TPU v7x, 512 devices: a whole 4x8x8 slice. The times are simulated.
512 devices in a mesh: ctx: 128 (over z_lo, y, x, core), tp: 4 (over z_hi).
Axes of the slice: x: 4, y: 8, z: 8 (z_hi: 4, z_lo: 2; z = z_hi * 2 + z_lo), core: 2. Of those that a mesh axis runs over, the one named last changes fastest.
Arguments:
- activations: bfloat16 [16384, 4096], P('ctx', 'tp'), may hold values from -6 to 6
- gradients: bfloat16 [16384, 4096], P('ctx', 'tp'), may hold values from -6 to 6
- basis_act: bfloat16 [4096, 2048], P('ctx', 'tp'), may hold values from -0.09375 to 0.09375
- basis_grad: bfloat16 [4096, 2048], P('ctx', 'tp'), may hold values from -0.09375 to 0.09375
- lengths: int32 [2], replicated, may hold values from 1024 to 8192, as said below
Outputs:
- eigenvalues: float32 [2048, 2048], P('ctx', 'tp')
Inputs may be any that keep to these rules, and one draw needn't show every extreme that they name: `lengths`: one sequence uses all 8192 slots in every draw.
All inputs are finite; a program needn't handle non-finite values.
Results may differ from a plain program's by a relative error of at most 0.0041.
Values may be sent and summed in bfloat16 or wider, within the bound.
No kernel may reach another device: no remote copies, remote signals or barrier semaphores. Data moves between devices by JAX's collectives and lax.ppermute only.
A program may use at most 64 MiB of HBM per device.

v0:
```python
import jax
import jax.numpy as jnp
from jax import lax
from jax.sharding import PartitionSpec as P

SEQS = 2


def add_rows(left, piece):
    return jnp.dot(left, piece, preferred_element_type=jnp.float32)


def on_device(activations, gradients, basis_act, basis_grad, lengths):
    full_act, full_grad = (
        lax.all_gather(activations, "tp", axis=1, tiled=True),
        lax.all_gather(gradients, "tp", axis=1, tiled=True),
    )
    tok_rows = full_act.shape[0]
    n_ctx = lax.axis_size("ctx")
    my_index = lax.axis_index("ctx")
    seq_len = tok_rows * n_ctx // SEQS
    slots = my_index * tok_rows + jnp.arange(tok_rows, dtype=jnp.int32)
    seq_index = slots // seq_len
    position = slots % seq_len
    seq_lengths = jnp.sum(
        jnp.where(
            seq_index[:, None] == jnp.arange(SEQS, dtype=jnp.int32)[None, :], lengths[None, :], 0
        ),
        axis=1,
    )
    valid = position < seq_lengths
    act_sum = add_rows(full_act, lax.all_gather(basis_act, "ctx", axis=0, tiled=True))
    grad_sum = add_rows(full_grad, lax.all_gather(basis_grad, "ctx", axis=0, tiled=True))
    rot_act = jnp.where(valid[:, None], act_sum, jnp.float32(0.0)).astype(jnp.bfloat16)
    rot_grad = grad_sum.astype(jnp.bfloat16)
    wide_grad = lax.all_gather(rot_grad, "tp", axis=1, tiled=True)
    partial_value = lax.dot_general(
        wide_grad, rot_act, (((0,), (0,)), ((), ())), preferred_element_type=jnp.float32
    )
    scale = lengths.astype(jnp.float32)
    received = lax.all_to_all(
        partial_value[:, None, :], "ctx", split_axis=0, concat_axis=1, tiled=True
    )
    own_rows = received.shape[0]
    columns = received.shape[2]
    per_seq = jnp.sum(received.reshape(own_rows, SEQS, n_ctx // SEQS, columns), axis=2)
    squared = per_seq * per_seq / scale[None, :, None]
    return jnp.sum(squared, axis=1) / jnp.float32(SEQS)


def solution(mesh):
    in_specs = (P("ctx", "tp"), P("ctx", "tp"), P("ctx", "tp"), P("ctx", "tp"), P())
    out_specs = P("ctx", "tp")
    return jax.shard_map(
        on_device, mesh=mesh, in_specs=in_specs, out_specs=out_specs, check_vma=False
    )
```

profile of v0, /device:TPU:1, one launch (start us, length us, event | category | flops | bytes accessed | tf_op | source)
XLA Modules:
  0.0 664.0 jit_solution(14674458826835503230)
XLA Ops:
  6.5 0.0 all-gather.5.cloned.1.call-start
  6.5 0.7 all-gather.5.cloned.1.call-update
  7.3 0.0 all-gather.7.cloned.1.call-start
  7.3 0.7 all-gather.7.cloned.1.call-update
  8.0 0.0 all-gather.9.cloned.1.call-start
  8.1 0.7 all-gather.9.cloned.1.call-update
  8.7 0.0 all-gather.11.cloned.1.call-start
  8.8 0.5 all-gather.11.cloned.1.call-update
  9.3 0.7 fusion.3
  10.1 41.7 %all-gather.5.cloned.1.call-done = bf16[128,4096]{1,0:T(8,128)(2,1)} async-done(((bf16[128,1024]{1,0:T(8,128)(2,1)}), bf16[128,4096]{1,0:T(8,128)(2,1)}) %all-gather.5.cloned.1.call-update) | async-done | bytes 1048592 | tf_op jit(solution)/shard_map/all_gather | solution.py:16
  51.8 218.5 %all-gather.7.cloned.1.call-done = bf16[4096,512]{1,0:T(8,128)(2,1)} async-done(((bf16[32,512]{1,0:T(8,128)(2,1)}), bf16[4096,512]{1,0:T(8,128)(2,1)}) %all-gather.7.cloned.1.call-update) | async-done | bytes 4194320 | tf_op jit(solution)/shard_map/all_gather | solution.py:33
  270.4 3.2 convolution_convert_fusion
  273.6 16.1 %all_gather.17 = bf16[128,2048]{1,0:T(8,128)(2,1)S(1)} all-gather(bf16[128,512]{1,0:T(8,128)(2,1)S(1)} %convolution_convert_fusion), channel_id=1, replica_groups=mesh['ctx'=128,'tp'=4] {'tp'}, dimensions={1}, use_global_device_ids=true | all-gather | bytes 655360 | tf_op jit(solution)/shard_map/all_gather | solution.py:36
  289.7 20.7 %all-gather.9.cloned.1.call-done = bf16[128,4096]{1,0:T(8,128)(2,1)} async-done(((bf16[128,1024]{1,0:T(8,128)(2,1)}), bf16[128,4096]{1,0:T(8,128)(2,1)}) %all-gather.9.cloned.1.call-update) | async-done | bytes 1048592 | tf_op jit(solution)/shard_map/all_gather | solution.py:15
  310.4 218.1 %all-gather.11.cloned.1.call-done = bf16[4096,512]{1,0:T(8,128)(2,1)} async-done(((bf16[32,512]{1,0:T(8,128)(2,1)}), bf16[4096,512]{1,0:T(8,128)(2,1)}) %all-gather.11.cloned.1.call-update) | async-done | bytes 4194320 | tf_op jit(solution)/shard_map/all_gather | solution.py:32
  528.5 5.9 convolution_bitcast_fusion
  534.4 8.4 %copy.7 = f32[2048,1,512]{2,1,0:T(1,128)} copy(f32[2048,1,512]{2,0,1:T(8,128)} %convolution_bitcast_fusion) | data formatting | bytes 8388608 | tf_op jit(solution)/shard_map/broadcast_in_dim | solution.py:42
  542.8 0.0 copy-start
  542.8 13.2 %all-to-all-start = ((f32[2048,1,512]{2,1,0:T(1,128)}), f32[2048,1,512]{2,1,0:T(1,128)}, u32[]{:S(2)}, u32[]{:S(2)}) async-start(f32[2048,1,512]{2,1,0:T(1,128)} %copy.7), calls=%async_computation | async-start | bytes 8388608 | tf_op jit(solution)/shard_map/all_to_all | solution.py:41
  556.0 0.0 copy-done
  556.0 97.7 %all-to-all-done = f32[2048,1,512]{2,1,0:T(1,128)} async-done(((f32[2048,1,512]{2,1,0:T(1,128)}), f32[2048,1,512]{2,1,0:T(1,128)}, u32[]{:S(2)}, u32[]{:S(2)}) %all-to-all-start) | async-done | bytes 4194336 | tf_op jit(solution)/shard_map/all_to_all | solution.py:41
  653.7 2.7 copy.8
  656.5 0.3 bitcast_reduce_fusion
  656.8 0.1 divide_reduce_fusion
  656.9 0.6 broadcast_multiply_fusion
  (3 shorter events, 0.0 us)
Async XLA Ops:
  6.5 45.3 %all-gather.5.cloned.1.call-start = ((), (), s32[]{:S(2)}) async-start(), calls=%async_computation.1 | async-start | bytes 1310720 | tf_op jit(solution)/shard_map/all_gather | solution.py:16
  7.3 263.1 %all-gather.7.cloned.1.call-start = ((), (), s32[]{:S(2)}) async-start(), calls=%async_computation.2 | async-start | bytes 4227072 | tf_op jit(solution)/shard_map/all_gather | solution.py:33
  8.0 302.4 %all-gather.9.cloned.1.call-start = ((), (), s32[]{:S(2)}) async-start(), calls=%async_computation.3 | async-start | bytes 1310720 | tf_op jit(solution)/shard_map/all_gather | solution.py:15
  8.7 519.7 %all-gather.11.cloned.1.call-start = ((), (), s32[]{:S(2)}) async-start(), calls=%async_computation.4 | async-start | bytes 4227072 | tf_op jit(solution)/shard_map/all_gather | solution.py:32
  542.8 13.2 %copy-start = (s32[2]{0:T(128)S(1)}, s32[2]{0:T(128)}, u32[]{:S(2)}) copy-start(s32[2]{0:T(128)} %param.9) | copy-start | bytes 28
  542.8 111.0 %all-to-all-start = ((f32[2048,1,512]{2,1,0:T(1,128)}), f32[2048,1,512]{2,1,0:T(1,128)}, u32[]{:S(2)}, u32[]{:S(2)}) async-start(f32[2048,1,512]{2,1,0:T(1,128)} %copy.7), calls=%async_computation | async-start | bytes 8388608 | tf_op jit(solution)/shard_map/all_to_all | solution.py:41
Sparse Core Ops, SparseCore 0:
  9.5 42.3 all-gather.4
  54.0 216.3 all-gather.6
  272.5 37.9 all-gather.8
  312.4 216.0 all-gather.10
where the time goes:
time: 664 us
  waiting for transfers between devices  599 us (90%)
  blocking collectives  16.1 us (2%)
  starting transfers between devices  13.3 us (2%)
  between operations  13.2 us (2%)
  local copies, waits for them, and re-layouts  11.2 us (2%)
  matrix products  9.12 us (1%)
    all_gather x1, waiting for transfers between devices, on_device(): lax.all_gather(basis_grad, 'ctx', axis=0, tiled=True)  219 us
    all_gather x1, waiting for transfers between devices, on_device(): lax.all_gather(basis_act, 'ctx', axis=0, tiled=True)  218 us
    all_to_all x1, waiting for transfers between devices, on_device(): lax.all_to_all(partial_value[:, None, :], 'ctx', split_axis=0, concat_axi...  97.7 us
    all_gather x1, waiting for transfers between devices, on_device(): lax.all_gather(gradients, 'tp', axis=1, tiled=True)  41.7 us
    all_gather x1, waiting for transfers between devices, on_device(): lax.all_gather(activations, 'tp', axis=1, tiled=True)  20.7 us
    all_gather x1, blocking collectives, on_device(): wide_grad = lax.all_gather(rot_grad, 'tp', axis=1, tiled=True)  16.1 us
  transfers between devices with their start and end apart: 5, of which 5 were waited for; matrix products, arithmetic and copies ran while one was open for 1% of the time, Pallas kernels for 0%

commit v1 on v0

v1 whole, which is shorter than its diff:
```python
import jax
import jax.numpy as jnp
from jax import lax
from jax.sharding import Mesh
from jax.sharding import PartitionSpec as P

SEQS = 2
F32 = jnp.float32
BF16 = jnp.bfloat16


def gather(value, axes, count):
    copies = jnp.broadcast_to(value[None], (count, *value.shape))
    return lax.all_to_all(copies, axes, 0, 0, tiled=True)


def on_device(activations, gradients, basis_act, basis_grad, lengths):
    n_zl, n_y, n_x, n_c, n_zh = (lax.axis_size(a) for a in ("zl", "y", "x", "c", "zh"))
    n_xc, y_lo = n_x * n_c, n_y // 2
    toks, feats = activations.shape
    rows, cols = basis_act.shape
    part = cols // n_xc

    tokens = lax.all_gather(
        jnp.concatenate([activations, gradients], axis=1), ("x", "c"), axis=0, tiled=True
    )

    piece_act = basis_act.reshape(rows, n_c, n_x, part).transpose(2, 1, 0, 3)
    lines = cols // (y_lo * n_xc)
    piece_grad = basis_grad.reshape(rows, y_lo, n_x, n_c, lines).transpose(2, 3, 0, 1, 4)
    pieces = jnp.concatenate([piece_act, piece_grad.reshape(n_x, n_c, rows, part)], axis=3)
    swap = []
    for q in range(n_zh):
        for y in range(y_lo):
            for zh in range(n_zh):
                swap.append((((q * y_lo) + y) * n_zh + zh, ((zh * y_lo) + y) * n_zh + q))
    pieces = lax.ppermute(pieces, ("zl", "y", "zh"), swap)
    pieces = jnp.broadcast_to(
        pieces.reshape(1, n_xc, rows, 2 * part), (n_zl * n_y, n_xc, rows, 2 * part)
    ).reshape(n_zl * n_y * n_xc, rows, 2 * part)
    basis = lax.all_to_all(pieces, ("zl", "y", "x", "c"), 0, 0, tiled=True)
    basis = basis.reshape(n_zh, y_lo * n_xc * rows, 2 * part)

    act = jnp.einsum("kfj,tf->kjt", basis, tokens[:, :feats], preferred_element_type=F32)
    grad = jnp.einsum("kfj,tf->kjt", basis, tokens[:, feats:], preferred_element_type=F32)
    partial = jnp.concatenate([act[:, :part], grad[:, part:]], axis=1)
    partial = lax.all_to_all(partial, "zh", 0, 0, tiled=True)
    rotated = jnp.sum(partial, axis=0)
    group = toks * n_xc
    position = lax.axis_index("y") * group + jnp.arange(group, dtype=jnp.int32)
    length = jnp.where(lax.axis_index("zl") == 0, lengths[0], lengths[1])
    valid = position < length
    rot_act = jnp.where(valid[None, :], rotated[:part], F32(0.0)).astype(BF16)
    rot_grad = rotated[part:].astype(BF16)

    wide_grad = lax.all_gather(rot_grad, "zh", axis=0, tiled=True)
    wide_act = lax.all_gather(rot_act, "x", axis=0, tiled=True)
    wide_act = gather(wide_act, "c", n_c).reshape(cols, group)
    share = lax.dot_general(
        wide_grad, wide_act, (((1,), (1,)), ((), ())), preferred_element_type=F32
    )
    share = share.astype(BF16).reshape(n_zl * n_y, -1, cols)
    received = lax.all_to_all(share, ("zl", "y"), 0, 0, tiled=True)
    received = received.astype(F32).reshape(SEQS, n_y, -1, cols)
    per_seq = jnp.sum(received, axis=1)
    scale = lengths.astype(F32)[:, None, None]
    return jnp.sum(per_seq * per_seq / scale, axis=0) / F32(SEQS)


def solution(mesh):
    split = Mesh(mesh.devices.reshape(2, 8, 4, 2, 4), ("zl", "y", "x", "c", "zh"))
    spec = P(("zl", "y", "x", "c"), "zh")
    return jax.shard_map(
        on_device, mesh=split, in_specs=(spec, spec, spec, spec, P()), out_specs=spec, check_vma=False
    )
```

time: 664 us -> 190 us (0.29)
  waiting for transfers between devices: 599 us -> 54.2 us
  blocking collectives: 16.1 us -> 86.6 us
  local copies, waits for them, and re-layouts: 11.2 us -> 3.02 us
    all_gather x4 -> x1, waiting for transfers between devices: 499 us -> 0.01 us  [on_device(): lax.all_gather(jnp.concatenate([activations, gradients], axis=1), ('x', '...]
    all_to_all x0 -> x1, blocking collectives: none -> 59.5 us  [on_device(): basis = lax.all_to_all(pieces, ('zl', 'y', 'x', 'c'), 0, 0, tiled=True)]
    all_to_all x1 -> x3, waiting for transfers between devices: 97.7 us -> 54.2 us  [the longest x1 46.5 us: on_device(): partial = lax.all_to_all(partial, 'zh', 0, 0, tiled=True)]
    all_gather x1 -> x2, blocking collectives: 16.1 us -> 27.1 us  [the longest x1 17.2 us: on_device(): wide_grad = lax.all_gather(rot_grad, 'zh', axis=0, tiled=True)]
    broadcast_in_dim x1 -> x2, local copies, waits for them, and re-layouts: 8.42 us -> 1.29 us  [the longest x1 1.1 us: gather(): copies = jnp.broadcast_to(value[None], (count, *value.shape))]
    all_to_all x1 -> x3, starting transfers between devices: 13.2 us -> 17.8 us  [the longest x1 7.51 us: gather(): return lax.all_to_all(copies, axes, 0, 0, tiled=True)]
  transfers between devices with their start and end apart: 5 -> 5, of which waited for: 5 -> 2; matrix products, arithmetic and copies ran while one was open for 1% -> 1% of each run, Pallas kernels for 0% -> 0%
where the time goes in v1:
time: 190 us; the launch traced here: 187 us
  blocking collectives  86.6 us (46%)
  waiting for transfers between devices  54.2 us (29%)
  starting transfers between devices  18.5 us (10%)
  between operations  14.8 us (8%)
  matrix products  5.87 us (3%)
  other arithmetic  4.44 us (2%)
  local copies, waits for them, and re-layouts  3.02 us (2%)
    all_to_all x1, blocking collectives, on_device(): basis = lax.all_to_all(pieces, ('zl', 'y', 'x', 'c'), 0, 0, tiled=True)  59.5 us
    all_to_all x1, waiting for transfers between devices, on_device(): partial = lax.all_to_all(partial, 'zh', 0, 0, tiled=True)  46.5 us
    all_gather x1, blocking collectives, on_device(): wide_grad = lax.all_gather(rot_grad, 'zh', axis=0, tiled=True)  17.2 us
    all_gather x1, blocking collectives, on_device(): wide_act = lax.all_gather(rot_act, 'x', axis=0, tiled=True)  9.9 us
    all_to_all x1, waiting for transfers between devices, on_device(): received = lax.all_to_all(share, ('zl', 'y'), 0, 0, tiled=True)  7.72 us
    all_to_all x1, starting transfers between devices, gather(): return lax.all_to_all(copies, axes, 0, 0, tiled=True)  7.51 us
    all_to_all x1, starting transfers between devices, on_device(): partial = lax.all_to_all(partial, 'zh', 0, 0, tiled=True)  6.78 us
  transfers between devices with their start and end apart: 5, of which 2 were waited for; matrix products, arithmetic and copies ran while one was open for 1% of the time, Pallas kernels for 0%

profile of v1, /device:TPU:1, one launch (start us, length us, event | category | flops | bytes accessed | tf_op | source)
XLA Modules:
  0.0 187.4 jit_solution(12353754927308030802)
XLA Ops:
  6.5 0.0 copy-start
  6.5 0.0 all-gather.2.cloned.1.call-start
  6.5 1.9 %pad_maximum_fusion.1 = bf16[128,2048]{1,0:T(8,128)(2,1)} fusion(bf16[128,1024]{1,0:T(8,128)(2,1)} %param.6, bf16[128,1024]{1,0:T(8,128)(2,1)} %param.5), kind=kLoop, calls=%fused_computation.8 | loop fusion | flops 1048576 | bytes 1048576 | tf_op jit(solution)/shard_map/concatenate | solution.py:25
  8.4 0.0 all-gather.2.cloned.1.call-update
  8.4 0.9 copy.17
  9.3 0.1 copy.19
  9.5 0.0 copy-done
  9.5 0.1 reshape.36
  9.6 0.1 pad_maximum_fusion.2
  9.7 0.7 collective-permute-start
  10.4 0.0 collective-permute-done
  10.4 0.2 broadcast_in_dim.28
  10.6 59.5 %all_to_all.20 = bf16[128,32,128]{2,1,0:T(8,128)(2,1)S(1)} all-to-all(bf16[128,32,128]{2,1,0:T(8,128)(2,1)S(1)} %bitcast.24), channel_id=1, replica_groups=mesh['zl'=2,'y'=8,'x'=4,'c'=2,'zh'=4] {'zl','y','x','c'}, dimensions={0} | all-to-all | bytes 2097152 | tf_op jit(solution)/shard_map/all_to_all | solution.py:41
  70.1 3.3 %fusion = f32[4,64,1024]{2,1,0:T(8,128)S(1)} fusion(bf16[1024,2048]{1,0:T(8,128)(2,1)} %all-gather.2.cloned.1.call-done, bf16[4,1024,128]{2,1,0:T(8,128)(2,1)S(1)} %bitcast.25), kind=kOutput, calls=%fused_computation.1 | convolution fusion | flops 536870912 | bytes 4194304 | tf_op jit(solution)/shard_map/kfj,tf->kjt/dot_general | solution.py:45
  73.4 0.0 copy-done.2
  73.4 1.3 fusion.1
  74.8 1.5 pad_maximum_fusion
  76.3 6.8 %all-to-all-start.1 = ((f32[4,128,1024]{2,1,0:T(8,128)}), f32[4,128,1024]{2,1,0:T(8,128)S(1)}, u32[]{:S(2)}, u32[]{:S(2)}) async-start(f32[4,128,1024]{2,1,0:T(8,128)} %pad_maximum_fusion), calls=%async_computation.1 | async-start | bytes 4194304 | tf_op jit(solution)/shard_map/all_to_all | solution.py:47
  83.1 0.0 copy-done.1
  83.1 0.6 fusion.5
  85.0 46.5 %all-to-all-done.1 = f32[4,128,1024]{2,1,0:T(8,128)S(1)} async-done(((f32[4,128,1024]{2,1,0:T(8,128)}), f32[4,128,1024]{2,1,0:T(8,128)S(1)}, u32[]{:S(2)}, u32[]{:S(2)}) %all-to-all-start.1) | async-done | bytes 2097184 | tf_op jit(solution)/shard_map/all_to_all | solution.py:47
  131.5 0.2 reduce_sum.27
  131.7 9.9 %all_gather.11 = bf16[256,1024]{1,0:T(8,128)(2,1)S(1)} all-gather(bf16[64,1024]{1,0:T(8,128)(2,1)S(1)} %get-tuple-element.5), channel_id=1, replica_groups=mesh['zl'=2,'y'=8,'x'=4,'c'=2,'zh'=4] {'x'}, dimensions={0}, use_global_device_ids=true | all-gather | bytes 655360 | tf_op jit(solution)/shard_map/all_gather | solution.py:57
  141.6 1.1 broadcast_in_dim.31
  142.7 7.5 %all-to-all-start.2 = ((bf16[2,256,1024]{2,1,0:T(8,128)(2,1)}), bf16[2,256,1024]{2,1,0:T(8,128)(2,1)S(1)}, u32[]{:S(2)}, u32[]{:S(2)}) async-start(bf16[2,256,1024]{2,1,0:T(8,128)(2,1)} %broadcast_in_dim.31), calls=%async_computation.2 | async-start | bytes 2097152 | tf_op jit(solution)/shard_map/all_to_all | solution.py:14
  150.2 17.2 %all_gather.10 = bf16[256,1024]{1,0:T(8,128)(2,1)S(1)} all-gather(bf16[64,1024]{1,0:T(8,128)(2,1)S(1)} %get-tuple-element.6), channel_id=1, replica_groups=mesh['zl'=2,'y'=8,'x'=4,'c'=2,'zh'=4] {'zh'}, dimensions={0}, use_global_device_ids=true | all-gather | bytes 655360 | tf_op jit(solution)/shard_map/all_gather | solution.py:56
  167.4 0.0 all-to-all-done.2
  167.4 1.2 convolution_convert_fusion
  168.6 3.5 %all-to-all-start.3 = ((bf16[16,16,512]{2,1,0:T(8,128)(2,1)}), bf16[16,16,512]{2,1,0:T(8,128)(2,1)S(1)}, u32[]{:S(2)}, u32[]{:S(2)}) async-start(bf16[16,16,512]{2,1,0:T(8,128)(2,1)} %bitcast.12), calls=%async_computation.3 | async-start | bytes 524288 | tf_op jit(solution)/shard_map/all_to_all | solution.py:63
  172.1 7.7 %all-to-all-done.3 = bf16[16,16,512]{2,1,0:T(8,128)(2,1)S(1)} async-done(((bf16[16,16,512]{2,1,0:T(8,128)(2,1)}), bf16[16,16,512]{2,1,0:T(8,128)(2,1)S(1)}, u32[]{:S(2)}, u32[]{:S(2)}) %all-to-all-start.3) | async-done | bytes 262176 | tf_op jit(solution)/shard_map/all_to_all | solution.py:63
  179.9 0.1 divide_reduce_fusion
  180.0 0.6 broadcast_multiply_fusion
  (9 shorter events, 0.1 us)
Async XLA Ops:
  6.5 2.9 %copy-start = (bf16[32,512]{1,0:T(8,128)(2,1)S(1)}, bf16[32,512]{1,0:T(8,128)(2,1)}, u32[]{:S(2)}) copy-start(bf16[32,512]{1,0:T(8,128)(2,1)} %param.7) | copy-start | bytes 98308
  6.5 63.5 %all-gather.2.cloned.1.call-start = ((), (), s32[]{:S(2)}) async-start(), calls=%async_computation.4 | async-start | bytes 4718592 | tf_op jit(solution)/shard_map/all_gather | solution.py:24
  9.7 0.7 collective-permute-start
  70.1 3.3 %copy-start.2 = (bf16[1024,2048]{1,0:T(8,128)(2,1)S(1)}, bf16[1024,2048]{1,0:T(8,128)(2,1)}, u32[]{:S(2)}) copy-start(bf16[1024,2048]{1,0:T(8,128)(2,1)} %all-gather.2.cloned.1.call-done) | copy-start | bytes 12582916
  76.3 6.8 %copy-start.1 = (s32[2]{0:T(128)S(1)}, s32[2]{0:T(128)}, u32[]{:S(2)}) copy-start(s32[2]{0:T(128)} %param.9) | copy-start | bytes 28
  76.3 55.2 %all-to-all-start.1 = ((f32[4,128,1024]{2,1,0:T(8,128)}), f32[4,128,1024]{2,1,0:T(8,128)S(1)}, u32[]{:S(2)}, u32[]{:S(2)}) async-start(f32[4,128,1024]{2,1,0:T(8,128)} %pad_maximum_fusion), calls=%async_computation.1 | async-start | bytes 4194304 | tf_op jit(solution)/shard_map/all_to_all | solution.py:47
  142.7 24.7 %all-to-all-start.2 = ((bf16[2,256,1024]{2,1,0:T(8,128)(2,1)}), bf16[2,256,1024]{2,1,0:T(8,128)(2,1)S(1)}, u32[]{:S(2)}, u32[]{:S(2)}) async-start(bf16[2,256,1024]{2,1,0:T(8,128)(2,1)} %broadcast_in_dim.31), calls=%async_computation.2 | async-start | bytes 2097152 | tf_op jit(solution)/shard_map/all_to_all | solution.py:14
  168.6 11.3 %all-to-all-start.3 = ((bf16[16,16,512]{2,1,0:T(8,128)(2,1)}), bf16[16,16,512]{2,1,0:T(8,128)(2,1)S(1)}, u32[]{:S(2)}, u32[]{:S(2)}) async-start(bf16[16,16,512]{2,1,0:T(8,128)(2,1)} %bitcast.12), calls=%async_computation.3 | async-start | bytes 524288 | tf_op jit(solution)/shard_map/all_to_all | solution.py:63
Sparse Core Ops, SparseCore 0:
  9.5 49.9 all-gather.1

commit v2 on v1

--- a/solution.py
+++ b/solution.py
@@ -7,11 +7,9 @@
 SEQS = 2
 F32 = jnp.float32
 BF16 = jnp.bfloat16
-
-
-def gather(value, axes, count):
-    copies = jnp.broadcast_to(value[None], (count, *value.shape))
-    return lax.all_to_all(copies, axes, 0, 0, tiled=True)
+F16 = jnp.float16
+TILE = 16
+TOP = 15
 
 
 def on_device(activations, gradients, basis_act, basis_grad, lengths):
@@ -25,7 +23,7 @@
         jnp.concatenate([activations, gradients], axis=1), ("x", "c"), axis=0, tiled=True
     )
 
-    piece_act = basis_act.reshape(rows, n_c, n_x, part).transpose(2, 1, 0, 3)
+    piece_act = basis_act.reshape(rows, n_x, n_c, part).transpose(1, 2, 0, 3)
     lines = cols // (y_lo * n_xc)
     piece_grad = basis_grad.reshape(rows, y_lo, n_x, n_c, lines).transpose(2, 3, 0, 1, 4)
     pieces = jnp.concatenate([piece_act, piece_grad.reshape(n_x, n_c, rows, part)], axis=3)
@@ -43,10 +41,22 @@
 
     act = jnp.einsum("kfj,tf->kjt", basis, tokens[:, :feats], preferred_element_type=F32)
     grad = jnp.einsum("kfj,tf->kjt", basis, tokens[:, feats:], preferred_element_type=F32)
-    partial = jnp.concatenate([act[:, :part], grad[:, part:]], axis=1)
-    partial = lax.all_to_all(partial, "zh", 0, 0, tiled=True)
-    rotated = jnp.sum(partial, axis=0)
     group = toks * n_xc
+    act, grad = act[:, :part], grad[:, part:]
+    largest = jnp.maximum(jnp.max(jnp.abs(act)), jnp.max(jnp.abs(grad)))
+    level = jnp.clip(jnp.ceil(jnp.log2(jnp.maximum(largest, F32(1e-30)))), -100.0, 100.0)
+    factor = jnp.exp2(F32(TOP) - level)
+    partial = jnp.concatenate(
+        [
+            (act * factor).astype(F16),
+            (grad * factor).astype(F16),
+            jnp.full((n_zh, TILE, group), level, F32).astype(F16),
+        ],
+        axis=1,
+    )
+    partial = lax.all_to_all(partial, "zh", 0, 0, tiled=True).astype(F32)
+    factors = jnp.exp2(partial[:, -TILE:, :] - F32(TOP))[:, :1, :1]
+    rotated = jnp.sum(partial[:, :-TILE] * factors, axis=0)
     position = lax.axis_index("y") * group + jnp.arange(group, dtype=jnp.int32)
     length = jnp.where(lax.axis_index("zl") == 0, lengths[0], lengths[1])
     valid = position < length
@@ -54,8 +64,7 @@
     rot_grad = rotated[part:].astype(BF16)
 
     wide_grad = lax.all_gather(rot_grad, "zh", axis=0, tiled=True)
-    wide_act = lax.all_gather(rot_act, "x", axis=0, tiled=True)
-    wide_act = gather(wide_act, "c", n_c).reshape(cols, group)
+    wide_act = lax.all_gather(rot_act, ("x", "c"), axis=0, tiled=True)
     share = lax.dot_general(
         wide_grad, wide_act, (((1,), (1,)), ((), ())), preferred_element_type=F32
     )

time: 190 us -> 166 us (0.87)
  waiting for transfers between devices: 54.2 us -> 41.6 us
  blocking collectives: 86.6 us -> 75.4 us
  starting transfers between devices: 18.5 us -> 15 us
  matrix products: 5.87 us -> 8.43 us
    all_to_all x2 -> x1, waiting for transfers between devices: 46.5 us -> 26.9 us  [on_device(): partial = lax.all_to_all(partial, 'zh', 0, 0, tiled=True).astype(F32)]
    all_gather x1 -> x0, blocking collectives: 9.9 us -> none  [on_device(): wide_act = lax.all_gather(rot_act, 'x', axis=0, tiled=True)]
    all_to_all x2 -> x1, starting transfers between devices: 14.3 us -> 6.65 us  [on_device(): partial = lax.all_to_all(partial, 'zh', 0, 0, tiled=True).astype(F32)]
    all_gather x0 -> x1, waiting for transfers between devices: none -> 5.66 us  [on_device(): wide_act = lax.all_gather(rot_act, ('x', 'c'), axis=0, tiled=True)]
    all_to_all x1, starting transfers between devices: 3.53 us -> 7.64 us  [on_device(): received = lax.all_to_all(share, ('zl', 'y'), 0, 0, tiled=True)]
  transfers between devices with their start and end apart: 5 -> 5, of which waited for: 2 -> 3; matrix products, arithmetic and copies ran while one was open for 1% -> 1% of each run, Pallas kernels for 0% -> 0%
where the time goes in v2:
time: 166 us; the launch traced here: 164 us
  blocking collectives  75.4 us (45%)
  waiting for transfers between devices  41.6 us (25%)
  between operations  16.2 us (10%)
  starting transfers between devices  15 us (9%)
  matrix products  8.43 us (5%)
  other arithmetic  5.68 us (3%)
  local copies, waits for them, and re-layouts  1.94 us (1%)
    all_to_all x1, blocking collectives, on_device(): basis = lax.all_to_all(pieces, ('zl', 'y', 'x', 'c'), 0, 0, tiled=True)  59.5 us
    all_to_all x1, waiting for transfers between devices, on_device(): partial = lax.all_to_all(partial, 'zh', 0, 0, tiled=True).astype(F32)  26.9 us
    all_gather x1, blocking collectives, on_device(): wide_grad = lax.all_gather(rot_grad, 'zh', axis=0, tiled=True)  16 us
    all_to_all x1, waiting for transfers between devices, on_device(): received = lax.all_to_all(share, ('zl', 'y'), 0, 0, tiled=True)  9.02 us
    all_to_all x1, starting transfers between devices, on_device(): received = lax.all_to_all(share, ('zl', 'y'), 0, 0, tiled=True)  7.64 us
    all_to_all x1, starting transfers between devices, on_device(): partial = lax.all_to_all(partial, 'zh', 0, 0, tiled=True).astype(F32)  6.65 us
    all_gather x1, waiting for transfers between devices, on_device(): wide_act = lax.all_gather(rot_act, ('x', 'c'), axis=0, tiled=True)  5.66 us
    dot_general x1, matrix products, on_device(): jnp.einsum('kfj,tf->kjt', basis, tokens[:, feats:], preferred_element_typ...  3.94 us
  transfers between devices with their start and end apart: 5, of which 3 were waited for; matrix products, arithmetic and copies ran while one was open for 1% of the time, Pallas kernels for 0%

profile of v2, /device:TPU:1, one launch (start us, length us, event | category | flops | bytes accessed | tf_op | source)
XLA Modules:
  0.0 164.2 jit_solution(14997250918237767134)
XLA Ops:
  6.5 0.0 all-gather.3.cloned.1.call-start
  6.5 1.9 %pad_maximum_fusion = bf16[128,2048]{1,0:T(8,128)(2,1)} fusion(bf16[128,1024]{1,0:T(8,128)(2,1)} %param.6, bf16[128,1024]{1,0:T(8,128)(2,1)} %param.5), kind=kLoop, calls=%fused_computation.14 | loop fusion | flops 1048576 | bytes 1048576 | tf_op jit(solution)/shard_map/concatenate | solution.py:23
  8.4 0.0 all-gather.3.cloned.1.call-update
  8.4 0.9 copy.24
  9.3 0.1 copy.27
  9.5 0.0 copy-done
  9.5 0.1 reshape.32
  9.6 0.1 pad_maximum_fusion.1
  9.7 0.7 collective-permute-start
  10.4 0.0 collective-permute-done
  10.4 0.2 broadcast_in_dim.25
  10.6 59.5 %all_to_all.15 = bf16[128,32,128]{2,1,0:T(8,128)(2,1)S(1)} all-to-all(bf16[128,32,128]{2,1,0:T(8,128)(2,1)S(1)} %bitcast.26), channel_id=1, replica_groups=mesh['zl'=2,'y'=8,'x'=4,'c'=2,'zh'=4] {'zl','y','x','c'}, dimensions={0} | all-to-all | bytes 2097152 | tf_op jit(solution)/shard_map/all_to_all | solution.py:39
  70.0 3.9 %abs_reduce_fusion = (f32[]{:T(128)}, f32[4,64,1024]{2,1,0:T(8,128)S(1)}) fusion(bf16[1024,2048]{1,0:T(8,128)(2,1)} %all-gather.3.cloned.1.call-done, bf16[4,1024,128]{2,1,0:T(8,128)(2,1)S(1)} %bitcast.27), kind=kOutput, calls=%fused_computation.12 | convolution fusion | flops 537395200 | bytes 4194308 | tf_op jit(solution)/shard_map/kfj,tf->kjt/dot_general | solution.py:43
  74.0 2.0 %abs_reduce_fusion.1 = (f32[]{:T(128)}, f32[4,64,1024]{2,1,0:T(8,128)S(1)}) fusion(bf16[1024,2048]{1,0:T(8,128)(2,1)S(1)} %copy-done.2, bf16[4,1024,128]{2,1,0:T(8,128)(2,1)S(1)} %bitcast.28), kind=kOutput, calls=%fused_computation.13 | convolution fusion | flops 537395200 | bytes 4194308 | tf_op jit(solution)/shard_map/kfj,tf->kjt/dot_general | solution.py:42
  77.4 0.3 multiply_convert_fusion
  77.7 0.0 copy-start.1
  77.7 1.4 maximum_maximum_fusion
  79.1 6.7 %all-to-all-start.1 = ((f16[4,144,1024]{2,1,0:T(8,128)(2,1)}), f16[4,144,1024]{2,1,0:T(8,128)(2,1)S(1)}, u32[]{:S(2)}, u32[]{:S(2)}) async-start(f16[4,144,1024]{2,1,0:T(8,128)(2,1)} %maximum_maximum_fusion), calls=%async_computation.1 | async-start | bytes 2359296 | tf_op jit(solution)/shard_map/all_to_all | solution.py:57
  85.7 0.6 fusion.9
  87.6 26.9 %all-to-all-done.1 = f16[4,144,1024]{2,1,0:T(8,128)(2,1)S(1)} async-done(((f16[4,144,1024]{2,1,0:T(8,128)(2,1)}), f16[4,144,1024]{2,1,0:T(8,128)(2,1)S(1)}, u32[]{:S(2)}, u32[]{:S(2)}) %all-to-all-start.1) | async-done | bytes 1179680 | tf_op jit(solution)/shard_map/all_to_all | solution.py:57
  114.5 0.2 convert_element_type.27
  114.7 0.1 fusion.8
  114.8 0.3 fusion
  115.1 0.7 fusion.5
  115.8 0.0 all-gather.5.cloned.1.call-update
  115.8 16.0 %all_gather.10 = bf16[256,1024]{1,0:T(8,128)(2,1)S(1)} all-gather(bf16[64,1024]{1,0:T(8,128)(2,1)S(1)} %get-tuple-element.6), channel_id=1, replica_groups=mesh['zl'=2,'y'=8,'x'=4,'c'=2,'zh'=4] {'zh'}, dimensions={0}, use_global_device_ids=true | all-gather | bytes 655360 | tf_op jit(solution)/shard_map/all_gather | solution.py:66
  131.8 5.7 %all-gather.5.cloned.1.call-done = bf16[512,1024]{1,0:T(8,128)(2,1)} async-done(((bf16[64,1024]{1,0:T(8,128)(2,1)}), bf16[512,1024]{1,0:T(8,128)(2,1)}) %all-gather.5.cloned.1.call-update) | async-done | bytes 1048592 | tf_op jit(solution)/shard_map/all_gather | solution.py:67
  137.5 2.5 %convolution_convert_fusion = bf16[256,512]{1,0:T(8,128)(2,1)} fusion(bf16[256,1024]{1,0:T(8,128)(2,1)S(1)} %all_gather.10, bf16[512,1024]{1,0:T(8,128)(2,1)} %all-gather.5.cloned.1.call-done), kind=kOutput, calls=%fused_computation.6 | convolution fusion | flops 268566528 | bytes 1835008 | tf_op jit(solution)/shard_map/dot_general | solution.py:68
  139.9 7.6 %all-to-all-start.2 = ((bf16[16,16,512]{2,1,0:T(8,128)(2,1)}), bf16[16,16,512]{2,1,0:T(8,128)(2,1)S(1)}, u32[]{:S(2)}, u32[]{:S(2)}) async-start(bf16[16,16,512]{2,1,0:T(8,128)(2,1)} %bitcast.11), calls=%async_computation.2 | async-start | bytes 524288 | tf_op jit(solution)/shard_map/all_to_all | solution.py:72
  147.6 9.0 %all-to-all-done.2 = bf16[16,16,512]{2,1,0:T(8,128)(2,1)S(1)} async-done(((bf16[16,16,512]{2,1,0:T(8,128)(2,1)}), bf16[16,16,512]{2,1,0:T(8,128)(2,1)S(1)}, u32[]{:S(2)}, u32[]{:S(2)}) %all-to-all-start.2) | async-done | bytes 262176 | tf_op jit(solution)/shard_map/all_to_all | solution.py:72
  156.7 0.1 divide_reduce_fusion
  156.8 0.6 broadcast_multiply_fusion
  (14 shorter events, 0.1 us)
Async XLA Ops:
  6.5 2.9 %copy-start = (bf16[32,512]{1,0:T(8,128)(2,1)S(1)}, bf16[32,512]{1,0:T(8,128)(2,1)}, u32[]{:S(2)}) copy-start(bf16[32,512]{1,0:T(8,128)(2,1)} %param.7) | copy-start | bytes 98308
  6.5 63.5 %all-gather.3.cloned.1.call-start = ((), (), s32[]{:S(2)}) async-start(), calls=%async_computation.3 | async-start | bytes 4718592 | tf_op jit(solution)/shard_map/all_gather | solution.py:22
  9.7 0.7 collective-permute-start
  70.0 3.9 %copy-start.2 = (bf16[1024,2048]{1,0:T(8,128)(2,1)S(1)}, bf16[1024,2048]{1,0:T(8,128)(2,1)}, u32[]{:S(2)}) copy-start(bf16[1024,2048]{1,0:T(8,128)(2,1)} %all-gather.3.cloned.1.call-done) | copy-start | bytes 12582916
  77.7 8.0 %copy-start.1 = (s32[2]{0:T(128)S(1)}, s32[2]{0:T(128)}, u32[]{:S(2)}) copy-start(s32[2]{0:T(128)} %param.9) | copy-start | bytes 28
  79.1 35.4 %all-to-all-start.1 = ((f16[4,144,1024]{2,1,0:T(8,128)(2,1)}), f16[4,144,1024]{2,1,0:T(8,128)(2,1)S(1)}, u32[]{:S(2)}, u32[]{:S(2)}) async-start(f16[4,144,1024]{2,1,0:T(8,128)(2,1)} %maximum_maximum_fusion), calls=%async_computation.1 | async-start | bytes 2359296 | tf_op jit(solution)/shard_map/all_to_all | solution.py:57
  85.7 51.8 %all-gather.5.cloned.1.call-start = ((), (), s32[]{:S(2)}) async-start(), calls=%async_computation.4 | async-start | bytes 1179648 | tf_op jit(solution)/shard_map/all_gather | solution.py:67
  139.9 16.7 %all-to-all-start.2 = ((bf16[16,16,512]{2,1,0:T(8,128)(2,1)}), bf16[16,16,512]{2,1,0:T(8,128)(2,1)S(1)}, u32[]{:S(2)}, u32[]{:S(2)}) async-start(bf16[16,16,512]{2,1,0:T(8,128)(2,1)} %bitcast.11), calls=%async_computation.2 | async-start | bytes 524288 | tf_op jit(solution)/shard_map/all_to_all | solution.py:72
Sparse Core Ops, SparseCore 0:
  9.5 50.2 all-gather.2
  116.0 21.4 all-gather.4

commit v3 on v1

v3 whole, which is shorter than its diff:
```python
import jax
import jax.numpy as jnp
from jax import lax
from jax.sharding import Mesh
from jax.sharding import PartitionSpec as P

SEQS = 2
F32 = jnp.float32
BF16 = jnp.bfloat16
F16 = jnp.float16
TILE = 16
TOP = 15


def exchange(value, axis, partner):
    return lax.ppermute(value, axis, [(i, partner(i)) for i in range(lax.axis_size(axis))])


def swap_if(condition, value, axis):
    low, high = jnp.split(value, 2, axis=axis)
    return jnp.where(condition, jnp.concatenate([high, low], axis=axis), value)


def on_device(activations, gradients, basis_act, basis_grad, lengths):
    n_zl, n_y, n_x, n_c, n_zh = (lax.axis_size(a) for a in ("zl", "y", "x", "c", "zh"))
    zl, y, x, c = (lax.axis_index(a) for a in ("zl", "y", "x", "c"))
    n_xc, y_lo = n_x * n_c, n_y // 2
    toks, feats = activations.shape
    rows, cols = basis_act.shape
    part = cols // n_xc
    group = toks * n_xc

    piece_act = basis_act.reshape(rows, n_c, n_x, part).transpose(2, 1, 0, 3)
    lines = cols // (y_lo * n_xc)
    piece_grad = basis_grad.reshape(rows, y_lo, n_x, n_c, lines).transpose(2, 3, 0, 1, 4)
    pieces = jnp.concatenate([piece_act, piece_grad.reshape(n_x, n_c, rows, part)], axis=3)
    swap = []
    for q in range(n_zh):
        for low in range(y_lo):
            for zh in range(n_zh):
                swap.append((((q * y_lo) + low) * n_zh + zh, ((zh * y_lo) + low) * n_zh + q))
    pieces = lax.ppermute(pieces, ("zl", "y", "zh"), swap)

    own = jnp.stack([activations, gradients])
    pair = jnp.stack([own, exchange(own, "x", lambda i: i ^ 1)])
    quad = jnp.concatenate([pair, exchange(pair, "x", lambda i: n_x - 1 - i)])
    other = exchange(quad, "c", lambda i: 1 - i)

    pieces = jnp.broadcast_to(
        pieces.reshape(1, n_xc, rows, 2 * part), (n_y, n_xc, rows, 2 * part)
    ).reshape(n_y * n_xc, rows, 2 * part)
    basis = lax.all_to_all(pieces, ("y", "x", "c"), 0, 0, tiled=True)
    basis = basis.reshape(n_y // y_lo, y_lo * n_xc * rows, 2 * part)
    far_basis = exchange(basis, "zl", lambda i: 1 - i)

    def rotate(which, first, last):
        def product(columns, blocks):
            out = jnp.einsum(
                "kfj,stf->kjst", columns, blocks[:, which], preferred_element_type=F32
            )
            return out[:, first:last].reshape(-1, last - first, group // n_c)

        halves = [
            jnp.concatenate([product(b, quad), product(b, other)], axis=2)
            for b in (basis, far_basis)
        ]
        return swap_if(zl == 1, jnp.concatenate(halves, axis=0), 0)

    act = rotate(0, 0, part)
    grad = rotate(1, part, 2 * part)
    largest = jnp.maximum(jnp.max(jnp.abs(act)), jnp.max(jnp.abs(grad)))
    level = jnp.clip(jnp.ceil(jnp.log2(jnp.maximum(largest, F32(1e-30)))), -100.0, 100.0)
    factor = jnp.exp2(F32(TOP) - level)
    level = jnp.full((n_zh, TILE, group), level, F32).astype(F16)
    act = jnp.concatenate([(act * factor).astype(F16), level], axis=1)
    grad = (grad * factor).astype(F16)
    act = lax.all_to_all(act, "zh", 0, 0, tiled=True)
    act, grad = lax.optimization_barrier((act, grad))
    grad = lax.all_to_all(grad, "zh", 0, 0, tiled=True).astype(F32)
    act = act.astype(F32)
    factors = jnp.exp2(act[:, -TILE:, :] - F32(TOP))[:, :1, :1]

    def in_order(value):
        blocks = jnp.split(value, n_xc, axis=1)
        blocks = [blocks[i] for i in (0, 1, 3, 2, 4, 5, 7, 6)]
        for condition, step in ((c == 1, n_x), (x >= 2, 2), (x % 2 == 1, 1)):
            blocks = [jnp.where(condition, blocks[i ^ step], blocks[i]) for i in range(n_xc)]
        return jnp.concatenate(blocks, axis=1)

    rot_act = in_order(jnp.sum(act[:, :-TILE] * factors, axis=0))
    rot_grad = in_order(jnp.sum(grad * factors, axis=0)).astype(BF16)
    block = jnp.arange(group, dtype=jnp.int32) // toks
    block = (block % n_x) * n_c + block // n_x
    position = y * group + block * toks + jnp.arange(group, dtype=jnp.int32) % toks
    length = jnp.where(zl == 0, lengths[0], lengths[1])
    valid = position < length
    rot_act = jnp.where(valid[None, :], rot_act, F32(0.0)).astype(BF16)

    wide_act = lax.all_gather(rot_act, "x", axis=0, tiled=True)
    wide_act = lax.all_to_all(
        jnp.broadcast_to(wide_act[None], (n_c, *wide_act.shape)), "c", 0, 0, tiled=True
    ).reshape(cols, group)
    wide_grad = lax.all_gather(rot_grad, "zh", axis=0, tiled=True)
    share = lax.dot_general(
        wide_grad, wide_act, (((1,), (1,)), ((), ())), preferred_element_type=F32
    )
    share = share.astype(BF16).reshape(n_zl * n_y, -1, cols)
    received = lax.all_to_all(share, ("zl", "y"), 0, 0, tiled=True)
    received = received.astype(F32).reshape(SEQS, n_y, -1, cols)
    per_seq = jnp.sum(received, axis=1)
    scale = lengths.astype(F32)[:, None, None]
    return jnp.sum(per_seq * per_seq / scale, axis=0) / F32(SEQS)


def solution(mesh):
    split = Mesh(mesh.devices.reshape(2, 8, 4, 2, 4), ("zl", "y", "x", "c", "zh"))
    spec = P(("zl", "y", "x", "c"), "zh")
    return jax.shard_map(
        on_device, mesh=split, in_specs=(spec, spec, spec, spec, P()), out_specs=spec, check_vma=False
    )
```

time: 190 us -> 190 us (level)
  blocking collectives: 86.6 us -> 24.4 us
  starting transfers between devices: 18.5 us -> 76 us
  between operations: 14.8 us -> 2.91 us
  matrix products: 5.87 us -> 15.3 us
  other arithmetic: 4.44 us -> 7.57 us
    all_to_all x1 -> x0, blocking collectives: 59.5 us -> none  [on_device(): basis = lax.all_to_all(pieces, ('zl', 'y', 'x', 'c'), 0, 0, tiled=True)]
    all_to_all x2 -> x4, starting transfers between devices: 14.3 us -> 47.3 us  [the longest x1 20.9 us: on_device(): basis = lax.all_to_all(pieces, ('y', 'x', 'c'), 0, 0, tiled=True)]
    ppermute x0 -> x4, starting transfers between devices: none -> 22.4 us  [exchange(): lax.ppermute(value, axis, [(i, partner(i)) for i in range(lax.axis_size(a...]
    ppermute x0 -> x4, waiting for transfers between devices: none -> 14.8 us  [exchange(): lax.ppermute(value, axis, [(i, partner(i)) for i in range(lax.axis_size(a...]
    all_to_all x2 -> x4, waiting for transfers between devices: 46.5 us -> 33.1 us  [the longest x1 12.6 us: on_device(): act = lax.all_to_all(act, 'zh', 0, 0, tiled=True)]
    dot_general x2 -> x8, matrix products: 4.69 us -> 14.2 us  [product(): jnp.einsum('kfj,stf->kjst', columns, blocks[:, which], preferred_element_...]
    all_gather x1, blocking collectives: 17.2 us -> 14.2 us  [on_device(): wide_grad = lax.all_gather(rot_grad, 'zh', axis=0, tiled=True)]
    all_to_all x1, starting transfers between devices: 3.53 us -> 5.56 us  [on_device(): received = lax.all_to_all(share, ('zl', 'y'), 0, 0, tiled=True)]
  transfers between devices with their start and end apart: 5 -> 10, of which waited for: 2 -> 6; matrix products, arithmetic and copies ran while one was open for 1% -> 7% of each run, Pallas kernels for 0% -> 0%
where the time goes in v3:
time: 190 us; the launch traced here: 186 us
  starting transfers between devices  76 us (40%)
  waiting for transfers between devices  55.8 us (29%)
  blocking collectives  24.4 us (13%)
  matrix products  15.3 us (8%)
  other arithmetic  7.57 us (4%)
  local copies, waits for them, and re-layouts  4.3 us (2%)
  between operations  2.91 us (2%)
    ppermute x4, starting transfers between devices, exchange(): lax.ppermute(value, axis, [(i, partner(i)) for i in range(lax.axis_size(a...  22.4 us
    all_to_all x1, starting transfers between devices, on_device(): basis = lax.all_to_all(pieces, ('y', 'x', 'c'), 0, 0, tiled=True)  20.9 us
    ppermute x4, waiting for transfers between devices, exchange(): lax.ppermute(value, axis, [(i, partner(i)) for i in range(lax.axis_size(a...  14.8 us
    all_gather x1, blocking collectives, on_device(): wide_grad = lax.all_gather(rot_grad, 'zh', axis=0, tiled=True)  14.2 us
    dot_general x8, matrix products, product(): jnp.einsum('kfj,stf->kjst', columns, blocks[:, which], preferred_element_...  14.2 us
    all_to_all x1, starting transfers between devices, on_device(): lax.all_to_all(jnp.broadcast_to(wide_act[None], (n_c, *wide_act.shape)),...  13.5 us
    all_to_all x1, waiting for transfers between devices, on_device(): act = lax.all_to_all(act, 'zh', 0, 0, tiled=True)  12.6 us
    all_to_all x1, waiting for transfers between devices, on_device(): basis = lax.all_to_all(pieces, ('y', 'x', 'c'), 0, 0, tiled=True)  11.8 us
  transfers between devices with their start and end apart: 10, of which 6 were waited for; matrix products, arithmetic and copies ran while one was open for 7% of the time, Pallas kernels for 0%

profile of v3, /device:TPU:1, one launch (start us, length us, event | category | flops | bytes accessed | tf_op | source)
XLA Modules:
  0.0 186.3 jit_solution(7120891455168341983)
XLA Ops:
  0.0 1.1 fusion.32
  1.1 3.9 %collective-permute-start.2 = (bf16[2,128,1024]{2,1,0:T(8,128)(2,1)S(1)}, bf16[2,128,1024]{2,1,0:T(8,128)(2,1)S(1)}, u32[]{:S(2)}, u32[]{:S(2)}) collective-permute-start(bf16[2,128,1024]{2,1,0:T(8,128)(2,1)S(1)} %get-tuple-element.32), channel_id=1, source_target_pairs={{0,8},{8,0},{16,24},{24,16},{1,9},{9,1},{17,25},{25,17},{2,10},{10... | collective-permute-start | bytes 1572872 | tf_op jit(solution)/shard_map/ppermute | solution.py:16
  5.1 6.6 %collective-permute-done.2 = bf16[2,128,1024]{2,1,0:T(8,128)(2,1)S(1)} collective-permute-done((bf16[2,128,1024]{2,1,0:T(8,128)(2,1)S(1)}, bf16[2,128,1024]{2,1,0:T(8,128)(2,1)S(1)}, u32[]{:S(2)}, u32[]{:S(2)}) %collective-permute-start.2) | collective-permute-done | bytes 524320 | tf_op jit(solution)/shard_map/ppermute | solution.py:16
  11.8 9.3 %collective-permute-start.3 = (bf16[2,2,128,1024]{3,2,0,1:T(8,128)(2,1)S(1)}, bf16[2,2,128,1024]{3,2,0,1:T(8,128)(2,1)}, u32[]{:S(2)}, u32[]{:S(2)}) collective-permute-start(bf16[2,2,128,1024]{3,2,0,1:T(8,128)(2,1)S(1)} %pad_maximum_fusion.1), channel_id=1, source_target_pairs={{0,24},{8,16},{16,8},{24,0},{1,25},{9,17},{17,9},{25,1},{2,26},{10... | collective-permute-start | bytes 3145736 | tf_op jit(solution)/shard_map/ppermute | solution.py:16
  22.3 0.9 broadcast_in_dim.29
  23.2 20.9 %all-to-all-start = ((bf16[64,32,128]{2,1,0:T(8,128)(2,1)}), bf16[64,32,128]{2,1,0:T(8,128)(2,1)S(1)}, u32[]{:S(2)}, u32[]{:S(2)}) async-start(bf16[64,32,128]{2,1,0:T(8,128)(2,1)} %bitcast.5), calls=%async_computation | async-start | bytes 1048576 | tf_op jit(solution)/shard_map/all_to_all | solution.py:52
  44.2 2.8 %pad_maximum_fusion = bf16[4,2,128,1024]{3,2,0,1:T(8,128)(2,1)} fusion(bf16[2,2,128,1024]{3,2,0,1:T(8,128)(2,1)} %collective-permute-done.3, bf16[1,2,128,1024]{3,2,0,1:T(8,128)(2,1)S(1)} %bitcast.94, bf16[1,2,128,1024]{3,2,0,1:T(8,128)(2,1)S(1)} %get-tuple-element.31), kind=kLoop, calls=%fused_computation | loop fusion | flops 2097152 | bytes 4194304 | tf_op jit(solution)/shard_map/concatenate | solution.py:46
  46.9 3.1 %collective-permute-start.4 = (bf16[4,2,128,1024]{3,2,0,1:T(8,128)(2,1)}, bf16[4,2,128,1024]{3,2,0,1:T(8,128)(2,1)}, u32[]{:S(2)}, u32[]{:S(2)}) collective-permute-start(bf16[4,2,128,1024]{3,2,0,1:T(8,128)(2,1)} %pad_maximum_fusion), channel_id=1, source_target_pairs={{0,4},{4,0},{1,5},{5,1},{2,6},{6,2},{3,7},{7,3},{8,12},{12,8},{9,1... | collective-permute-start | bytes 6291464 | tf_op jit(solution)/shard_map/ppermute | solution.py:16
  50.0 11.8 %all-to-all-done = bf16[64,32,128]{2,1,0:T(8,128)(2,1)S(1)} async-done(((bf16[64,32,128]{2,1,0:T(8,128)(2,1)}), bf16[64,32,128]{2,1,0:T(8,128)(2,1)S(1)}, u32[]{:S(2)}, u32[]{:S(2)}) %all-to-all-start) | async-done | bytes 524320 | tf_op jit(solution)/shard_map/all_to_all | solution.py:52
  62.1 6.1 %collective-permute-start.1 = (bf16[2,1024,128]{1,2,0:T(8,128)(2,1)S(1)}, bf16[2,1024,128]{1,2,0:T(8,128)(2,1)S(1)}, u32[]{:S(2)}, u32[]{:S(2)}) collective-permute-start(bf16[2,1024,128]{1,2,0:T(8,128)(2,1)S(1)} %copy.49), channel_id=1, source_target_pairs={{0,256},{256,0},{1,257},{257,1},{2,258},{258,2},{3,259},{259,3},{4... | collective-permute-start | bytes 1572872 | tf_op jit(solution)/shard_map/ppermute | solution.py:16
  68.2 1.9 %convolution_bitcast_fusion.5 = f32[2,4,8,8,128]{4,3,2,1,0:T(8,128)S(1)} fusion(bf16[4,2,128,1024]{3,2,0,1:T(8,128)(2,1)} %pad_maximum_fusion, bf16[2,1024,128,1]{2,1,3,0:T(8,128)(2,1)S(1)} %bitcast.89), kind=kOutput, calls=%fused_computation.7 | convolution fusion | flops 134217728 | bytes 1835008 | tf_op jit(solution)/shard_map/kfj,stf->kjst/dot_general | solution.py:58
  70.1 1.7 convolution_bitcast_fusion.7
  71.9 8.2 %collective-permute-done.1 = bf16[2,1024,128]{1,2,0:T(8,128)(2,1)S(1)} collective-permute-done((bf16[2,1024,128]{1,2,0:T(8,128)(2,1)S(1)}, bf16[2,1024,128]{1,2,0:T(8,128)(2,1)S(1)}, u32[]{:S(2)}, u32[]{:S(2)}) %collective-permute-start.1) | collective-permute-done | bytes 524320 | tf_op jit(solution)/shard_map/ppermute | solution.py:16
  80.1 1.7 convolution_bitcast_fusion.1
  81.9 1.7 convolution_bitcast_fusion.3
  83.6 1.9 %convolution_bitcast_fusion.4 = f32[2,4,8,8,128]{4,3,2,1,0:T(8,128)S(1)} fusion(bf16[4,2,128,1024]{3,2,0,1:T(8,128)(2,1)} %collective-permute-done.4, bf16[2,1024,128,1]{2,1,3,0:T(8,128)(2,1)S(1)} %bitcast.91), kind=kOutput, calls=%fused_computation.6 | convolution fusion | flops 134217728 | bytes 1835008 | tf_op jit(solution)/shard_map/kfj,stf->kjst/dot_general | solution.py:58
  85.6 1.7 convolution_bitcast_fusion
  87.4 1.7 convolution_bitcast_fusion.6
  89.1 1.7 convolution_bitcast_fusion.2
  93.1 1.0 concatenate.51
  94.0 7.4 %all-to-all-start.1 = ((f16[4,80,1024]{2,1,0:T(8,128)(2,1)}), f16[4,80,1024]{2,1,0:T(8,128)(2,1)S(1)}, u32[]{:S(2)}, u32[]{:S(2)}) async-start(f16[4,80,1024]{2,1,0:T(8,128)(2,1)} %concatenate.51), calls=%async_computation.1 | async-start | bytes 1310720 | tf_op jit(solution)/shard_map/all_to_all | solution.py:77
  101.4 0.9 multiply_convert_fusion
  102.3 12.6 %all-to-all-done.1 = f16[4,80,1024]{2,1,0:T(8,128)(2,1)S(1)} async-done(((f16[4,80,1024]{2,1,0:T(8,128)(2,1)}), f16[4,80,1024]{2,1,0:T(8,128)(2,1)S(1)}, u32[]{:S(2)}, u32[]{:S(2)}) %all-to-all-start.1) | async-done | bytes 655392 | tf_op jit(solution)/shard_map/all_to_all | solution.py:77
  114.9 5.5 %all-to-all-start.2 = ((f16[4,64,1024]{2,1,0:T(8,128)(2,1)}), f16[4,64,1024]{2,1,0:T(8,128)(2,1)S(1)}, u32[]{:S(2)}, u32[]{:S(2)}) async-start(f16[4,64,1024]{2,1,0:T(8,128)(2,1)} %multiply_convert_fusion), calls=%async_computation.2 | async-start | bytes 1048576 | tf_op jit(solution)/shard_map/all_to_all | solution.py:79
  122.5 8.7 %all-to-all-done.2 = f16[4,64,1024]{2,1,0:T(8,128)(2,1)S(1)} async-done(((f16[4,64,1024]{2,1,0:T(8,128)(2,1)}), f16[4,64,1024]{2,1,0:T(8,128)(2,1)S(1)}, u32[]{:S(2)}, u32[]{:S(2)}) %all-to-all-start.2) | async-done | bytes 524320 | tf_op jit(solution)/shard_map/all_to_all | solution.py:79
  131.7 10.2 %all_gather.7 = bf16[256,1024]{1,0:T(8,128)(2,1)S(1)} all-gather(bf16[64,1024]{1,0:T(8,128)(2,1)S(1)} %select_convert_fusion), channel_id=1, replica_groups=mesh['zl'=2,'y'=8,'x'=4,'c'=2,'zh'=4] {'x'}, dimensions={0}, use_global_device_ids=true | all-gather | bytes 655360 | tf_op jit(solution)/shard_map/all_gather | solution.py:99
  141.9 1.1 broadcast_in_dim.32
  143.0 13.5 %all-to-all-start.3 = ((bf16[2,256,1024]{2,1,0:T(8,128)(2,1)}), bf16[2,256,1024]{2,1,0:T(8,128)(2,1)S(1)}, u32[]{:S(2)}, u32[]{:S(2)}) async-start(bf16[2,256,1024]{2,1,0:T(8,128)(2,1)} %broadcast_in_dim.32), calls=%async_computation.3 | async-start | bytes 2097152 | tf_op jit(solution)/shard_map/all_to_all | solution.py:100
  156.8 14.2 %all_gather.6 = bf16[256,1024]{1,0:T(8,128)(2,1)S(1)} all-gather(bf16[64,1024]{1,0:T(8,128)(2,1)S(1)} %constant_dynamic-update-slice_fusion), channel_id=1, replica_groups=mesh['zl'=2,'y'=8,'x'=4,'c'=2,'zh'=4] {'zh'}, dimensions={0}, use_global_device_ids=true | all-gather | bytes 655360 | tf_op jit(solution)/shard_map/all_gather | solution.py:103
  171.0 1.2 convolution_convert_fusion
  172.2 5.6 %all-to-all-start.4 = ((bf16[16,16,512]{2,1,0:T(8,128)(2,1)}), bf16[16,16,512]{2,1,0:T(8,128)(2,1)S(1)}, u32[]{:S(2)}, u32[]{:S(2)}) async-start(bf16[16,16,512]{2,1,0:T(8,128)(2,1)} %bitcast.31), calls=%async_computation.4 | async-start | bytes 524288 | tf_op jit(solution)/shard_map/all_to_all | solution.py:108
  177.7 7.8 %all-to-all-done.4 = bf16[16,16,512]{2,1,0:T(8,128)(2,1)S(1)} async-done(((bf16[16,16,512]{2,1,0:T(8,128)(2,1)}), bf16[16,16,512]{2,1,0:T(8,128)(2,1)S(1)}, u32[]{:S(2)}, u32[]{:S(2)}) %all-to-all-start.4) | async-done | bytes 262176 | tf_op jit(solution)/shard_map/all_to_all | solution.py:108
  (56 shorter events, 4.8 us)
Async XLA Ops:
  0.0 21.1 %copy-start = (bf16[32,512]{1,0:T(8,128)(2,1)S(1)}, bf16[32,512]{1,0:T(8,128)(2,1)}, u32[]{:S(2)}) copy-start(bf16[32,512]{1,0:T(8,128)(2,1)} %param.8) | copy-start | bytes 98308
  0.0 21.4 %copy-start.1 = (bf16[32,512]{1,0:T(8,128)(2,1)S(1)}, bf16[32,512]{1,0:T(8,128)(2,1)}, u32[]{:S(2)}) copy-start(bf16[32,512]{1,0:T(8,128)(2,1)} %param.7) | copy-start | bytes 98308
  1.1 10.6 %collective-permute-start.2 = (bf16[2,128,1024]{2,1,0:T(8,128)(2,1)S(1)}, bf16[2,128,1024]{2,1,0:T(8,128)(2,1)S(1)}, u32[]{:S(2)}, u32[]{:S(2)}) collective-permute-start(bf16[2,128,1024]{2,1,0:T(8,128)(2,1)S(1)} %get-tuple-element.32), channel_id=1, source_target_pairs={{0,8},{8,0},{16,24},{24,16},{1,9},{9,1},{17,25},{25,17},{2,10},{10... | collective-permute-start | bytes 1572872 | tf_op jit(solution)/shard_map/ppermute | solution.py:16
  11.8 32.3 %collective-permute-start.3 = (bf16[2,2,128,1024]{3,2,0,1:T(8,128)(2,1)S(1)}, bf16[2,2,128,1024]{3,2,0,1:T(8,128)(2,1)}, u32[]{:S(2)}, u32[]{:S(2)}) collective-permute-start(bf16[2,2,128,1024]{3,2,0,1:T(8,128)(2,1)S(1)} %pad_maximum_fusion.1), channel_id=1, source_target_pairs={{0,24},{8,16},{16,8},{24,0},{1,25},{9,17},{17,9},{25,1},{2,26},{10... | collective-permute-start | bytes 3145736 | tf_op jit(solution)/shard_map/ppermute | solution.py:16
  21.6 0.7 collective-permute-start
  23.2 38.6 %all-to-all-start = ((bf16[64,32,128]{2,1,0:T(8,128)(2,1)}), bf16[64,32,128]{2,1,0:T(8,128)(2,1)S(1)}, u32[]{:S(2)}, u32[]{:S(2)}) async-start(bf16[64,32,128]{2,1,0:T(8,128)(2,1)} %bitcast.5), calls=%async_computation | async-start | bytes 1048576 | tf_op jit(solution)/shard_map/all_to_all | solution.py:52
  46.9 36.7 %collective-permute-start.4 = (bf16[4,2,128,1024]{3,2,0,1:T(8,128)(2,1)}, bf16[4,2,128,1024]{3,2,0,1:T(8,128)(2,1)}, u32[]{:S(2)}, u32[]{:S(2)}) collective-permute-start(bf16[4,2,128,1024]{3,2,0,1:T(8,128)(2,1)} %pad_maximum_fusion), channel_id=1, source_target_pairs={{0,4},{4,0},{1,5},{5,1},{2,6},{6,2},{3,7},{7,3},{8,12},{12,8},{9,1... | collective-permute-start | bytes 6291464 | tf_op jit(solution)/shard_map/ppermute | solution.py:16
  62.1 18.1 %collective-permute-start.1 = (bf16[2,1024,128]{1,2,0:T(8,128)(2,1)S(1)}, bf16[2,1024,128]{1,2,0:T(8,128)(2,1)S(1)}, u32[]{:S(2)}, u32[]{:S(2)}) collective-permute-start(bf16[2,1024,128]{1,2,0:T(8,128)(2,1)S(1)} %copy.49), channel_id=1, source_target_pairs={{0,256},{256,0},{1,257},{257,1},{2,258},{258,2},{3,259},{259,3},{4... | collective-permute-start | bytes 1572872 | tf_op jit(solution)/shard_map/ppermute | solution.py:16
  94.0 26.4 %copy-start.2 = (s32[2]{0:T(128)S(1)}, s32[2]{0:T(128)}, u32[]{:S(2)}) copy-start(s32[2]{0:T(128)} %param.9) | copy-start | bytes 28
  94.0 20.9 %all-to-all-start.1 = ((f16[4,80,1024]{2,1,0:T(8,128)(2,1)}), f16[4,80,1024]{2,1,0:T(8,128)(2,1)S(1)}, u32[]{:S(2)}, u32[]{:S(2)}) async-start(f16[4,80,1024]{2,1,0:T(8,128)(2,1)} %concatenate.51), calls=%async_computation.1 | async-start | bytes 1310720 | tf_op jit(solution)/shard_map/all_to_all | solution.py:77
  114.9 16.3 %all-to-all-start.2 = ((f16[4,64,1024]{2,1,0:T(8,128)(2,1)}), f16[4,64,1024]{2,1,0:T(8,128)(2,1)S(1)}, u32[]{:S(2)}, u32[]{:S(2)}) async-start(f16[4,64,1024]{2,1,0:T(8,128)(2,1)} %multiply_convert_fusion), calls=%async_computation.2 | async-start | bytes 1048576 | tf_op jit(solution)/shard_map/all_to_all | solution.py:79
  143.0 28.0 %all-to-all-start.3 = ((bf16[2,256,1024]{2,1,0:T(8,128)(2,1)}), bf16[2,256,1024]{2,1,0:T(8,128)(2,1)S(1)}, u32[]{:S(2)}, u32[]{:S(2)}) async-start(bf16[2,256,1024]{2,1,0:T(8,128)(2,1)} %broadcast_in_dim.32), calls=%async_computation.3 | async-start | bytes 2097152 | tf_op jit(solution)/shard_map/all_to_all | solution.py:100
  172.2 13.4 %all-to-all-start.4 = ((bf16[16,16,512]{2,1,0:T(8,128)(2,1)}), bf16[16,16,512]{2,1,0:T(8,128)(2,1)S(1)}, u32[]{:S(2)}, u32[]{:S(2)}) async-start(bf16[16,16,512]{2,1,0:T(8,128)(2,1)} %bitcast.31), calls=%async_computation.4 | async-start | bytes 524288 | tf_op jit(solution)/shard_map/all_to_all | solution.py:108

commit v4 on v3

v4 whole, which is shorter than its diff:
```python
import jax
import jax.numpy as jnp
from jax import lax
from jax.experimental import pallas as pl
from jax.experimental.pallas import tpu as pltpu
from jax.sharding import Mesh
from jax.sharding import PartitionSpec as P

SEQS = 2
F32 = jnp.float32
BF16 = jnp.bfloat16
F16 = jnp.float16
TILE = 16
TOP = 15
XORS = (0, 1, 3, 2)


def exchange(value, axis, partner):
    return lax.ppermute(value, axis, [(i, partner(i)) for i in range(lax.axis_size(axis))])


def rotate_kernel(place, basis, far_basis, pair, far, core_pair, core_far, act, grad, most, turned):
    n_zl, n_k = 2, basis.shape[0]
    part, toks = basis.shape[2] // 2, pair.shape[2]
    x, c, zl = place[0], place[1], place[2]
    for k in range(n_zl * n_k):
        block = (basis if k < n_k else far_basis)[k % n_k].T
        turned[0, pl.ds(k * part, part)] = block[:part]
        turned[1, pl.ds(k * part, part)] = block[part:]
    largest = jnp.zeros((n_zl * n_k * part, toks), F32)
    for slot, xor in enumerate(XORS):
        mine, other = ((pair, core_pair), (far, core_far))[slot // 2]
        first = (x ^ xor) * 2
        for which, out_ref in enumerate((act, grad)):
            rows = jnp.concatenate([mine[slot % 2, which], other[slot % 2, which]], axis=0)
            out = lax.dot_general(
                turned[which], rows, (((1,), (1,)), ((), ())), preferred_element_type=F32
            )
            for half, core in enumerate((c, 1 - c)):
                value = out[:, half * toks : (half + 1) * toks]
                largest = jnp.maximum(largest, jnp.abs(value))
                lanes = pl.ds(pl.multiple_of((first + core) * toks, toks), toks)
                for k in range(n_zl * n_k):
                    column = (zl ^ (k // n_k)) * n_k + k % n_k
                    out_ref[column, :, lanes] = value[k * part : (k + 1) * part]
    most[...] = jnp.max(largest.reshape(-1, 8, toks), axis=0)


def rotate(place, basis, far_basis, *tokens):
    n_k, feats, wide = basis.shape
    toks = tokens[0].shape[2]
    n_k, part, group = 2 * n_k, wide // 2, 8 * toks
    out = jax.ShapeDtypeStruct((n_k, part, group), F32)
    vmem = pl.BlockSpec(memory_space=pltpu.VMEM)
    return pl.pallas_call(
        rotate_kernel,
        out_shape=(out, out, jax.ShapeDtypeStruct((8, toks), F32)),
        in_specs=[pl.BlockSpec(memory_space=pltpu.SMEM)] + [vmem] * 6,
        out_specs=(vmem, vmem, vmem),
        scratch_shapes=[pltpu.VMEM((2, n_k * part, feats), BF16)],
        compiler_params=pltpu.CompilerParams(vmem_limit_bytes=32 * 2**20),
        cost_estimate=pl.CostEstimate(
            flops=2 * n_k * wide * feats * group, bytes_accessed=8 * 2**20, transcendentals=0
        ),
        name="rotate",
    )(place, basis, far_basis, *tokens)


def on_device(activations, gradients, basis_act, basis_grad, lengths):
    n_zl, n_y, n_x, n_c, n_zh = (lax.axis_size(a) for a in ("zl", "y", "x", "c", "zh"))
    zl, y, x, c = (lax.axis_index(a) for a in ("zl", "y", "x", "c"))
    n_xc, y_lo = n_x * n_c, n_y // 2
    toks, feats = activations.shape
    rows, cols = basis_act.shape
    part = cols // n_xc
    group = toks * n_xc

    piece_act = basis_act.reshape(rows, n_c, n_x, part).transpose(2, 1, 0, 3)
    lines = cols // (y_lo * n_xc)
    piece_grad = basis_grad.reshape(rows, y_lo, n_x, n_c, lines).transpose(2, 3, 0, 1, 4)
    pieces = jnp.concatenate([piece_act, piece_grad.reshape(n_x, n_c, rows, part)], axis=3)
    own = jnp.stack([activations, gradients])
    pieces, own = lax.optimization_barrier((pieces.reshape(n_xc, rows, 2 * part), own))
    swap = []
    for q in range(n_zh):
        for low in range(y_lo):
            for zh in range(n_zh):
                swap.append((((q * y_lo) + low) * n_zh + zh, ((zh * y_lo) + low) * n_zh + q))
    pieces = lax.ppermute(pieces, ("zl", "y", "zh"), swap)

    near = exchange(own, "x", lambda i: i ^ 1)
    near, pieces = lax.optimization_barrier((near, pieces))
    pair = jnp.stack([own, near])
    far = exchange(pair, "x", lambda i: n_x - 1 - i)
    core_pair = exchange(pair, "c", lambda i: 1 - i)
    pieces = jnp.broadcast_to(pieces[None], (n_y, n_xc, rows, 2 * part))
    basis = lax.all_to_all(pieces.reshape(-1, rows, 2 * part), ("y", "x", "c"), 0, 0, tiled=True)
    basis = basis.reshape(n_y // y_lo, y_lo * n_xc * rows, 2 * part)
    basis, far = lax.optimization_barrier((basis, far))
    far_basis = exchange(basis, "zl", lambda i: 1 - i)
    core_far = exchange(far, "c", lambda i: 1 - i)

    place = jnp.stack([x, c, zl]).astype(jnp.int32)
    act, grad, most = rotate(place, basis, far_basis, pair, far, core_pair, core_far)
    largest = jnp.max(most)
    level = jnp.clip(jnp.ceil(jnp.log2(jnp.maximum(largest, F32(1e-30)))), -100.0, 100.0)
    factor = jnp.exp2(F32(TOP) - level)
    level = jnp.full((n_zh, TILE, group), level, F32).astype(F16)
    act = jnp.concatenate([(act * factor).astype(F16), level], axis=1)
    grad = (grad * factor).astype(F16)
    act = lax.all_to_all(act, "zh", 0, 0, tiled=True)
    act, grad = lax.optimization_barrier((act, grad))
    grad = lax.all_to_all(grad, "zh", 0, 0, tiled=True)
    act = act.astype(F32)
    factors = jnp.exp2(act[:, -TILE:, :] - F32(TOP))[:, :1, :1]
    rot_act = jnp.sum(act[:, :-TILE] * factors, axis=0)
    position = y * group + jnp.arange(group, dtype=jnp.int32)
    length = jnp.where(zl == 0, lengths[0], lengths[1])
    valid = position < length
    rot_act = jnp.where(valid[None, :], rot_act, F32(0.0)).astype(BF16)
    wide_act = lax.all_gather(rot_act, "x", axis=0, tiled=True)
    wide_act, grad = lax.optimization_barrier((wide_act, grad))
    far_act = exchange(wide_act, "c", lambda i: 1 - i)
    rot_grad = jnp.sum(grad.astype(F32) * factors, axis=0).astype(BF16)
    wide_grad = lax.all_gather(rot_grad, "zh", axis=0, tiled=True)

    def product(columns):
        return lax.dot_general(
            wide_grad, columns, (((1,), (1,)), ((), ())), preferred_element_type=F32
        ).astype(BF16)

    near_share, far_share = product(wide_act), product(far_act)
    share = jnp.concatenate(
        [jnp.where(c == 0, near_share, far_share), jnp.where(c == 0, far_share, near_share)],
        axis=1,
    )
    received = lax.all_to_all(
        share.reshape(n_zl * n_y, -1, cols), ("zl", "y"), 0, 0, tiled=True
    )
    received = received.astype(F32).reshape(SEQS, n_y, -1, cols)
    per_seq = jnp.sum(received, axis=1)
    scale = lengths.astype(F32)[:, None, None]
    return jnp.sum(per_seq * per_seq / scale, axis=0) / F32(SEQS)


def solution(mesh):
    split = Mesh(mesh.devices.reshape(2, 8, 4, 2, 4), ("zl", "y", "x", "c", "zh"))
    spec = P(("zl", "y", "x", "c"), "zh")
    return jax.shard_map(
        on_device, mesh=split, in_specs=(spec, spec, spec, spec, P()), out_specs=spec, check_vma=False
    )
```

time: 190 us -> 169 us (0.89)
  starting transfers between devices: 76 us -> 61.3 us
  matrix products: 15.3 us -> 0.68 us
  local copies, waits for them, and re-layouts: 4.3 us -> 8.34 us
  blocking collectives: 24.4 us -> 27.5 us
  Pallas kernels: 0 us -> 3.06 us
  other arithmetic: 7.57 us -> 5.63 us
    all_to_all x4 -> x3, starting transfers between devices: 45.5 us -> 22.3 us  [the longest x1 9.72 us: on_device(): lax.all_to_all(pieces.reshape(-1, rows, 2 * part), ('y', 'x', 'c'), 0, 0,...]
    dot_general x9 -> x2, matrix products: 15.3 us -> 0.68 us  [product(): lax.dot_general(wide_grad, columns, (((1,), (1,)), ((), ())), preferred_e...]
    ppermute x4 -> x6, starting transfers between devices: 22.4 us -> 28.5 us  [exchange(): lax.ppermute(value, axis, [(i, partner(i)) for i in range(lax.axis_size(a...]
    all_to_all x4 -> x3, waiting for transfers between devices: 28.4 us -> 24 us  [the longest x1 16.2 us: on_device(): lax.all_to_all(pieces.reshape(-1, rows, 2 * part), ('y', 'x', 'c'), 0, 0,...]
    unnamed x11 -> x9, local copies, waits for them, and re-layouts: 0.21 us -> 4.06 us
    ppermute x4 -> x6, waiting for transfers between devices: 14.8 us -> 18 us  [exchange(): lax.ppermute(value, axis, [(i, partner(i)) for i in range(lax.axis_size(a...]
    pallas_call x0 -> x1, Pallas kernels: none -> 3.06 us  [rotate(): pl.pallas_call(rotate_kernel, out_shape=(out, out, jax.ShapeDtypeStruct((...]
    concatenate x3 -> x1, other arithmetic: 2.82 us -> 0.02 us  [on_device(): jnp.concatenate([jnp.where(c == 0, near_share, far_share), jnp.where(c ==...]
  transfers between devices with their start and end apart: 10 -> 11, of which waited for: 6 -> 5; matrix products, arithmetic and copies ran while one was open for 7% -> 2% of each run, Pallas kernels for 0% -> 0%
where the time goes in v4:
time: 169 us; the launch traced here: 166 us
  starting transfers between devices  61.3 us (36%)
  waiting for transfers between devices  56.8 us (34%)
  blocking collectives  27.5 us (16%)
  local copies, waits for them, and re-layouts  8.34 us (5%)
  other arithmetic  5.63 us (3%)
  Pallas kernels  3.06 us (2%)
  between operations  2.3 us (1%)
    ppermute x6, starting transfers between devices, exchange(): lax.ppermute(value, axis, [(i, partner(i)) for i in range(lax.axis_size(a...  28.5 us
    ppermute x6, waiting for transfers between devices, exchange(): lax.ppermute(value, axis, [(i, partner(i)) for i in range(lax.axis_size(a...  18 us
    all_gather x1, blocking collectives, on_device(): wide_grad = lax.all_gather(rot_grad, 'zh', axis=0, tiled=True)  16.3 us
    all_to_all x1, waiting for transfers between devices, on_device(): lax.all_to_all(pieces.reshape(-1, rows, 2 * part), ('y', 'x', 'c'), 0, 0,...  16.2 us
    all_to_all x1, waiting for transfers between devices, on_device(): act = lax.all_to_all(act, 'zh', 0, 0, tiled=True)  14.7 us
    all_gather x1, blocking collectives, on_device(): wide_act = lax.all_gather(rot_act, 'x', axis=0, tiled=True)  11.2 us
    all_to_all x1, starting transfers between devices, on_device(): act = lax.all_to_all(act, 'zh', 0, 0, tiled=True)  9.77 us
    all_to_all x1, starting transfers between devices, on_device(): lax.all_to_all(pieces.reshape(-1, rows, 2 * part), ('y', 'x', 'c'), 0, 0,...  9.72 us
  transfers between devices with their start and end apart: 11, of which 5 were waited for; matrix products, arithmetic and copies ran while one was open for 2% of the time, Pallas kernels for 0%

profile of v4, /device:TPU:1, one launch (start us, length us, event | category | flops | bytes accessed | tf_op | source)
XLA Modules:
  0.0 165.5 jit_solution(16903458558379059480)
XLA Ops:
  0.0 0.9 copy.16
  1.0 0.9 reshape.33
  1.9 1.1 pad_maximum_fusion.1
  3.1 3.9 %collective-permute-start = (bf16[2,128,1024]{2,1,0:T(8,128)(2,1)S(1)}, bf16[2,128,1024]{2,1,0:T(8,128)(2,1)S(1)}, u32[]{:S(2)}, u32[]{:S(2)}) collective-permute-start(bf16[2,128,1024]{2,1,0:T(8,128)(2,1)S(1)} %pad_maximum_fusion.1), channel_id=1, source_target_pairs={{0,8},{8,0},{16,24},{24,16},{1,9},{9,1},{17,25},{25,17},{2,10},{10... | collective-permute-start | bytes 1572872 | tf_op jit(solution)/shard_map/ppermute | solution.py:19
  7.0 0.7 collective-permute-start.1
  7.7 5.9 %collective-permute-done = bf16[2,128,1024]{2,1,0:T(8,128)(2,1)S(1)} collective-permute-done((bf16[2,128,1024]{2,1,0:T(8,128)(2,1)S(1)}, bf16[2,128,1024]{2,1,0:T(8,128)(2,1)S(1)}, u32[]{:S(2)}, u32[]{:S(2)}) %collective-permute-start) | collective-permute-done | bytes 524320 | tf_op jit(solution)/shard_map/ppermute | solution.py:19
  13.8 9.3 %collective-permute-start.2 = (bf16[2,2,128,1024]{3,2,1,0:T(8,128)(2,1)S(1)}, bf16[2,2,128,1024]{3,2,1,0:T(8,128)(2,1)S(1)}, u32[]{:S(2)}, u32[]{:S(2)}) collective-permute-start(bf16[2,2,128,1024]{3,2,1,0:T(8,128)(2,1)S(1)} %pad_maximum_fusion.pair), channel_id=1, source_target_pairs={{0,24},{8,16},{16,8},{24,0},{1,25},{9,17},{17,9},{25,1},{2,26},{10... | collective-permute-start | bytes 3145736 | tf_op jit(solution)/shard_map/ppermute | solution.py:19
  23.1 0.9 broadcast_in_dim.22
  24.0 9.7 %all-to-all-start = ((bf16[64,32,128]{2,1,0:T(8,128)(2,1)}), bf16[64,32,128]{2,1,0:T(8,128)(2,1)S(1)}, u32[]{:S(2)}, u32[]{:S(2)}) async-start(bf16[64,32,128]{2,1,0:T(8,128)(2,1)} %bitcast.12), calls=%async_computation | async-start | bytes 1048576 | tf_op jit(solution)/shard_map/all_to_all | solution.py:97
  33.7 2.4 %collective-permute-start.4 = (bf16[2,2,128,1024]{3,2,1,0:T(8,128)(2,1)S(1)}, bf16[2,2,128,1024]{3,2,1,0:T(8,128)(2,1)}, u32[]{:S(2)}, u32[]{:S(2)}) collective-permute-start(bf16[2,2,128,1024]{3,2,1,0:T(8,128)(2,1)S(1)} %pad_maximum_fusion.pair), channel_id=1, source_target_pairs={{0,4},{4,0},{1,5},{5,1},{2,6},{6,2},{3,7},{7,3},{8,12},{12,8},{9,1... | collective-permute-start | bytes 3145736 | tf_op jit(solution)/shard_map/ppermute | solution.py:19
  36.1 16.2 %all-to-all-done = bf16[64,32,128]{2,1,0:T(8,128)(2,1)S(1)} async-done(((bf16[64,32,128]{2,1,0:T(8,128)(2,1)}), bf16[64,32,128]{2,1,0:T(8,128)(2,1)S(1)}, u32[]{:S(2)}, u32[]{:S(2)}) %all-to-all-start) | async-done | bytes 524320 | tf_op jit(solution)/shard_map/all_to_all | solution.py:97
  52.3 2.3 %collective-permute-start.5 = (bf16[2,2,128,1024]{3,2,1,0:T(8,128)(2,1)S(1)}, bf16[2,2,128,1024]{3,2,1,0:T(8,128)(2,1)}, u32[]{:S(2)}, u32[]{:S(2)}) collective-permute-start(bf16[2,2,128,1024]{3,2,1,0:T(8,128)(2,1)S(1)} %collective-permute-done.2.far), channel_id=1, source_target_pairs={{0,4},{4,0},{1,5},{5,1},{2,6},{6,2},{3,7},{7,3},{8,12},{12,8},{9,1... | collective-permute-start | bytes 3145736 | tf_op jit(solution)/shard_map/ppermute | solution.py:19
  54.6 1.0 copy-done.1
  55.6 4.8 %collective-permute-start.3 = (bf16[2,1024,128]{2,1,0:T(8,128)(2,1)S(1)}, bf16[2,1024,128]{2,1,0:T(8,128)(2,1)S(1)}, u32[]{:S(2)}, u32[]{:S(2)}) collective-permute-start(bf16[2,1024,128]{2,1,0:T(8,128)(2,1)S(1)} %bitcast.25), channel_id=1, source_target_pairs={{0,256},{256,0},{1,257},{257,1},{2,258},{258,2},{3,259},{259,3},{4... | collective-permute-start | bytes 1572872 | tf_op jit(solution)/shard_map/ppermute | solution.py:19
  60.6 12.1 %collective-permute-done.3.far_basis = bf16[2,1024,128]{2,1,0:T(8,128)(2,1)S(1)} collective-permute-done((bf16[2,1024,128]{2,1,0:T(8,128)(2,1)S(1)}, bf16[2,1024,128]{2,1,0:T(8,128)(2,1)S(1)}, u32[]{:S(2)}, u32[]{:S(2)}) %collective-permute-start.3) | collective-permute-done | bytes 524320 | tf_op jit(solution)/shard_map/ppermute | solution.py:19
  72.7 1.2 copy-done.2
  73.9 3.1 %rotate.1 = (f32[4,64,1024]{2,1,0:T(8,128)S(1)}, f32[4,64,1024]{2,1,0:T(8,128)S(1)}, f32[8,128]{1,0:T(8,128)S(1)}) custom-call(s32[3]{0:T(128)S(1)} %pad_add_fusion.place, bf16[2,1024,128]{2,1,0:T(8,128)(2,1)S(1)} %bitcast.26, bf16[2,1024,128]{2,1,0:T(8,128)(2,1)S(1)} %collective-permute-done.3.far_basis, ...), custom_call_target="tpu_custom_call" | custom-call | flops 1073741824 | bytes 8388608 | tf_op jit(solution)/shard_map/rotate/pallas_call | solution.py:55
  77.0 1.0 copy-done
  77.9 0.7 reduce_max.9
  79.4 1.3 multiply_convert_fusion.1
  80.7 1.0 concatenate.17
  81.7 9.8 %all-to-all-start.1 = ((f16[4,80,1024]{2,1,0:T(8,128)(2,1)}), f16[4,80,1024]{2,1,0:T(8,128)(2,1)S(1)}, u32[]{:S(2)}, u32[]{:S(2)}) async-start(f16[4,80,1024]{2,1,0:T(8,128)(2,1)} %concatenate.17), calls=%async_computation.1 | async-start | bytes 1310720 | tf_op jit(solution)/shard_map/all_to_all | solution.py:111
  93.3 0.9 multiply_convert_fusion
  94.2 14.7 %all-to-all-done.1 = f16[4,80,1024]{2,1,0:T(8,128)(2,1)S(1)} async-done(((f16[4,80,1024]{2,1,0:T(8,128)(2,1)}), f16[4,80,1024]{2,1,0:T(8,128)(2,1)S(1)}, u32[]{:S(2)}, u32[]{:S(2)}) %all-to-all-start.1) | async-done | bytes 655392 | tf_op jit(solution)/shard_map/all_to_all | solution.py:111
  108.9 4.5 %all-to-all-start.2 = ((f16[4,64,1024]{2,1,0:T(8,128)(2,1)}), f16[4,64,1024]{2,1,0:T(8,128)(2,1)S(1)}, u32[]{:S(2)}, u32[]{:S(2)}) async-start(f16[4,64,1024]{2,1,0:T(8,128)(2,1)} %multiply_convert_fusion), calls=%async_computation.2 | async-start | bytes 1048576 | tf_op jit(solution)/shard_map/all_to_all | solution.py:113
  113.9 11.2 %all_gather.6 = bf16[256,1024]{1,0:T(8,128)(2,1)S(1)} all-gather(bf16[64,1024]{1,0:T(8,128)(2,1)S(1)} %select_convert_fusion), channel_id=1, replica_groups=mesh['zl'=2,'y'=8,'x'=4,'c'=2,'zh'=4] {'x'}, dimensions={0}, use_global_device_ids=true | all-gather | bytes 655360 | tf_op jit(solution)/shard_map/all_gather | solution.py:121
  125.1 5.7 %collective-permute-start.6 = (bf16[256,1024]{1,0:T(8,128)(2,1)S(1)}, bf16[256,1024]{1,0:T(8,128)(2,1)S(1)}, u32[]{:S(2)}, u32[]{:S(2)}) collective-permute-start(bf16[256,1024]{1,0:T(8,128)(2,1)S(1)} %all_gather.6), channel_id=1, source_target_pairs={{0,4},{4,0},{1,5},{5,1},{2,6},{6,2},{3,7},{7,3},{8,12},{12,8},{9,1... | collective-permute-start | bytes 1572872 | tf_op jit(solution)/shard_map/ppermute | solution.py:19
  131.0 16.3 %all_gather.7 = bf16[256,1024]{1,0:T(8,128)(2,1)S(1)} all-gather(bf16[64,1024]{1,0:T(8,128)(2,1)S(1)} %multiply_reduce_fusion), channel_id=1, replica_groups=mesh['zl'=2,'y'=8,'x'=4,'c'=2,'zh'=4] {'zh'}, dimensions={0}, use_global_device_ids=true | all-gather | bytes 655360 | tf_op jit(solution)/shard_map/all_gather | solution.py:125
  148.0 0.8 copy.19
  148.9 8.2 %all-to-all-start.3 = ((bf16[16,16,512]{2,1,0:T(8,128)(2,1)}), bf16[16,16,512]{2,1,0:T(8,128)(2,1)S(1)}, u32[]{:S(2)}, u32[]{:S(2)}) async-start(bf16[16,16,512]{2,1,0:T(8,128)(2,1)} %bitcast.16), calls=%async_computation.3 | async-start | bytes 524288 | tf_op jit(solution)/shard_map/all_to_all | solution.py:137
  157.0 7.7 %all-to-all-done.3 = bf16[16,16,512]{2,1,0:T(8,128)(2,1)S(1)} async-done(((bf16[16,16,512]{2,1,0:T(8,128)(2,1)}), bf16[16,16,512]{2,1,0:T(8,128)(2,1)S(1)}, u32[]{:S(2)}, u32[]{:S(2)}) %all-to-all-start.3) | async-done | bytes 262176 | tf_op jit(solution)/shard_map/all_to_all | solution.py:137
  164.9 0.6 broadcast_multiply_fusion
  (31 shorter events, 2.5 us)
Async XLA Ops:
  3.1 10.6 %collective-permute-start = (bf16[2,128,1024]{2,1,0:T(8,128)(2,1)S(1)}, bf16[2,128,1024]{2,1,0:T(8,128)(2,1)S(1)}, u32[]{:S(2)}, u32[]{:S(2)}) collective-permute-start(bf16[2,128,1024]{2,1,0:T(8,128)(2,1)S(1)} %pad_maximum_fusion.1), channel_id=1, source_target_pairs={{0,8},{8,0},{16,24},{24,16},{1,9},{9,1},{17,25},{25,17},{2,10},{10... | collective-permute-start | bytes 1572872 | tf_op jit(solution)/shard_map/ppermute | solution.py:19
  7.0 0.7 collective-permute-start.1
  13.8 38.6 %collective-permute-start.2 = (bf16[2,2,128,1024]{3,2,1,0:T(8,128)(2,1)S(1)}, bf16[2,2,128,1024]{3,2,1,0:T(8,128)(2,1)S(1)}, u32[]{:S(2)}, u32[]{:S(2)}) collective-permute-start(bf16[2,2,128,1024]{3,2,1,0:T(8,128)(2,1)S(1)} %pad_maximum_fusion.pair), channel_id=1, source_target_pairs={{0,24},{8,16},{16,8},{24,0},{1,25},{9,17},{17,9},{25,1},{2,26},{10... | collective-permute-start | bytes 3145736 | tf_op jit(solution)/shard_map/ppermute | solution.py:19
  24.0 28.3 %all-to-all-start = ((bf16[64,32,128]{2,1,0:T(8,128)(2,1)}), bf16[64,32,128]{2,1,0:T(8,128)(2,1)S(1)}, u32[]{:S(2)}, u32[]{:S(2)}) async-start(bf16[64,32,128]{2,1,0:T(8,128)(2,1)} %bitcast.12), calls=%async_computation | async-start | bytes 1048576 | tf_op jit(solution)/shard_map/all_to_all | solution.py:97
  33.7 26.8 %collective-permute-start.4 = (bf16[2,2,128,1024]{3,2,1,0:T(8,128)(2,1)S(1)}, bf16[2,2,128,1024]{3,2,1,0:T(8,128)(2,1)}, u32[]{:S(2)}, u32[]{:S(2)}) collective-permute-start(bf16[2,2,128,1024]{3,2,1,0:T(8,128)(2,1)S(1)} %pad_maximum_fusion.pair), channel_id=1, source_target_pairs={{0,4},{4,0},{1,5},{5,1},{2,6},{6,2},{3,7},{7,3},{8,12},{12,8},{9,1... | collective-permute-start | bytes 3145736 | tf_op jit(solution)/shard_map/ppermute | solution.py:19
  52.3 20.3 %collective-permute-start.5 = (bf16[2,2,128,1024]{3,2,1,0:T(8,128)(2,1)S(1)}, bf16[2,2,128,1024]{3,2,1,0:T(8,128)(2,1)}, u32[]{:S(2)}, u32[]{:S(2)}) collective-permute-start(bf16[2,2,128,1024]{3,2,1,0:T(8,128)(2,1)S(1)} %collective-permute-done.2.far), channel_id=1, source_target_pairs={{0,4},{4,0},{1,5},{5,1},{2,6},{6,2},{3,7},{7,3},{8,12},{12,8},{9,1... | collective-permute-start | bytes 3145736 | tf_op jit(solution)/shard_map/ppermute | solution.py:19
  54.6 1.0 copy-start.1
  55.6 17.0 %collective-permute-start.3 = (bf16[2,1024,128]{2,1,0:T(8,128)(2,1)S(1)}, bf16[2,1024,128]{2,1,0:T(8,128)(2,1)S(1)}, u32[]{:S(2)}, u32[]{:S(2)}) collective-permute-start(bf16[2,1024,128]{2,1,0:T(8,128)(2,1)S(1)} %bitcast.25), channel_id=1, source_target_pairs={{0,256},{256,0},{1,257},{257,1},{2,258},{258,2},{3,259},{259,3},{4... | collective-permute-start | bytes 1572872 | tf_op jit(solution)/shard_map/ppermute | solution.py:19
  72.6 1.2 copy-start.2
  76.9 1.0 copy-start
  80.7 10.7 %copy-start.3 = (s32[2]{0:T(128)S(1)}, s32[2]{0:T(128)}, u32[]{:S(2)}) copy-start(s32[2]{0:T(128)} %param.9) | copy-start | bytes 28
  81.7 27.3 %all-to-all-start.1 = ((f16[4,80,1024]{2,1,0:T(8,128)(2,1)}), f16[4,80,1024]{2,1,0:T(8,128)(2,1)S(1)}, u32[]{:S(2)}, u32[]{:S(2)}) async-start(f16[4,80,1024]{2,1,0:T(8,128)(2,1)} %concatenate.17), calls=%async_computation.1 | async-start | bytes 1310720 | tf_op jit(solution)/shard_map/all_to_all | solution.py:111
  108.9 16.2 %all-to-all-start.2 = ((f16[4,64,1024]{2,1,0:T(8,128)(2,1)}), f16[4,64,1024]{2,1,0:T(8,128)(2,1)S(1)}, u32[]{:S(2)}, u32[]{:S(2)}) async-start(f16[4,64,1024]{2,1,0:T(8,128)(2,1)} %multiply_convert_fusion), calls=%async_computation.2 | async-start | bytes 1048576 | tf_op jit(solution)/shard_map/all_to_all | solution.py:113
  125.1 22.5 %collective-permute-start.6 = (bf16[256,1024]{1,0:T(8,128)(2,1)S(1)}, bf16[256,1024]{1,0:T(8,128)(2,1)S(1)}, u32[]{:S(2)}, u32[]{:S(2)}) collective-permute-start(bf16[256,1024]{1,0:T(8,128)(2,1)S(1)} %all_gather.6), channel_id=1, source_target_pairs={{0,4},{4,0},{1,5},{5,1},{2,6},{6,2},{3,7},{7,3},{8,12},{12,8},{9,1... | collective-permute-start | bytes 1572872 | tf_op jit(solution)/shard_map/ppermute | solution.py:19
  148.9 15.9 %all-to-all-start.3 = ((bf16[16,16,512]{2,1,0:T(8,128)(2,1)}), bf16[16,16,512]{2,1,0:T(8,128)(2,1)S(1)}, u32[]{:S(2)}, u32[]{:S(2)}) async-start(bf16[16,16,512]{2,1,0:T(8,128)(2,1)} %bitcast.16), calls=%async_computation.3 | async-start | bytes 524288 | tf_op jit(solution)/shard_map/all_to_all | solution.py:137

commit v5 on v1

v5 whole, which is shorter than its diff:
```python
import jax
import jax.numpy as jnp
from jax import lax
from jax.experimental import pallas as pl
from jax.experimental.pallas import tpu as pltpu
from jax.sharding import Mesh
from jax.sharding import PartitionSpec as P

SEQS = 2
F32 = jnp.float32
BF16 = jnp.bfloat16
F16 = jnp.float16
TILE = 16
TOP = 15
VMEM = pl.BlockSpec(memory_space=pltpu.VMEM)
SMEM = pl.BlockSpec(memory_space=pltpu.SMEM)


def shift(value, axis, step):
    n = lax.axis_size(axis)
    return lax.ppermute(value, axis, [(i, (i + step) % n) for i in range(n)])


def spread(value, outer, n_x, inner, run):
    width = value.shape[1]
    source = lax.broadcasted_iota(jnp.int32, (width, width), 0)
    target = lax.broadcasted_iota(jnp.int32, (width, width), 1)
    at_run, at_inner = source % run, source // run % inner
    at_x, at_outer = source // (run * inner) % n_x, source // (run * inner * n_x)
    moved = ((at_x * inner + at_inner) * outer + at_outer) * run + at_run
    ones = (moved == target).astype(F32).astype(BF16)
    return jnp.dot(value, ones, preferred_element_type=F32).astype(BF16)


def prepare_kernel(y_lo, n_c, act, grad, basis_act, basis_grad, tokens, bases):
    n_x, _, toks, width = tokens.shape
    rows = basis_act.shape[0]
    both = jnp.concatenate([act[...], grad[...]], axis=0)
    both = spread(both, y_lo, n_x, n_c, width // (y_lo * n_c))
    for x in range(n_x):
        for which in range(2):
            tokens[x, which] = both[which * toks : (which + 1) * toks, x * width : (x + 1) * width]
    bases[0] = basis_act[...]
    bases[1] = spread(basis_grad[...], y_lo, n_x, 1, basis_grad.shape[1] // (y_lo * n_x))


def prepare(y_lo, n_x, n_c, act, grad, basis_act, basis_grad):
    toks, feats = act.shape
    return pl.pallas_call(
        lambda *refs: prepare_kernel(y_lo, n_c, *refs),
        out_shape=(
            jax.ShapeDtypeStruct((n_x, 2, toks, feats // n_x), BF16),
            jax.ShapeDtypeStruct((2, *basis_act.shape), BF16),
        ),
        in_specs=[VMEM] * 4,
        out_specs=(VMEM, VMEM),
        compiler_params=pltpu.CompilerParams(vmem_limit_bytes=32 * 2**20),
        cost_estimate=pl.CostEstimate(
            flops=4 * toks * feats * feats, bytes_accessed=2**20, transcendentals=0
        ),
        name="prepare",
    )(act, grad, basis_act, basis_grad)


def rotate_kernel(place, mine, up, down, far_act, far_grad, basis, core_basis, out):
    n_x, _, toks, width = mine.shape
    rows, cols = basis.shape[2], basis.shape[3]
    n_zh = 4
    per, half = basis.shape[0] // n_zh, width // 2
    zh, c = place[0], place[1]
    near, far = (pl.ds(pl.multiple_of(core * half, half), half) for core in (c, 1 - c))
    sums = []
    for which in range(2):
        total = None
        for step, block in enumerate((mine, down, None, up)):
            owner = pl.ds(((zh + step) % n_zh) * per, per)
            left = []
            for lanes in (near, far):
                if block is None:
                    piece = (far_act, far_grad)[which][:, :, lanes]
                else:
                    piece = block[:, which, :, lanes]
                left.append(piece.reshape(n_x * toks, half))
            right = [b[owner, which].reshape(per * rows, cols) for b in (basis, core_basis)]
            product = jnp.dot(
                jnp.concatenate(left, axis=1),
                jnp.concatenate(right, axis=0),
                preferred_element_type=F32,
            )
            total = product if total is None else total + product
        sums.append(total)
    largest = jnp.max(jnp.maximum(jnp.abs(sums[0]), jnp.abs(sums[1])), axis=0, keepdims=True)
    largest = jnp.max(largest, axis=1, keepdims=True)
    level = jnp.clip(jnp.ceil(jnp.log2(jnp.maximum(largest, 1e-30))), -100.0, 100.0)
    factor = jnp.exp2(F32(TOP) - level)
    group, part = n_x * toks, cols // n_x
    for x in range(n_x):
        for which in range(2):
            value = sums[which][:, x * part : (x + 1) * part] * factor
            out[x, pl.ds(which * group, group)] = value
        out[x, pl.ds(2 * group, TILE)] = jnp.broadcast_to(level, (TILE, part))


def rotate(place, *arrays):
    n_x, _, toks, width = arrays[0].shape
    cols = arrays[-1].shape[3]
    return pl.pallas_call(
        rotate_kernel,
        out_shape=jax.ShapeDtypeStruct((n_x, 2 * n_x * toks + TILE, cols // n_x), F32),
        in_specs=[SMEM] + [VMEM] * len(arrays),
        out_specs=VMEM,
        compiler_params=pltpu.CompilerParams(vmem_limit_bytes=40 * 2**20),
        cost_estimate=pl.CostEstimate(
            flops=16 * n_x * toks * width * cols, bytes_accessed=8 * 2**20, transcendentals=0
        ),
        name="rotate",
    )(place, *arrays)


def on_device(activations, gradients, basis_act, basis_grad, lengths):
    n_zl, n_y, n_x, n_c, n_zh = (lax.axis_size(a) for a in ("zl", "y", "x", "c", "zh"))
    zl, y, c, zh = (lax.axis_index(a) for a in ("zl", "y", "c", "zh"))
    toks = activations.shape[0]
    rows, cols = basis_act.shape
    part, group = cols // n_x, n_x * toks

    tokens, bases = prepare(n_y // 2, n_x, n_c, activations, gradients, basis_act, basis_grad)
    mine = lax.all_to_all(tokens, "x", 0, 0, tiled=True)
    mine, bases = lax.optimization_barrier((mine, bases))
    up, down = shift(mine, "zh", 1), shift(mine, "zh", -1)
    far_act, far_grad = shift(up[:, 0], "zh", 1), shift(down[:, 1], "zh", -1)

    copies = jnp.broadcast_to(bases[None], (n_zl * n_y, *bases.shape))
    basis = lax.all_to_all(copies, ("zl", "y"), 0, 0, tiled=True)
    core_basis = shift(basis, "c", 1)

    place = jnp.stack([zh, c]).astype(jnp.int32)
    partial = rotate(place, mine, up, down, far_act, far_grad, basis, core_basis)
    partial = lax.all_to_all(partial.astype(F16), "x", 0, 0, tiled=True).astype(F32)
    factors = jnp.exp2(partial[:, 2 * group :, :] - F32(TOP))[:, :1, :1]
    rotated = jnp.sum(partial[:, : 2 * group] * factors, axis=0)
    index = jnp.arange(group, dtype=jnp.int32)
    position = ((y * n_x + index // toks) * n_c + c) * toks + index % toks
    length = jnp.where(zl == 0, lengths[0], lengths[1])
    valid = position < length
    rot_act = jnp.where(valid[:, None], rotated[:group], F32(0.0)).astype(BF16)
    rot_grad = rotated[group:].astype(BF16)

    wide_act = lax.all_to_all(
        jnp.broadcast_to(rot_act[None], (n_x, group, part)), "x", 0, 0, tiled=True
    )
    wide_grad = lax.all_gather(rot_grad, "zh", axis=0)
    share = jnp.einsum("ktg,xta->kgxa", wide_grad, wide_act, preferred_element_type=F32)
    share = share.astype(BF16).reshape(n_zl * n_y * n_c, -1, cols)
    received = lax.all_to_all(share, ("zl", "y", "c"), 0, 0, tiled=True)
    received = received.astype(F32).reshape(SEQS, n_y * n_c, -1, cols)
    per_seq = jnp.sum(received, axis=1)
    scale = lengths.astype(F32)[:, None, None]
    return jnp.sum(per_seq * per_seq / scale, axis=0) / F32(SEQS)


def solution(mesh):
    split = Mesh(mesh.devices.reshape(2, 8, 4, 2, 4), ("zl", "y", "x", "c", "zh"))
    spec = P(("zl", "y", "x", "c"), "zh")
    return jax.shard_map(
        on_device, mesh=split, in_specs=(spec, spec, spec, spec, P()), out_specs=spec, check_vma=False
    )
```

time: 190 us -> 181 us (0.953)
  blocking collectives: 86.6 us -> 24.9 us
  starting transfers between devices: 18.5 us -> 60.5 us
  waiting for transfers between devices: 54.2 us -> 73.3 us
  between operations: 14.8 us -> 1.48 us
  local copies, waits for them, and re-layouts: 3.02 us -> 12.7 us
  matrix products: 5.87 us -> 0.46 us
  Pallas kernels: 0 us -> 3.07 us
    all_to_all x1, blocking collectives: 59.5 us -> 11.6 us  [on_device(): mine = lax.all_to_all(tokens, 'x', 0, 0, tiled=True)]
    ppermute x1 -> x5, waiting for transfers between devices: 0.01 us -> 30.9 us  [shift(): return lax.ppermute(value, axis, [(i, (i + step) % n) for i in range(n)])]
    ppermute x1 -> x5, starting transfers between devices: 0.66 us -> 28.6 us  [shift(): return lax.ppermute(value, axis, [(i, (i + step) % n) for i in range(n)])]
    all_to_all x3 -> x4, starting transfers between devices: 17.8 us -> 31.9 us  [the longest x1 14.5 us: on_device(): received = lax.all_to_all(share, ('zl', 'y', 'c'), 0, 0, tiled=True)]
    all_gather x2 -> x1, blocking collectives: 27.1 us -> 13.3 us  [on_device(): wide_grad = lax.all_gather(rot_grad, 'zh', axis=0)]
    all_to_all x3 -> x4, waiting for transfers between devices: 54.2 us -> 42.5 us  [the longest x1 16.6 us: on_device(): received = lax.all_to_all(share, ('zl', 'y', 'c'), 0, 0, tiled=True)]
    dot_general x3 -> x1, matrix products: 5.87 us -> 0.46 us  [on_device(): jnp.einsum('ktg,xta->kgxa', wide_grad, wide_act, preferred_element_type=F32)]
    unnamed x7 -> x14, local copies, waits for them, and re-layouts: 0.89 us -> 4.98 us
  transfers between devices with their start and end apart: 5 -> 9, of which waited for: 2 -> 5; matrix products, arithmetic and copies ran while one was open for 1% -> 3% of each run, Pallas kernels for 0% -> 0%
where the time goes in v5:
time: 181 us; the launch traced here: 179 us
  waiting for transfers between devices  73.3 us (40%)
  starting transfers between devices  60.5 us (33%)
  blocking collectives  24.9 us (14%)
  local copies, waits for them, and re-layouts  12.7 us (7%)
  Pallas kernels  3.07 us (2%)
  other arithmetic  2.6 us (1%)
    ppermute x5, waiting for transfers between devices, shift(): return lax.ppermute(value, axis, [(i, (i + step) % n) for i in range(n)])  30.9 us
    ppermute x5, starting transfers between devices, shift(): return lax.ppermute(value, axis, [(i, (i + step) % n) for i in range(n)])  28.6 us
    all_to_all x1, waiting for transfers between devices, on_device(): received = lax.all_to_all(share, ('zl', 'y', 'c'), 0, 0, tiled=True)  16.6 us
    all_to_all x1, starting transfers between devices, on_device(): received = lax.all_to_all(share, ('zl', 'y', 'c'), 0, 0, tiled=True)  14.5 us
    all_to_all x1, waiting for transfers between devices, on_device(): basis = lax.all_to_all(copies, ('zl', 'y'), 0, 0, tiled=True)  14.4 us
    all_gather x1, blocking collectives, on_device(): wide_grad = lax.all_gather(rot_grad, 'zh', axis=0)  13.3 us
    all_to_all x1, blocking collectives, on_device(): mine = lax.all_to_all(tokens, 'x', 0, 0, tiled=True)  11.6 us
    all_to_all x1, waiting for transfers between devices, on_device(): lax.all_to_all(partial.astype(F16), 'x', 0, 0, tiled=True).astype(F32)  11.5 us
  transfers between devices with their start and end apart: 9, of which 5 were waited for; matrix products, arithmetic and copies ran while one was open for 3% of the time, Pallas kernels for 0%

profile of v5, /device:TPU:1, one launch (start us, length us, event | category | flops | bytes accessed | tf_op | source)
XLA Modules:
  0.0 179.1 jit_solution(4398922888831133530)
XLA Ops:
  0.0 0.9 copy-done
  1.0 0.9 copy-done.1
  1.9 0.8 copy-done.2
  2.7 0.8 copy-done.3
  3.4 1.0 prepare.1
  4.4 11.6 %all_to_all.25.mine = bf16[4,2,128,256]{3,2,1,0:T(8,128)(2,1)S(1)} all-to-all(bf16[4,2,128,256]{3,2,1,0:T(8,128)(2,1)S(1)} %get-tuple-element.9), channel_id=1, replica_groups=mesh['zl'=2,'y'=8,'x'=4,'c'=2,'zh'=4] {'x'}, dimensions={0} | all-to-all | bytes 1048576 | tf_op jit(solution)/shard_map/all_to_all | solution.py:128
  16.0 1.1 broadcast_in_dim.16
  17.1 10.4 %all-to-all-start.1 = ((bf16[16,2,32,512]{3,2,1,0:T(8,128)(2,1)}), bf16[16,2,32,512]{3,2,1,0:T(8,128)(2,1)S(1)}, u32[]{:S(2)}, u32[]{:S(2)}) async-start(bf16[16,2,32,512]{3,2,1,0:T(8,128)(2,1)} %broadcast_in_dim.16), calls=%async_computation.1 | async-start | bytes 2097152 | tf_op jit(solution)/shard_map/all_to_all | solution.py:134
  27.5 0.9 copy.22
  28.3 9.8 %collective-permute-start.1 = (bf16[4,2,128,256]{3,2,0,1:T(8,128)(2,1)}, bf16[4,2,128,256]{3,2,0,1:T(8,128)(2,1)S(1)}, u32[]{:S(2)}, u32[]{:S(2)}) collective-permute-start(bf16[4,2,128,256]{3,2,0,1:T(8,128)(2,1)} %copy.22), channel_id=1, source_target_pairs={{0,3},{1,0},{2,1},{3,2},{4,7},{5,4},{6,5},{7,6},{8,11},{9,8},{10,9... | collective-permute-start | bytes 1572872 | tf_op jit(solution)/shard_map/ppermute | solution.py:21
  38.1 14.4 %all-to-all-done.1.basis = bf16[16,2,32,512]{3,2,1,0:T(8,128)(2,1)S(1)} async-done(((bf16[16,2,32,512]{3,2,1,0:T(8,128)(2,1)}), bf16[16,2,32,512]{3,2,1,0:T(8,128)(2,1)S(1)}, u32[]{:S(2)}, u32[]{:S(2)}) %all-to-all-start.1) | async-done | bytes 1048608 | tf_op jit(solution)/shard_map/all_to_all | solution.py:134
  52.5 4.8 %collective-permute-start.4 = (bf16[16,2,32,512]{3,2,1,0:T(8,128)(2,1)S(1)}, bf16[16,2,32,512]{3,2,1,0:T(8,128)(2,1)S(1)}, u32[]{:S(2)}, u32[]{:S(2)}) collective-permute-start(bf16[16,2,32,512]{3,2,1,0:T(8,128)(2,1)S(1)} %all-to-all-done.1.basis), channel_id=1, source_target_pairs={{0,4},{4,0},{1,5},{5,1},{2,6},{6,2},{3,7},{7,3},{8,12},{12,8},{9,1... | collective-permute-start | bytes 3145736 | tf_op jit(solution)/shard_map/ppermute | solution.py:21
  57.3 6.2 %collective-permute-start = (bf16[4,2,128,256]{3,2,0,1:T(8,128)(2,1)}, bf16[4,2,128,256]{3,2,0,1:T(8,128)(2,1)S(1)}, u32[]{:S(2)}, u32[]{:S(2)}) collective-permute-start(bf16[4,2,128,256]{3,2,0,1:T(8,128)(2,1)} %copy.22), channel_id=1, source_target_pairs={{0,1},{1,2},{2,3},{3,0},{4,5},{5,6},{6,7},{7,4},{8,9},{9,10},{10,1... | collective-permute-start | bytes 1572872 | tf_op jit(solution)/shard_map/ppermute | solution.py:21
  63.5 0.8 copy-done.4
  64.3 6.0 %collective-permute-start.3 = (bf16[4,128,256]{2,1,0:T(8,128)(2,1)S(1)}, bf16[4,128,256]{2,1,0:T(8,128)(2,1)S(1)}, u32[]{:S(2)}, u32[]{:S(2)}) collective-permute-start(bf16[4,128,256]{2,1,0:T(8,128)(2,1)S(1)} %slice_bitcast_fusion), channel_id=1, source_target_pairs={{0,3},{1,0},{2,1},{3,2},{4,7},{5,4},{6,5},{7,6},{8,11},{9,8},{10,9... | collective-permute-start | bytes 786440 | tf_op jit(solution)/shard_map/ppermute | solution.py:21
  70.3 21.1 %collective-permute-done = bf16[4,2,128,256]{3,2,0,1:T(8,128)(2,1)S(1)} collective-permute-done((bf16[4,2,128,256]{3,2,0,1:T(8,128)(2,1)}, bf16[4,2,128,256]{3,2,0,1:T(8,128)(2,1)S(1)}, u32[]{:S(2)}, u32[]{:S(2)}) %collective-permute-start) | collective-permute-done | bytes 524320 | tf_op jit(solution)/shard_map/ppermute | solution.py:21
  91.4 0.8 copy-done.5
  92.1 0.7 slice_bitcast_fusion.1
  92.9 1.9 %collective-permute-start.2 = (bf16[4,128,256]{2,1,0:T(8,128)(2,1)}, bf16[4,128,256]{2,1,0:T(8,128)(2,1)S(1)}, u32[]{:S(2)}, u32[]{:S(2)}) collective-permute-start(bf16[4,128,256]{2,1,0:T(8,128)(2,1)} %slice_bitcast_fusion.1), channel_id=1, source_target_pairs={{0,1},{1,2},{2,3},{3,0},{4,5},{5,6},{6,7},{7,4},{8,9},{9,10},{10,1... | collective-permute-start | bytes 786440 | tf_op jit(solution)/shard_map/ppermute | solution.py:21
  94.9 1.1 copy.25.down
  95.9 1.1 copy.24.up
  97.0 9.7 %collective-permute-done.2.far_act = bf16[4,128,256]{2,1,0:T(8,128)(2,1)S(1)} collective-permute-done((bf16[4,128,256]{2,1,0:T(8,128)(2,1)}, bf16[4,128,256]{2,1,0:T(8,128)(2,1)S(1)}, u32[]{:S(2)}, u32[]{:S(2)}) %collective-permute-start.2) | collective-permute-done | bytes 262176 | tf_op jit(solution)/shard_map/ppermute | solution.py:21
  106.8 2.1 %rotate.1 = f32[4,1040,128]{2,1,0:T(8,128)S(1)} custom-call(s32[2]{0:T(128)S(1)} %pad_add_fusion.place, bf16[4,2,128,256]{3,2,1,0:T(8,128)(2,1)S(1)} %all_to_all.25.mine, bf16[4,2,128,256]{3,2,1,0:T(8,128)(2,1)S(1)} %copy.24.up, bf16[4,2,128,256]{3,2,1,0:T(8,128)(2,1)S(1)} %copy.25.down, bf16[4,128,256]{2,1,0:T(8,128)(2,1)S(1)} %collective-permute-done.2.far_act, ...), custom_call_target="tpu_custom_call" | custom-call | flops 1073741824 | bytes 8388608 | tf_op jit(solution)/shard_map/rotate/pallas_call | solution.py:107
  108.9 1.1 convert_element_type.17
  110.0 3.5 %all-to-all-start.2 = ((f16[4,1040,128]{2,1,0:T(8,128)(2,1)}), f16[4,1040,128]{2,1,0:T(8,128)(2,1)S(1)}, u32[]{:S(2)}, u32[]{:S(2)}) async-start(f16[4,1040,128]{2,1,0:T(8,128)(2,1)} %convert_element_type.17), calls=%async_computation.2 | async-start | bytes 2129920 | tf_op jit(solution)/shard_map/all_to_all | solution.py:139
  115.5 11.5 %all-to-all-done.2 = f16[4,1040,128]{2,1,0:T(8,128)(2,1)S(1)} async-done(((f16[4,1040,128]{2,1,0:T(8,128)(2,1)}), f16[4,1040,128]{2,1,0:T(8,128)(2,1)S(1)}, u32[]{:S(2)}, u32[]{:S(2)}) %all-to-all-start.2) | async-done | bytes 1064992 | tf_op jit(solution)/shard_map/all_to_all | solution.py:139
  127.6 0.9 broadcast_in_dim.29
  128.5 3.5 %all-to-all-start.3 = ((bf16[4,512,128]{2,1,0:T(8,128)(2,1)}), bf16[4,512,128]{2,1,0:T(8,128)(2,1)S(1)}, u32[]{:S(2)}, u32[]{:S(2)}) async-start(bf16[4,512,128]{2,1,0:T(8,128)(2,1)} %broadcast_in_dim.29), calls=%async_computation.3 | async-start | bytes 1048576 | tf_op jit(solution)/shard_map/all_to_all | solution.py:149
  132.0 13.3 %all-gather = bf16[2048,128]{1,0:T(8,128)(2,1)S(1)} all-gather(bf16[512,128]{1,0:T(8,128)(2,1)S(1)} %get-tuple-element.14), channel_id=2, replica_groups=mesh['zl'=2,'y'=8,'x'=4,'c'=2,'zh'=4] {'zh'}, dimensions={0}, use_global_device_ids=true | all-gather | bytes 655360 | tf_op jit(solution)/shard_map/all_gather | solution.py:152
  146.2 1.0 reshape.38
  147.2 14.5 %all-to-all-start.4 = ((bf16[32,16,512]{2,1,0:T(8,128)(2,1)}), bf16[32,16,512]{2,1,0:T(8,128)(2,1)S(1)}, u32[]{:S(2)}, u32[]{:S(2)}) async-start(bf16[32,16,512]{2,1,0:T(8,128)(2,1)} %reshape.38), calls=%async_computation.4 | async-start | bytes 1048576 | tf_op jit(solution)/shard_map/all_to_all | solution.py:155
  161.7 16.6 %all-to-all-done.4 = bf16[32,16,512]{2,1,0:T(8,128)(2,1)S(1)} async-done(((bf16[32,16,512]{2,1,0:T(8,128)(2,1)}), bf16[32,16,512]{2,1,0:T(8,128)(2,1)S(1)}, u32[]{:S(2)}, u32[]{:S(2)}) %all-to-all-start.4) | async-done | bytes 524320 | tf_op jit(solution)/shard_map/all_to_all | solution.py:155
  (27 shorter events, 3.1 us)
Async XLA Ops:
  0.0 0.9 copy-start
  1.0 0.9 copy-start.1
  1.9 0.8 copy-start.2
  2.7 0.8 copy-start.3
  17.1 35.4 %all-to-all-start.1 = ((bf16[16,2,32,512]{3,2,1,0:T(8,128)(2,1)}), bf16[16,2,32,512]{3,2,1,0:T(8,128)(2,1)S(1)}, u32[]{:S(2)}, u32[]{:S(2)}) async-start(bf16[16,2,32,512]{3,2,1,0:T(8,128)(2,1)} %broadcast_in_dim.16), calls=%async_computation.1 | async-start | bytes 2097152 | tf_op jit(solution)/shard_map/all_to_all | solution.py:134
  28.3 35.1 %collective-permute-start.1 = (bf16[4,2,128,256]{3,2,0,1:T(8,128)(2,1)}, bf16[4,2,128,256]{3,2,0,1:T(8,128)(2,1)S(1)}, u32[]{:S(2)}, u32[]{:S(2)}) collective-permute-start(bf16[4,2,128,256]{3,2,0,1:T(8,128)(2,1)} %copy.22), channel_id=1, source_target_pairs={{0,3},{1,0},{2,1},{3,2},{4,7},{5,4},{6,5},{7,6},{8,11},{9,8},{10,9... | collective-permute-start | bytes 1572872 | tf_op jit(solution)/shard_map/ppermute | solution.py:21
  52.5 54.3 %collective-permute-start.4 = (bf16[16,2,32,512]{3,2,1,0:T(8,128)(2,1)S(1)}, bf16[16,2,32,512]{3,2,1,0:T(8,128)(2,1)S(1)}, u32[]{:S(2)}, u32[]{:S(2)}) collective-permute-start(bf16[16,2,32,512]{3,2,1,0:T(8,128)(2,1)S(1)} %all-to-all-done.1.basis), channel_id=1, source_target_pairs={{0,4},{4,0},{1,5},{5,1},{2,6},{6,2},{3,7},{7,3},{8,12},{12,8},{9,1... | collective-permute-start | bytes 3145736 | tf_op jit(solution)/shard_map/ppermute | solution.py:21
  57.3 34.1 %collective-permute-start = (bf16[4,2,128,256]{3,2,0,1:T(8,128)(2,1)}, bf16[4,2,128,256]{3,2,0,1:T(8,128)(2,1)S(1)}, u32[]{:S(2)}, u32[]{:S(2)}) collective-permute-start(bf16[4,2,128,256]{3,2,0,1:T(8,128)(2,1)} %copy.22), channel_id=1, source_target_pairs={{0,1},{1,2},{2,3},{3,0},{4,5},{5,6},{6,7},{7,4},{8,9},{9,10},{10,1... | collective-permute-start | bytes 1572872 | tf_op jit(solution)/shard_map/ppermute | solution.py:21
  63.5 0.8 copy-start.4
  64.3 32.8 %collective-permute-start.3 = (bf16[4,128,256]{2,1,0:T(8,128)(2,1)S(1)}, bf16[4,128,256]{2,1,0:T(8,128)(2,1)S(1)}, u32[]{:S(2)}, u32[]{:S(2)}) collective-permute-start(bf16[4,128,256]{2,1,0:T(8,128)(2,1)S(1)} %slice_bitcast_fusion), channel_id=1, source_target_pairs={{0,3},{1,0},{2,1},{3,2},{4,7},{5,4},{6,5},{7,6},{8,11},{9,8},{10,9... | collective-permute-start | bytes 786440 | tf_op jit(solution)/shard_map/ppermute | solution.py:21
  91.4 0.8 copy-start.5
  92.9 13.9 %collective-permute-start.2 = (bf16[4,128,256]{2,1,0:T(8,128)(2,1)}, bf16[4,128,256]{2,1,0:T(8,128)(2,1)S(1)}, u32[]{:S(2)}, u32[]{:S(2)}) collective-permute-start(bf16[4,128,256]{2,1,0:T(8,128)(2,1)} %slice_bitcast_fusion.1), channel_id=1, source_target_pairs={{0,1},{1,2},{2,3},{3,0},{4,5},{5,6},{6,7},{7,4},{8,9},{9,10},{10,1... | collective-permute-start | bytes 786440 | tf_op jit(solution)/shard_map/ppermute | solution.py:21
  108.9 4.7 %copy-start.6 = (s32[2]{0:T(128)S(1)}, s32[2]{0:T(128)}, u32[]{:S(2)}) copy-start(s32[2]{0:T(128)} %param.9) | copy-start | bytes 28
  110.0 17.0 %all-to-all-start.2 = ((f16[4,1040,128]{2,1,0:T(8,128)(2,1)}), f16[4,1040,128]{2,1,0:T(8,128)(2,1)S(1)}, u32[]{:S(2)}, u32[]{:S(2)}) async-start(f16[4,1040,128]{2,1,0:T(8,128)(2,1)} %convert_element_type.17), calls=%async_computation.2 | async-start | bytes 2129920 | tf_op jit(solution)/shard_map/all_to_all | solution.py:139
  128.5 16.8 %all-to-all-start.3 = ((bf16[4,512,128]{2,1,0:T(8,128)(2,1)}), bf16[4,512,128]{2,1,0:T(8,128)(2,1)S(1)}, u32[]{:S(2)}, u32[]{:S(2)}) async-start(bf16[4,512,128]{2,1,0:T(8,128)(2,1)} %broadcast_in_dim.29), calls=%async_computation.3 | async-start | bytes 1048576 | tf_op jit(solution)/shard_map/all_to_all | solution.py:149
  147.2 31.1 %all-to-all-start.4 = ((bf16[32,16,512]{2,1,0:T(8,128)(2,1)}), bf16[32,16,512]{2,1,0:T(8,128)(2,1)S(1)}, u32[]{:S(2)}, u32[]{:S(2)}) async-start(bf16[32,16,512]{2,1,0:T(8,128)(2,1)} %reshape.38), calls=%async_computation.4 | async-start | bytes 1048576 | tf_op jit(solution)/shard_map/all_to_all | solution.py:155

commit v6 on v1

v6 whole, which is shorter than its diff:
```python
import jax
import jax.numpy as jnp
from jax import lax
from jax.experimental import pallas as pl
from jax.experimental.pallas import tpu as pltpu
from jax.sharding import Mesh
from jax.sharding import PartitionSpec as P

SEQS = 2
F32 = jnp.float32
BF16 = jnp.bfloat16
F16 = jnp.float16
TILE = 16
ROWS = 32
XORS = (0, 1, 3, 2)
TOP = 15
VMEM = pl.BlockSpec(memory_space=pltpu.VMEM)
SMEM = pl.BlockSpec(memory_space=pltpu.SMEM)


def send(value, axis, target):
    return lax.ppermute(value, axis, [(i, target(i)) for i in range(lax.axis_size(axis))])


def prepare_kernel(act_hbm, grad_hbm, act_out, grad_out, held, sems):
    copies = [
        pltpu.make_async_copy(ref, held.at[i], sems.at[i]) for i, ref in enumerate((act_hbm, grad_hbm))
    ]
    for copy in copies:
        copy.start()
    n_x, _, part = act_out.shape
    cols = held.shape[2]
    lines = part // n_x
    source = lax.broadcasted_iota(jnp.int32, (cols, cols), 0)
    target = lax.broadcasted_iota(jnp.int32, (cols, cols), 1)
    upper = source // lines
    moved = (upper % n_x * n_x + upper // n_x) * lines + source % lines
    ones = (moved == target).astype(F32).astype(BF16)
    copies[0].wait()
    for x in range(n_x):
        act_out[x] = held[0, :, x * part : (x + 1) * part]
    copies[1].wait()
    grad = jnp.dot(held[1], ones, preferred_element_type=F32).astype(BF16)
    for x in range(n_x):
        grad_out[x] = grad[:, x * part : (x + 1) * part]


def prepare(n_x, act, grad):
    rows, cols = act.shape
    hbm = pl.BlockSpec(memory_space=pl.ANY)
    out = jax.ShapeDtypeStruct((n_x, rows, cols // n_x), BF16)
    return pl.pallas_call(
        prepare_kernel,
        out_shape=(out, out),
        in_specs=[hbm, hbm],
        out_specs=(VMEM, VMEM),
        scratch_shapes=[pltpu.VMEM((2, rows, cols), BF16), pltpu.SemaphoreType.DMA((2,))],
        compiler_params=pltpu.CompilerParams(vmem_limit_bytes=32 * 2**20),
        cost_estimate=pl.CostEstimate(
            flops=2 * rows * cols * cols, bytes_accessed=2**17, transcendentals=0
        ),
        name="prepare",
    )(act, grad)


def rotate_kernel(which, place, pair, far, basis, core_basis, out, whole):
    n_k, _, part = basis.shape
    toks = pair.shape[2]
    group = 2 * pair.shape[0] * toks
    rows = ROWS
    x, c, zh = place[0], place[1], place[2]
    for k in range(n_k):
        for i in range(basis.shape[1] // rows):
            for ref, core in ((basis, c), (core_basis, 1 - c)):
                at = pl.ds(pl.multiple_of((2 * i + core) * rows, rows), rows)
                whole[at, pl.ds(k * part, part)] = ref[k, pl.ds(i * rows, rows)]
    largest = jnp.zeros((toks, n_k * part), F32)
    for slot, xor in enumerate(XORS):
        tokens = (pair, far)[slot // 2][slot % 2, which]
        value = jnp.dot(tokens, whole[...], preferred_element_type=F32)
        largest = jnp.maximum(largest, jnp.abs(value))
        at = pl.ds(pl.multiple_of((x ^ xor) * toks, toks), toks)
        for k in range(n_k):
            out[(k - zh) % n_k if which == 0 else k, at] = value[:, k * part : (k + 1) * part]
    largest = jnp.max(jnp.max(largest, axis=0, keepdims=True), axis=1, keepdims=True)
    level = jnp.clip(jnp.ceil(jnp.log2(jnp.maximum(largest, 1e-30))), -100.0, 100.0)
    factor = jnp.exp2(TOP - level)
    for k in range(n_k):
        out[k, pl.ds(0, group)] = out[k, pl.ds(0, group)] * factor
        out[k, pl.ds(group, TILE)] = jnp.broadcast_to(level, (TILE, part))


def rotate(which, place, pair, far, basis, core_basis):
    n_k, depth, part = basis.shape
    group = 4 * pair.shape[2]
    return pl.pallas_call(
        lambda *refs: rotate_kernel(which, *refs),
        out_shape=jax.ShapeDtypeStruct((n_k, group + TILE, part), F32),
        in_specs=[SMEM] + [VMEM] * 4,
        out_specs=VMEM,
        scratch_shapes=[pltpu.VMEM((2 * depth, n_k * part), BF16)],
        compiler_params=pltpu.CompilerParams(vmem_limit_bytes=32 * 2**20),
        cost_estimate=pl.CostEstimate(
            flops=4 * depth * n_k * part * group, bytes_accessed=4 * 2**20, transcendentals=0
        ),
        name="rotate",
    )(place, pair, far, basis, core_basis)


def on_device(activations, gradients, basis_act, basis_grad, lengths):
    n_zl, n_y, n_x, n_c, n_zh = (lax.axis_size(a) for a in ("zl", "y", "x", "c", "zh"))
    zl, y, x, c, zh = (lax.axis_index(a) for a in ("zl", "y", "x", "c", "zh"))
    y_lo = n_y // 2
    toks = activations.shape[0]
    rows, cols = basis_act.shape
    part, group = cols // n_x, n_x * toks

    pieces = jnp.stack(prepare(n_x, basis_act, basis_grad))
    swap = []
    for q in range(n_zh):
        for low in range(y_lo):
            for h in range(n_zh):
                swap.append((((q * y_lo) + low) * n_zh + h, ((h * y_lo) + low) * n_zh + q))
    pieces = lax.ppermute(pieces, ("zl", "y", "zh"), swap)

    own = jnp.stack([activations, gradients])
    near = send(own, "x", lambda i: i ^ 1)
    near, pieces = lax.optimization_barrier((near, pieces))
    pair = jnp.stack([own, near])
    far = send(pair, "x", lambda i: n_x - 1 - i)

    def spread(value):
        value = jnp.broadcast_to(value[None], (n_zl * n_y, *value.shape))
        value = value.reshape(-1, rows, part)
        value = lax.all_to_all(value, ("zl", "y", "x"), 0, 0, tiled=True)
        return value.reshape(n_zh, -1, part)

    def total(parts):
        sums = 0.0
        for value in parts:
            value = value.astype(F32)
            sums += value[:group] * jnp.exp2(value[group : group + 1, :1] - TOP)
        return sums

    place = jnp.stack([x, c, zh]).astype(jnp.int32)
    basis = spread(pieces[0])
    basis, far, pieces = lax.optimization_barrier((basis, far, pieces))
    core_basis = send(basis, "c", lambda i: 1 - i)
    basis_2 = spread(pieces[1])

    act = rotate(0, place, pair, far, basis, core_basis)
    parts = [act[0]]
    for step in range(1, n_zh):
        parts.append(send(act[step].astype(F16), "zh", lambda i: (i + step) % n_zh))
    index = jnp.arange(group, dtype=jnp.int32)
    position = ((y * n_x + index // toks) * n_c + c) * toks + index % toks
    valid = position < jnp.where(zl == 0, lengths[0], lengths[1])
    rot_act = jnp.where(valid[:, None], total(parts), F32(0.0)).astype(BF16)
    basis_2, rot_act = lax.optimization_barrier((basis_2, rot_act))
    core_basis_2 = send(basis_2, "c", lambda i: 1 - i)
    wide_act = lax.all_gather(rot_act, "x", axis=0)

    grad = rotate(1, place, pair, far, basis_2, core_basis_2)
    grad = lax.all_to_all(grad.astype(F16), "zh", 0, 0, tiled=True)
    rot_grad = total([grad[k] for k in range(n_zh)]).astype(BF16)
    wide_grad = lax.all_gather(rot_grad, "zh", axis=0)

    share = jnp.einsum("ktg,xta->kgxa", wide_grad, wide_act, preferred_element_type=F32)
    share = share.astype(BF16).reshape(n_zl * n_y * n_c, -1, cols)
    received = lax.all_to_all(share, ("zl", "y", "c"), 0, 0, tiled=True)
    received = received.astype(F32).reshape(SEQS, n_y * n_c, -1, cols)
    per_seq = jnp.sum(received, axis=1)
    scale = lengths.astype(F32)[:, None, None]
    return jnp.sum(per_seq * per_seq / scale, axis=0) / F32(SEQS)


def solution(mesh):
    split = Mesh(mesh.devices.reshape(2, 8, 4, 2, 4), ("zl", "y", "x", "c", "zh"))
    spec = P(("zl", "y", "x", "c"), "zh")
    return jax.shard_map(
        on_device, mesh=split, in_specs=(spec, spec, spec, spec, P()), out_specs=spec, check_vma=False
    )
```

time: 190 us -> 175 us (0.921)
  starting transfers between devices: 18.5 us -> 64.4 us
  blocking collectives: 86.6 us -> 53.6 us
  waiting for transfers between devices: 54.2 us -> 33.3 us
  between operations: 14.8 us -> 7.03 us
  matrix products: 5.87 us -> 0.46 us
  Pallas kernels: 0 us -> 4.3 us
  local copies, waits for them, and re-layouts: 3.02 us -> 7.21 us
    ppermute x0 -> x7, starting transfers between devices: none -> 37.9 us  [send(): lax.ppermute(value, axis, [(i, target(i)) for i in range(lax.axis_size(ax...]
    all_to_all x3, waiting for transfers between devices: 54.2 us -> 19.7 us  [the longest x1 16.6 us: on_device(): received = lax.all_to_all(share, ('zl', 'y', 'c'), 0, 0, tiled=True)]
    all_to_all x1, blocking collectives: 59.5 us -> 26.1 us  [spread(): value = lax.all_to_all(value, ('zl', 'y', 'x'), 0, 0, tiled=True)]
    ppermute x0 -> x7, waiting for transfers between devices: none -> 13.7 us  [send(): lax.ppermute(value, axis, [(i, target(i)) for i in range(lax.axis_size(ax...]
    all_to_all x3, starting transfers between devices: 17.8 us -> 25.8 us  [the longest x1 12.7 us: spread(): value = lax.all_to_all(value, ('zl', 'y', 'x'), 0, 0, tiled=True)]
    dot_general x3 -> x1, matrix products: 5.87 us -> 0.46 us  [on_device(): jnp.einsum('ktg,xta->kgxa', wide_grad, wide_act, preferred_element_type=F32)]
    pallas_call x0 -> x3, Pallas kernels: none -> 4.3 us  [the longest x2 3.8 us: rotate(): pl.pallas_call(lambda *refs: rotate_kernel(which, *refs), out_shape=jax.S...]
    slice x1 -> x9, local copies, waits for them, and re-layouts: 0.58 us -> 4.69 us  [the longest x8 4.1 us: total(): sums += value[:group] * jnp.exp2(value[group:group + 1, :1] - TOP)]
  transfers between devices with their start and end apart: 5 -> 11, of which waited for: 2 -> 7; matrix products, arithmetic and copies ran while one was open for 1% -> 2% of each run, Pallas kernels for 0% -> 2%
where the time goes in v6:
time: 175 us; the launch traced here: 174 us
  starting transfers between devices  64.4 us (37%)
  blocking collectives  53.6 us (31%)
  waiting for transfers between devices  33.3 us (19%)
  local copies, waits for them, and re-layouts  7.21 us (4%)
  between operations  7.03 us (4%)
  Pallas kernels  4.3 us (2%)
  other arithmetic  3.45 us (2%)
    ppermute x7, starting transfers between devices, send(): lax.ppermute(value, axis, [(i, target(i)) for i in range(lax.axis_size(ax...  37.9 us
    all_to_all x1, blocking collectives, spread(): value = lax.all_to_all(value, ('zl', 'y', 'x'), 0, 0, tiled=True)  26.1 us
    all_to_all x1, waiting for transfers between devices, on_device(): received = lax.all_to_all(share, ('zl', 'y', 'c'), 0, 0, tiled=True)  16.6 us
    all_gather x1, blocking collectives, on_device(): wide_grad = lax.all_gather(rot_grad, 'zh', axis=0)  16.3 us
    ppermute x7, waiting for transfers between devices, send(): lax.ppermute(value, axis, [(i, target(i)) for i in range(lax.axis_size(ax...  13.7 us
    all_to_all x1, starting transfers between devices, spread(): value = lax.all_to_all(value, ('zl', 'y', 'x'), 0, 0, tiled=True)  12.7 us
    all_gather x1, blocking collectives, on_device(): wide_act = lax.all_gather(rot_act, 'x', axis=0)  11.3 us
    all_to_all x1, starting transfers between devices, on_device(): received = lax.all_to_all(share, ('zl', 'y', 'c'), 0, 0, tiled=True)  8.53 us
  transfers between devices with their start and end apart: 11, of which 7 were waited for; matrix products, arithmetic and copies ran while one was open for 2% of the time, Pallas kernels for 2%

profile of v6, /device:TPU:1, one launch (start us, length us, event | category | flops | bytes accessed | tf_op | source)
XLA Modules:
  0.0 173.8 jit_solution(2524733677718566915)
XLA Ops:
  0.0 1.1 fusion.28
  1.1 3.9 %collective-permute-start = (bf16[2,128,1024]{2,1,0:T(8,128)(2,1)S(1)}, bf16[2,128,1024]{2,1,0:T(8,128)(2,1)S(1)}, u32[]{:S(2)}, u32[]{:S(2)}) collective-permute-start(bf16[2,128,1024]{2,1,0:T(8,128)(2,1)S(1)} %get-tuple-element.35), channel_id=1, source_target_pairs={{0,8},{8,0},{16,24},{24,16},{1,9},{9,1},{17,25},{25,17},{2,10},{10... | collective-permute-start | bytes 1572872 | tf_op jit(solution)/shard_map/ppermute | solution.py:22
  5.6 0.7 collective-permute-start.1
  6.3 5.4 %collective-permute-done = bf16[2,128,1024]{2,1,0:T(8,128)(2,1)S(1)} collective-permute-done((bf16[2,128,1024]{2,1,0:T(8,128)(2,1)S(1)}, bf16[2,128,1024]{2,1,0:T(8,128)(2,1)S(1)}, u32[]{:S(2)}, u32[]{:S(2)}) %collective-permute-start) | collective-permute-done | bytes 524320 | tf_op jit(solution)/shard_map/ppermute | solution.py:22
  11.8 9.3 %collective-permute-start.2 = (bf16[2,2,128,1024]{3,2,1,0:T(8,128)(2,1)S(1)}, bf16[2,2,128,1024]{3,2,1,0:T(8,128)(2,1)S(1)}, u32[]{:S(2)}, u32[]{:S(2)}) collective-permute-start(bf16[2,2,128,1024]{3,2,1,0:T(8,128)(2,1)S(1)} %pad_maximum_fusion.refs_1_), channel_id=1, source_target_pairs={{0,24},{8,16},{16,8},{24,0},{1,25},{9,17},{17,9},{25,1},{2,26},{10... | collective-permute-start | bytes 3145736 | tf_op jit(solution)/shard_map/ppermute | solution.py:22
  21.2 26.1 %all_to_all.20 = bf16[64,32,128]{2,1,0:T(8,128)(2,1)S(1)} all-to-all(bf16[64,32,128]{2,1,0:T(8,128)(2,1)S(1)} %bitcast.68), channel_id=1, replica_groups=mesh['zl'=2,'y'=8,'x'=4,'c'=2,'zh'=4] {'zl','y','x'}, dimensions={0} | all-to-all | bytes 1048576 | tf_op jit(solution)/shard_map/all_to_all | solution.py:135
  47.3 6.1 %collective-permute-start.3 = (bf16[4,512,128]{2,1,0:T(8,128)(2,1)S(1)}, bf16[4,512,128]{2,1,0:T(8,128)(2,1)}, u32[]{:S(2)}, u32[]{:S(2)}) collective-permute-start(bf16[4,512,128]{2,1,0:T(8,128)(2,1)S(1)} %bitcast.62), channel_id=1, source_target_pairs={{0,4},{4,0},{1,5},{5,1},{2,6},{6,2},{3,7},{7,3},{8,12},{12,8},{9,1... | collective-permute-start | bytes 1572872 | tf_op jit(solution)/shard_map/ppermute | solution.py:22
  53.4 0.9 broadcast_in_dim.31
  54.3 12.7 %all-to-all-start.1 = ((bf16[64,32,128]{2,1,0:T(8,128)(2,1)}), bf16[64,32,128]{2,1,0:T(8,128)(2,1)S(1)}, u32[]{:S(2)}, u32[]{:S(2)}) async-start(bf16[64,32,128]{2,1,0:T(8,128)(2,1)} %bitcast.67), calls=%async_computation.1 | async-start | bytes 1048576 | tf_op jit(solution)/shard_map/all_to_all | solution.py:135
  67.1 0.6 fusion.29
  69.0 2.2 %rotate.2 = f32[4,528,128]{2,1,0:T(8,128)S(1)} custom-call(s32[3]{0:T(128)S(1)} %pad_add_fusion.refs_0_, bf16[2,2,128,1024]{3,2,1,0:T(8,128)(2,1)S(1)} %pad_maximum_fusion.refs_1_, bf16[2,2,128,1024]{3,2,1,0:T(8,128)(2,1)S(1)} %collective-permute-done.2.refs_2_, bf16[4,512,128]{2,1,0:T(8,128)(2,1)S(1)} %bitcast.63, ...), custom_call_target="tpu_custom_call" | custom-call | flops 536870912 | bytes 4194304 | tf_op jit(solution)/shard_map/rotate/pallas_call | solution.py:96
  71.3 4.5 %collective-permute-start.4 = (f16[528,128]{1,0:T(8,128)(2,1)S(1)}, f16[528,128]{1,0:T(8,128)(2,1)S(1)}, u32[]{:S(2)}, u32[]{:S(2)}) collective-permute-start(f16[528,128]{1,0:T(8,128)(2,1)S(1)} %get-tuple-element.31), channel_id=1, source_target_pairs={{0,1},{1,2},{2,3},{3,0},{4,5},{5,6},{6,7},{7,4},{8,9},{9,10},{10,1... | collective-permute-start | bytes 405512 | tf_op jit(solution)/shard_map/ppermute | solution.py:22
  75.9 7.9 %collective-permute-start.5 = (f16[528,128]{1,0:T(8,128)(2,1)S(1)}, f16[528,128]{1,0:T(8,128)(2,1)S(1)}, u32[]{:S(2)}, u32[]{:S(2)}) collective-permute-start(f16[528,128]{1,0:T(8,128)(2,1)S(1)} %get-tuple-element.33), channel_id=1, source_target_pairs={{0,2},{1,3},{2,0},{3,1},{4,6},{5,7},{6,4},{7,5},{8,10},{9,11},{10,... | collective-permute-start | bytes 405512 | tf_op jit(solution)/shard_map/ppermute | solution.py:22
  83.8 3.4 %collective-permute-start.6 = (f16[528,128]{1,0:T(8,128)(2,1)S(1)}, f16[528,128]{1,0:T(8,128)(2,1)S(1)}, u32[]{:S(2)}, u32[]{:S(2)}) collective-permute-start(f16[528,128]{1,0:T(8,128)(2,1)S(1)} %get-tuple-element.32), channel_id=1, source_target_pairs={{0,3},{1,0},{2,1},{3,2},{4,7},{5,4},{6,5},{7,6},{8,11},{9,8},{10,9... | collective-permute-start | bytes 405512 | tf_op jit(solution)/shard_map/ppermute | solution.py:22
  87.3 0.5 slice.123
  88.5 0.7 collective-permute-done.4
  89.2 0.5 slice.126
  90.4 3.2 %collective-permute-done.5 = f16[528,128]{1,0:T(8,128)(2,1)S(1)} collective-permute-done((f16[528,128]{1,0:T(8,128)(2,1)S(1)}, f16[528,128]{1,0:T(8,128)(2,1)S(1)}, u32[]{:S(2)}, u32[]{:S(2)}) %collective-permute-start.5) | collective-permute-done | bytes 135200 | tf_op jit(solution)/shard_map/ppermute | solution.py:22
  93.6 0.5 slice.129
  94.9 2.8 %collective-permute-done.6 = f16[528,128]{1,0:T(8,128)(2,1)S(1)} collective-permute-done((f16[528,128]{1,0:T(8,128)(2,1)S(1)}, f16[528,128]{1,0:T(8,128)(2,1)S(1)}, u32[]{:S(2)}, u32[]{:S(2)}) %collective-permute-start.6) | collective-permute-done | bytes 135200 | tf_op jit(solution)/shard_map/ppermute | solution.py:22
  99.1 2.7 %collective-permute-start.7 = (bf16[4,512,128]{2,1,0:T(8,128)(2,1)S(1)}, bf16[4,512,128]{2,1,0:T(8,128)(2,1)S(1)}, u32[]{:S(2)}, u32[]{:S(2)}) collective-permute-start(bf16[4,512,128]{2,1,0:T(8,128)(2,1)S(1)} %bitcast.60), channel_id=1, source_target_pairs={{0,4},{4,0},{1,5},{5,1},{2,6},{6,2},{3,7},{7,3},{8,12},{12,8},{9,1... | collective-permute-start | bytes 1572872 | tf_op jit(solution)/shard_map/ppermute | solution.py:22
  101.8 1.5 collective-permute-done.7.refs_4_
  103.3 1.6 rotate.3
  104.9 0.9 convert_element_type.68
  105.8 4.5 %all-to-all-start.2 = ((f16[4,528,128]{2,1,0:T(8,128)(2,1)}), f16[4,528,128]{2,1,0:T(8,128)(2,1)S(1)}, u32[]{:S(2)}, u32[]{:S(2)}) async-start(f16[4,528,128]{2,1,0:T(8,128)(2,1)} %convert_element_type.68), calls=%async_computation.2 | async-start | bytes 1081344 | tf_op jit(solution)/shard_map/all_to_all | solution.py:164
  110.3 11.3 %all-gather = bf16[2048,128]{1,0:T(8,128)(2,1)S(1)} all-gather(bf16[512,128]{1,0:T(8,128)(2,1)S(1)} %fusion.7), channel_id=2, replica_groups=mesh['zl'=2,'y'=8,'x'=4,'c'=2,'zh'=4] {'x'}, dimensions={0}, use_global_device_ids=true | all-gather | bytes 655360 | tf_op jit(solution)/shard_map/all_gather | solution.py:161
  121.6 3.1 %all-to-all-done.2 = f16[4,528,128]{2,1,0:T(8,128)(2,1)S(1)} async-done(((f16[4,528,128]{2,1,0:T(8,128)(2,1)}), f16[4,528,128]{2,1,0:T(8,128)(2,1)S(1)}, u32[]{:S(2)}, u32[]{:S(2)}) %all-to-all-start.2) | async-done | bytes 540704 | tf_op jit(solution)/shard_map/all_to_all | solution.py:164
  129.8 16.3 %all_gather.13 = bf16[4,512,128]{2,1,0:T(8,128)(2,1)S(1)} all-gather(bf16[1,512,128]{2,1,0:T(8,128)(2,1)S(1)} %fusion.2), channel_id=1, replica_groups=mesh['zl'=2,'y'=8,'x'=4,'c'=2,'zh'=4] {'zh'}, dimensions={0}, use_global_device_ids=true | all-gather | bytes 655360 | tf_op jit(solution)/shard_map/all_gather | solution.py:166
  146.9 1.0 reshape.76
  147.9 8.5 %all-to-all-start.3 = ((bf16[32,16,512]{2,1,0:T(8,128)(2,1)}), bf16[32,16,512]{2,1,0:T(8,128)(2,1)S(1)}, u32[]{:S(2)}, u32[]{:S(2)}) async-start(bf16[32,16,512]{2,1,0:T(8,128)(2,1)} %reshape.76), calls=%async_computation.3 | async-start | bytes 1048576 | tf_op jit(solution)/shard_map/all_to_all | solution.py:170
  156.5 16.6 %all-to-all-done.3 = bf16[32,16,512]{2,1,0:T(8,128)(2,1)S(1)} async-done(((bf16[32,16,512]{2,1,0:T(8,128)(2,1)}), bf16[32,16,512]{2,1,0:T(8,128)(2,1)S(1)}, u32[]{:S(2)}, u32[]{:S(2)}) %all-to-all-start.3) | async-done | bytes 524320 | tf_op jit(solution)/shard_map/all_to_all | solution.py:170
  173.2 0.6 broadcast_multiply_fusion
  (37 shorter events, 5.0 us)
Async XLA Ops:
  0.0 5.1 %copy-start = (bf16[32,512]{1,0:T(8,128)(2,1)S(1)}, bf16[32,512]{1,0:T(8,128)(2,1)}, u32[]{:S(2)}) copy-start(bf16[32,512]{1,0:T(8,128)(2,1)} %act_hbm.1) | copy-start | bytes 98308
  0.0 5.1 %copy-start.1 = (bf16[32,512]{1,0:T(8,128)(2,1)S(1)}, bf16[32,512]{1,0:T(8,128)(2,1)}, u32[]{:S(2)}) copy-start(bf16[32,512]{1,0:T(8,128)(2,1)} %grad_hbm.1) | copy-start | bytes 98308
  1.1 10.6 %collective-permute-start = (bf16[2,128,1024]{2,1,0:T(8,128)(2,1)S(1)}, bf16[2,128,1024]{2,1,0:T(8,128)(2,1)S(1)}, u32[]{:S(2)}, u32[]{:S(2)}) collective-permute-start(bf16[2,128,1024]{2,1,0:T(8,128)(2,1)S(1)} %get-tuple-element.35), channel_id=1, source_target_pairs={{0,8},{8,0},{16,24},{24,16},{1,9},{9,1},{17,25},{25,17},{2,10},{10... | collective-permute-start | bytes 1572872 | tf_op jit(solution)/shard_map/ppermute | solution.py:22
  5.6 0.7 collective-permute-start.1
  11.8 35.5 %collective-permute-start.2 = (bf16[2,2,128,1024]{3,2,1,0:T(8,128)(2,1)S(1)}, bf16[2,2,128,1024]{3,2,1,0:T(8,128)(2,1)S(1)}, u32[]{:S(2)}, u32[]{:S(2)}) collective-permute-start(bf16[2,2,128,1024]{3,2,1,0:T(8,128)(2,1)S(1)} %pad_maximum_fusion.refs_1_), channel_id=1, source_target_pairs={{0,24},{8,16},{16,8},{24,0},{1,25},{9,17},{17,9},{25,1},{2,26},{10... | collective-permute-start | bytes 3145736 | tf_op jit(solution)/shard_map/ppermute | solution.py:22
  47.3 19.8 %copy-start.2 = (s32[2]{0:T(128)S(1)}, s32[2]{0:T(128)}, u32[]{:S(2)}) copy-start(s32[2]{0:T(128)} %param.9) | copy-start | bytes 28
  47.3 21.7 %collective-permute-start.3 = (bf16[4,512,128]{2,1,0:T(8,128)(2,1)S(1)}, bf16[4,512,128]{2,1,0:T(8,128)(2,1)}, u32[]{:S(2)}, u32[]{:S(2)}) collective-permute-start(bf16[4,512,128]{2,1,0:T(8,128)(2,1)S(1)} %bitcast.62), channel_id=1, source_target_pairs={{0,4},{4,0},{1,5},{5,1},{2,6},{6,2},{3,7},{7,3},{8,12},{12,8},{9,1... | collective-permute-start | bytes 1572872 | tf_op jit(solution)/shard_map/ppermute | solution.py:22
  54.3 44.7 %all-to-all-start.1 = ((bf16[64,32,128]{2,1,0:T(8,128)(2,1)}), bf16[64,32,128]{2,1,0:T(8,128)(2,1)S(1)}, u32[]{:S(2)}, u32[]{:S(2)}) async-start(bf16[64,32,128]{2,1,0:T(8,128)(2,1)} %bitcast.67), calls=%async_computation.1 | async-start | bytes 1048576 | tf_op jit(solution)/shard_map/all_to_all | solution.py:135
  71.3 17.9 %collective-permute-start.4 = (f16[528,128]{1,0:T(8,128)(2,1)S(1)}, f16[528,128]{1,0:T(8,128)(2,1)S(1)}, u32[]{:S(2)}, u32[]{:S(2)}) collective-permute-start(f16[528,128]{1,0:T(8,128)(2,1)S(1)} %get-tuple-element.31), channel_id=1, source_target_pairs={{0,1},{1,2},{2,3},{3,0},{4,5},{5,6},{6,7},{7,4},{8,9},{9,10},{10,1... | collective-permute-start | bytes 405512 | tf_op jit(solution)/shard_map/ppermute | solution.py:22
  75.9 17.7 %collective-permute-start.5 = (f16[528,128]{1,0:T(8,128)(2,1)S(1)}, f16[528,128]{1,0:T(8,128)(2,1)S(1)}, u32[]{:S(2)}, u32[]{:S(2)}) collective-permute-start(f16[528,128]{1,0:T(8,128)(2,1)S(1)} %get-tuple-element.33), channel_id=1, source_target_pairs={{0,2},{1,3},{2,0},{3,1},{4,6},{5,7},{6,4},{7,5},{8,10},{9,11},{10,... | collective-permute-start | bytes 405512 | tf_op jit(solution)/shard_map/ppermute | solution.py:22
  83.8 13.8 %collective-permute-start.6 = (f16[528,128]{1,0:T(8,128)(2,1)S(1)}, f16[528,128]{1,0:T(8,128)(2,1)S(1)}, u32[]{:S(2)}, u32[]{:S(2)}) collective-permute-start(f16[528,128]{1,0:T(8,128)(2,1)S(1)} %get-tuple-element.32), channel_id=1, source_target_pairs={{0,3},{1,0},{2,1},{3,2},{4,7},{5,4},{6,5},{7,6},{8,11},{9,8},{10,9... | collective-permute-start | bytes 405512 | tf_op jit(solution)/shard_map/ppermute | solution.py:22
  99.1 4.2 %collective-permute-start.7 = (bf16[4,512,128]{2,1,0:T(8,128)(2,1)S(1)}, bf16[4,512,128]{2,1,0:T(8,128)(2,1)S(1)}, u32[]{:S(2)}, u32[]{:S(2)}) collective-permute-start(bf16[4,512,128]{2,1,0:T(8,128)(2,1)S(1)} %bitcast.60), channel_id=1, source_target_pairs={{0,4},{4,0},{1,5},{5,1},{2,6},{6,2},{3,7},{7,3},{8,12},{12,8},{9,1... | collective-permute-start | bytes 1572872 | tf_op jit(solution)/shard_map/ppermute | solution.py:22
  105.8 18.9 %all-to-all-start.2 = ((f16[4,528,128]{2,1,0:T(8,128)(2,1)}), f16[4,528,128]{2,1,0:T(8,128)(2,1)S(1)}, u32[]{:S(2)}, u32[]{:S(2)}) async-start(f16[4,528,128]{2,1,0:T(8,128)(2,1)} %convert_element_type.68), calls=%async_computation.2 | async-start | bytes 1081344 | tf_op jit(solution)/shard_map/all_to_all | solution.py:164
  147.9 25.1 %all-to-all-start.3 = ((bf16[32,16,512]{2,1,0:T(8,128)(2,1)}), bf16[32,16,512]{2,1,0:T(8,128)(2,1)S(1)}, u32[]{:S(2)}, u32[]{:S(2)}) async-start(bf16[32,16,512]{2,1,0:T(8,128)(2,1)} %reshape.76), calls=%async_computation.3 | async-start | bytes 1048576 | tf_op jit(solution)/shard_map/all_to_all | solution.py:170

commit v7 on v5

v7 whole, which is shorter than its diff:
```python
import jax
import jax.numpy as jnp
from jax import lax
from jax.experimental import pallas as pl
from jax.experimental.pallas import tpu as pltpu
from jax.sharding import Mesh
from jax.sharding import PartitionSpec as P

SEQS = 2
F32 = jnp.float32
BF16 = jnp.bfloat16
F16 = jnp.float16
TILE = 16
TOP = 15
VMEM = pl.BlockSpec(memory_space=pltpu.VMEM)
SMEM = pl.BlockSpec(memory_space=pltpu.SMEM)


def shift(value, axis, step):
    n = lax.axis_size(axis)
    return lax.ppermute(value, axis, [(i, (i + step) % n) for i in range(n)])


def spread(value, outer, n_x, inner, run):
    width = value.shape[1]
    source = lax.broadcasted_iota(jnp.int32, (width, width), 0)
    target = lax.broadcasted_iota(jnp.int32, (width, width), 1)
    at_run, at_inner = source % run, source // run % inner
    at_x, at_outer = source // (run * inner) % n_x, source // (run * inner * n_x)
    moved = ((at_x * inner + at_inner) * outer + at_outer) * run + at_run
    ones = (moved == target).astype(F32).astype(BF16)
    return jnp.dot(value, ones, preferred_element_type=F32).astype(BF16)


def prepare_kernel(y_lo, n_c, *refs):
    inputs, (tokens, bases), held, sems = refs[:4], refs[4:6], refs[6:10], refs[10]
    sorted_tokens, out_sems = refs[11:]
    copies = [
        pltpu.make_async_copy(ref, kept, sems.at[i]) for i, (ref, kept) in enumerate(zip(inputs, held))
    ]
    for copy in copies:
        copy.start()
    n_x, n_zh, _, toks, width = tokens.shape
    run = width // (y_lo * n_c)
    for copy in copies:
        copy.wait()
    for which in range(2):
        moved = spread(held[which][...], y_lo, n_x, n_c, run)
        for x in range(n_x):
            sorted_tokens[x, which] = moved[:, x * width : (x + 1) * width]
    copies = [
        pltpu.make_async_copy(sorted_tokens.at[x], tokens.at[x, zh], out_sems.at[x, zh])
        for x in range(n_x)
        for zh in range(n_zh)
    ]
    for copy in copies:
        copy.start()
    bases[0] = held[2][...]
    bases[1] = spread(held[3][...], y_lo, n_x, 1, bases.shape[2] // (y_lo * n_x))
    for copy in copies:
        copy.wait()


def prepare(y_lo, n_x, n_c, n_zh, *arrays):
    toks, feats = arrays[0].shape
    return pl.pallas_call(
        lambda *refs: prepare_kernel(y_lo, n_c, *refs),
        out_shape=(
            jax.ShapeDtypeStruct((n_x, n_zh, 2, toks, feats // n_x), BF16),
            jax.ShapeDtypeStruct((2, *arrays[2].shape), BF16),
        ),
        in_specs=[pl.BlockSpec(memory_space=pl.ANY)] * 4,
        out_specs=(pl.BlockSpec(memory_space=pl.ANY), VMEM),
        scratch_shapes=[
            *[pltpu.VMEM(a.shape, BF16) for a in arrays],
            pltpu.SemaphoreType.DMA((4,)),
            pltpu.VMEM((n_x, 2, toks, feats // n_x), BF16),
            pltpu.SemaphoreType.DMA((n_x, n_zh)),
        ],
        compiler_params=pltpu.CompilerParams(vmem_limit_bytes=60 * 2**20),
        cost_estimate=pl.CostEstimate(
            flops=4 * toks * feats * feats, bytes_accessed=2**20, transcendentals=0
        ),
        name="prepare",
    )(*arrays)


def rotate_kernel(place, tokens, basis, far_basis, core_basis, core_far_basis, out):
    n_x, n_zh, _, toks, width = tokens.shape
    n_y, _, rows, cols = basis.shape
    per, half = n_y * 2 // n_zh, width // 2
    zl, c = place[0], place[1]
    near, far = (pl.ds(pl.multiple_of(core * half, half), half) for core in (c, 1 - c))
    sums = []
    for which in range(2):
        total = None
        for side, bases in ((zl, (basis, core_basis)), (1 - zl, (far_basis, core_far_basis))):
            for upper in range(n_y // per):
                owner = side * (n_y // per) + upper
                left = [
                    tokens[:, owner, which, :, lanes].reshape(n_x * toks, half)
                    for lanes in (near, far)
                ]
                right = [
                    ref[upper * per : (upper + 1) * per, which].reshape(per * rows, cols)
                    for ref in bases
                ]
                product = jnp.dot(
                    jnp.concatenate(left, axis=1),
                    jnp.concatenate(right, axis=0),
                    preferred_element_type=F32,
                )
                total = product if total is None else total + product
        sums.append(total)
    largest = jnp.max(jnp.maximum(jnp.abs(sums[0]), jnp.abs(sums[1])), axis=0, keepdims=True)
    largest = jnp.max(largest, axis=1, keepdims=True)
    level = jnp.clip(jnp.ceil(jnp.log2(jnp.maximum(largest, 1e-30))), -100.0, 100.0)
    factor = jnp.exp2(F32(TOP) - level)
    group, part = n_x * toks, cols // n_x
    for x in range(n_x):
        for which in range(2):
            value = sums[which][:, x * part : (x + 1) * part] * factor
            out[x, pl.ds(which * group, group)] = value
        out[x, pl.ds(2 * group, TILE)] = jnp.broadcast_to(level, (TILE, part))


def rotate(place, *arrays):
    n_x, n_zh, _, toks, width = arrays[0].shape
    cols = arrays[-1].shape[3]
    return pl.pallas_call(
        rotate_kernel,
        out_shape=jax.ShapeDtypeStruct((n_x, 2 * n_x * toks + TILE, cols // n_x), F32),
        in_specs=[SMEM] + [VMEM] * len(arrays),
        out_specs=VMEM,
        compiler_params=pltpu.CompilerParams(vmem_limit_bytes=40 * 2**20),
        cost_estimate=pl.CostEstimate(
            flops=4 * n_x * n_zh * toks * width * cols, bytes_accessed=8 * 2**20, transcendentals=0
        ),
        name="rotate",
    )(place, *arrays)


def on_device(activations, gradients, basis_act, basis_grad, lengths):
    n_zl, n_y, n_x, n_c, n_zh = (lax.axis_size(a) for a in ("zl", "y", "x", "c", "zh"))
    zl, y, c = (lax.axis_index(a) for a in ("zl", "y", "c"))
    toks = activations.shape[0]
    cols = basis_act.shape[1]
    part, group = cols // n_x, n_x * toks

    tokens, bases = prepare(n_y // 2, n_x, n_c, n_zh, activations, gradients, basis_act, basis_grad)
    tokens = lax.all_to_all(
        tokens.reshape(n_x * n_zh, *tokens.shape[2:]), ("x", "zh"), 0, 0, tiled=True
    ).reshape(tokens.shape)

    basis = lax.all_gather(bases, "y", axis=0)
    far_basis = shift(basis, "zl", 1)
    core_basis = shift(basis, "c", 1)
    core_far_basis = shift(far_basis, "c", 1)

    place = jnp.stack([zl, c]).astype(jnp.int32)
    partial = rotate(place, tokens, basis, far_basis, core_basis, core_far_basis)
    partial = lax.all_to_all(partial.astype(F16), "x", 0, 0, tiled=True).astype(F32)
    factors = jnp.exp2(partial[:, None, 2 * group :] - F32(TOP))
    partial = partial[:, : 2 * group].reshape(n_x, 2 * group // TILE, TILE, part)
    rotated = jnp.sum(partial * factors, axis=0).reshape(2 * group, part)
    index = jnp.arange(group, dtype=jnp.int32)
    position = ((y * n_x + index // toks) * n_c + c) * toks + index % toks
    length = jnp.where(zl == 0, lengths[0], lengths[1])
    valid = position < length
    rot_act = jnp.where(valid[:, None], rotated[:group], F32(0.0)).astype(BF16)
    rot_grad = rotated[group:].astype(BF16)

    wide_act = lax.all_to_all(
        jnp.broadcast_to(rot_act[None], (n_x, group, part)), "x", 0, 0, tiled=True
    )
    wide_grad = lax.all_gather(rot_grad, "zh", axis=0)
    share = jnp.einsum("ktg,xta->kgxa", wide_grad, wide_act, preferred_element_type=F32)
    share = share.astype(BF16).reshape(n_zl * n_y * n_c, -1, cols)
    received = lax.all_to_all(share, ("zl", "y", "c"), 0, 0, tiled=True)
    received = received.astype(F32).reshape(SEQS, n_y * n_c, -1, cols)
    per_seq = jnp.sum(received, axis=1)
    scale = lengths.astype(F32)[:, None, None]
    return jnp.sum(per_seq * per_seq / scale, axis=0) / F32(SEQS)


def solution(mesh):
    split = Mesh(mesh.devices.reshape(2, 8, 4, 2, 4), ("zl", "y", "x", "c", "zh"))
    spec = P(("zl", "y", "x", "c"), "zh")
    return jax.shard_map(
        on_device, mesh=split, in_specs=(spec, spec, spec, spec, P()), out_specs=spec, check_vma=False
    )
```

time: 181 us -> 157 us (0.87)
  waiting for transfers between devices: 73.3 us -> 55.3 us
  blocking collectives: 24.9 us -> 37.7 us
  starting transfers between devices: 60.5 us -> 48.2 us
  local copies, waits for them, and re-layouts: 12.7 us -> 2.87 us
  Pallas kernels: 3.07 us -> 7.24 us
    all_gather x0 -> x1, blocking collectives: none -> 22.7 us  [on_device(): basis = lax.all_gather(bases, 'y', axis=0)]
    ppermute x5 -> x3, starting transfers between devices: 28.6 us -> 14 us  [shift(): return lax.ppermute(value, axis, [(i, (i + step) % n) for i in range(n)])]
    all_to_all x1, waiting for transfers between devices: 14.4 us -> 0.01 us  [on_device(): lax.all_to_all(tokens.reshape(n_x * n_zh, *tokens.shape[2:]), ('x', 'zh')...]
    all_to_all x1 -> x0, blocking collectives: 11.6 us -> none  [on_device(): mine = lax.all_to_all(tokens, 'x', 0, 0, tiled=True)]
    unnamed x14 -> x4, local copies, waits for them, and re-layouts: 4.98 us -> 0.01 us
    ppermute x5 -> x3, waiting for transfers between devices: 30.9 us -> 25.9 us  [shift(): return lax.ppermute(value, axis, [(i, (i + step) % n) for i in range(n)])]
    pallas_call x1, Pallas kernels: 1.01 us -> 4.51 us  [prepare(): pl.pallas_call(lambda *refs: prepare_kernel(y_lo, n_c, *refs), out_shape=...]
    all_to_all x1, starting transfers between devices: 10.4 us -> 13.6 us  [on_device(): lax.all_to_all(tokens.reshape(n_x * n_zh, *tokens.shape[2:]), ('x', 'zh')...]
  transfers between devices with their start and end apart: 9 -> 7, of which waited for: 5 -> 4; matrix products, arithmetic and copies ran while one was open for 3% -> 0% of each run, Pallas kernels for 0% -> 0%
where the time goes in v7:
time: 157 us; the launch traced here: 156 us
  waiting for transfers between devices  55.3 us (35%)
  starting transfers between devices  48.2 us (31%)
  blocking collectives  37.7 us (24%)
  Pallas kernels  7.24 us (5%)
  local copies, waits for them, and re-layouts  2.87 us (2%)
  other arithmetic  2.42 us (2%)
    ppermute x3, waiting for transfers between devices, shift(): return lax.ppermute(value, axis, [(i, (i + step) % n) for i in range(n)])  25.9 us
    all_gather x1, blocking collectives, on_device(): basis = lax.all_gather(bases, 'y', axis=0)  22.7 us
    all_to_all x1, waiting for transfers between devices, on_device(): received = lax.all_to_all(share, ('zl', 'y', 'c'), 0, 0, tiled=True)  16.6 us
    all_gather x1, blocking collectives, on_device(): wide_grad = lax.all_gather(rot_grad, 'zh', axis=0)  15 us
    ppermute x3, starting transfers between devices, shift(): return lax.ppermute(value, axis, [(i, (i + step) % n) for i in range(n)])  14 us
    all_to_all x1, starting transfers between devices, on_device(): lax.all_to_all(tokens.reshape(n_x * n_zh, *tokens.shape[2:]), ('x', 'zh')...  13.6 us
    all_to_all x1, starting transfers between devices, on_device(): received = lax.all_to_all(share, ('zl', 'y', 'c'), 0, 0, tiled=True)  12.9 us
    all_to_all x1, waiting for transfers between devices, on_device(): lax.all_to_all(partial.astype(F16), 'x', 0, 0, tiled=True).astype(F32)  12.9 us
  transfers between devices with their start and end apart: 7, of which 4 were waited for; matrix products, arithmetic and copies ran while one was open for 0% of the time, Pallas kernels for 0%

profile of v7, /device:TPU:1, one launch (start us, length us, event | category | flops | bytes accessed | tf_op | source)
XLA Modules:
  0.0 155.5 jit_solution(6909908540480622418)
XLA Ops:
  0.0 4.5 %prepare.1 = (bf16[4,4,2,128,256]{4,3,2,1,0:T(8,128)(2,1)}, bf16[2,32,512]{2,1,0:T(8,128)(2,1)}) custom-call(bf16[128,1024]{1,0:T(8,128)(2,1)} %refs_0_.1, bf16[128,1024]{1,0:T(8,128)(2,1)} %refs_1_.1, bf16[32,512]{1,0:T(8,128)(2,1)} %refs_2_.1, bf16[32,512]{1,0:T(8,128)(2,1)} %refs_3_.1), custom_call_target="tpu_custom_call" | custom-call | flops 536870912 | bytes 1048576 | tf_op jit(solution)/shard_map/prepare/pallas_call | solution.py:66
  4.5 13.6 %all-to-all-start = ((bf16[16,2,128,256]{3,2,1,0:T(8,128)(2,1)}), bf16[16,2,128,256]{3,2,1,0:T(8,128)(2,1)S(1)}, u32[]{:S(2)}, u32[]{:S(2)}) async-start(bf16[16,2,128,256]{3,2,1,0:T(8,128)(2,1)} %bitcast.26), calls=%async_computation | async-start | bytes 4194304 | tf_op jit(solution)/shard_map/all_to_all | solution.py:151
  18.1 22.7 %all-gather = bf16[16,32,512]{2,1,0:T(8,128)(2,1)S(1)} all-gather(bf16[2,32,512]{2,1,0:T(8,128)(2,1)S(1)} %copy-done), channel_id=2, replica_groups=mesh['zl'=2,'y'=8,'x'=4,'c'=2,'zh'=4] {'y'}, dimensions={0}, use_global_device_ids=true | all-gather | bytes 589824 | tf_op jit(solution)/shard_map/all_gather | solution.py:155
  40.8 3.1 %collective-permute-start = (bf16[8,2,32,512]{3,2,1,0:T(8,128)(2,1)S(1)}, bf16[8,2,32,512]{3,2,1,0:T(8,128)(2,1)S(1)}, u32[]{:S(2)}, u32[]{:S(2)}) collective-permute-start(bf16[8,2,32,512]{3,2,1,0:T(8,128)(2,1)S(1)} %bitcast.22), channel_id=1, source_target_pairs={{0,256},{256,0},{1,257},{257,1},{2,258},{258,2},{3,259},{259,3},{4... | collective-permute-start | bytes 1572872 | tf_op jit(solution)/shard_map/ppermute | solution.py:21
  43.9 7.5 %collective-permute-start.1 = (bf16[8,2,32,512]{3,2,1,0:T(8,128)(2,1)S(1)}, bf16[8,2,32,512]{3,2,1,0:T(8,128)(2,1)}, u32[]{:S(2)}, u32[]{:S(2)}) collective-permute-start(bf16[8,2,32,512]{3,2,1,0:T(8,128)(2,1)S(1)} %bitcast.23), channel_id=1, source_target_pairs={{0,4},{4,0},{1,5},{5,1},{2,6},{6,2},{3,7},{7,3},{8,12},{12,8},{9,1... | collective-permute-start | bytes 1572872 | tf_op jit(solution)/shard_map/ppermute | solution.py:21
  51.4 24.3 %collective-permute-done.far_basis = bf16[8,2,32,512]{3,2,1,0:T(8,128)(2,1)S(1)} collective-permute-done((bf16[8,2,32,512]{3,2,1,0:T(8,128)(2,1)S(1)}, bf16[8,2,32,512]{3,2,1,0:T(8,128)(2,1)S(1)}, u32[]{:S(2)}, u32[]{:S(2)}) %collective-permute-start) | collective-permute-done | bytes 524320 | tf_op jit(solution)/shard_map/ppermute | solution.py:21
  75.8 3.4 %collective-permute-start.2 = (bf16[8,2,32,512]{3,2,1,0:T(8,128)(2,1)S(1)}, bf16[8,2,32,512]{3,2,1,0:T(8,128)(2,1)}, u32[]{:S(2)}, u32[]{:S(2)}) collective-permute-start(bf16[8,2,32,512]{3,2,1,0:T(8,128)(2,1)S(1)} %collective-permute-done.far_basis), channel_id=1, source_target_pairs={{0,4},{4,0},{1,5},{5,1},{2,6},{6,2},{3,7},{7,3},{8,12},{12,8},{9,1... | collective-permute-start | bytes 1572872 | tf_op jit(solution)/shard_map/ppermute | solution.py:21
  79.2 0.1 pad_add_fusion.place
  79.3 0.0 collective-permute-done.1.core_basis
  79.3 1.6 %collective-permute-done.2.core_far_basis = bf16[8,2,32,512]{3,2,1,0:T(8,128)(2,1)} collective-permute-done((bf16[8,2,32,512]{3,2,1,0:T(8,128)(2,1)S(1)}, bf16[8,2,32,512]{3,2,1,0:T(8,128)(2,1)}, u32[]{:S(2)}, u32[]{:S(2)}) %collective-permute-start.2) | collective-permute-done | bytes 524320 | tf_op jit(solution)/shard_map/ppermute | solution.py:21
  80.8 0.0 all-to-all-done
  80.8 2.7 %rotate.1 = f32[4,1040,128]{2,1,0:T(8,128)S(1)} custom-call(s32[2]{0:T(128)S(1)} %pad_add_fusion.place, bf16[4,4,2,128,256]{4,3,2,1,0:T(8,128)(2,1)S(1)} %bitcast.21, bf16[8,2,32,512]{3,2,1,0:T(8,128)(2,1)S(1)} %bitcast.24, bf16[8,2,32,512]{3,2,1,0:T(8,128)(2,1)S(1)} %collective-permute-done.far_basis, ...), custom_call_target="tpu_custom_call" | custom-call | flops 1073741824 | bytes 8388608 | tf_op jit(solution)/shard_map/rotate/pallas_call | solution.py:130
  83.6 0.0 copy-start.1
  83.6 1.1 convert_element_type.23
  84.7 4.2 %all-to-all-start.1 = ((f16[4,1040,128]{2,1,0:T(8,128)(2,1)}), f16[4,1040,128]{2,1,0:T(8,128)(2,1)S(1)}, u32[]{:S(2)}, u32[]{:S(2)}) async-start(f16[4,1040,128]{2,1,0:T(8,128)(2,1)} %convert_element_type.23), calls=%async_computation.1 | async-start | bytes 2129920 | tf_op jit(solution)/shard_map/all_to_all | solution.py:162
  88.9 0.6 fusion.18
  90.8 12.9 %all-to-all-done.1 = f16[4,1040,128]{2,1,0:T(8,128)(2,1)S(1)} async-done(((f16[4,1040,128]{2,1,0:T(8,128)(2,1)}), f16[4,1040,128]{2,1,0:T(8,128)(2,1)S(1)}, u32[]{:S(2)}, u32[]{:S(2)}) %all-to-all-start.1) | async-done | bytes 1064992 | tf_op jit(solution)/shard_map/all_to_all | solution.py:162
  103.6 0.1 convert_element_type.24
  103.8 0.1 fusion
  103.9 0.1 fusion.2
  104.1 0.9 broadcast_in_dim.23
  104.9 3.5 %all-to-all-start.2 = ((bf16[4,512,128]{2,1,0:T(8,128)(2,1)}), bf16[4,512,128]{2,1,0:T(8,128)(2,1)S(1)}, u32[]{:S(2)}, u32[]{:S(2)}) async-start(bf16[4,512,128]{2,1,0:T(8,128)(2,1)} %broadcast_in_dim.23), calls=%async_computation.2 | async-start | bytes 1048576 | tf_op jit(solution)/shard_map/all_to_all | solution.py:173
  108.4 15.0 %all-gather.1 = bf16[2048,128]{1,0:T(8,128)(2,1)S(1)} all-gather(bf16[512,128]{1,0:T(8,128)(2,1)S(1)} %get-tuple-element.10), channel_id=3, replica_groups=mesh['zl'=2,'y'=8,'x'=4,'c'=2,'zh'=4] {'zh'}, dimensions={0}, use_global_device_ids=true | all-gather | bytes 655360 | tf_op jit(solution)/shard_map/all_gather | solution.py:176
  123.4 0.0 all-to-all-done.2
  123.4 0.5 convolution_convert_fusion
  123.9 0.4 copy.11
  124.3 1.0 reshape.71
  125.3 12.9 %all-to-all-start.3 = ((bf16[32,16,512]{2,1,0:T(8,128)(2,1)}), bf16[32,16,512]{2,1,0:T(8,128)(2,1)S(1)}, u32[]{:S(2)}, u32[]{:S(2)}) async-start(bf16[32,16,512]{2,1,0:T(8,128)(2,1)} %reshape.71), calls=%async_computation.3 | async-start | bytes 1048576 | tf_op jit(solution)/shard_map/all_to_all | solution.py:179
  138.2 16.6 %all-to-all-done.3 = bf16[32,16,512]{2,1,0:T(8,128)(2,1)S(1)} async-done(((bf16[32,16,512]{2,1,0:T(8,128)(2,1)}), bf16[32,16,512]{2,1,0:T(8,128)(2,1)S(1)}, u32[]{:S(2)}, u32[]{:S(2)}) %all-to-all-start.3) | async-done | bytes 524320 | tf_op jit(solution)/shard_map/all_to_all | solution.py:179
  154.7 0.1 convert_reduce_fusion
  154.8 0.1 divide_reduce_fusion
  154.9 0.6 broadcast_multiply_fusion
  (6 shorter events, 0.0 us)
Async XLA Ops:
  4.5 13.6 %copy-start = (bf16[2,32,512]{2,1,0:T(8,128)(2,1)S(1)}, bf16[2,32,512]{2,1,0:T(8,128)(2,1)}, u32[]{:S(2)}) copy-start(bf16[2,32,512]{2,1,0:T(8,128)(2,1)} %get-tuple-element.8) | copy-start | bytes 196612
  4.5 76.3 %all-to-all-start = ((bf16[16,2,128,256]{3,2,1,0:T(8,128)(2,1)}), bf16[16,2,128,256]{3,2,1,0:T(8,128)(2,1)S(1)}, u32[]{:S(2)}, u32[]{:S(2)}) async-start(bf16[16,2,128,256]{3,2,1,0:T(8,128)(2,1)} %bitcast.26), calls=%async_computation | async-start | bytes 4194304 | tf_op jit(solution)/shard_map/all_to_all | solution.py:151
  40.8 35.0 %collective-permute-start = (bf16[8,2,32,512]{3,2,1,0:T(8,128)(2,1)S(1)}, bf16[8,2,32,512]{3,2,1,0:T(8,128)(2,1)S(1)}, u32[]{:S(2)}, u32[]{:S(2)}) collective-permute-start(bf16[8,2,32,512]{3,2,1,0:T(8,128)(2,1)S(1)} %bitcast.22), channel_id=1, source_target_pairs={{0,256},{256,0},{1,257},{257,1},{2,258},{258,2},{3,259},{259,3},{4... | collective-permute-start | bytes 1572872 | tf_op jit(solution)/shard_map/ppermute | solution.py:21
  43.9 35.4 %collective-permute-start.1 = (bf16[8,2,32,512]{3,2,1,0:T(8,128)(2,1)S(1)}, bf16[8,2,32,512]{3,2,1,0:T(8,128)(2,1)}, u32[]{:S(2)}, u32[]{:S(2)}) collective-permute-start(bf16[8,2,32,512]{3,2,1,0:T(8,128)(2,1)S(1)} %bitcast.23), channel_id=1, source_target_pairs={{0,4},{4,0},{1,5},{5,1},{2,6},{6,2},{3,7},{7,3},{8,12},{12,8},{9,1... | collective-permute-start | bytes 1572872 | tf_op jit(solution)/shard_map/ppermute | solution.py:21
  75.8 5.0 %collective-permute-start.2 = (bf16[8,2,32,512]{3,2,1,0:T(8,128)(2,1)S(1)}, bf16[8,2,32,512]{3,2,1,0:T(8,128)(2,1)}, u32[]{:S(2)}, u32[]{:S(2)}) collective-permute-start(bf16[8,2,32,512]{3,2,1,0:T(8,128)(2,1)S(1)} %collective-permute-done.far_basis), channel_id=1, source_target_pairs={{0,4},{4,0},{1,5},{5,1},{2,6},{6,2},{3,7},{7,3},{8,12},{12,8},{9,1... | collective-permute-start | bytes 1572872 | tf_op jit(solution)/shard_map/ppermute | solution.py:21
  83.6 5.4 %copy-start.1 = (s32[2]{0:T(128)S(1)}, s32[2]{0:T(128)}, u32[]{:S(2)}) copy-start(s32[2]{0:T(128)} %param.9) | copy-start | bytes 28
  84.7 18.9 %all-to-all-start.1 = ((f16[4,1040,128]{2,1,0:T(8,128)(2,1)}), f16[4,1040,128]{2,1,0:T(8,128)(2,1)S(1)}, u32[]{:S(2)}, u32[]{:S(2)}) async-start(f16[4,1040,128]{2,1,0:T(8,128)(2,1)} %convert_element_type.23), calls=%async_computation.1 | async-start | bytes 2129920 | tf_op jit(solution)/shard_map/all_to_all | solution.py:162
  104.9 18.4 %all-to-all-start.2 = ((bf16[4,512,128]{2,1,0:T(8,128)(2,1)}), bf16[4,512,128]{2,1,0:T(8,128)(2,1)S(1)}, u32[]{:S(2)}, u32[]{:S(2)}) async-start(bf16[4,512,128]{2,1,0:T(8,128)(2,1)} %broadcast_in_dim.23), calls=%async_computation.2 | async-start | bytes 1048576 | tf_op jit(solution)/shard_map/all_to_all | solution.py:173
  125.3 29.5 %all-to-all-start.3 = ((bf16[32,16,512]{2,1,0:T(8,128)(2,1)}), bf16[32,16,512]{2,1,0:T(8,128)(2,1)S(1)}, u32[]{:S(2)}, u32[]{:S(2)}) async-start(bf16[32,16,512]{2,1,0:T(8,128)(2,1)} %reshape.71), calls=%async_computation.3 | async-start | bytes 1048576 | tf_op jit(solution)/shard_map/all_to_all | solution.py:179

commit v8 on v7

--- a/solution.py
+++ b/solution.py
@@ -21,14 +21,17 @@
     return lax.ppermute(value, axis, [(i, (i + step) % n) for i in range(n)])
 
 
-def spread(value, outer, n_x, inner, run):
-    width = value.shape[1]
+def sorting(width, outer, n_x, inner):
+    run = width // (outer * n_x * inner)
     source = lax.broadcasted_iota(jnp.int32, (width, width), 0)
     target = lax.broadcasted_iota(jnp.int32, (width, width), 1)
     at_run, at_inner = source % run, source // run % inner
     at_x, at_outer = source // (run * inner) % n_x, source // (run * inner * n_x)
     moved = ((at_x * inner + at_inner) * outer + at_outer) * run + at_run
-    ones = (moved == target).astype(F32).astype(BF16)
+    return (moved == target).astype(F32).astype(BF16)
+
+
+def spread(value, ones):
     return jnp.dot(value, ones, preferred_element_type=F32).astype(BF16)
 
 
@@ -41,23 +44,25 @@
     for copy in copies:
         copy.start()
     n_x, n_zh, _, toks, width = tokens.shape
-    run = width // (y_lo * n_c)
+    cols = bases.shape[2]
+    by_x = sorting(n_x * width, y_lo, n_x, n_c)
+    by_owner = sorting(cols, y_lo, n_x, n_c)
     for copy in copies:
         copy.wait()
-    for which in range(2):
-        moved = spread(held[which][...], y_lo, n_x, n_c, run)
-        for x in range(n_x):
-            sorted_tokens[x, which] = moved[:, x * width : (x + 1) * width]
-    copies = [
-        pltpu.make_async_copy(sorted_tokens.at[x], tokens.at[x, zh], out_sems.at[x, zh])
-        for x in range(n_x)
-        for zh in range(n_zh)
-    ]
-    for copy in copies:
-        copy.start()
+    both = jnp.concatenate([held[0][...], held[1][...]], axis=0)
+    sent = []
+    for x in range(n_x):
+        moved = spread(both, by_x[:, x * width : (x + 1) * width])
+        for which in range(2):
+            sorted_tokens[x, which] = moved[which * toks : (which + 1) * toks]
+        for zh in range(n_zh):
+            sent.append(
+                pltpu.make_async_copy(sorted_tokens.at[x], tokens.at[x, zh], out_sems.at[x, zh])
+            )
+            sent[-1].start()
     bases[0] = held[2][...]
-    bases[1] = spread(held[3][...], y_lo, n_x, 1, bases.shape[2] // (y_lo * n_x))
-    for copy in copies:
+    bases[1] = spread(held[3][...], by_owner)
+    for copy in sent:
         copy.wait()
 
 
@@ -140,6 +145,37 @@
     )(place, *arrays)
 
 
+def share_kernel(grad, act, out):
+    n_k, _, part = grad.shape
+    n_x, n_c = act.shape[:2]
+    half = part // n_c
+    turned = [grad[k].T for k in range(n_k)]
+    total = None
+    for core in range(n_c):
+        left = jnp.concatenate([t[core * half : (core + 1) * half] for t in turned], axis=0)
+        right = jnp.concatenate([act[x, core] for x in range(n_x)], axis=1)
+        product = jnp.dot(left, right, preferred_element_type=F32)
+        total = product if total is None else total + product
+    out[...] = total.astype(BF16)
+
+
+def share_of(grad, act):
+    n_k, group, part = grad.shape
+    n_x, n_c = act.shape[:2]
+    rows, cols = n_k * part // n_c, n_x * part
+    return pl.pallas_call(
+        share_kernel,
+        out_shape=jax.ShapeDtypeStruct((rows, cols), BF16),
+        in_specs=[VMEM, VMEM],
+        out_specs=VMEM,
+        compiler_params=pltpu.CompilerParams(vmem_limit_bytes=32 * 2**20),
+        cost_estimate=pl.CostEstimate(
+            flops=2 * n_c * rows * cols * group, bytes_accessed=2 * 2**20, transcendentals=0
+        ),
+        name="share",
+    )(grad, act)
+
+
 def on_device(activations, gradients, basis_act, basis_grad, lengths):
     n_zl, n_y, n_x, n_c, n_zh = (lax.axis_size(a) for a in ("zl", "y", "x", "c", "zh"))
     zl, y, c = (lax.axis_index(a) for a in ("zl", "y", "c"))
@@ -148,13 +184,14 @@
     part, group = cols // n_x, n_x * toks
 
     tokens, bases = prepare(n_y // 2, n_x, n_c, n_zh, activations, gradients, basis_act, basis_grad)
+    far_bases = shift(bases, "zl", 1)
     tokens = lax.all_to_all(
         tokens.reshape(n_x * n_zh, *tokens.shape[2:]), ("x", "zh"), 0, 0, tiled=True
     ).reshape(tokens.shape)
 
     basis = lax.all_gather(bases, "y", axis=0)
-    far_basis = shift(basis, "zl", 1)
     core_basis = shift(basis, "c", 1)
+    far_basis = lax.all_gather(far_bases, "y", axis=0)
     core_far_basis = shift(far_basis, "c", 1)
 
     place = jnp.stack([zl, c]).astype(jnp.int32)
@@ -168,16 +205,19 @@
     length = jnp.where(zl == 0, lengths[0], lengths[1])
     valid = position < length
     rot_act = jnp.where(valid[:, None], rotated[:group], F32(0.0)).astype(BF16)
-    rot_grad = rotated[group:].astype(BF16)
-
+    mine = jnp.stack([rot_act, rotated[group:].astype(BF16)])
+    other = shift(mine, "c", 1)
+
+    lane = jnp.arange(part, dtype=jnp.int32)
+    rot_grad = jnp.where(lane // (part // n_c) == c, mine[1], jnp.roll(other[1], part // n_c, axis=1))
+    both_act = jnp.where(c == 0, jnp.stack([mine[0], other[0]]), jnp.stack([other[0], mine[0]]))
     wide_act = lax.all_to_all(
-        jnp.broadcast_to(rot_act[None], (n_x, group, part)), "x", 0, 0, tiled=True
+        jnp.broadcast_to(both_act[None], (n_x, *both_act.shape)), "x", 0, 0, tiled=True
     )
     wide_grad = lax.all_gather(rot_grad, "zh", axis=0)
-    share = jnp.einsum("ktg,xta->kgxa", wide_grad, wide_act, preferred_element_type=F32)
-    share = share.astype(BF16).reshape(n_zl * n_y * n_c, -1, cols)
-    received = lax.all_to_all(share, ("zl", "y", "c"), 0, 0, tiled=True)
-    received = received.astype(F32).reshape(SEQS, n_y * n_c, -1, cols)
+    share = share_of(wide_grad, wide_act).reshape(n_zl * n_y, -1, cols)
+    received = lax.all_to_all(share, ("zl", "y"), 0, 0, tiled=True)
+    received = received.astype(F32).reshape(SEQS, n_y, -1, cols)
     per_seq = jnp.sum(received, axis=1)
     scale = lengths.astype(F32)[:, None, None]
     return jnp.sum(per_seq * per_seq / scale, axis=0) / F32(SEQS)

time: 157 us -> 166 us (1.057)
  the two profiles are of different devices: /device:TPU:1 before, /device:TPU:10 now
where the time goes in v8:
time: 166 us
  blocking collectives  70.7 us (43%)
  starting transfers between devices  41.1 us (25%)
  waiting for transfers between devices  40.4 us (24%)
  Pallas kernels  7.54 us (5%)
  other arithmetic  2.56 us (2%)
  local copies, waits for them, and re-layouts  1.84 us (1%)
    all_gather x1, blocking collectives, on_device(): far_basis = lax.all_gather(far_bases, 'y', axis=0)  26.2 us
    all_gather x1, blocking collectives, on_device(): basis = lax.all_gather(bases, 'y', axis=0)  26.1 us
    ppermute x4, waiting for transfers between devices, shift(): return lax.ppermute(value, axis, [(i, (i + step) % n) for i in range(n)])  19.1 us
    all_gather x1, blocking collectives, on_device(): wide_grad = lax.all_gather(rot_grad, 'zh', axis=0)  18.4 us
    all_to_all x1, starting transfers between devices, on_device(): lax.all_to_all(tokens.reshape(n_x * n_zh, *tokens.shape[2:]), ('x', 'zh')...  13.4 us
    all_to_all x1, waiting for transfers between devices, on_device(): lax.all_to_all(partial.astype(F16), 'x', 0, 0, tiled=True).astype(F32)  12.2 us
    ppermute x4, starting transfers between devices, shift(): return lax.ppermute(value, axis, [(i, (i + step) % n) for i in range(n)])  9.12 us
    all_to_all x1, waiting for transfers between devices, on_device(): received = lax.all_to_all(share, ('zl', 'y'), 0, 0, tiled=True)  9.04 us
  transfers between devices with their start and end apart: 8, of which 5 were waited for; matrix products, arithmetic and copies ran while one was open for 1% of the time, Pallas kernels for 0%

profile of v8, /device:TPU:10, one launch (start us, length us, event | category | flops | bytes accessed | tf_op | source)
XLA Modules:
  0.0 165.6 jit_solution(17892506478327666197)
XLA Ops:
  0.0 3.6 %prepare.1 = (bf16[4,4,2,128,256]{4,3,2,1,0:T(8,128)(2,1)}, bf16[2,32,512]{2,1,0:T(8,128)(2,1)}) custom-call(bf16[128,1024]{1,0:T(8,128)(2,1)} %refs_0_.1, bf16[128,1024]{1,0:T(8,128)(2,1)} %refs_1_.1, bf16[32,512]{1,0:T(8,128)(2,1)} %refs_2_.1, bf16[32,512]{1,0:T(8,128)(2,1)} %refs_3_.1), custom_call_target="tpu_custom_call" | custom-call | flops 536870912 | bytes 1048576 | tf_op jit(solution)/shard_map/prepare/pallas_call | solution.py:71
  3.6 13.4 %all-to-all-start = ((bf16[16,2,128,256]{3,2,1,0:T(8,128)(2,1)}), bf16[16,2,128,256]{3,2,1,0:T(8,128)(2,1)S(1)}, u32[]{:S(2)}, u32[]{:S(2)}) async-start(bf16[16,2,128,256]{3,2,1,0:T(8,128)(2,1)} %bitcast.27), calls=%async_computation | async-start | bytes 4194304 | tf_op jit(solution)/shard_map/all_to_all | solution.py:188
  17.1 3.4 %collective-permute-start = (bf16[2,32,512]{2,1,0:T(8,128)(2,1)S(1)}, bf16[2,32,512]{2,1,0:T(8,128)(2,1)S(1)}, u32[]{:S(2)}, u32[]{:S(2)}) collective-permute-start(bf16[2,32,512]{2,1,0:T(8,128)(2,1)S(1)} %copy-done), channel_id=1, source_target_pairs={{0,256},{256,0},{1,257},{257,1},{2,258},{258,2},{3,259},{259,3},{4... | collective-permute-start | bytes 196616 | tf_op jit(solution)/shard_map/ppermute | solution.py:21
  20.5 26.1 %all-gather = bf16[16,32,512]{2,1,0:T(8,128)(2,1)S(1)} all-gather(bf16[2,32,512]{2,1,0:T(8,128)(2,1)S(1)} %copy-done), channel_id=2, replica_groups=mesh['zl'=2,'y'=8,'x'=4,'c'=2,'zh'=4] {'y'}, dimensions={0}, use_global_device_ids=true | all-gather | bytes 589824 | tf_op jit(solution)/shard_map/all_gather | solution.py:192
  46.6 1.9 %collective-permute-start.1 = (bf16[8,2,32,512]{3,2,1,0:T(8,128)(2,1)S(1)}, bf16[8,2,32,512]{3,2,1,0:T(8,128)(2,1)}, u32[]{:S(2)}, u32[]{:S(2)}) collective-permute-start(bf16[8,2,32,512]{3,2,1,0:T(8,128)(2,1)S(1)} %bitcast.23), channel_id=1, source_target_pairs={{0,4},{4,0},{1,5},{5,1},{2,6},{6,2},{3,7},{7,3},{8,12},{12,8},{9,1... | collective-permute-start | bytes 1572872 | tf_op jit(solution)/shard_map/ppermute | solution.py:21
  48.5 15.7 %collective-permute-done = bf16[2,32,512]{2,1,0:T(8,128)(2,1)S(1)} collective-permute-done((bf16[2,32,512]{2,1,0:T(8,128)(2,1)S(1)}, bf16[2,32,512]{2,1,0:T(8,128)(2,1)S(1)}, u32[]{:S(2)}, u32[]{:S(2)}) %collective-permute-start) | collective-permute-done | bytes 65568 | tf_op jit(solution)/shard_map/ppermute | solution.py:21
  64.2 26.2 %all-gather.1 = bf16[16,32,512]{2,1,0:T(8,128)(2,1)S(1)} all-gather(bf16[2,32,512]{2,1,0:T(8,128)(2,1)S(1)} %collective-permute-done), channel_id=3, replica_groups=mesh['zl'=2,'y'=8,'x'=4,'c'=2,'zh'=4] {'y'}, dimensions={0}, use_global_device_ids=true | all-gather | bytes 589824 | tf_op jit(solution)/shard_map/all_gather | solution.py:194
  90.4 1.9 %collective-permute-start.2 = (bf16[8,2,32,512]{3,2,1,0:T(8,128)(2,1)S(1)}, bf16[8,2,32,512]{3,2,1,0:T(8,128)(2,1)}, u32[]{:S(2)}, u32[]{:S(2)}) collective-permute-start(bf16[8,2,32,512]{3,2,1,0:T(8,128)(2,1)S(1)} %bitcast.25), channel_id=1, source_target_pairs={{0,4},{4,0},{1,5},{5,1},{2,6},{6,2},{3,7},{7,3},{8,12},{12,8},{9,1... | collective-permute-start | bytes 1572872 | tf_op jit(solution)/shard_map/ppermute | solution.py:21
  92.3 0.1 pad_add_fusion.place
  92.4 1.9 %collective-permute-done.2.core_far_basis = bf16[8,2,32,512]{3,2,1,0:T(8,128)(2,1)} collective-permute-done((bf16[8,2,32,512]{3,2,1,0:T(8,128)(2,1)S(1)}, bf16[8,2,32,512]{3,2,1,0:T(8,128)(2,1)}, u32[]{:S(2)}, u32[]{:S(2)}) %collective-permute-start.2) | collective-permute-done | bytes 524320 | tf_op jit(solution)/shard_map/ppermute | solution.py:21
  94.3 0.0 all-to-all-done
  94.3 2.7 %rotate.1 = f32[4,1040,128]{2,1,0:T(8,128)S(1)} custom-call(s32[2]{0:T(128)S(1)} %pad_add_fusion.place, bf16[4,4,2,128,256]{4,3,2,1,0:T(8,128)(2,1)S(1)} %bitcast.21, bf16[8,2,32,512]{3,2,1,0:T(8,128)(2,1)S(1)} %bitcast.24, bf16[8,2,32,512]{3,2,1,0:T(8,128)(2,1)S(1)} %bitcast.26, bf16[8,2,32,512]{3,2,1,0:T(8,128)(2,1)} %collective-permute-done.1.core_basis, ...), custom_call_target="tpu_custom_call" | custom-call | flops 1073741824 | bytes 8388608 | tf_op jit(solution)/shard_map/rotate/pallas_call | solution.py:135
  97.0 0.0 copy-start.1
  97.0 1.1 convert_element_type.23
  98.2 5.2 %all-to-all-start.1 = ((f16[4,1040,128]{2,1,0:T(8,128)(2,1)}), f16[4,1040,128]{2,1,0:T(8,128)(2,1)S(1)}, u32[]{:S(2)}, u32[]{:S(2)}) async-start(f16[4,1040,128]{2,1,0:T(8,128)(2,1)} %convert_element_type.23), calls=%async_computation.1 | async-start | bytes 2129920 | tf_op jit(solution)/shard_map/all_to_all | solution.py:199
  103.3 0.6 fusion.23
  105.2 12.2 %all-to-all-done.1 = f16[4,1040,128]{2,1,0:T(8,128)(2,1)S(1)} async-done(((f16[4,1040,128]{2,1,0:T(8,128)(2,1)}), f16[4,1040,128]{2,1,0:T(8,128)(2,1)S(1)}, u32[]{:S(2)}, u32[]{:S(2)}) %all-to-all-start.1) | async-done | bytes 1064992 | tf_op jit(solution)/shard_map/all_to_all | solution.py:199
  117.5 0.1 convert_element_type.24
  117.6 0.1 fusion
  117.8 0.1 fusion.4
  117.9 1.9 %collective-permute-start.3 = (bf16[2,512,128]{2,1,0:T(8,128)(2,1)S(1)}, bf16[2,512,128]{2,1,0:T(8,128)(2,1)S(1)}, u32[]{:S(2)}, u32[]{:S(2)}) collective-permute-start(bf16[2,512,128]{2,1,0:T(8,128)(2,1)S(1)} %pad_maximum_fusion.1), channel_id=1, source_target_pairs={{0,4},{4,0},{1,5},{5,1},{2,6},{6,2},{3,7},{7,3},{8,12},{12,8},{9,1... | collective-permute-start | bytes 786440 | tf_op jit(solution)/shard_map/ppermute | solution.py:21
  119.9 1.5 collective-permute-done.3
  121.4 1.1 broadcast_in_dim.28
  122.5 4.9 %all-to-all-start.2 = ((bf16[4,2,512,128]{3,2,1,0:T(8,128)(2,1)}), bf16[4,2,512,128]{3,2,1,0:T(8,128)(2,1)S(1)}, u32[]{:S(2)}, u32[]{:S(2)}) async-start(bf16[4,2,512,128]{3,2,1,0:T(8,128)(2,1)} %broadcast_in_dim.28), calls=%async_computation.2 | async-start | bytes 2097152 | tf_op jit(solution)/shard_map/all_to_all | solution.py:214
  127.5 0.1 fusion.22
  127.6 0.1 maximum_select_fusion
  127.7 18.4 %all-gather.2 = bf16[2048,128]{1,0:T(8,128)(2,1)S(1)} all-gather(bf16[512,128]{1,0:T(8,128)(2,1)S(1)} %maximum_select_fusion), channel_id=4, replica_groups=mesh['zl'=2,'y'=8,'x'=4,'c'=2,'zh'=4] {'zh'}, dimensions={0}, use_global_device_ids=true | all-gather | bytes 655360 | tf_op jit(solution)/shard_map/all_gather | solution.py:217
  146.1 1.2 share.1
  147.3 8.4 %all-to-all-start.3 = ((bf16[16,16,512]{2,1,0:T(8,128)(2,1)}), bf16[16,16,512]{2,1,0:T(8,128)(2,1)S(1)}, u32[]{:S(2)}, u32[]{:S(2)}) async-start(bf16[16,16,512]{2,1,0:T(8,128)(2,1)} %bitcast.13), calls=%async_computation.3 | async-start | bytes 524288 | tf_op jit(solution)/shard_map/all_to_all | solution.py:219
  155.8 9.0 %all-to-all-done.3 = bf16[16,16,512]{2,1,0:T(8,128)(2,1)S(1)} async-done(((bf16[16,16,512]{2,1,0:T(8,128)(2,1)}), bf16[16,16,512]{2,1,0:T(8,128)(2,1)S(1)}, u32[]{:S(2)}, u32[]{:S(2)}) %all-to-all-start.3) | async-done | bytes 262176 | tf_op jit(solution)/shard_map/all_to_all | solution.py:219
  164.9 0.1 divide_reduce_fusion
  164.9 0.6 broadcast_multiply_fusion
  (13 shorter events, 0.2 us)
Async XLA Ops:
  3.6 13.5 %copy-start = (bf16[2,32,512]{2,1,0:T(8,128)(2,1)S(1)}, bf16[2,32,512]{2,1,0:T(8,128)(2,1)}, u32[]{:S(2)}) copy-start(bf16[2,32,512]{2,1,0:T(8,128)(2,1)} %get-tuple-element.8) | copy-start | bytes 196612
  3.6 90.7 %all-to-all-start = ((bf16[16,2,128,256]{3,2,1,0:T(8,128)(2,1)}), bf16[16,2,128,256]{3,2,1,0:T(8,128)(2,1)S(1)}, u32[]{:S(2)}, u32[]{:S(2)}) async-start(bf16[16,2,128,256]{3,2,1,0:T(8,128)(2,1)} %bitcast.27), calls=%async_computation | async-start | bytes 4194304 | tf_op jit(solution)/shard_map/all_to_all | solution.py:188
  17.1 47.1 %collective-permute-start = (bf16[2,32,512]{2,1,0:T(8,128)(2,1)S(1)}, bf16[2,32,512]{2,1,0:T(8,128)(2,1)S(1)}, u32[]{:S(2)}, u32[]{:S(2)}) collective-permute-start(bf16[2,32,512]{2,1,0:T(8,128)(2,1)S(1)} %copy-done), channel_id=1, source_target_pairs={{0,256},{256,0},{1,257},{257,1},{2,258},{258,2},{3,259},{259,3},{4... | collective-permute-start | bytes 196616 | tf_op jit(solution)/shard_map/ppermute | solution.py:21
  46.6 45.8 %collective-permute-start.1 = (bf16[8,2,32,512]{3,2,1,0:T(8,128)(2,1)S(1)}, bf16[8,2,32,512]{3,2,1,0:T(8,128)(2,1)}, u32[]{:S(2)}, u32[]{:S(2)}) collective-permute-start(bf16[8,2,32,512]{3,2,1,0:T(8,128)(2,1)S(1)} %bitcast.23), channel_id=1, source_target_pairs={{0,4},{4,0},{1,5},{5,1},{2,6},{6,2},{3,7},{7,3},{8,12},{12,8},{9,1... | collective-permute-start | bytes 1572872 | tf_op jit(solution)/shard_map/ppermute | solution.py:21
  90.4 3.9 %collective-permute-start.2 = (bf16[8,2,32,512]{3,2,1,0:T(8,128)(2,1)S(1)}, bf16[8,2,32,512]{3,2,1,0:T(8,128)(2,1)}, u32[]{:S(2)}, u32[]{:S(2)}) collective-permute-start(bf16[8,2,32,512]{3,2,1,0:T(8,128)(2,1)S(1)} %bitcast.25), channel_id=1, source_target_pairs={{0,4},{4,0},{1,5},{5,1},{2,6},{6,2},{3,7},{7,3},{8,12},{12,8},{9,1... | collective-permute-start | bytes 1572872 | tf_op jit(solution)/shard_map/ppermute | solution.py:21
  97.0 6.3 %copy-start.1 = (s32[2]{0:T(128)S(1)}, s32[2]{0:T(128)}, u32[]{:S(2)}) copy-start(s32[2]{0:T(128)} %param.9) | copy-start | bytes 28
  98.2 19.3 %all-to-all-start.1 = ((f16[4,1040,128]{2,1,0:T(8,128)(2,1)}), f16[4,1040,128]{2,1,0:T(8,128)(2,1)S(1)}, u32[]{:S(2)}, u32[]{:S(2)}) async-start(f16[4,1040,128]{2,1,0:T(8,128)(2,1)} %convert_element_type.23), calls=%async_computation.1 | async-start | bytes 2129920 | tf_op jit(solution)/shard_map/all_to_all | solution.py:199
  117.9 3.4 %collective-permute-start.3 = (bf16[2,512,128]{2,1,0:T(8,128)(2,1)S(1)}, bf16[2,512,128]{2,1,0:T(8,128)(2,1)S(1)}, u32[]{:S(2)}, u32[]{:S(2)}) collective-permute-start(bf16[2,512,128]{2,1,0:T(8,128)(2,1)S(1)} %pad_maximum_fusion.1), channel_id=1, source_target_pairs={{0,4},{4,0},{1,5},{5,1},{2,6},{6,2},{3,7},{7,3},{8,12},{12,8},{9,1... | collective-permute-start | bytes 786440 | tf_op jit(solution)/shard_map/ppermute | solution.py:21
  122.5 23.6 %all-to-all-start.2 = ((bf16[4,2,512,128]{3,2,1,0:T(8,128)(2,1)}), bf16[4,2,512,128]{3,2,1,0:T(8,128)(2,1)S(1)}, u32[]{:S(2)}, u32[]{:S(2)}) async-start(bf16[4,2,512,128]{3,2,1,0:T(8,128)(2,1)} %broadcast_in_dim.28), calls=%async_computation.2 | async-start | bytes 2097152 | tf_op jit(solution)/shard_map/all_to_all | solution.py:214
  147.3 17.5 %all-to-all-start.3 = ((bf16[16,16,512]{2,1,0:T(8,128)(2,1)}), bf16[16,16,512]{2,1,0:T(8,128)(2,1)S(1)}, u32[]{:S(2)}, u32[]{:S(2)}) async-start(bf16[16,16,512]{2,1,0:T(8,128)(2,1)} %bitcast.13), calls=%async_computation.3 | async-start | bytes 524288 | tf_op jit(solution)/shard_map/all_to_all | solution.py:219

commit v9 on v8

--- a/solution.py
+++ b/solution.py
@@ -90,79 +90,82 @@
     )(*arrays)
 
 
-def rotate_kernel(place, tokens, basis, far_basis, core_basis, core_far_basis, out):
+def rotate_kernel(which, place, tokens, basis, core_basis, far_basis, core_far_basis, out):
     n_x, n_zh, _, toks, width = tokens.shape
-    n_y, _, rows, cols = basis.shape
+    _, n_y, rows, cols = basis.shape
     per, half = n_y * 2 // n_zh, width // 2
     zl, c = place[0], place[1]
     near, far = (pl.ds(pl.multiple_of(core * half, half), half) for core in (c, 1 - c))
-    sums = []
-    for which in range(2):
-        total = None
-        for side, bases in ((zl, (basis, core_basis)), (1 - zl, (far_basis, core_far_basis))):
-            for upper in range(n_y // per):
-                owner = side * (n_y // per) + upper
-                left = [
-                    tokens[:, owner, which, :, lanes].reshape(n_x * toks, half)
-                    for lanes in (near, far)
-                ]
-                right = [
-                    ref[upper * per : (upper + 1) * per, which].reshape(per * rows, cols)
-                    for ref in bases
-                ]
-                product = jnp.dot(
-                    jnp.concatenate(left, axis=1),
-                    jnp.concatenate(right, axis=0),
-                    preferred_element_type=F32,
-                )
-                total = product if total is None else total + product
-        sums.append(total)
-    largest = jnp.max(jnp.maximum(jnp.abs(sums[0]), jnp.abs(sums[1])), axis=0, keepdims=True)
-    largest = jnp.max(largest, axis=1, keepdims=True)
+    total = None
+    sides = (
+        (zl, (basis.at[which], core_basis.at[which])),
+        (1 - zl, (far_basis, core_far_basis)),
+    )
+    for side, bases in sides:
+        for upper in range(n_y // per):
+            owner = side * (n_y // per) + upper
+            left = [
+                tokens[:, owner, which, :, lanes].reshape(n_x * toks, half) for lanes in (near, far)
+            ]
+            right = [
+                ref[upper * per : (upper + 1) * per].reshape(per * rows, cols) for ref in bases
+            ]
+            product = jnp.dot(
+                jnp.concatenate(left, axis=1),
+                jnp.concatenate(right, axis=0),
+                preferred_element_type=F32,
+            )
+            total = product if total is None else total + product
+    largest = jnp.max(jnp.max(jnp.abs(total), axis=0, keepdims=True), axis=1, keepdims=True)
     level = jnp.clip(jnp.ceil(jnp.log2(jnp.maximum(largest, 1e-30))), -100.0, 100.0)
-    factor = jnp.exp2(F32(TOP) - level)
+    total = total * jnp.exp2(F32(TOP) - level)
     group, part = n_x * toks, cols // n_x
-    for x in range(n_x):
-        for which in range(2):
-            value = sums[which][:, x * part : (x + 1) * part] * factor
-            out[x, pl.ds(which * group, group)] = value
-        out[x, pl.ds(2 * group, TILE)] = jnp.broadcast_to(level, (TILE, part))
-
-
-def rotate(place, *arrays):
+    for i in range(out.shape[0]):
+        if which == 0:
+            value = total[:, i * part : (i + 1) * part]
+        else:
+            value = total[:, i * part // 2 : (i + 1) * part // 2]
+            value = jnp.concatenate([value[: group // 2], value[group // 2 :]], axis=1)
+        out[i, pl.ds(0, value.shape[0])] = value
+        out[i, pl.ds(value.shape[0], TILE)] = jnp.broadcast_to(level, (TILE, part))
+
+
+def rotate(which, place, *arrays):
     n_x, n_zh, _, toks, width = arrays[0].shape
-    cols = arrays[-1].shape[3]
+    cols = arrays[-1].shape[2]
+    pieces = n_x * (1 + which)
+    depth = n_x * toks // (1 + which) + TILE
     return pl.pallas_call(
-        rotate_kernel,
-        out_shape=jax.ShapeDtypeStruct((n_x, 2 * n_x * toks + TILE, cols // n_x), F32),
+        lambda *refs: rotate_kernel(which, *refs),
+        out_shape=jax.ShapeDtypeStruct((pieces, depth, cols // n_x), F32),
         in_specs=[SMEM] + [VMEM] * len(arrays),
         out_specs=VMEM,
         compiler_params=pltpu.CompilerParams(vmem_limit_bytes=40 * 2**20),
         cost_estimate=pl.CostEstimate(
-            flops=4 * n_x * n_zh * toks * width * cols, bytes_accessed=8 * 2**20, transcendentals=0
+            flops=2 * n_x * n_zh * toks * width * cols, bytes_accessed=4 * 2**20, transcendentals=0
         ),
         name="rotate",
     )(place, *arrays)
 
 
 def share_kernel(grad, act, out):
-    n_k, _, part = grad.shape
-    n_x, n_c = act.shape[:2]
-    half = part // n_c
-    turned = [grad[k].T for k in range(n_k)]
+    n_k, n_c, depth, part = grad.shape
+    n_x, half = act.shape[0], part // 2
     total = None
     for core in range(n_c):
-        left = jnp.concatenate([t[core * half : (core + 1) * half] for t in turned], axis=0)
-        right = jnp.concatenate([act[x, core] for x in range(n_x)], axis=1)
-        product = jnp.dot(left, right, preferred_element_type=F32)
-        total = product if total is None else total + product
+        turned = [grad[k, core].T for k in range(n_k)]
+        for side in range(2):
+            left = jnp.concatenate([t[side * half : (side + 1) * half] for t in turned], axis=0)
+            tokens = slice(side * depth, (side + 1) * depth)
+            right = jnp.concatenate([act[x, core, tokens] for x in range(n_x)], axis=1)
+            product = jnp.dot(left, right, preferred_element_type=F32)
+            total = product if total is None else total + product
     out[...] = total.astype(BF16)
 
 
 def share_of(grad, act):
-    n_k, group, part = grad.shape
-    n_x, n_c = act.shape[:2]
-    rows, cols = n_k * part // n_c, n_x * part
+    n_k, n_c, depth, part = grad.shape
+    rows, cols = n_k * part // 2, act.shape[0] * part
     return pl.pallas_call(
         share_kernel,
         out_shape=jax.ShapeDtypeStruct((rows, cols), BF16),
@@ -170,10 +173,18 @@
         out_specs=VMEM,
         compiler_params=pltpu.CompilerParams(vmem_limit_bytes=32 * 2**20),
         cost_estimate=pl.CostEstimate(
-            flops=2 * n_c * rows * cols * group, bytes_accessed=2 * 2**20, transcendentals=0
+            flops=4 * n_c * rows * cols * depth, bytes_accessed=2 * 2**20, transcendentals=0
         ),
         name="share",
     )(grad, act)
+
+
+def total_of(partial, axes, n_x):
+    partial = lax.all_to_all(partial.astype(F16), axes, 0, 0, tiled=True).astype(F32)
+    factors = jnp.exp2(partial[:, None, -TILE:] - F32(TOP))
+    partial = partial[:, :-TILE].reshape(len(partial), -1, TILE, partial.shape[2]) * factors
+    partial = partial.reshape(n_x, -1, *partial.shape[1:])
+    return jnp.sum(partial, axis=0).reshape(partial.shape[1], -1, partial.shape[4])
 
 
 def on_device(activations, gradients, basis_act, basis_grad, lengths):
@@ -181,36 +192,34 @@
     zl, y, c = (lax.axis_index(a) for a in ("zl", "y", "c"))
     toks = activations.shape[0]
     cols = basis_act.shape[1]
-    part, group = cols // n_x, n_x * toks
+    group = n_x * toks
 
     tokens, bases = prepare(n_y // 2, n_x, n_c, n_zh, activations, gradients, basis_act, basis_grad)
-    far_bases = shift(bases, "zl", 1)
     tokens = lax.all_to_all(
         tokens.reshape(n_x * n_zh, *tokens.shape[2:]), ("x", "zh"), 0, 0, tiled=True
     ).reshape(tokens.shape)
 
-    basis = lax.all_gather(bases, "y", axis=0)
+    basis = lax.all_gather(bases, "y", axis=1)
     core_basis = shift(basis, "c", 1)
-    far_basis = lax.all_gather(far_bases, "y", axis=0)
-    core_far_basis = shift(far_basis, "c", 1)
+    far_act = shift(basis[0], "zl", 1)
+    far_grad = shift(basis[1], "zl", 1)
+    core_far_act, core_far_grad = shift(far_act, "c", 1), shift(far_grad, "c", 1)
 
     place = jnp.stack([zl, c]).astype(jnp.int32)
-    partial = rotate(place, tokens, basis, far_basis, core_basis, core_far_basis)
-    partial = lax.all_to_all(partial.astype(F16), "x", 0, 0, tiled=True).astype(F32)
-    factors = jnp.exp2(partial[:, None, 2 * group :] - F32(TOP))
-    partial = partial[:, : 2 * group].reshape(n_x, 2 * group // TILE, TILE, part)
-    rotated = jnp.sum(partial * factors, axis=0).reshape(2 * group, part)
+    act = rotate(0, place, tokens, basis, core_basis, far_act, core_far_act)
+    rot_act = total_of(act, "x", n_x)[0]
+    grad = rotate(1, place, tokens, basis, core_basis, far_grad, core_far_grad)
+    rot_grad = total_of(grad, ("x", "c"), n_x).astype(BF16)
     index = jnp.arange(group, dtype=jnp.int32)
     position = ((y * n_x + index // toks) * n_c + c) * toks + index % toks
     length = jnp.where(zl == 0, lengths[0], lengths[1])
     valid = position < length
-    rot_act = jnp.where(valid[:, None], rotated[:group], F32(0.0)).astype(BF16)
-    mine = jnp.stack([rot_act, rotated[group:].astype(BF16)])
-    other = shift(mine, "c", 1)
-
-    lane = jnp.arange(part, dtype=jnp.int32)
-    rot_grad = jnp.where(lane // (part // n_c) == c, mine[1], jnp.roll(other[1], part // n_c, axis=1))
-    both_act = jnp.where(c == 0, jnp.stack([mine[0], other[0]]), jnp.stack([other[0], mine[0]]))
+    rot_act = jnp.where(valid[:, None], rot_act, F32(0.0)).astype(BF16)
+    other_act = shift(rot_act, "c", 1)
+
+    both_act = jnp.where(
+        c == 0, jnp.stack([rot_act, other_act]), jnp.stack([other_act, rot_act])
+    )
     wide_act = lax.all_to_all(
         jnp.broadcast_to(both_act[None], (n_x, *both_act.shape)), "x", 0, 0, tiled=True
     )

time: 166 us -> 149 us (0.90)
  blocking collectives: 70.7 us -> 45.3 us
  starting transfers between devices: 41.1 us -> 49.3 us
  waiting for transfers between devices: 40.4 us -> 36.8 us
  other arithmetic: 2.56 us -> 4.29 us
    all_gather x2 -> x1, blocking collectives: 52.3 us -> 26.2 us  [on_device(): basis = lax.all_gather(bases, 'y', axis=1)]
    all_to_all x1 -> x2, waiting for transfers between devices: 12.2 us -> 6.11 us  [total_of(): lax.all_to_all(partial.astype(F16), axes, 0, 0, tiled=True).astype(F32)]
    all_to_all x1 -> x2, starting transfers between devices: 5.18 us -> 9.97 us  [total_of(): lax.all_to_all(partial.astype(F16), axes, 0, 0, tiled=True).astype(F32)]
    ppermute x4 -> x6, starting transfers between devices: 9.12 us -> 13.6 us  [shift(): return lax.ppermute(value, axis, [(i, (i + step) % n) for i in range(n)])]
    ppermute x4 -> x6, waiting for transfers between devices: 19.1 us -> 21.6 us  [shift(): return lax.ppermute(value, axis, [(i, (i + step) % n) for i in range(n)])]
    convert_element_type x3 -> x6, other arithmetic: 1.39 us -> 3.24 us  [the longest x2 1.78 us: total_of(): partial.astype(F16)]
    pallas_call x1 -> x2, Pallas kernels: 2.72 us -> 4.08 us  [rotate(): pl.pallas_call(lambda *refs: rotate_kernel(which, *refs), out_shape=jax.S...]
  transfers between devices with their start and end apart: 8 -> 11, of which waited for: 5 -> 6; matrix products, arithmetic and copies ran while one was open for 1% -> 3% of each run, Pallas kernels for 0% -> 3%
where the time goes in v9:
time: 149 us
  starting transfers between devices  49.3 us (33%)
  blocking collectives  45.3 us (30%)
  waiting for transfers between devices  36.8 us (25%)
  Pallas kernels  8.89 us (6%)
  other arithmetic  4.29 us (3%)
  local copies, waits for them, and re-layouts  2.58 us (2%)
    all_gather x1, blocking collectives, on_device(): basis = lax.all_gather(bases, 'y', axis=1)  26.2 us
    ppermute x6, waiting for transfers between devices, shift(): return lax.ppermute(value, axis, [(i, (i + step) % n) for i in range(n)])  21.6 us
    all_gather x1, blocking collectives, on_device(): wide_grad = lax.all_gather(rot_grad, 'zh', axis=0)  19 us
    ppermute x6, starting transfers between devices, shift(): return lax.ppermute(value, axis, [(i, (i + step) % n) for i in range(n)])  13.6 us
    all_to_all x1, starting transfers between devices, on_device(): lax.all_to_all(tokens.reshape(n_x * n_zh, *tokens.shape[2:]), ('x', 'zh')...  13.4 us
    all_to_all x2, starting transfers between devices, total_of(): lax.all_to_all(partial.astype(F16), axes, 0, 0, tiled=True).astype(F32)  9.97 us
    all_to_all x1, waiting for transfers between devices, on_device(): received = lax.all_to_all(share, ('zl', 'y'), 0, 0, tiled=True)  9.04 us
    all_to_all x1, starting transfers between devices, on_device(): received = lax.all_to_all(share, ('zl', 'y'), 0, 0, tiled=True)  7.38 us
  transfers between devices with their start and end apart: 11, of which 6 were waited for; matrix products, arithmetic and copies ran while one was open for 3% of the time, Pallas kernels for 3%

profile of v9, /device:TPU:10, one launch (start us, length us, event | category | flops | bytes accessed | tf_op | source)
XLA Modules:
  0.0 148.6 jit_solution(15533126876043609074)
XLA Ops:
  0.0 3.6 %prepare.1 = (bf16[4,4,2,128,256]{4,3,2,1,0:T(8,128)(2,1)}, bf16[2,32,512]{2,1,0:T(8,128)(2,1)}) custom-call(bf16[128,1024]{1,0:T(8,128)(2,1)} %refs_0_.1, bf16[128,1024]{1,0:T(8,128)(2,1)} %refs_1_.1, bf16[32,512]{1,0:T(8,128)(2,1)} %refs_2_.1, bf16[32,512]{1,0:T(8,128)(2,1)} %refs_3_.1), custom_call_target="tpu_custom_call" | custom-call | flops 536870912 | bytes 1048576 | tf_op jit(solution)/shard_map/prepare/pallas_call | solution.py:71
  3.6 13.4 %all-to-all-start = ((bf16[16,2,128,256]{3,2,1,0:T(8,128)(2,1)}), bf16[16,2,128,256]{3,2,1,0:T(8,128)(2,1)S(1)}, u32[]{:S(2)}, u32[]{:S(2)}) async-start(bf16[16,2,128,256]{3,2,1,0:T(8,128)(2,1)} %bitcast.29), calls=%async_computation | async-start | bytes 4194304 | tf_op jit(solution)/shard_map/all_to_all | solution.py:198
  17.1 26.2 %all-gather = bf16[2,256,512]{2,1,0:T(8,128)(2,1)S(1)} all-gather(bf16[2,32,512]{2,1,0:T(8,128)(2,1)S(1)} %copy-done), channel_id=2, replica_groups=mesh['zl'=2,'y'=8,'x'=4,'c'=2,'zh'=4] {'y'}, dimensions={1}, use_global_device_ids=true | all-gather | bytes 589824 | tf_op jit(solution)/shard_map/all_gather | solution.py:202
  43.3 0.7 fusion.19
  44.1 3.2 %collective-permute-start.3 = (bf16[8,32,512]{2,1,0:T(8,128)(2,1)S(1)}, bf16[8,32,512]{2,1,0:T(8,128)(2,1)}, u32[]{:S(2)}, u32[]{:S(2)}) collective-permute-start(bf16[8,32,512]{2,1,0:T(8,128)(2,1)S(1)} %bitcast.32), channel_id=1, source_target_pairs={{0,256},{256,0},{1,257},{257,1},{2,258},{258,2},{3,259},{259,3},{4... | collective-permute-start | bytes 786440 | tf_op jit(solution)/shard_map/ppermute | solution.py:21
  47.3 1.9 %collective-permute-start = (bf16[2,8,32,512]{3,2,1,0:T(8,128)(2,1)S(1)}, bf16[2,8,32,512]{3,2,1,0:T(8,128)(2,1)S(1)}, u32[]{:S(2)}, u32[]{:S(2)}) collective-permute-start(bf16[2,8,32,512]{3,2,1,0:T(8,128)(2,1)S(1)} %bitcast.25), channel_id=1, source_target_pairs={{0,4},{4,0},{1,5},{5,1},{2,6},{6,2},{3,7},{7,3},{8,12},{12,8},{9,1... | collective-permute-start | bytes 1572872 | tf_op jit(solution)/shard_map/ppermute | solution.py:21
  49.2 20.3 %collective-permute-done.3.refs_4_ = bf16[8,32,512]{2,1,0:T(8,128)(2,1)} collective-permute-done((bf16[8,32,512]{2,1,0:T(8,128)(2,1)S(1)}, bf16[8,32,512]{2,1,0:T(8,128)(2,1)}, u32[]{:S(2)}, u32[]{:S(2)}) %collective-permute-start.3) | collective-permute-done | bytes 262176 | tf_op jit(solution)/shard_map/ppermute | solution.py:21
  69.6 1.9 %collective-permute-start.4 = (bf16[8,32,512]{2,1,0:T(8,128)(2,1)}, bf16[8,32,512]{2,1,0:T(8,128)(2,1)}, u32[]{:S(2)}, u32[]{:S(2)}) collective-permute-start(bf16[8,32,512]{2,1,0:T(8,128)(2,1)} %collective-permute-done.3.refs_4_), channel_id=1, source_target_pairs={{0,4},{4,0},{1,5},{5,1},{2,6},{6,2},{3,7},{7,3},{8,12},{12,8},{9,1... | collective-permute-start | bytes 786440 | tf_op jit(solution)/shard_map/ppermute | solution.py:21
  71.5 2.5 %collective-permute-start.1 = (bf16[8,32,512]{2,1,0:T(8,128)(2,1)}, bf16[8,32,512]{2,1,0:T(8,128)(2,1)S(1)}, u32[]{:S(2)}, u32[]{:S(2)}) collective-permute-start(bf16[8,32,512]{2,1,0:T(8,128)(2,1)} %bitcast.5), channel_id=1, source_target_pairs={{0,256},{256,0},{1,257},{257,1},{2,258},{258,2},{3,259},{259,3},{4... | collective-permute-start | bytes 786440 | tf_op jit(solution)/shard_map/ppermute | solution.py:21
  74.1 1.9 %rotate.3 = f32[4,528,128]{2,1,0:T(8,128)S(1)} custom-call(s32[2]{0:T(128)S(1)} %pad_add_fusion.refs_0_, bf16[4,4,2,128,256]{4,3,2,1,0:T(8,128)(2,1)S(1)} %bitcast.23, bf16[2,8,32,512]{3,2,1,0:T(8,128)(2,1)S(1)} %bitcast.26, bf16[2,8,32,512]{3,2,1,0:T(8,128)(2,1)S(1)} %collective-permute-done.refs_3_, bf16[8,32,512]{2,1,0:T(8,128)(2,1)} %collective-permute-done.3.refs_4_, ...), custom_call_target="tpu_custom_call" | custom-call | flops 536870912 | bytes 4194304 | tf_op jit(solution)/shard_map/rotate/pallas_call | solution.py:138
  76.1 0.9 convert_element_type.48
  77.0 5.1 %all-to-all-start.2 = ((f16[4,528,128]{2,1,0:T(8,128)(2,1)}), f16[4,528,128]{2,1,0:T(8,128)(2,1)}, u32[]{:S(2)}, u32[]{:S(2)}) async-start(f16[4,528,128]{2,1,0:T(8,128)(2,1)} %convert_element_type.48), calls=%async_computation.2 | async-start | bytes 1081344 | tf_op jit(solution)/shard_map/all_to_all | solution.py:183
  82.0 0.3 collective-permute-done.1.refs_4_
  82.3 1.9 %collective-permute-start.2 = (bf16[8,32,512]{2,1,0:T(8,128)(2,1)S(1)}, bf16[8,32,512]{2,1,0:T(8,128)(2,1)}, u32[]{:S(2)}, u32[]{:S(2)}) collective-permute-start(bf16[8,32,512]{2,1,0:T(8,128)(2,1)S(1)} %collective-permute-done.1.refs_4_), channel_id=1, source_target_pairs={{0,4},{4,0},{1,5},{5,1},{2,6},{6,2},{3,7},{7,3},{8,12},{12,8},{9,1... | collective-permute-start | bytes 786440 | tf_op jit(solution)/shard_map/ppermute | solution.py:21
  84.2 0.7 fusion.20
  86.2 2.2 %rotate.2 = f32[8,272,128]{2,1,0:T(8,128)S(1)} custom-call(s32[2]{0:T(128)S(1)} %pad_add_fusion.refs_0_, bf16[4,4,2,128,256]{4,3,2,1,0:T(8,128)(2,1)S(1)} %bitcast.24, bf16[2,8,32,512]{3,2,1,0:T(8,128)(2,1)S(1)} %bitcast.27, bf16[2,8,32,512]{3,2,1,0:T(8,128)(2,1)S(1)} %collective-permute-done.refs_3_, ...), custom_call_target="tpu_custom_call" | custom-call | flops 536870912 | bytes 4194304 | tf_op jit(solution)/shard_map/rotate/pallas_call | solution.py:138
  88.4 0.9 convert_element_type.44
  89.2 1.5 all-to-all-done.2
  90.7 4.9 %all-to-all-start.1 = ((f16[8,272,128]{2,1,0:T(8,128)(2,1)}), f16[8,272,128]{2,1,0:T(8,128)(2,1)S(1)}, u32[]{:S(2)}, u32[]{:S(2)}) async-start(f16[8,272,128]{2,1,0:T(8,128)(2,1)} %convert_element_type.44), calls=%async_computation.1 | async-start | bytes 1114112 | tf_op jit(solution)/shard_map/all_to_all | solution.py:183
  95.6 1.1 convert_element_type.49
  96.8 0.1 select_convert_fusion
  97.0 2.1 %collective-permute-start.5 = (bf16[512,128]{1,0:T(8,128)(2,1)S(1)}, bf16[512,128]{1,0:T(8,128)(2,1)S(1)}, u32[]{:S(2)}, u32[]{:S(2)}) collective-permute-start(bf16[512,128]{1,0:T(8,128)(2,1)S(1)} %select_convert_fusion), channel_id=1, source_target_pairs={{0,4},{4,0},{1,5},{5,1},{2,6},{6,2},{3,7},{7,3},{8,12},{12,8},{9,1... | collective-permute-start | bytes 393224 | tf_op jit(solution)/shard_map/ppermute | solution.py:21
  99.0 0.1 fusion.1
  99.2 1.0 collective-permute-done.5
  100.3 4.6 %all-to-all-done.1 = f16[8,272,128]{2,1,0:T(8,128)(2,1)S(1)} async-done(((f16[8,272,128]{2,1,0:T(8,128)(2,1)}), f16[8,272,128]{2,1,0:T(8,128)(2,1)S(1)}, u32[]{:S(2)}, u32[]{:S(2)}) %all-to-all-start.1) | async-done | bytes 557088 | tf_op jit(solution)/shard_map/all_to_all | solution.py:183
  104.9 1.1 broadcast_in_dim.30
  106.0 4.9 %all-to-all-start.3 = ((bf16[4,2,512,128]{3,2,1,0:T(8,128)(2,1)}), bf16[4,2,512,128]{3,2,1,0:T(8,128)(2,1)S(1)}, u32[]{:S(2)}, u32[]{:S(2)}) async-start(bf16[4,2,512,128]{3,2,1,0:T(8,128)(2,1)} %broadcast_in_dim.30), calls=%async_computation.3 | async-start | bytes 2097152 | tf_op jit(solution)/shard_map/all_to_all | solution.py:223
  111.2 19.0 %all_gather.12.grad = bf16[4,2,256,128]{3,2,1,0:T(8,128)(2,1)S(1)} all-gather(bf16[1,2,256,128]{3,2,1,0:T(8,128)(2,1)S(1)} %bitcast.30), channel_id=1, replica_groups=mesh['zl'=2,'y'=8,'x'=4,'c'=2,'zh'=4] {'zh'}, dimensions={0}, use_global_device_ids=true | all-gather | bytes 655360 | tf_op jit(solution)/shard_map/all_gather | solution.py:226
  130.2 1.2 share.1
  131.4 7.4 %all-to-all-start.4 = ((bf16[16,16,512]{2,1,0:T(8,128)(2,1)}), bf16[16,16,512]{2,1,0:T(8,128)(2,1)S(1)}, u32[]{:S(2)}, u32[]{:S(2)}) async-start(bf16[16,16,512]{2,1,0:T(8,128)(2,1)} %bitcast.15), calls=%async_computation.4 | async-start | bytes 524288 | tf_op jit(solution)/shard_map/all_to_all | solution.py:228
  138.8 9.0 %all-to-all-done.4 = bf16[16,16,512]{2,1,0:T(8,128)(2,1)S(1)} async-done(((bf16[16,16,512]{2,1,0:T(8,128)(2,1)}), bf16[16,16,512]{2,1,0:T(8,128)(2,1)S(1)}, u32[]{:S(2)}, u32[]{:S(2)}) %all-to-all-start.4) | async-done | bytes 262176 | tf_op jit(solution)/shard_map/all_to_all | solution.py:228
  148.0 0.6 broadcast_multiply_fusion
  (21 shorter events, 0.6 us)
Async XLA Ops:
  3.6 13.5 %copy-start = (bf16[2,32,512]{2,1,0:T(8,128)(2,1)S(1)}, bf16[2,32,512]{2,1,0:T(8,128)(2,1)}, u32[]{:S(2)}) copy-start(bf16[2,32,512]{2,1,0:T(8,128)(2,1)} %get-tuple-element.8) | copy-start | bytes 196612
  3.6 70.5 %all-to-all-start = ((bf16[16,2,128,256]{3,2,1,0:T(8,128)(2,1)}), bf16[16,2,128,256]{3,2,1,0:T(8,128)(2,1)S(1)}, u32[]{:S(2)}, u32[]{:S(2)}) async-start(bf16[16,2,128,256]{3,2,1,0:T(8,128)(2,1)} %bitcast.29), calls=%async_computation | async-start | bytes 4194304 | tf_op jit(solution)/shard_map/all_to_all | solution.py:198
  44.1 25.5 %collective-permute-start.3 = (bf16[8,32,512]{2,1,0:T(8,128)(2,1)S(1)}, bf16[8,32,512]{2,1,0:T(8,128)(2,1)}, u32[]{:S(2)}, u32[]{:S(2)}) collective-permute-start(bf16[8,32,512]{2,1,0:T(8,128)(2,1)S(1)} %bitcast.32), channel_id=1, source_target_pairs={{0,256},{256,0},{1,257},{257,1},{2,258},{258,2},{3,259},{259,3},{4... | collective-permute-start | bytes 786440 | tf_op jit(solution)/shard_map/ppermute | solution.py:21
  47.3 26.8 %collective-permute-start = (bf16[2,8,32,512]{3,2,1,0:T(8,128)(2,1)S(1)}, bf16[2,8,32,512]{3,2,1,0:T(8,128)(2,1)S(1)}, u32[]{:S(2)}, u32[]{:S(2)}) collective-permute-start(bf16[2,8,32,512]{3,2,1,0:T(8,128)(2,1)S(1)} %bitcast.25), channel_id=1, source_target_pairs={{0,4},{4,0},{1,5},{5,1},{2,6},{6,2},{3,7},{7,3},{8,12},{12,8},{9,1... | collective-permute-start | bytes 1572872 | tf_op jit(solution)/shard_map/ppermute | solution.py:21
  69.6 4.6 %collective-permute-start.4 = (bf16[8,32,512]{2,1,0:T(8,128)(2,1)}, bf16[8,32,512]{2,1,0:T(8,128)(2,1)}, u32[]{:S(2)}, u32[]{:S(2)}) collective-permute-start(bf16[8,32,512]{2,1,0:T(8,128)(2,1)} %collective-permute-done.3.refs_4_), channel_id=1, source_target_pairs={{0,4},{4,0},{1,5},{5,1},{2,6},{6,2},{3,7},{7,3},{8,12},{12,8},{9,1... | collective-permute-start | bytes 786440 | tf_op jit(solution)/shard_map/ppermute | solution.py:21
  71.5 10.8 %collective-permute-start.1 = (bf16[8,32,512]{2,1,0:T(8,128)(2,1)}, bf16[8,32,512]{2,1,0:T(8,128)(2,1)S(1)}, u32[]{:S(2)}, u32[]{:S(2)}) collective-permute-start(bf16[8,32,512]{2,1,0:T(8,128)(2,1)} %bitcast.5), channel_id=1, source_target_pairs={{0,256},{256,0},{1,257},{257,1},{2,258},{258,2},{3,259},{259,3},{4... | collective-permute-start | bytes 786440 | tf_op jit(solution)/shard_map/ppermute | solution.py:21
  76.0 8.2 %copy-start.1 = (s32[2]{0:T(128)S(1)}, s32[2]{0:T(128)}, u32[]{:S(2)}) copy-start(s32[2]{0:T(128)} %param.9) | copy-start | bytes 28
  77.0 13.7 %all-to-all-start.2 = ((f16[4,528,128]{2,1,0:T(8,128)(2,1)}), f16[4,528,128]{2,1,0:T(8,128)(2,1)}, u32[]{:S(2)}, u32[]{:S(2)}) async-start(f16[4,528,128]{2,1,0:T(8,128)(2,1)} %convert_element_type.48), calls=%async_computation.2 | async-start | bytes 1081344 | tf_op jit(solution)/shard_map/all_to_all | solution.py:183
  82.3 3.9 %collective-permute-start.2 = (bf16[8,32,512]{2,1,0:T(8,128)(2,1)S(1)}, bf16[8,32,512]{2,1,0:T(8,128)(2,1)}, u32[]{:S(2)}, u32[]{:S(2)}) collective-permute-start(bf16[8,32,512]{2,1,0:T(8,128)(2,1)S(1)} %collective-permute-done.1.refs_4_), channel_id=1, source_target_pairs={{0,4},{4,0},{1,5},{5,1},{2,6},{6,2},{3,7},{7,3},{8,12},{12,8},{9,1... | collective-permute-start | bytes 786440 | tf_op jit(solution)/shard_map/ppermute | solution.py:21
  90.7 14.2 %all-to-all-start.1 = ((f16[8,272,128]{2,1,0:T(8,128)(2,1)}), f16[8,272,128]{2,1,0:T(8,128)(2,1)S(1)}, u32[]{:S(2)}, u32[]{:S(2)}) async-start(f16[8,272,128]{2,1,0:T(8,128)(2,1)} %convert_element_type.44), calls=%async_computation.1 | async-start | bytes 1114112 | tf_op jit(solution)/shard_map/all_to_all | solution.py:183
  97.0 3.2 %collective-permute-start.5 = (bf16[512,128]{1,0:T(8,128)(2,1)S(1)}, bf16[512,128]{1,0:T(8,128)(2,1)S(1)}, u32[]{:S(2)}, u32[]{:S(2)}) collective-permute-start(bf16[512,128]{1,0:T(8,128)(2,1)S(1)} %select_convert_fusion), channel_id=1, source_target_pairs={{0,4},{4,0},{1,5},{5,1},{2,6},{6,2},{3,7},{7,3},{8,12},{12,8},{9,1... | collective-permute-start | bytes 393224 | tf_op jit(solution)/shard_map/ppermute | solution.py:21
  106.0 24.2 %all-to-all-start.3 = ((bf16[4,2,512,128]{3,2,1,0:T(8,128)(2,1)}), bf16[4,2,512,128]{3,2,1,0:T(8,128)(2,1)S(1)}, u32[]{:S(2)}, u32[]{:S(2)}) async-start(bf16[4,2,512,128]{3,2,1,0:T(8,128)(2,1)} %broadcast_in_dim.30), calls=%async_computation.3 | async-start | bytes 2097152 | tf_op jit(solution)/shard_map/all_to_all | solution.py:223
  131.4 16.4 %all-to-all-start.4 = ((bf16[16,16,512]{2,1,0:T(8,128)(2,1)}), bf16[16,16,512]{2,1,0:T(8,128)(2,1)S(1)}, u32[]{:S(2)}, u32[]{:S(2)}) async-start(bf16[16,16,512]{2,1,0:T(8,128)(2,1)} %bitcast.15), calls=%async_computation.4 | async-start | bytes 524288 | tf_op jit(solution)/shard_map/all_to_all | solution.py:228

commit v10 on v9

v10 whole, which is shorter than its diff:
```python
import jax
import jax.numpy as jnp
from jax import lax
from jax.experimental import pallas as pl
from jax.experimental.pallas import tpu as pltpu
from jax.sharding import Mesh
from jax.sharding import PartitionSpec as P

SEQS = 2
F32 = jnp.float32
BF16 = jnp.bfloat16
F16 = jnp.float16
TILE = 16
TOP = 15
VMEM = pl.BlockSpec(memory_space=pltpu.VMEM)
SMEM = pl.BlockSpec(memory_space=pltpu.SMEM)


def shift(value, axis, step):
    n = lax.axis_size(axis)
    return lax.ppermute(value, axis, [(i, (i + step) % n) for i in range(n)])


def sorting(width, outer, n_x, inner):
    run = width // (outer * n_x * inner)
    source = lax.broadcasted_iota(jnp.int32, (width, width), 0)
    target = lax.broadcasted_iota(jnp.int32, (width, width), 1)
    at_run, at_inner = source % run, source // run % inner
    at_x, at_outer = source // (run * inner) % n_x, source // (run * inner * n_x)
    moved = ((at_x * inner + at_inner) * outer + at_outer) * run + at_run
    return (moved == target).astype(F32).astype(BF16)


def spread(value, ones):
    return jnp.dot(value, ones, preferred_element_type=F32).astype(BF16)


def bases_kernel(y_lo, n_x, n_c, act, grad, out, held, sems):
    copies = [
        pltpu.make_async_copy(ref, held.at[i], sems.at[i]) for i, ref in enumerate((act, grad))
    ]
    for copy in copies:
        copy.start()
    by_owner = sorting(held.shape[2], y_lo, n_x, n_c)
    for copy in copies:
        copy.wait()
    out[0] = held[0]
    out[1] = spread(held[1], by_owner)


def arrange_bases(y_lo, n_x, n_c, act, grad):
    return pl.pallas_call(
        lambda *refs: bases_kernel(y_lo, n_x, n_c, *refs),
        out_shape=jax.ShapeDtypeStruct((2, *act.shape), BF16),
        in_specs=[pl.BlockSpec(memory_space=pl.ANY)] * 2,
        out_specs=VMEM,
        scratch_shapes=[pltpu.VMEM((2, *act.shape), BF16), pltpu.SemaphoreType.DMA((2,))],
        compiler_params=pltpu.CompilerParams(vmem_limit_bytes=60 * 2**20),
        cost_estimate=pl.CostEstimate(
            flops=2 * act.shape[0] * act.shape[1] ** 2, bytes_accessed=2**17, transcendentals=0
        ),
        name="arrange_bases",
    )(act, grad)


def tokens_kernel(y_lo, n_c, act, grad, tokens, held, in_sems, moved, out_sems):
    copies = [
        pltpu.make_async_copy(ref, held.at[i], in_sems.at[i]) for i, ref in enumerate((act, grad))
    ]
    for copy in copies:
        copy.start()
    n_x, n_zh, _, toks, width = tokens.shape
    by_x = sorting(n_x * width, y_lo, n_x, n_c)
    for copy in copies:
        copy.wait()
    both = held[...].reshape(2 * toks, n_x * width)
    sent = []
    for x in range(n_x):
        part = spread(both, by_x[:, x * width : (x + 1) * width])
        moved[x] = part.reshape(2, toks, width)
        for zh in range(n_zh):
            sent.append(pltpu.make_async_copy(moved.at[x], tokens.at[x, zh], out_sems.at[x, zh]))
            sent[-1].start()
    for copy in sent:
        copy.wait()


def arrange_tokens(y_lo, n_x, n_c, n_zh, act, grad):
    toks, feats = act.shape
    return pl.pallas_call(
        lambda *refs: tokens_kernel(y_lo, n_c, *refs),
        out_shape=jax.ShapeDtypeStruct((n_x, n_zh, 2, toks, feats // n_x), BF16),
        in_specs=[pl.BlockSpec(memory_space=pl.ANY)] * 2,
        out_specs=pl.BlockSpec(memory_space=pl.ANY),
        scratch_shapes=[
            pltpu.VMEM((2, toks, feats), BF16),
            pltpu.SemaphoreType.DMA((2,)),
            pltpu.VMEM((n_x, 2, toks, feats // n_x), BF16),
            pltpu.SemaphoreType.DMA((n_x, n_zh)),
        ],
        compiler_params=pltpu.CompilerParams(vmem_limit_bytes=60 * 2**20),
        cost_estimate=pl.CostEstimate(
            flops=4 * toks * feats * feats, bytes_accessed=2**20, transcendentals=0
        ),
        name="arrange_tokens",
    )(act, grad)


def rotate_kernel(which, place, lengths, tokens, low, high, core_low, core_high, out, whole):
    n_x, n_zh, _, toks, width = tokens.shape
    rows, cols = low.shape[4], low.shape[5]
    group, part = n_x * toks, cols // n_x
    zl, y, c = place[0], place[1], place[2]
    for one, pair in enumerate(((low, core_low), (high, core_high))):
        for two in range(2):
            for four in range(2):
                from_y = y ^ (four * 4 + two * 2 + one)
                for far in range(2):
                    owner = (zl ^ far) * 2 + from_y // 4
                    for ref, core in zip(pair, (c, 1 - c)):
                        at = pl.multiple_of((core * 4 + from_y % 4) * rows, rows)
                        whole[owner, pl.ds(at, rows)] = ref[two, four, far, which]
    total = None
    for owner in range(n_zh):
        left = tokens[:, owner, which].reshape(group, width)
        product = jnp.dot(left, whole[owner], preferred_element_type=F32)
        total = product if total is None else total + product
    if which == 0:
        index = lax.broadcasted_iota(jnp.int32, (group, 1), 0)
        position = ((y * n_x + index // toks) * 2 + c) * toks + index % toks
        total = jnp.where(position < lengths[zl], total, 0.0)
    largest = jnp.max(jnp.max(jnp.abs(total), axis=0, keepdims=True), axis=1, keepdims=True)
    level = jnp.clip(jnp.ceil(jnp.log2(jnp.maximum(largest, 1e-30))), -100.0, 100.0)
    total = total * jnp.exp2(F32(TOP) - level)
    for i in range(out.shape[0]):
        if which == 0:
            value = total[:, i * part : (i + 1) * part]
        else:
            value = total[:, i * part // 2 : (i + 1) * part // 2]
            value = jnp.concatenate([value[: group // 2], value[group // 2 :]], axis=1)
        out[i, pl.ds(0, value.shape[0])] = value
        out[i, pl.ds(value.shape[0], TILE)] = jnp.broadcast_to(level, (TILE, part))


def rotate(which, place, lengths, *arrays):
    n_x, n_zh, _, toks, width = arrays[0].shape
    cols = arrays[1].shape[5]
    pieces = n_x * (1 + which)
    depth = n_x * toks // (1 + which) + TILE
    return pl.pallas_call(
        lambda *refs: rotate_kernel(which, *refs),
        out_shape=jax.ShapeDtypeStruct((pieces, depth, cols // n_x), F32),
        in_specs=[SMEM] * 2 + [VMEM] * len(arrays),
        out_specs=VMEM,
        scratch_shapes=[pltpu.VMEM((n_zh, width, cols), BF16)],
        compiler_params=pltpu.CompilerParams(vmem_limit_bytes=40 * 2**20),
        cost_estimate=pl.CostEstimate(
            flops=2 * n_x * n_zh * toks * width * cols, bytes_accessed=4 * 2**20, transcendentals=0
        ),
        name="rotate",
    )(place, lengths, *arrays)


def share_kernel(grad, act, out):
    n_k, n_c, depth, part = grad.shape
    n_x, half = act.shape[0], part // 2
    total = None
    for core in range(n_c):
        turned = [grad[k, core].T for k in range(n_k)]
        for side in range(2):
            left = jnp.concatenate([t[side * half : (side + 1) * half] for t in turned], axis=0)
            tokens = slice(side * depth, (side + 1) * depth)
            right = jnp.concatenate([act[x, core, tokens] for x in range(n_x)], axis=1)
            product = jnp.dot(left, right, preferred_element_type=F32)
            total = product if total is None else total + product
    out[...] = total.astype(BF16)


def share_of(grad, act):
    n_k, n_c, depth, part = grad.shape
    rows, cols = n_k * part // 2, act.shape[0] * part
    return pl.pallas_call(
        share_kernel,
        out_shape=jax.ShapeDtypeStruct((rows, cols), BF16),
        in_specs=[VMEM, VMEM],
        out_specs=VMEM,
        compiler_params=pltpu.CompilerParams(vmem_limit_bytes=32 * 2**20),
        cost_estimate=pl.CostEstimate(
            flops=4 * n_c * rows * cols * depth, bytes_accessed=2 * 2**20, transcendentals=0
        ),
        name="share",
    )(grad, act)


def total_of(partial, axes, n_x):
    partial = lax.all_to_all(partial.astype(F16), axes, 0, 0, tiled=True).astype(F32)
    factors = jnp.exp2(partial[:, None, -TILE:] - F32(TOP))
    partial = partial[:, :-TILE].reshape(len(partial), -1, TILE, partial.shape[2]) * factors
    partial = partial.reshape(n_x, -1, *partial.shape[1:])
    return jnp.sum(partial, axis=0).reshape(partial.shape[1], -1, partial.shape[4])


def on_device(activations, gradients, basis_act, basis_grad, lengths):
    n_zl, n_y, n_x, n_c, n_zh = (lax.axis_size(a) for a in ("zl", "y", "x", "c", "zh"))
    zl, y, c = (lax.axis_index(a) for a in ("zl", "y", "c"))
    cols = basis_act.shape[1]

    def partner(value, step):
        return lax.ppermute(value, "y", [(i, i ^ step) for i in range(n_y)])

    bases = arrange_bases(n_y // 2, n_x, n_c, basis_act, basis_grad)
    tokens = arrange_tokens(n_y // 2, n_x, n_c, n_zh, activations, gradients)
    far_bases, tokens = lax.optimization_barrier((shift(bases, "zl", 1), tokens))
    low = jnp.stack([bases, far_bases])
    low = jnp.stack([low, partner(low, 4)])
    low = jnp.stack([low, partner(low, 2)])
    high = partner(low, 1)
    core_low, core_high = shift(low, "c", 1), shift(high, "c", 1)

    tokens = lax.all_to_all(
        tokens.reshape(n_x * n_zh, *tokens.shape[2:]), ("x", "zh"), 0, 0, tiled=True
    ).reshape(tokens.shape)

    place = jnp.stack([zl, y, c]).astype(jnp.int32)
    arrays = (lengths, tokens, low, high, core_low, core_high)
    rot_act = total_of(rotate(0, place, *arrays), "x", n_x)[0].astype(BF16)
    grad = rotate(1, place, *arrays)
    rot_grad = total_of(grad, ("x", "c"), n_x).astype(BF16)
    other_act = shift(rot_act, "c", 1)

    both_act = jnp.where(
        c == 0, jnp.stack([rot_act, other_act]), jnp.stack([other_act, rot_act])
    )
    wide_act = lax.all_to_all(
        jnp.broadcast_to(both_act[None], (n_x, *both_act.shape)), "x", 0, 0, tiled=True
    )
    wide_grad = lax.all_gather(rot_grad, "zh", axis=0)
    share = share_of(wide_grad, wide_act).reshape(n_zl * n_y, -1, cols)
    received = lax.all_to_all(share, ("zl", "y"), 0, 0, tiled=True)
    received = received.astype(F32).reshape(SEQS, n_y, -1, cols)
    per_seq = jnp.sum(received, axis=1)
    scale = lengths.astype(F32)[:, None, None]
    return jnp.sum(per_seq * per_seq / scale, axis=0) / F32(SEQS)


def solution(mesh):
    split = Mesh(mesh.devices.reshape(2, 8, 4, 2, 4), ("zl", "y", "x", "c", "zh"))
    spec = P(("zl", "y", "x", "c"), "zh")
    return jax.shard_map(
        on_device, mesh=split, in_specs=(spec, spec, spec, spec, P()), out_specs=spec, check_vma=False
    )
```

time: 149 us -> 144 us (0.966)
  the two profiles are of different devices: /device:TPU:10 before, /device:TPU:8 now
where the time goes in v10:
time: 144 us; the launch traced here: 143 us
  starting transfers between devices  55.6 us (39%)
  waiting for transfers between devices  53.7 us (37%)
  blocking collectives  17.9 us (12%)
  Pallas kernels  10.4 us (7%)
  other arithmetic  4.11 us (3%)
    ppermute x3, waiting for transfers between devices, partner(): return lax.ppermute(value, 'y', [(i, i ^ step) for i in range(n_y)])  24.6 us
    all_gather x1, blocking collectives, on_device(): wide_grad = lax.all_gather(rot_grad, 'zh', axis=0)  17.9 us
    ppermute x3, starting transfers between devices, partner(): return lax.ppermute(value, 'y', [(i, i ^ step) for i in range(n_y)])  14.2 us
    all_to_all x1, starting transfers between devices, on_device(): lax.all_to_all(tokens.reshape(n_x * n_zh, *tokens.shape[2:]), ('x', 'zh')...  12.1 us
    all_to_all x2, waiting for transfers between devices, total_of(): lax.all_to_all(partial.astype(F16), axes, 0, 0, tiled=True).astype(F32)  12 us
    ppermute x4, starting transfers between devices, shift(): return lax.ppermute(value, axis, [(i, (i + step) % n) for i in range(n)])  10.4 us
    all_to_all x1, waiting for transfers between devices, on_device(): received = lax.all_to_all(share, ('zl', 'y'), 0, 0, tiled=True)  9.42 us
    all_to_all x2, starting transfers between devices, total_of(): lax.all_to_all(partial.astype(F16), axes, 0, 0, tiled=True).astype(F32)  7.68 us
  transfers between devices with their start and end apart: 12, of which 9 were waited for; matrix products, arithmetic and copies ran while one was open for 2% of the time, Pallas kernels for 4%

profile of v10, /device:TPU:8, one launch (start us, length us, event | category | flops | bytes accessed | tf_op | source)
XLA Modules:
  0.0 143.1 jit_solution(13229772196716091666)
XLA Ops:
  0.0 1.6 %arrange_bases.1 = bf16[2,32,512]{2,1,0:T(8,128)(2,1)} custom-call(bf16[32,512]{1,0:T(8,128)(2,1)} %refs_0_.2, bf16[32,512]{1,0:T(8,128)(2,1)} %refs_1_.4), custom_call_target="tpu_custom_call" | custom-call | flops 16777216 | bytes 131072 | tf_op jit(solution)/shard_map/arrange_bases/pallas_call | solution.py:52
  1.6 4.3 %collective-permute-start = (bf16[2,32,512]{2,1,0:T(8,128)(2,1)}, bf16[2,32,512]{2,1,0:T(8,128)(2,1)S(1)}, u32[]{:S(2)}, u32[]{:S(2)}) collective-permute-start(bf16[2,32,512]{2,1,0:T(8,128)(2,1)} %arrange_bases.1), channel_id=1, source_target_pairs={{0,256},{256,0},{1,257},{257,1},{2,258},{258,2},{3,259},{259,3},{4... | collective-permute-start | bytes 196616 | tf_op jit(solution)/shard_map/ppermute | solution.py:21
  5.9 2.9 %arrange_tokens.1 = bf16[4,4,2,128,256]{4,3,2,1,0:T(8,128)(2,1)} custom-call(bf16[128,1024]{1,0:T(8,128)(2,1)} %refs_0_.3, bf16[128,1024]{1,0:T(8,128)(2,1)} %refs_1_.5), custom_call_target="tpu_custom_call" | custom-call | flops 536870912 | bytes 1048576 | tf_op jit(solution)/shard_map/arrange_tokens/pallas_call | solution.py:90
  8.9 12.1 %all-to-all-start = ((bf16[16,2,128,256]{3,2,1,0:T(8,128)(2,1)}), bf16[16,2,128,256]{3,2,1,0:T(8,128)(2,1)S(1)}, u32[]{:S(2)}, u32[]{:S(2)}) async-start(bf16[16,2,128,256]{3,2,1,0:T(8,128)(2,1)} %bitcast.26), calls=%async_computation | async-start | bytes 4194304 | tf_op jit(solution)/shard_map/all_to_all | solution.py:220
  21.0 6.8 %collective-permute-start.1 = (bf16[2,2,32,512]{3,2,1,0:T(8,128)(2,1)S(1)}, bf16[2,2,32,512]{3,2,1,0:T(8,128)(2,1)S(1)}, u32[]{:S(2)}, u32[]{:S(2)}) collective-permute-start(bf16[2,2,32,512]{3,2,1,0:T(8,128)(2,1)S(1)} %get-tuple-element.12), channel_id=1, source_target_pairs={{0,128},{32,160},{64,192},{96,224},{128,0},{160,32},{192,64},{224,... | collective-permute-start | bytes 393224 | tf_op jit(solution)/shard_map/ppermute | solution.py:209
  27.9 6.3 %collective-permute-done.1 = bf16[2,2,32,512]{3,2,1,0:T(8,128)(2,1)S(1)} collective-permute-done((bf16[2,2,32,512]{3,2,1,0:T(8,128)(2,1)S(1)}, bf16[2,2,32,512]{3,2,1,0:T(8,128)(2,1)S(1)}, u32[]{:S(2)}, u32[]{:S(2)}) %collective-permute-start.1) | collective-permute-done | bytes 131104 | tf_op jit(solution)/shard_map/ppermute | solution.py:209
  34.2 4.2 %collective-permute-start.2 = (bf16[2,2,2,32,512]{4,3,2,1,0:T(8,128)(2,1)S(1)}, bf16[2,2,2,32,512]{4,3,2,1,0:T(8,128)(2,1)S(1)}, u32[]{:S(2)}, u32[]{:S(2)}) collective-permute-start(bf16[2,2,2,32,512]{4,3,2,1,0:T(8,128)(2,1)S(1)} %get-tuple-element.10), channel_id=1, source_target_pairs={{0,64},{32,96},{64,0},{96,32},{128,192},{160,224},{192,128},{224,1... | collective-permute-start | bytes 786440 | tf_op jit(solution)/shard_map/ppermute | solution.py:209
  38.4 8.8 %collective-permute-done.2 = bf16[2,2,2,32,512]{4,3,2,1,0:T(8,128)(2,1)S(1)} collective-permute-done((bf16[2,2,2,32,512]{4,3,2,1,0:T(8,128)(2,1)S(1)}, bf16[2,2,2,32,512]{4,3,2,1,0:T(8,128)(2,1)S(1)}, u32[]{:S(2)}, u32[]{:S(2)}) %collective-permute-start.2) | collective-permute-done | bytes 262176 | tf_op jit(solution)/shard_map/ppermute | solution.py:209
  47.3 3.2 %collective-permute-start.3 = (bf16[2,2,2,2,32,512]{5,4,3,2,1,0:T(8,128)(2,1)S(1)}, bf16[2,2,2,2,32,512]{5,4,3,2,1,0:T(8,128)(2,1)S(1)}, u32[]{:S(2)}, u32[]{:S(2)}) collective-permute-start(bf16[2,2,2,2,32,512]{5,4,3,2,1,0:T(8,128)(2,1)S(1)} %pad_maximum_fusion.refs_3_), channel_id=1, source_target_pairs={{0,32},{32,0},{64,96},{96,64},{128,160},{160,128},{192,224},{224,1... | collective-permute-start | bytes 1572872 | tf_op jit(solution)/shard_map/ppermute | solution.py:209
  50.5 1.9 %collective-permute-start.4 = (bf16[2,2,2,2,32,512]{5,4,3,2,1,0:T(8,128)(2,1)S(1)}, bf16[2,2,2,2,32,512]{5,4,3,2,1,0:T(8,128)(2,1)}, u32[]{:S(2)}, u32[]{:S(2)}) collective-permute-start(bf16[2,2,2,2,32,512]{5,4,3,2,1,0:T(8,128)(2,1)S(1)} %pad_maximum_fusion.refs_3_), channel_id=1, source_target_pairs={{0,4},{4,0},{1,5},{5,1},{2,6},{6,2},{3,7},{7,3},{8,12},{12,8},{9,1... | collective-permute-start | bytes 1572872 | tf_op jit(solution)/shard_map/ppermute | solution.py:21
  52.5 9.5 %collective-permute-done.3.refs_4_ = bf16[2,2,2,2,32,512]{5,4,3,2,1,0:T(8,128)(2,1)S(1)} collective-permute-done((bf16[2,2,2,2,32,512]{5,4,3,2,1,0:T(8,128)(2,1)S(1)}, bf16[2,2,2,2,32,512]{5,4,3,2,1,0:T(8,128)(2,1)S(1)}, u32[]{:S(2)}, u32[]{:S(2)}) %collective-permute-start.3) | collective-permute-done | bytes 524320 | tf_op jit(solution)/shard_map/ppermute | solution.py:209
  62.0 1.9 %collective-permute-start.5 = (bf16[2,2,2,2,32,512]{5,4,3,2,1,0:T(8,128)(2,1)S(1)}, bf16[2,2,2,2,32,512]{5,4,3,2,1,0:T(8,128)(2,1)}, u32[]{:S(2)}, u32[]{:S(2)}) collective-permute-start(bf16[2,2,2,2,32,512]{5,4,3,2,1,0:T(8,128)(2,1)S(1)} %collective-permute-done.3.refs_4_), channel_id=1, source_target_pairs={{0,4},{4,0},{1,5},{5,1},{2,6},{6,2},{3,7},{7,3},{8,12},{12,8},{9,1... | collective-permute-start | bytes 1572872 | tf_op jit(solution)/shard_map/ppermute | solution.py:21
  64.0 1.9 %collective-permute-done.5.refs_6_ = bf16[2,2,2,2,32,512]{5,4,3,2,1,0:T(8,128)(2,1)} collective-permute-done((bf16[2,2,2,2,32,512]{5,4,3,2,1,0:T(8,128)(2,1)S(1)}, bf16[2,2,2,2,32,512]{5,4,3,2,1,0:T(8,128)(2,1)}, u32[]{:S(2)}, u32[]{:S(2)}) %collective-permute-start.5) | collective-permute-done | bytes 524320 | tf_op jit(solution)/shard_map/ppermute | solution.py:21
  65.9 4.7 %all-to-all-done = bf16[16,2,128,256]{3,2,1,0:T(8,128)(2,1)S(1)} async-done(((bf16[16,2,128,256]{3,2,1,0:T(8,128)(2,1)}), bf16[16,2,128,256]{3,2,1,0:T(8,128)(2,1)S(1)}, u32[]{:S(2)}, u32[]{:S(2)}) %all-to-all-start) | async-done | bytes 2097184 | tf_op jit(solution)/shard_map/all_to_all | solution.py:220
  70.6 2.2 %rotate.3 = f32[4,528,128]{2,1,0:T(8,128)S(1)} custom-call(s32[3]{0:T(128)S(1)} %pad_add_fusion.refs_0_, s32[2]{0:T(128)S(1)} %copy-done, bf16[4,4,2,128,256]{4,3,2,1,0:T(8,128)(2,1)S(1)} %bitcast.24, bf16[2,2,2,2,32,512]{5,4,3,2,1,0:T(8,128)(2,1)S(1)} %pad_maximum_fusion.refs_3_, bf16[2,2,2,2,32,512]{5,4,3,2,1,0:T(8,128)(2,1)S(1)} %collective-permute-done.3.refs_4_, ...), custom_call_target="tpu_custom_call" | custom-call | flops 536870912 | bytes 4194304 | tf_op jit(solution)/shard_map/rotate/pallas_call | solution.py:150
  72.8 0.9 convert_element_type.49
  73.7 4.1 %all-to-all-start.2 = ((f16[4,528,128]{2,1,0:T(8,128)(2,1)}), f16[4,528,128]{2,1,0:T(8,128)(2,1)}, u32[]{:S(2)}, u32[]{:S(2)}) async-start(f16[4,528,128]{2,1,0:T(8,128)(2,1)} %convert_element_type.49), calls=%async_computation.2 | async-start | bytes 1081344 | tf_op jit(solution)/shard_map/all_to_all | solution.py:196
  77.8 2.5 %rotate.2 = f32[8,272,128]{2,1,0:T(8,128)S(1)} custom-call(s32[3]{0:T(128)S(1)} %pad_add_fusion.refs_0_, s32[2]{0:T(128)S(1)} %copy-done, bf16[4,4,2,128,256]{4,3,2,1,0:T(8,128)(2,1)S(1)} %bitcast.25, bf16[2,2,2,2,32,512]{5,4,3,2,1,0:T(8,128)(2,1)S(1)} %pad_maximum_fusion.refs_3_, bf16[2,2,2,2,32,512]{5,4,3,2,1,0:T(8,128)(2,1)S(1)} %collective-permute-done.3.refs_4_, ...), custom_call_target="tpu_custom_call" | custom-call | flops 536870912 | bytes 4194304 | tf_op jit(solution)/shard_map/rotate/pallas_call | solution.py:150
  80.4 0.9 convert_element_type.45
  81.2 6.0 %all-to-all-done.2 = f16[4,528,128]{2,1,0:T(8,128)(2,1)} async-done(((f16[4,528,128]{2,1,0:T(8,128)(2,1)}), f16[4,528,128]{2,1,0:T(8,128)(2,1)}, u32[]{:S(2)}, u32[]{:S(2)}) %all-to-all-start.2) | async-done | bytes 540704 | tf_op jit(solution)/shard_map/all_to_all | solution.py:196
  87.2 3.5 %all-to-all-start.1 = ((f16[8,272,128]{2,1,0:T(8,128)(2,1)}), f16[8,272,128]{2,1,0:T(8,128)(2,1)S(1)}, u32[]{:S(2)}, u32[]{:S(2)}) async-start(f16[8,272,128]{2,1,0:T(8,128)(2,1)} %convert_element_type.45), calls=%async_computation.1 | async-start | bytes 1114112 | tf_op jit(solution)/shard_map/all_to_all | solution.py:196
  90.7 1.1 convert_element_type.50
  92.0 2.3 %collective-permute-start.6 = (bf16[512,128]{1,0:T(8,128)(2,1)S(1)}, bf16[512,128]{1,0:T(8,128)(2,1)S(1)}, u32[]{:S(2)}, u32[]{:S(2)}) collective-permute-start(bf16[512,128]{1,0:T(8,128)(2,1)S(1)} %fusion), channel_id=1, source_target_pairs={{0,4},{4,0},{1,5},{5,1},{2,6},{6,2},{3,7},{7,3},{8,12},{12,8},{9,1... | collective-permute-start | bytes 393224 | tf_op jit(solution)/shard_map/ppermute | solution.py:21
  94.3 1.0 collective-permute-done.6
  95.3 6.1 %all-to-all-done.1 = f16[8,272,128]{2,1,0:T(8,128)(2,1)S(1)} async-done(((f16[8,272,128]{2,1,0:T(8,128)(2,1)}), f16[8,272,128]{2,1,0:T(8,128)(2,1)S(1)}, u32[]{:S(2)}, u32[]{:S(2)}) %all-to-all-start.1) | async-done | bytes 557088 | tf_op jit(solution)/shard_map/all_to_all | solution.py:196
  101.4 1.1 broadcast_in_dim.2
  102.5 3.5 %all-to-all-start.3 = ((bf16[4,2,512,128]{3,2,1,0:T(8,128)(2,1)}), bf16[4,2,512,128]{3,2,1,0:T(8,128)(2,1)S(1)}, u32[]{:S(2)}, u32[]{:S(2)}) async-start(bf16[4,2,512,128]{3,2,1,0:T(8,128)(2,1)} %broadcast_in_dim.2), calls=%async_computation.3 | async-start | bytes 2097152 | tf_op jit(solution)/shard_map/all_to_all | solution.py:234
  106.3 17.9 %all_gather.4.grad = bf16[4,2,256,128]{3,2,1,0:T(8,128)(2,1)S(1)} all-gather(bf16[1,2,256,128]{3,2,1,0:T(8,128)(2,1)S(1)} %bitcast.29), channel_id=1, replica_groups=mesh['zl'=2,'y'=8,'x'=4,'c'=2,'zh'=4] {'zh'}, dimensions={0}, use_global_device_ids=true | all-gather | bytes 655360 | tf_op jit(solution)/shard_map/all_gather | solution.py:237
  124.1 1.2 share.1
  125.3 7.6 %all-to-all-start.4 = ((bf16[16,16,512]{2,1,0:T(8,128)(2,1)}), bf16[16,16,512]{2,1,0:T(8,128)(2,1)S(1)}, u32[]{:S(2)}, u32[]{:S(2)}) async-start(bf16[16,16,512]{2,1,0:T(8,128)(2,1)} %bitcast.17), calls=%async_computation.4 | async-start | bytes 524288 | tf_op jit(solution)/shard_map/all_to_all | solution.py:239
  133.0 9.4 %all-to-all-done.4 = bf16[16,16,512]{2,1,0:T(8,128)(2,1)S(1)} async-done(((bf16[16,16,512]{2,1,0:T(8,128)(2,1)}), bf16[16,16,512]{2,1,0:T(8,128)(2,1)S(1)}, u32[]{:S(2)}, u32[]{:S(2)}) %all-to-all-start.4) | async-done | bytes 262176 | tf_op jit(solution)/shard_map/all_to_all | solution.py:239
  142.5 0.6 broadcast_multiply_fusion
  (21 shorter events, 0.7 us)
Async XLA Ops:
  1.6 7.2 %collective-permute-start = (bf16[2,32,512]{2,1,0:T(8,128)(2,1)}, bf16[2,32,512]{2,1,0:T(8,128)(2,1)S(1)}, u32[]{:S(2)}, u32[]{:S(2)}) collective-permute-start(bf16[2,32,512]{2,1,0:T(8,128)(2,1)} %arrange_bases.1), channel_id=1, source_target_pairs={{0,256},{256,0},{1,257},{257,1},{2,258},{258,2},{3,259},{259,3},{4... | collective-permute-start | bytes 196616 | tf_op jit(solution)/shard_map/ppermute | solution.py:21
  8.9 12.1 %copy-start.1 = (bf16[2,32,512]{2,1,0:T(8,128)(2,1)S(1)}, bf16[2,32,512]{2,1,0:T(8,128)(2,1)}, u32[]{:S(2)}) copy-start(bf16[2,32,512]{2,1,0:T(8,128)(2,1)} %arrange_bases.1) | copy-start | bytes 196612
  8.9 61.7 %all-to-all-start = ((bf16[16,2,128,256]{3,2,1,0:T(8,128)(2,1)}), bf16[16,2,128,256]{3,2,1,0:T(8,128)(2,1)S(1)}, u32[]{:S(2)}, u32[]{:S(2)}) async-start(bf16[16,2,128,256]{3,2,1,0:T(8,128)(2,1)} %bitcast.26), calls=%async_computation | async-start | bytes 4194304 | tf_op jit(solution)/shard_map/all_to_all | solution.py:220
  21.0 49.6 %copy-start = (s32[2]{0:T(128)S(1)}, s32[2]{0:T(128)}, u32[]{:S(2)}) copy-start(s32[2]{0:T(128)} %refs_1_.7) | copy-start | bytes 28
  21.0 13.1 %collective-permute-start.1 = (bf16[2,2,32,512]{3,2,1,0:T(8,128)(2,1)S(1)}, bf16[2,2,32,512]{3,2,1,0:T(8,128)(2,1)S(1)}, u32[]{:S(2)}, u32[]{:S(2)}) collective-permute-start(bf16[2,2,32,512]{3,2,1,0:T(8,128)(2,1)S(1)} %get-tuple-element.12), channel_id=1, source_target_pairs={{0,128},{32,160},{64,192},{96,224},{128,0},{160,32},{192,64},{224,... | collective-permute-start | bytes 393224 | tf_op jit(solution)/shard_map/ppermute | solution.py:209
  34.2 13.0 %collective-permute-start.2 = (bf16[2,2,2,32,512]{4,3,2,1,0:T(8,128)(2,1)S(1)}, bf16[2,2,2,32,512]{4,3,2,1,0:T(8,128)(2,1)S(1)}, u32[]{:S(2)}, u32[]{:S(2)}) collective-permute-start(bf16[2,2,2,32,512]{4,3,2,1,0:T(8,128)(2,1)S(1)} %get-tuple-element.10), channel_id=1, source_target_pairs={{0,64},{32,96},{64,0},{96,32},{128,192},{160,224},{192,128},{224,1... | collective-permute-start | bytes 786440 | tf_op jit(solution)/shard_map/ppermute | solution.py:209
  47.3 14.7 %collective-permute-start.3 = (bf16[2,2,2,2,32,512]{5,4,3,2,1,0:T(8,128)(2,1)S(1)}, bf16[2,2,2,2,32,512]{5,4,3,2,1,0:T(8,128)(2,1)S(1)}, u32[]{:S(2)}, u32[]{:S(2)}) collective-permute-start(bf16[2,2,2,2,32,512]{5,4,3,2,1,0:T(8,128)(2,1)S(1)} %pad_maximum_fusion.refs_3_), channel_id=1, source_target_pairs={{0,32},{32,0},{64,96},{96,64},{128,160},{160,128},{192,224},{224,1... | collective-permute-start | bytes 1572872 | tf_op jit(solution)/shard_map/ppermute | solution.py:209
  50.5 13.4 %collective-permute-start.4 = (bf16[2,2,2,2,32,512]{5,4,3,2,1,0:T(8,128)(2,1)S(1)}, bf16[2,2,2,2,32,512]{5,4,3,2,1,0:T(8,128)(2,1)}, u32[]{:S(2)}, u32[]{:S(2)}) collective-permute-start(bf16[2,2,2,2,32,512]{5,4,3,2,1,0:T(8,128)(2,1)S(1)} %pad_maximum_fusion.refs_3_), channel_id=1, source_target_pairs={{0,4},{4,0},{1,5},{5,1},{2,6},{6,2},{3,7},{7,3},{8,12},{12,8},{9,1... | collective-permute-start | bytes 1572872 | tf_op jit(solution)/shard_map/ppermute | solution.py:21
  62.0 3.9 %collective-permute-start.5 = (bf16[2,2,2,2,32,512]{5,4,3,2,1,0:T(8,128)(2,1)S(1)}, bf16[2,2,2,2,32,512]{5,4,3,2,1,0:T(8,128)(2,1)}, u32[]{:S(2)}, u32[]{:S(2)}) collective-permute-start(bf16[2,2,2,2,32,512]{5,4,3,2,1,0:T(8,128)(2,1)S(1)} %collective-permute-done.3.refs_4_), channel_id=1, source_target_pairs={{0,4},{4,0},{1,5},{5,1},{2,6},{6,2},{3,7},{7,3},{8,12},{12,8},{9,1... | collective-permute-start | bytes 1572872 | tf_op jit(solution)/shard_map/ppermute | solution.py:21
  73.7 13.5 %all-to-all-start.2 = ((f16[4,528,128]{2,1,0:T(8,128)(2,1)}), f16[4,528,128]{2,1,0:T(8,128)(2,1)}, u32[]{:S(2)}, u32[]{:S(2)}) async-start(f16[4,528,128]{2,1,0:T(8,128)(2,1)} %convert_element_type.49), calls=%async_computation.2 | async-start | bytes 1081344 | tf_op jit(solution)/shard_map/all_to_all | solution.py:196
  87.2 14.2 %all-to-all-start.1 = ((f16[8,272,128]{2,1,0:T(8,128)(2,1)}), f16[8,272,128]{2,1,0:T(8,128)(2,1)S(1)}, u32[]{:S(2)}, u32[]{:S(2)}) async-start(f16[8,272,128]{2,1,0:T(8,128)(2,1)} %convert_element_type.45), calls=%async_computation.1 | async-start | bytes 1114112 | tf_op jit(solution)/shard_map/all_to_all | solution.py:196
  92.0 3.3 %collective-permute-start.6 = (bf16[512,128]{1,0:T(8,128)(2,1)S(1)}, bf16[512,128]{1,0:T(8,128)(2,1)S(1)}, u32[]{:S(2)}, u32[]{:S(2)}) collective-permute-start(bf16[512,128]{1,0:T(8,128)(2,1)S(1)} %fusion), channel_id=1, source_target_pairs={{0,4},{4,0},{1,5},{5,1},{2,6},{6,2},{3,7},{7,3},{8,12},{12,8},{9,1... | collective-permute-start | bytes 393224 | tf_op jit(solution)/shard_map/ppermute | solution.py:21
  102.5 21.7 %all-to-all-start.3 = ((bf16[4,2,512,128]{3,2,1,0:T(8,128)(2,1)}), bf16[4,2,512,128]{3,2,1,0:T(8,128)(2,1)S(1)}, u32[]{:S(2)}, u32[]{:S(2)}) async-start(bf16[4,2,512,128]{3,2,1,0:T(8,128)(2,1)} %broadcast_in_dim.2), calls=%async_computation.3 | async-start | bytes 2097152 | tf_op jit(solution)/shard_map/all_to_all | solution.py:234
  125.3 17.1 %all-to-all-start.4 = ((bf16[16,16,512]{2,1,0:T(8,128)(2,1)}), bf16[16,16,512]{2,1,0:T(8,128)(2,1)S(1)}, u32[]{:S(2)}, u32[]{:S(2)}) async-start(bf16[16,16,512]{2,1,0:T(8,128)(2,1)} %bitcast.17), calls=%async_computation.4 | async-start | bytes 524288 | tf_op jit(solution)/shard_map/all_to_all | solution.py:239

commit v11 on v10

--- a/solution.py
+++ b/solution.py
@@ -106,56 +106,57 @@
     )(act, grad)
 
 
-def rotate_kernel(which, place, lengths, tokens, low, high, core_low, core_high, out, whole):
+def rotate_kernel(place, lengths, tokens, low, high, core_low, core_high, out, whole):
     n_x, n_zh, _, toks, width = tokens.shape
     rows, cols = low.shape[4], low.shape[5]
     group, part = n_x * toks, cols // n_x
     zl, y, c = place[0], place[1], place[2]
-    for one, pair in enumerate(((low, core_low), (high, core_high))):
-        for two in range(2):
-            for four in range(2):
-                from_y = y ^ (four * 4 + two * 2 + one)
-                for far in range(2):
-                    owner = (zl ^ far) * 2 + from_y // 4
-                    for ref, core in zip(pair, (c, 1 - c)):
-                        at = pl.multiple_of((core * 4 + from_y % 4) * rows, rows)
-                        whole[owner, pl.ds(at, rows)] = ref[two, four, far, which]
-    total = None
-    for owner in range(n_zh):
-        left = tokens[:, owner, which].reshape(group, width)
-        product = jnp.dot(left, whole[owner], preferred_element_type=F32)
-        total = product if total is None else total + product
-    if which == 0:
-        index = lax.broadcasted_iota(jnp.int32, (group, 1), 0)
-        position = ((y * n_x + index // toks) * 2 + c) * toks + index % toks
-        total = jnp.where(position < lengths[zl], total, 0.0)
-    largest = jnp.max(jnp.max(jnp.abs(total), axis=0, keepdims=True), axis=1, keepdims=True)
+    sums = []
+    for which in range(2):
+        for one, pair in enumerate(((low, core_low), (high, core_high))):
+            for two in range(2):
+                for four in range(2):
+                    from_y = y ^ (four * 4 + two * 2 + one)
+                    for far in range(2):
+                        owner = (zl ^ far) * 2 + from_y // 4
+                        for ref, core in zip(pair, (c, 1 - c)):
+                            at = pl.multiple_of((core * 4 + from_y % 4) * rows, rows)
+                            whole[which, owner, pl.ds(at, rows)] = ref[two, four, far, which]
+        total = None
+        for owner in range(n_zh):
+            left = tokens[:, owner, which].reshape(group, width)
+            product = jnp.dot(left, whole[which, owner], preferred_element_type=F32)
+            total = product if total is None else total + product
+        sums.append(total)
+    index = lax.broadcasted_iota(jnp.int32, (group, 1), 0)
+    position = ((y * n_x + index // toks) * 2 + c) * toks + index % toks
+    sums[0] = jnp.where(position < lengths[zl], sums[0], 0.0)
+    largest = jnp.max(jnp.maximum(jnp.abs(sums[0]), jnp.abs(sums[1])), axis=0, keepdims=True)
+    largest = jnp.max(largest, axis=1, keepdims=True)
     level = jnp.clip(jnp.ceil(jnp.log2(jnp.maximum(largest, 1e-30))), -100.0, 100.0)
-    total = total * jnp.exp2(F32(TOP) - level)
-    for i in range(out.shape[0]):
-        if which == 0:
-            value = total[:, i * part : (i + 1) * part]
-        else:
-            value = total[:, i * part // 2 : (i + 1) * part // 2]
-            value = jnp.concatenate([value[: group // 2], value[group // 2 :]], axis=1)
-        out[i, pl.ds(0, value.shape[0])] = value
-        out[i, pl.ds(value.shape[0], TILE)] = jnp.broadcast_to(level, (TILE, part))
-
-
-def rotate(which, place, lengths, *arrays):
+    act, grad = (total * jnp.exp2(F32(TOP) - level) for total in sums)
+    half = group // 2
+    for x in range(n_x):
+        for core in range(2):
+            piece = 2 * x + core
+            out[piece, pl.ds(0, half)] = act[core * half : (core + 1) * half, x * part : (x + 1) * part]
+            value = grad[:, piece * part // 2 : (piece + 1) * part // 2]
+            out[piece, pl.ds(half, half)] = jnp.concatenate([value[:half], value[half:]], axis=1)
+            out[piece, pl.ds(group, TILE)] = jnp.broadcast_to(level, (TILE, part))
+
+
+def rotate(place, lengths, *arrays):
     n_x, n_zh, _, toks, width = arrays[0].shape
     cols = arrays[1].shape[5]
-    pieces = n_x * (1 + which)
-    depth = n_x * toks // (1 + which) + TILE
-    return pl.pallas_call(
-        lambda *refs: rotate_kernel(which, *refs),
-        out_shape=jax.ShapeDtypeStruct((pieces, depth, cols // n_x), F32),
+    return pl.pallas_call(
+        rotate_kernel,
+        out_shape=jax.ShapeDtypeStruct((2 * n_x, n_x * toks + TILE, cols // n_x), F32),
         in_specs=[SMEM] * 2 + [VMEM] * len(arrays),
         out_specs=VMEM,
-        scratch_shapes=[pltpu.VMEM((n_zh, width, cols), BF16)],
+        scratch_shapes=[pltpu.VMEM((2, n_zh, width, cols), BF16)],
         compiler_params=pltpu.CompilerParams(vmem_limit_bytes=40 * 2**20),
         cost_estimate=pl.CostEstimate(
-            flops=2 * n_x * n_zh * toks * width * cols, bytes_accessed=4 * 2**20, transcendentals=0
+            flops=4 * n_x * n_zh * toks * width * cols, bytes_accessed=8 * 2**20, transcendentals=0
         ),
         name="rotate",
     )(place, lengths, *arrays)
@@ -169,8 +170,7 @@
         turned = [grad[k, core].T for k in range(n_k)]
         for side in range(2):
             left = jnp.concatenate([t[side * half : (side + 1) * half] for t in turned], axis=0)
-            tokens = slice(side * depth, (side + 1) * depth)
-            right = jnp.concatenate([act[x, core, tokens] for x in range(n_x)], axis=1)
+            right = jnp.concatenate([act[x, side, core] for x in range(n_x)], axis=1)
             product = jnp.dot(left, right, preferred_element_type=F32)
             total = product if total is None else total + product
     out[...] = total.astype(BF16)
@@ -192,18 +192,10 @@
     )(grad, act)
 
 
-def total_of(partial, axes, n_x):
-    partial = lax.all_to_all(partial.astype(F16), axes, 0, 0, tiled=True).astype(F32)
-    factors = jnp.exp2(partial[:, None, -TILE:] - F32(TOP))
-    partial = partial[:, :-TILE].reshape(len(partial), -1, TILE, partial.shape[2]) * factors
-    partial = partial.reshape(n_x, -1, *partial.shape[1:])
-    return jnp.sum(partial, axis=0).reshape(partial.shape[1], -1, partial.shape[4])
-
-
 def on_device(activations, gradients, basis_act, basis_grad, lengths):
     n_zl, n_y, n_x, n_c, n_zh = (lax.axis_size(a) for a in ("zl", "y", "x", "c", "zh"))
     zl, y, c = (lax.axis_index(a) for a in ("zl", "y", "c"))
-    cols = basis_act.shape[1]
+    cols, group = basis_act.shape[1], n_x * activations.shape[0]
 
     def partner(value, step):
         return lax.ppermute(value, "y", [(i, i ^ step) for i in range(n_y)])
@@ -223,17 +215,17 @@
 
     place = jnp.stack([zl, y, c]).astype(jnp.int32)
     arrays = (lengths, tokens, low, high, core_low, core_high)
-    rot_act = total_of(rotate(0, place, *arrays), "x", n_x)[0].astype(BF16)
-    grad = rotate(1, place, *arrays)
-    rot_grad = total_of(grad, ("x", "c"), n_x).astype(BF16)
-    other_act = shift(rot_act, "c", 1)
-
-    both_act = jnp.where(
-        c == 0, jnp.stack([rot_act, other_act]), jnp.stack([other_act, rot_act])
-    )
+    partial = rotate(place, *arrays).astype(F16)
+    partial = lax.all_to_all(partial, ("x", "c"), 0, 0, tiled=True)
+    factors = jnp.exp2(partial[:, None, -TILE:].astype(F32) - F32(TOP))
+    partial = partial[:, :-TILE].reshape(n_x * n_c, -1, TILE, partial.shape[2]).astype(F32)
+    partial = (partial * factors).reshape(n_x, n_c, *partial.shape[1:])
+    rotated = jnp.sum(partial, axis=0).astype(BF16).reshape(n_c, group, -1)
+    rot_act, rot_grad = rotated[:, : group // 2], rotated[:, group // 2 :]
+
     wide_act = lax.all_to_all(
-        jnp.broadcast_to(both_act[None], (n_x, *both_act.shape)), "x", 0, 0, tiled=True
-    )
+        jnp.broadcast_to(rot_act[None], (n_x * n_c, *rot_act.shape)), ("x", "c"), 0, 0, tiled=True
+    ).reshape(n_x, n_c, *rot_act.shape)
     wide_grad = lax.all_gather(rot_grad, "zh", axis=0)
     share = share_of(wide_grad, wide_act).reshape(n_zl * n_y, -1, cols)
     received = lax.all_to_all(share, ("zl", "y"), 0, 0, tiled=True)

time: 144 us -> 138 us (0.958)
  blocking collectives: 17.9 us -> 38.3 us
  waiting for transfers between devices: 53.7 us -> 41.2 us
  starting transfers between devices: 55.6 us -> 46.3 us
  other arithmetic: 4.11 us -> 1.3 us
  Pallas kernels: 10.4 us -> 8.82 us
    all_to_all x0 -> x1, blocking collectives: none -> 19.6 us  [on_device(): partial = lax.all_to_all(partial, ('x', 'c'), 0, 0, tiled=True)]
    all_to_all x3 -> x1, waiting for transfers between devices: 12 us -> 0.01 us  [on_device(): lax.all_to_all(jnp.broadcast_to(rot_act[None], (n_x * n_c, *rot_act.shape...]
    all_to_all x3 -> x1, starting transfers between devices: 11.2 us -> 3.56 us  [on_device(): lax.all_to_all(jnp.broadcast_to(rot_act[None], (n_x * n_c, *rot_act.shape...]
    convert_element_type x4 -> x1, other arithmetic: 2.97 us -> 0.14 us  [on_device(): partial = rotate(place, *arrays).astype(F16)]
    ppermute x4 -> x3, starting transfers between devices: 10.4 us -> 8.11 us  [shift(): return lax.ppermute(value, axis, [(i, (i + step) % n) for i in range(n)])]
    pallas_call x2 -> x1, Pallas kernels: 4.7 us -> 3.09 us  [rotate(): pl.pallas_call(rotate_kernel, out_shape=jax.ShapeDtypeStruct((2 * n_x, n_...]
    ppermute x4 -> x3, waiting for transfers between devices: 2.89 us -> 1.93 us  [shift(): return lax.ppermute(value, axis, [(i, (i + step) % n) for i in range(n)])]
  transfers between devices with their start and end apart: 12 -> 9, of which waited for: 9 -> 6; matrix products, arithmetic and copies ran while one was open for 2% -> 0% of each run, Pallas kernels for 4% -> 2%
where the time goes in v11:
time: 138 us
  starting transfers between devices  46.3 us (34%)
  waiting for transfers between devices  41.2 us (30%)
  blocking collectives  38.3 us (28%)
  Pallas kernels  8.82 us (6%)
  local copies, waits for them, and re-layouts  1.41 us (1%)
    ppermute x3, waiting for transfers between devices, partner(): return lax.ppermute(value, 'y', [(i, i ^ step) for i in range(n_y)])  24.6 us
    all_to_all x1, blocking collectives, on_device(): partial = lax.all_to_all(partial, ('x', 'c'), 0, 0, tiled=True)  19.6 us
    all_gather x1, blocking collectives, on_device(): wide_grad = lax.all_gather(rot_grad, 'zh', axis=0)  18.7 us
    ppermute x3, starting transfers between devices, partner(): return lax.ppermute(value, 'y', [(i, i ^ step) for i in range(n_y)])  14.2 us
    all_to_all x1, starting transfers between devices, on_device(): lax.all_to_all(tokens.reshape(n_x * n_zh, *tokens.shape[2:]), ('x', 'zh')...  12.1 us
    all_to_all x1, waiting for transfers between devices, on_device(): received = lax.all_to_all(share, ('zl', 'y'), 0, 0, tiled=True)  9.85 us
    all_to_all x1, starting transfers between devices, on_device(): received = lax.all_to_all(share, ('zl', 'y'), 0, 0, tiled=True)  8.31 us
    ppermute x3, starting transfers between devices, shift(): return lax.ppermute(value, axis, [(i, (i + step) % n) for i in range(n)])  8.11 us
  transfers between devices with their start and end apart: 9, of which 6 were waited for; matrix products, arithmetic and copies ran while one was open for 0% of the time, Pallas kernels for 2%

profile of v11, /device:TPU:8, one launch (start us, length us, event | category | flops | bytes accessed | tf_op | source)
XLA Modules:
  0.0 137.5 jit_solution(11072919813784670539)
XLA Ops:
  0.0 1.6 %arrange_bases.1 = bf16[2,32,512]{2,1,0:T(8,128)(2,1)} custom-call(bf16[32,512]{1,0:T(8,128)(2,1)} %refs_0_.2, bf16[32,512]{1,0:T(8,128)(2,1)} %refs_1_.2), custom_call_target="tpu_custom_call" | custom-call | flops 16777216 | bytes 131072 | tf_op jit(solution)/shard_map/arrange_bases/pallas_call | solution.py:52
  1.6 4.3 %collective-permute-start = (bf16[2,32,512]{2,1,0:T(8,128)(2,1)}, bf16[2,32,512]{2,1,0:T(8,128)(2,1)S(1)}, u32[]{:S(2)}, u32[]{:S(2)}) collective-permute-start(bf16[2,32,512]{2,1,0:T(8,128)(2,1)} %arrange_bases.1), channel_id=1, source_target_pairs={{0,256},{256,0},{1,257},{257,1},{2,258},{258,2},{3,259},{259,3},{4... | collective-permute-start | bytes 196616 | tf_op jit(solution)/shard_map/ppermute | solution.py:21
  5.9 2.9 %arrange_tokens.1 = bf16[4,4,2,128,256]{4,3,2,1,0:T(8,128)(2,1)} custom-call(bf16[128,1024]{1,0:T(8,128)(2,1)} %refs_0_.3, bf16[128,1024]{1,0:T(8,128)(2,1)} %refs_1_.3), custom_call_target="tpu_custom_call" | custom-call | flops 536870912 | bytes 1048576 | tf_op jit(solution)/shard_map/arrange_tokens/pallas_call | solution.py:90
  8.9 0.0 collective-permute-done
  8.9 12.1 %all-to-all-start = ((bf16[16,2,128,256]{3,2,1,0:T(8,128)(2,1)}), bf16[16,2,128,256]{3,2,1,0:T(8,128)(2,1)S(1)}, u32[]{:S(2)}, u32[]{:S(2)}) async-start(bf16[16,2,128,256]{3,2,1,0:T(8,128)(2,1)} %bitcast.26), calls=%async_computation | async-start | bytes 4194304 | tf_op jit(solution)/shard_map/all_to_all | solution.py:212
  21.0 0.0 copy-start
  21.0 6.8 %collective-permute-start.1 = (bf16[2,2,32,512]{3,2,1,0:T(8,128)(2,1)S(1)}, bf16[2,2,32,512]{3,2,1,0:T(8,128)(2,1)S(1)}, u32[]{:S(2)}, u32[]{:S(2)}) collective-permute-start(bf16[2,2,32,512]{3,2,1,0:T(8,128)(2,1)S(1)} %get-tuple-element.14), channel_id=1, source_target_pairs={{0,128},{32,160},{64,192},{96,224},{128,0},{160,32},{192,64},{224,... | collective-permute-start | bytes 393224 | tf_op jit(solution)/shard_map/ppermute | solution.py:201
  27.9 6.3 %collective-permute-done.1 = bf16[2,2,32,512]{3,2,1,0:T(8,128)(2,1)S(1)} collective-permute-done((bf16[2,2,32,512]{3,2,1,0:T(8,128)(2,1)S(1)}, bf16[2,2,32,512]{3,2,1,0:T(8,128)(2,1)S(1)}, u32[]{:S(2)}, u32[]{:S(2)}) %collective-permute-start.1) | collective-permute-done | bytes 131104 | tf_op jit(solution)/shard_map/ppermute | solution.py:201
  34.2 4.2 %collective-permute-start.2 = (bf16[2,2,2,32,512]{4,3,2,1,0:T(8,128)(2,1)S(1)}, bf16[2,2,2,32,512]{4,3,2,1,0:T(8,128)(2,1)S(1)}, u32[]{:S(2)}, u32[]{:S(2)}) collective-permute-start(bf16[2,2,2,32,512]{4,3,2,1,0:T(8,128)(2,1)S(1)} %get-tuple-element.12), channel_id=1, source_target_pairs={{0,64},{32,96},{64,0},{96,32},{128,192},{160,224},{192,128},{224,1... | collective-permute-start | bytes 786440 | tf_op jit(solution)/shard_map/ppermute | solution.py:201
  38.4 8.8 %collective-permute-done.2 = bf16[2,2,2,32,512]{4,3,2,1,0:T(8,128)(2,1)S(1)} collective-permute-done((bf16[2,2,2,32,512]{4,3,2,1,0:T(8,128)(2,1)S(1)}, bf16[2,2,2,32,512]{4,3,2,1,0:T(8,128)(2,1)S(1)}, u32[]{:S(2)}, u32[]{:S(2)}) %collective-permute-start.2) | collective-permute-done | bytes 262176 | tf_op jit(solution)/shard_map/ppermute | solution.py:201
  47.2 0.1 pad_maximum_fusion.low
  47.3 3.2 %collective-permute-start.3 = (bf16[2,2,2,2,32,512]{5,4,3,2,1,0:T(8,128)(2,1)S(1)}, bf16[2,2,2,2,32,512]{5,4,3,2,1,0:T(8,128)(2,1)S(1)}, u32[]{:S(2)}, u32[]{:S(2)}) collective-permute-start(bf16[2,2,2,2,32,512]{5,4,3,2,1,0:T(8,128)(2,1)S(1)} %pad_maximum_fusion.low), channel_id=1, source_target_pairs={{0,32},{32,0},{64,96},{96,64},{128,160},{160,128},{192,224},{224,1... | collective-permute-start | bytes 1572872 | tf_op jit(solution)/shard_map/ppermute | solution.py:201
  50.5 1.9 %collective-permute-start.4 = (bf16[2,2,2,2,32,512]{5,4,3,2,1,0:T(8,128)(2,1)S(1)}, bf16[2,2,2,2,32,512]{5,4,3,2,1,0:T(8,128)(2,1)}, u32[]{:S(2)}, u32[]{:S(2)}) collective-permute-start(bf16[2,2,2,2,32,512]{5,4,3,2,1,0:T(8,128)(2,1)S(1)} %pad_maximum_fusion.low), channel_id=1, source_target_pairs={{0,4},{4,0},{1,5},{5,1},{2,6},{6,2},{3,7},{7,3},{8,12},{12,8},{9,1... | collective-permute-start | bytes 1572872 | tf_op jit(solution)/shard_map/ppermute | solution.py:21
  52.5 9.5 %collective-permute-done.3.high = bf16[2,2,2,2,32,512]{5,4,3,2,1,0:T(8,128)(2,1)S(1)} collective-permute-done((bf16[2,2,2,2,32,512]{5,4,3,2,1,0:T(8,128)(2,1)S(1)}, bf16[2,2,2,2,32,512]{5,4,3,2,1,0:T(8,128)(2,1)S(1)}, u32[]{:S(2)}, u32[]{:S(2)}) %collective-permute-start.3) | collective-permute-done | bytes 524320 | tf_op jit(solution)/shard_map/ppermute | solution.py:201
  62.0 1.9 %collective-permute-start.5 = (bf16[2,2,2,2,32,512]{5,4,3,2,1,0:T(8,128)(2,1)S(1)}, bf16[2,2,2,2,32,512]{5,4,3,2,1,0:T(8,128)(2,1)}, u32[]{:S(2)}, u32[]{:S(2)}) collective-permute-start(bf16[2,2,2,2,32,512]{5,4,3,2,1,0:T(8,128)(2,1)S(1)} %collective-permute-done.3.high), channel_id=1, source_target_pairs={{0,4},{4,0},{1,5},{5,1},{2,6},{6,2},{3,7},{7,3},{8,12},{12,8},{9,1... | collective-permute-start | bytes 1572872 | tf_op jit(solution)/shard_map/ppermute | solution.py:21
  63.9 0.1 pad_add_fusion.place
  64.0 1.9 %collective-permute-done.5.core_high = bf16[2,2,2,2,32,512]{5,4,3,2,1,0:T(8,128)(2,1)} collective-permute-done((bf16[2,2,2,2,32,512]{5,4,3,2,1,0:T(8,128)(2,1)S(1)}, bf16[2,2,2,2,32,512]{5,4,3,2,1,0:T(8,128)(2,1)}, u32[]{:S(2)}, u32[]{:S(2)}) %collective-permute-start.5) | collective-permute-done | bytes 524320 | tf_op jit(solution)/shard_map/ppermute | solution.py:21
  65.9 4.7 %all-to-all-done = bf16[16,2,128,256]{3,2,1,0:T(8,128)(2,1)S(1)} async-done(((bf16[16,2,128,256]{3,2,1,0:T(8,128)(2,1)}), bf16[16,2,128,256]{3,2,1,0:T(8,128)(2,1)S(1)}, u32[]{:S(2)}, u32[]{:S(2)}) %all-to-all-start) | async-done | bytes 2097184 | tf_op jit(solution)/shard_map/all_to_all | solution.py:212
  70.6 3.1 %rotate.1 = f32[8,528,128]{2,1,0:T(8,128)S(1)} custom-call(s32[3]{0:T(128)S(1)} %pad_add_fusion.place, s32[2]{0:T(128)S(1)} %copy-done, bf16[4,4,2,128,256]{4,3,2,1,0:T(8,128)(2,1)S(1)} %bitcast.23, bf16[2,2,2,2,32,512]{5,4,3,2,1,0:T(8,128)(2,1)S(1)} %pad_maximum_fusion.low, bf16[2,2,2,2,32,512]{5,4,3,2,1,0:T(8,128)(2,1)S(1)} %collective-permute-done.3.high, ...), custom_call_target="tpu_custom_call" | custom-call | flops 1073741824 | bytes 8388608 | tf_op jit(solution)/shard_map/rotate/pallas_call | solution.py:151
  73.7 0.1 convert_element_type.25
  73.9 19.6 %all_to_all.20 = f16[8,528,128]{2,1,0:T(8,128)(2,1)S(1)} all-to-all(f16[8,528,128]{2,1,0:T(8,128)(2,1)S(1)} %convert_element_type.25), channel_id=1, replica_groups=mesh['zl'=2,'y'=8,'x'=4,'c'=2,'zh'=4] {'x','c'}, dimensions={0} | all-to-all | bytes 2162688 | tf_op jit(solution)/shard_map/all_to_all | solution.py:219
  93.5 0.2 slice.16
  93.7 0.2 fusion
  94.0 1.2 broadcast_in_dim.2
  95.1 3.6 %all-to-all-start.2 = ((bf16[8,2,256,128]{3,2,1,0:T(8,128)(2,1)}), bf16[8,2,256,128]{3,2,1,0:T(8,128)(2,1)S(1)}, u32[]{:S(2)}, u32[]{:S(2)}) async-start(bf16[8,2,256,128]{3,2,1,0:T(8,128)(2,1)} %broadcast_in_dim.2), calls=%async_computation.2 | async-start | bytes 2097152 | tf_op jit(solution)/shard_map/all_to_all | solution.py:226
  98.7 18.7 %all-gather = bf16[8,256,128]{2,1,0:T(8,128)(2,1)S(1)} all-gather(bf16[2,256,128]{2,1,0:T(8,128)(2,1)S(1)} %get-tuple-element.10), channel_id=2, replica_groups=mesh['zl'=2,'y'=8,'x'=4,'c'=2,'zh'=4] {'zh'}, dimensions={0}, use_global_device_ids=true | all-gather | bytes 655360 | tf_op jit(solution)/shard_map/all_gather | solution.py:229
  117.4 0.0 all-to-all-done.2
  117.4 1.2 share.1
  118.6 8.3 %all-to-all-start.3 = ((bf16[16,16,512]{2,1,0:T(8,128)(2,1)}), bf16[16,16,512]{2,1,0:T(8,128)(2,1)S(1)}, u32[]{:S(2)}, u32[]{:S(2)}) async-start(bf16[16,16,512]{2,1,0:T(8,128)(2,1)} %bitcast.16), calls=%async_computation.3 | async-start | bytes 524288 | tf_op jit(solution)/shard_map/all_to_all | solution.py:231
  126.9 9.9 %all-to-all-done.3 = bf16[16,16,512]{2,1,0:T(8,128)(2,1)S(1)} async-done(((bf16[16,16,512]{2,1,0:T(8,128)(2,1)}), bf16[16,16,512]{2,1,0:T(8,128)(2,1)S(1)}, u32[]{:S(2)}, u32[]{:S(2)}) %all-to-all-start.3) | async-done | bytes 262176 | tf_op jit(solution)/shard_map/all_to_all | solution.py:231
  136.8 0.1 divide_reduce_fusion
  136.9 0.6 broadcast_multiply_fusion
  (10 shorter events, 0.1 us)
Async XLA Ops:
  1.6 7.2 %collective-permute-start = (bf16[2,32,512]{2,1,0:T(8,128)(2,1)}, bf16[2,32,512]{2,1,0:T(8,128)(2,1)S(1)}, u32[]{:S(2)}, u32[]{:S(2)}) collective-permute-start(bf16[2,32,512]{2,1,0:T(8,128)(2,1)} %arrange_bases.1), channel_id=1, source_target_pairs={{0,256},{256,0},{1,257},{257,1},{2,258},{258,2},{3,259},{259,3},{4... | collective-permute-start | bytes 196616 | tf_op jit(solution)/shard_map/ppermute | solution.py:21
  8.9 12.2 %copy-start.1 = (bf16[2,32,512]{2,1,0:T(8,128)(2,1)S(1)}, bf16[2,32,512]{2,1,0:T(8,128)(2,1)}, u32[]{:S(2)}) copy-start(bf16[2,32,512]{2,1,0:T(8,128)(2,1)} %arrange_bases.1) | copy-start | bytes 196612
  8.9 61.8 %all-to-all-start = ((bf16[16,2,128,256]{3,2,1,0:T(8,128)(2,1)}), bf16[16,2,128,256]{3,2,1,0:T(8,128)(2,1)S(1)}, u32[]{:S(2)}, u32[]{:S(2)}) async-start(bf16[16,2,128,256]{3,2,1,0:T(8,128)(2,1)} %bitcast.26), calls=%async_computation | async-start | bytes 4194304 | tf_op jit(solution)/shard_map/all_to_all | solution.py:212
  21.0 49.6 %copy-start = (s32[2]{0:T(128)S(1)}, s32[2]{0:T(128)}, u32[]{:S(2)}) copy-start(s32[2]{0:T(128)} %lengths.1) | copy-start | bytes 28
  21.0 13.1 %collective-permute-start.1 = (bf16[2,2,32,512]{3,2,1,0:T(8,128)(2,1)S(1)}, bf16[2,2,32,512]{3,2,1,0:T(8,128)(2,1)S(1)}, u32[]{:S(2)}, u32[]{:S(2)}) collective-permute-start(bf16[2,2,32,512]{3,2,1,0:T(8,128)(2,1)S(1)} %get-tuple-element.14), channel_id=1, source_target_pairs={{0,128},{32,160},{64,192},{96,224},{128,0},{160,32},{192,64},{224,... | collective-permute-start | bytes 393224 | tf_op jit(solution)/shard_map/ppermute | solution.py:201
  34.2 13.0 %collective-permute-start.2 = (bf16[2,2,2,32,512]{4,3,2,1,0:T(8,128)(2,1)S(1)}, bf16[2,2,2,32,512]{4,3,2,1,0:T(8,128)(2,1)S(1)}, u32[]{:S(2)}, u32[]{:S(2)}) collective-permute-start(bf16[2,2,2,32,512]{4,3,2,1,0:T(8,128)(2,1)S(1)} %get-tuple-element.12), channel_id=1, source_target_pairs={{0,64},{32,96},{64,0},{96,32},{128,192},{160,224},{192,128},{224,1... | collective-permute-start | bytes 786440 | tf_op jit(solution)/shard_map/ppermute | solution.py:201
  47.3 14.7 %collective-permute-start.3 = (bf16[2,2,2,2,32,512]{5,4,3,2,1,0:T(8,128)(2,1)S(1)}, bf16[2,2,2,2,32,512]{5,4,3,2,1,0:T(8,128)(2,1)S(1)}, u32[]{:S(2)}, u32[]{:S(2)}) collective-permute-start(bf16[2,2,2,2,32,512]{5,4,3,2,1,0:T(8,128)(2,1)S(1)} %pad_maximum_fusion.low), channel_id=1, source_target_pairs={{0,32},{32,0},{64,96},{96,64},{128,160},{160,128},{192,224},{224,1... | collective-permute-start | bytes 1572872 | tf_op jit(solution)/shard_map/ppermute | solution.py:201
  50.5 13.4 %collective-permute-start.4 = (bf16[2,2,2,2,32,512]{5,4,3,2,1,0:T(8,128)(2,1)S(1)}, bf16[2,2,2,2,32,512]{5,4,3,2,1,0:T(8,128)(2,1)}, u32[]{:S(2)}, u32[]{:S(2)}) collective-permute-start(bf16[2,2,2,2,32,512]{5,4,3,2,1,0:T(8,128)(2,1)S(1)} %pad_maximum_fusion.low), channel_id=1, source_target_pairs={{0,4},{4,0},{1,5},{5,1},{2,6},{6,2},{3,7},{7,3},{8,12},{12,8},{9,1... | collective-permute-start | bytes 1572872 | tf_op jit(solution)/shard_map/ppermute | solution.py:21
  62.0 3.9 %collective-permute-start.5 = (bf16[2,2,2,2,32,512]{5,4,3,2,1,0:T(8,128)(2,1)S(1)}, bf16[2,2,2,2,32,512]{5,4,3,2,1,0:T(8,128)(2,1)}, u32[]{:S(2)}, u32[]{:S(2)}) collective-permute-start(bf16[2,2,2,2,32,512]{5,4,3,2,1,0:T(8,128)(2,1)S(1)} %collective-permute-done.3.high), channel_id=1, source_target_pairs={{0,4},{4,0},{1,5},{5,1},{2,6},{6,2},{3,7},{7,3},{8,12},{12,8},{9,1... | collective-permute-start | bytes 1572872 | tf_op jit(solution)/shard_map/ppermute | solution.py:21
  95.1 22.3 %all-to-all-start.2 = ((bf16[8,2,256,128]{3,2,1,0:T(8,128)(2,1)}), bf16[8,2,256,128]{3,2,1,0:T(8,128)(2,1)S(1)}, u32[]{:S(2)}, u32[]{:S(2)}) async-start(bf16[8,2,256,128]{3,2,1,0:T(8,128)(2,1)} %broadcast_in_dim.2), calls=%async_computation.2 | async-start | bytes 2097152 | tf_op jit(solution)/shard_map/all_to_all | solution.py:226
  118.6 18.2 %all-to-all-start.3 = ((bf16[16,16,512]{2,1,0:T(8,128)(2,1)}), bf16[16,16,512]{2,1,0:T(8,128)(2,1)S(1)}, u32[]{:S(2)}, u32[]{:S(2)}) async-start(bf16[16,16,512]{2,1,0:T(8,128)(2,1)} %bitcast.16), calls=%async_computation.3 | async-start | bytes 524288 | tf_op jit(solution)/shard_map/all_to_all | solution.py:231

commit v12 on v11

--- a/solution.py
+++ b/solution.py
@@ -162,34 +162,37 @@
     )(place, lengths, *arrays)
 
 
-def share_kernel(grad, act, out):
+def share_kernel(place, grad, act, core_act, out):
     n_k, n_c, depth, part = grad.shape
     n_x, half = act.shape[0], part // 2
+    c = place[2]
     total = None
     for core in range(n_c):
         turned = [grad[k, core].T for k in range(n_k)]
-        for side in range(2):
-            left = jnp.concatenate([t[side * half : (side + 1) * half] for t in turned], axis=0)
-            right = jnp.concatenate([act[x, side, core] for x in range(n_x)], axis=1)
+        low = jnp.concatenate([t[:half] for t in turned], axis=0)
+        high = jnp.concatenate([t[half:] for t in turned], axis=0)
+        sides = ((jnp.where(c == 0, low, high), act), (jnp.where(c == 0, high, low), core_act))
+        for left, tokens in sides:
+            right = jnp.concatenate([tokens[x, core] for x in range(n_x)], axis=1)
             product = jnp.dot(left, right, preferred_element_type=F32)
             total = product if total is None else total + product
     out[...] = total.astype(BF16)
 
 
-def share_of(grad, act):
+def share_of(place, grad, act, core_act):
     n_k, n_c, depth, part = grad.shape
     rows, cols = n_k * part // 2, act.shape[0] * part
     return pl.pallas_call(
         share_kernel,
         out_shape=jax.ShapeDtypeStruct((rows, cols), BF16),
-        in_specs=[VMEM, VMEM],
+        in_specs=[SMEM] + [VMEM] * 3,
         out_specs=VMEM,
         compiler_params=pltpu.CompilerParams(vmem_limit_bytes=32 * 2**20),
         cost_estimate=pl.CostEstimate(
             flops=4 * n_c * rows * cols * depth, bytes_accessed=2 * 2**20, transcendentals=0
         ),
         name="share",
-    )(grad, act)
+    )(place, grad, act, core_act)
 
 
 def on_device(activations, gradients, basis_act, basis_grad, lengths):
@@ -223,11 +226,12 @@
     rotated = jnp.sum(partial, axis=0).astype(BF16).reshape(n_c, group, -1)
     rot_act, rot_grad = rotated[:, : group // 2], rotated[:, group // 2 :]
 
-    wide_act = lax.all_to_all(
-        jnp.broadcast_to(rot_act[None], (n_x * n_c, *rot_act.shape)), ("x", "c"), 0, 0, tiled=True
-    ).reshape(n_x, n_c, *rot_act.shape)
-    wide_grad = lax.all_gather(rot_grad, "zh", axis=0)
-    share = share_of(wide_grad, wide_act).reshape(n_zl * n_y, -1, cols)
+    wide_grad = lax.all_to_all(
+        jnp.broadcast_to(rot_grad[None], (n_zh, *rot_grad.shape)), "zh", 0, 0, tiled=True
+    )
+    wide_act = lax.all_gather(rot_act, "x", axis=0)
+    core_act = shift(wide_act, "c", 1)
+    share = share_of(place, wide_grad, wide_act, core_act).reshape(n_zl * n_y, -1, cols)
     received = lax.all_to_all(share, ("zl", "y"), 0, 0, tiled=True)
     received = received.astype(F32).reshape(SEQS, n_y, -1, cols)
     per_seq = jnp.sum(received, axis=1)

time: 138 us -> 139 us (level)
  the two profiles are of different devices: /device:TPU:8 before, /device:TPU:1 now
where the time goes in v12:
time: 139 us; the launch traced here: 137 us
  starting transfers between devices  60.3 us (43%)
  waiting for transfers between devices  34.3 us (25%)
  blocking collectives  30.7 us (22%)
  Pallas kernels  9.36 us (7%)
    all_to_all x1, blocking collectives, on_device(): partial = lax.all_to_all(partial, ('x', 'c'), 0, 0, tiled=True)  20.4 us
    ppermute x3, waiting for transfers between devices, partner(): return lax.ppermute(value, 'y', [(i, i ^ step) for i in range(n_y)])  19.8 us
    ppermute x4, starting transfers between devices, shift(): return lax.ppermute(value, axis, [(i, (i + step) % n) for i in range(n)])  18.3 us
    ppermute x3, starting transfers between devices, partner(): return lax.ppermute(value, 'y', [(i, i ^ step) for i in range(n_y)])  17.7 us
    all_to_all x1, starting transfers between devices, on_device(): lax.all_to_all(tokens.reshape(n_x * n_zh, *tokens.shape[2:]), ('x', 'zh')...  11.8 us
    all_gather x1, blocking collectives, on_device(): wide_act = lax.all_gather(rot_act, 'x', axis=0)  10.3 us
    all_to_all x1, waiting for transfers between devices, on_device(): received = lax.all_to_all(share, ('zl', 'y'), 0, 0, tiled=True)  8.9 us
    all_to_all x1, starting transfers between devices, on_device(): received = lax.all_to_all(share, ('zl', 'y'), 0, 0, tiled=True)  7.73 us
  transfers between devices with their start and end apart: 10, of which 7 were waited for; matrix products, arithmetic and copies ran while one was open for 0% of the time, Pallas kernels for 2%

profile of v12, /device:TPU:1, one launch (start us, length us, event | category | flops | bytes accessed | tf_op | source)
XLA Modules:
  0.0 137.3 jit_solution(7420904953968056440)
XLA Ops:
  0.0 1.6 %arrange_bases.1 = bf16[2,32,512]{2,1,0:T(8,128)(2,1)} custom-call(bf16[32,512]{1,0:T(8,128)(2,1)} %refs_0_.2, bf16[32,512]{1,0:T(8,128)(2,1)} %refs_1_.2), custom_call_target="tpu_custom_call" | custom-call | flops 16777216 | bytes 131072 | tf_op jit(solution)/shard_map/arrange_bases/pallas_call | solution.py:52
  1.6 4.8 %collective-permute-start = (bf16[2,32,512]{2,1,0:T(8,128)(2,1)}, bf16[2,32,512]{2,1,0:T(8,128)(2,1)S(1)}, u32[]{:S(2)}, u32[]{:S(2)}) collective-permute-start(bf16[2,32,512]{2,1,0:T(8,128)(2,1)} %arrange_bases.1), channel_id=1, source_target_pairs={{0,256},{256,0},{1,257},{257,1},{2,258},{258,2},{3,259},{259,3},{4... | collective-permute-start | bytes 196616 | tf_op jit(solution)/shard_map/ppermute | solution.py:21
  6.4 2.9 %arrange_tokens.1 = bf16[4,4,2,128,256]{4,3,2,1,0:T(8,128)(2,1)} custom-call(bf16[128,1024]{1,0:T(8,128)(2,1)} %refs_0_.3, bf16[128,1024]{1,0:T(8,128)(2,1)} %refs_1_.3), custom_call_target="tpu_custom_call" | custom-call | flops 536870912 | bytes 1048576 | tf_op jit(solution)/shard_map/arrange_tokens/pallas_call | solution.py:90
  9.4 11.8 %all-to-all-start = ((bf16[16,2,128,256]{3,2,1,0:T(8,128)(2,1)}), bf16[16,2,128,256]{3,2,1,0:T(8,128)(2,1)S(1)}, u32[]{:S(2)}, u32[]{:S(2)}) async-start(bf16[16,2,128,256]{3,2,1,0:T(8,128)(2,1)} %bitcast.25), calls=%async_computation | async-start | bytes 4194304 | tf_op jit(solution)/shard_map/all_to_all | solution.py:215
  21.3 0.0 copy-start
  21.3 7.5 %collective-permute-start.1 = (bf16[2,2,32,512]{3,2,1,0:T(8,128)(2,1)S(1)}, bf16[2,2,32,512]{3,2,1,0:T(8,128)(2,1)S(1)}, u32[]{:S(2)}, u32[]{:S(2)}) collective-permute-start(bf16[2,2,32,512]{3,2,1,0:T(8,128)(2,1)S(1)} %get-tuple-element.14), channel_id=1, source_target_pairs={{0,128},{32,160},{64,192},{96,224},{128,0},{160,32},{192,64},{224,... | collective-permute-start | bytes 393224 | tf_op jit(solution)/shard_map/ppermute | solution.py:204
  28.8 2.4 %collective-permute-done.1 = bf16[2,2,32,512]{3,2,1,0:T(8,128)(2,1)S(1)} collective-permute-done((bf16[2,2,32,512]{3,2,1,0:T(8,128)(2,1)S(1)}, bf16[2,2,32,512]{3,2,1,0:T(8,128)(2,1)S(1)}, u32[]{:S(2)}, u32[]{:S(2)}) %collective-permute-start.1) | collective-permute-done | bytes 131104 | tf_op jit(solution)/shard_map/ppermute | solution.py:204
  31.3 8.3 %collective-permute-start.2 = (bf16[2,2,2,32,512]{4,3,2,1,0:T(8,128)(2,1)S(1)}, bf16[2,2,2,32,512]{4,3,2,1,0:T(8,128)(2,1)S(1)}, u32[]{:S(2)}, u32[]{:S(2)}) collective-permute-start(bf16[2,2,2,32,512]{4,3,2,1,0:T(8,128)(2,1)S(1)} %get-tuple-element.12), channel_id=1, source_target_pairs={{0,64},{32,96},{64,0},{96,32},{128,192},{160,224},{192,128},{224,1... | collective-permute-start | bytes 786440 | tf_op jit(solution)/shard_map/ppermute | solution.py:204
  39.6 8.9 %collective-permute-done.2 = bf16[2,2,2,32,512]{4,3,2,1,0:T(8,128)(2,1)S(1)} collective-permute-done((bf16[2,2,2,32,512]{4,3,2,1,0:T(8,128)(2,1)S(1)}, bf16[2,2,2,32,512]{4,3,2,1,0:T(8,128)(2,1)S(1)}, u32[]{:S(2)}, u32[]{:S(2)}) %collective-permute-start.2) | collective-permute-done | bytes 262176 | tf_op jit(solution)/shard_map/ppermute | solution.py:204
  48.5 0.1 pad_maximum_fusion.low
  48.5 1.9 %collective-permute-start.3 = (bf16[2,2,2,2,32,512]{5,4,3,2,1,0:T(8,128)(2,1)S(1)}, bf16[2,2,2,2,32,512]{5,4,3,2,1,0:T(8,128)(2,1)S(1)}, u32[]{:S(2)}, u32[]{:S(2)}) collective-permute-start(bf16[2,2,2,2,32,512]{5,4,3,2,1,0:T(8,128)(2,1)S(1)} %pad_maximum_fusion.low), channel_id=1, source_target_pairs={{0,32},{32,0},{64,96},{96,64},{128,160},{160,128},{192,224},{224,1... | collective-permute-start | bytes 1572872 | tf_op jit(solution)/shard_map/ppermute | solution.py:204
  50.4 3.8 %collective-permute-start.4 = (bf16[2,2,2,2,32,512]{5,4,3,2,1,0:T(8,128)(2,1)S(1)}, bf16[2,2,2,2,32,512]{5,4,3,2,1,0:T(8,128)(2,1)}, u32[]{:S(2)}, u32[]{:S(2)}) collective-permute-start(bf16[2,2,2,2,32,512]{5,4,3,2,1,0:T(8,128)(2,1)S(1)} %pad_maximum_fusion.low), channel_id=1, source_target_pairs={{0,4},{4,0},{1,5},{5,1},{2,6},{6,2},{3,7},{7,3},{8,12},{12,8},{9,1... | collective-permute-start | bytes 1572872 | tf_op jit(solution)/shard_map/ppermute | solution.py:21
  54.2 8.5 %collective-permute-done.3.high = bf16[2,2,2,2,32,512]{5,4,3,2,1,0:T(8,128)(2,1)S(1)} collective-permute-done((bf16[2,2,2,2,32,512]{5,4,3,2,1,0:T(8,128)(2,1)S(1)}, bf16[2,2,2,2,32,512]{5,4,3,2,1,0:T(8,128)(2,1)S(1)}, u32[]{:S(2)}, u32[]{:S(2)}) %collective-permute-start.3) | collective-permute-done | bytes 524320 | tf_op jit(solution)/shard_map/ppermute | solution.py:204
  62.7 4.0 %collective-permute-start.5 = (bf16[2,2,2,2,32,512]{5,4,3,2,1,0:T(8,128)(2,1)S(1)}, bf16[2,2,2,2,32,512]{5,4,3,2,1,0:T(8,128)(2,1)}, u32[]{:S(2)}, u32[]{:S(2)}) collective-permute-start(bf16[2,2,2,2,32,512]{5,4,3,2,1,0:T(8,128)(2,1)S(1)} %collective-permute-done.3.high), channel_id=1, source_target_pairs={{0,4},{4,0},{1,5},{5,1},{2,6},{6,2},{3,7},{7,3},{8,12},{12,8},{9,1... | collective-permute-start | bytes 1572872 | tf_op jit(solution)/shard_map/ppermute | solution.py:21
  66.7 0.1 pad_add_fusion.place
  66.7 1.6 %collective-permute-done.5.core_high = bf16[2,2,2,2,32,512]{5,4,3,2,1,0:T(8,128)(2,1)} collective-permute-done((bf16[2,2,2,2,32,512]{5,4,3,2,1,0:T(8,128)(2,1)S(1)}, bf16[2,2,2,2,32,512]{5,4,3,2,1,0:T(8,128)(2,1)}, u32[]{:S(2)}, u32[]{:S(2)}) %collective-permute-start.5) | collective-permute-done | bytes 524320 | tf_op jit(solution)/shard_map/ppermute | solution.py:21
  68.3 2.4 %all-to-all-done = bf16[16,2,128,256]{3,2,1,0:T(8,128)(2,1)S(1)} async-done(((bf16[16,2,128,256]{3,2,1,0:T(8,128)(2,1)}), bf16[16,2,128,256]{3,2,1,0:T(8,128)(2,1)S(1)}, u32[]{:S(2)}, u32[]{:S(2)}) %all-to-all-start) | async-done | bytes 2097184 | tf_op jit(solution)/shard_map/all_to_all | solution.py:215
  70.8 3.1 %rotate.1 = f32[8,528,128]{2,1,0:T(8,128)S(1)} custom-call(s32[3]{0:T(128)S(1)} %pad_add_fusion.place, s32[2]{0:T(128)S(1)} %copy-done, bf16[4,4,2,128,256]{4,3,2,1,0:T(8,128)(2,1)S(1)} %bitcast.22, bf16[2,2,2,2,32,512]{5,4,3,2,1,0:T(8,128)(2,1)S(1)} %pad_maximum_fusion.low, bf16[2,2,2,2,32,512]{5,4,3,2,1,0:T(8,128)(2,1)S(1)} %collective-permute-done.3.high, ...), custom_call_target="tpu_custom_call" | custom-call | flops 1073741824 | bytes 8388608 | tf_op jit(solution)/shard_map/rotate/pallas_call | solution.py:151
  73.9 0.1 convert_element_type.25
  74.0 20.4 %all_to_all.20 = f16[8,528,128]{2,1,0:T(8,128)(2,1)S(1)} all-to-all(f16[8,528,128]{2,1,0:T(8,128)(2,1)S(1)} %convert_element_type.25), channel_id=1, replica_groups=mesh['zl'=2,'y'=8,'x'=4,'c'=2,'zh'=4] {'x','c'}, dimensions={0} | all-to-all | bytes 2162688 | tf_op jit(solution)/shard_map/all_to_all | solution.py:222
  94.4 0.2 slice.16
  94.7 0.2 fusion
  94.9 0.9 broadcast_in_dim.2
  95.8 4.8 %all-to-all-start.2 = ((bf16[4,2,256,128]{3,2,1,0:T(8,128)(2,1)}), bf16[4,2,256,128]{3,2,1,0:T(8,128)(2,1)S(1)}, u32[]{:S(2)}, u32[]{:S(2)}) async-start(bf16[4,2,256,128]{3,2,1,0:T(8,128)(2,1)} %broadcast_in_dim.2), calls=%async_computation.2 | async-start | bytes 1048576 | tf_op jit(solution)/shard_map/all_to_all | solution.py:229
  100.5 10.3 %all-gather = bf16[8,256,128]{2,1,0:T(8,128)(2,1)S(1)} all-gather(bf16[2,256,128]{2,1,0:T(8,128)(2,1)S(1)} %get-tuple-element.9), channel_id=2, replica_groups=mesh['zl'=2,'y'=8,'x'=4,'c'=2,'zh'=4] {'x'}, dimensions={0}, use_global_device_ids=true | all-gather | bytes 655360 | tf_op jit(solution)/shard_map/all_gather | solution.py:232
  110.8 5.8 %collective-permute-start.6 = (bf16[4,2,256,128]{3,2,1,0:T(8,128)(2,1)S(1)}, bf16[4,2,256,128]{3,2,1,0:T(8,128)(2,1)S(1)}, u32[]{:S(2)}, u32[]{:S(2)}) collective-permute-start(bf16[4,2,256,128]{3,2,1,0:T(8,128)(2,1)S(1)} %bitcast.23), channel_id=1, source_target_pairs={{0,4},{4,0},{1,5},{5,1},{2,6},{6,2},{3,7},{7,3},{8,12},{12,8},{9,1... | collective-permute-start | bytes 1572872 | tf_op jit(solution)/shard_map/ppermute | solution.py:21
  116.6 1.5 %collective-permute-done.6.core_act = bf16[4,2,256,128]{3,2,1,0:T(8,128)(2,1)S(1)} collective-permute-done((bf16[4,2,256,128]{3,2,1,0:T(8,128)(2,1)S(1)}, bf16[4,2,256,128]{3,2,1,0:T(8,128)(2,1)S(1)}, u32[]{:S(2)}, u32[]{:S(2)}) %collective-permute-start.6) | collective-permute-done | bytes 524320 | tf_op jit(solution)/shard_map/ppermute | solution.py:21
  118.1 1.7 %share.1 = bf16[256,512]{1,0:T(8,128)(2,1)} custom-call(s32[3]{0:T(128)S(1)} %pad_add_fusion.place, bf16[4,2,256,128]{3,2,1,0:T(8,128)(2,1)S(1)} %all-to-all-done.2.grad, bf16[4,2,256,128]{3,2,1,0:T(8,128)(2,1)S(1)} %bitcast.24, bf16[4,2,256,128]{3,2,1,0:T(8,128)(2,1)S(1)} %collective-permute-done.6.core_act), custom_call_target="tpu_custom_call" | custom-call | flops 268435456 | bytes 2097152 | tf_op jit(solution)/shard_map/share/pallas_call | solution.py:185
  119.9 7.7 %all-to-all-start.3 = ((bf16[16,16,512]{2,1,0:T(8,128)(2,1)}), bf16[16,16,512]{2,1,0:T(8,128)(2,1)S(1)}, u32[]{:S(2)}, u32[]{:S(2)}) async-start(bf16[16,16,512]{2,1,0:T(8,128)(2,1)} %bitcast.15), calls=%async_computation.3 | async-start | bytes 524288 | tf_op jit(solution)/shard_map/all_to_all | solution.py:235
  127.6 8.9 %all-to-all-done.3 = bf16[16,16,512]{2,1,0:T(8,128)(2,1)S(1)} async-done(((bf16[16,16,512]{2,1,0:T(8,128)(2,1)}), bf16[16,16,512]{2,1,0:T(8,128)(2,1)S(1)}, u32[]{:S(2)}, u32[]{:S(2)}) %all-to-all-start.3) | async-done | bytes 262176 | tf_op jit(solution)/shard_map/all_to_all | solution.py:235
  136.5 0.1 divide_reduce_fusion
  136.6 0.6 broadcast_multiply_fusion
  (12 shorter events, 0.2 us)
Async XLA Ops:
  1.6 7.8 %collective-permute-start = (bf16[2,32,512]{2,1,0:T(8,128)(2,1)}, bf16[2,32,512]{2,1,0:T(8,128)(2,1)S(1)}, u32[]{:S(2)}, u32[]{:S(2)}) collective-permute-start(bf16[2,32,512]{2,1,0:T(8,128)(2,1)} %arrange_bases.1), channel_id=1, source_target_pairs={{0,256},{256,0},{1,257},{257,1},{2,258},{258,2},{3,259},{259,3},{4... | collective-permute-start | bytes 196616 | tf_op jit(solution)/shard_map/ppermute | solution.py:21
  9.4 11.9 %copy-start.1 = (bf16[2,32,512]{2,1,0:T(8,128)(2,1)S(1)}, bf16[2,32,512]{2,1,0:T(8,128)(2,1)}, u32[]{:S(2)}) copy-start(bf16[2,32,512]{2,1,0:T(8,128)(2,1)} %arrange_bases.1) | copy-start | bytes 196612
  9.4 61.3 %all-to-all-start = ((bf16[16,2,128,256]{3,2,1,0:T(8,128)(2,1)}), bf16[16,2,128,256]{3,2,1,0:T(8,128)(2,1)S(1)}, u32[]{:S(2)}, u32[]{:S(2)}) async-start(bf16[16,2,128,256]{3,2,1,0:T(8,128)(2,1)} %bitcast.25), calls=%async_computation | async-start | bytes 4194304 | tf_op jit(solution)/shard_map/all_to_all | solution.py:215
  21.3 49.5 %copy-start = (s32[2]{0:T(128)S(1)}, s32[2]{0:T(128)}, u32[]{:S(2)}) copy-start(s32[2]{0:T(128)} %lengths.1) | copy-start | bytes 28
  21.3 9.9 %collective-permute-start.1 = (bf16[2,2,32,512]{3,2,1,0:T(8,128)(2,1)S(1)}, bf16[2,2,32,512]{3,2,1,0:T(8,128)(2,1)S(1)}, u32[]{:S(2)}, u32[]{:S(2)}) collective-permute-start(bf16[2,2,32,512]{3,2,1,0:T(8,128)(2,1)S(1)} %get-tuple-element.14), channel_id=1, source_target_pairs={{0,128},{32,160},{64,192},{96,224},{128,0},{160,32},{192,64},{224,... | collective-permute-start | bytes 393224 | tf_op jit(solution)/shard_map/ppermute | solution.py:204
  31.3 17.2 %collective-permute-start.2 = (bf16[2,2,2,32,512]{4,3,2,1,0:T(8,128)(2,1)S(1)}, bf16[2,2,2,32,512]{4,3,2,1,0:T(8,128)(2,1)S(1)}, u32[]{:S(2)}, u32[]{:S(2)}) collective-permute-start(bf16[2,2,2,32,512]{4,3,2,1,0:T(8,128)(2,1)S(1)} %get-tuple-element.12), channel_id=1, source_target_pairs={{0,64},{32,96},{64,0},{96,32},{128,192},{160,224},{192,128},{224,1... | collective-permute-start | bytes 786440 | tf_op jit(solution)/shard_map/ppermute | solution.py:204
  48.5 14.2 %collective-permute-start.3 = (bf16[2,2,2,2,32,512]{5,4,3,2,1,0:T(8,128)(2,1)S(1)}, bf16[2,2,2,2,32,512]{5,4,3,2,1,0:T(8,128)(2,1)S(1)}, u32[]{:S(2)}, u32[]{:S(2)}) collective-permute-start(bf16[2,2,2,2,32,512]{5,4,3,2,1,0:T(8,128)(2,1)S(1)} %pad_maximum_fusion.low), channel_id=1, source_target_pairs={{0,32},{32,0},{64,96},{96,64},{128,160},{160,128},{192,224},{224,1... | collective-permute-start | bytes 1572872 | tf_op jit(solution)/shard_map/ppermute | solution.py:204
  50.4 16.3 %collective-permute-start.4 = (bf16[2,2,2,2,32,512]{5,4,3,2,1,0:T(8,128)(2,1)S(1)}, bf16[2,2,2,2,32,512]{5,4,3,2,1,0:T(8,128)(2,1)}, u32[]{:S(2)}, u32[]{:S(2)}) collective-permute-start(bf16[2,2,2,2,32,512]{5,4,3,2,1,0:T(8,128)(2,1)S(1)} %pad_maximum_fusion.low), channel_id=1, source_target_pairs={{0,4},{4,0},{1,5},{5,1},{2,6},{6,2},{3,7},{7,3},{8,12},{12,8},{9,1... | collective-permute-start | bytes 1572872 | tf_op jit(solution)/shard_map/ppermute | solution.py:21
  62.7 5.6 %collective-permute-start.5 = (bf16[2,2,2,2,32,512]{5,4,3,2,1,0:T(8,128)(2,1)S(1)}, bf16[2,2,2,2,32,512]{5,4,3,2,1,0:T(8,128)(2,1)}, u32[]{:S(2)}, u32[]{:S(2)}) collective-permute-start(bf16[2,2,2,2,32,512]{5,4,3,2,1,0:T(8,128)(2,1)S(1)} %collective-permute-done.3.high), channel_id=1, source_target_pairs={{0,4},{4,0},{1,5},{5,1},{2,6},{6,2},{3,7},{7,3},{8,12},{12,8},{9,1... | collective-permute-start | bytes 1572872 | tf_op jit(solution)/shard_map/ppermute | solution.py:21
  95.8 22.4 %all-to-all-start.2 = ((bf16[4,2,256,128]{3,2,1,0:T(8,128)(2,1)}), bf16[4,2,256,128]{3,2,1,0:T(8,128)(2,1)S(1)}, u32[]{:S(2)}, u32[]{:S(2)}) async-start(bf16[4,2,256,128]{3,2,1,0:T(8,128)(2,1)} %broadcast_in_dim.2), calls=%async_computation.2 | async-start | bytes 1048576 | tf_op jit(solution)/shard_map/all_to_all | solution.py:229
  110.8 7.3 %collective-permute-start.6 = (bf16[4,2,256,128]{3,2,1,0:T(8,128)(2,1)S(1)}, bf16[4,2,256,128]{3,2,1,0:T(8,128)(2,1)S(1)}, u32[]{:S(2)}, u32[]{:S(2)}) collective-permute-start(bf16[4,2,256,128]{3,2,1,0:T(8,128)(2,1)S(1)} %bitcast.23), channel_id=1, source_target_pairs={{0,4},{4,0},{1,5},{5,1},{2,6},{6,2},{3,7},{7,3},{8,12},{12,8},{9,1... | collective-permute-start | bytes 1572872 | tf_op jit(solution)/shard_map/ppermute | solution.py:21
  119.9 16.7 %all-to-all-start.3 = ((bf16[16,16,512]{2,1,0:T(8,128)(2,1)}), bf16[16,16,512]{2,1,0:T(8,128)(2,1)S(1)}, u32[]{:S(2)}, u32[]{:S(2)}) async-start(bf16[16,16,512]{2,1,0:T(8,128)(2,1)} %bitcast.15), calls=%async_computation.3 | async-start | bytes 524288 | tf_op jit(solution)/shard_map/all_to_all | solution.py:235

commit v13 on v10

v13 whole, which is shorter than its diff:
```python
import jax
import jax.numpy as jnp
from jax import lax
from jax.experimental import pallas as pl
from jax.experimental.pallas import tpu as pltpu
from jax.sharding import Mesh
from jax.sharding import PartitionSpec as P

SEQS = 2
F32 = jnp.float32
BF16 = jnp.bfloat16
F16 = jnp.float16
TILE = 16
TOP = 15
VMEM = pl.BlockSpec(memory_space=pltpu.VMEM)
SMEM = pl.BlockSpec(memory_space=pltpu.SMEM)


def sorting(width, outer, n_x, inner):
    run = width // (outer * n_x * inner)
    source = lax.broadcasted_iota(jnp.int32, (width, width), 0)
    target = lax.broadcasted_iota(jnp.int32, (width, width), 1)
    at_run, at_inner = source % run, source // run % inner
    at_x, at_outer = source // (run * inner) % n_x, source // (run * inner * n_x)
    moved = ((at_x * inner + at_inner) * outer + at_outer) * run + at_run
    return (moved == target).astype(F32).astype(BF16)


def spread(value, ones):
    return jnp.dot(value, ones, preferred_element_type=F32).astype(BF16)


def bases_kernel(y_lo, n_x, n_c, act, grad, out, held, sems):
    copies = [
        pltpu.make_async_copy(ref, held.at[i], sems.at[i]) for i, ref in enumerate((act, grad))
    ]
    for copy in copies:
        copy.start()
    by_owner = sorting(held.shape[2], y_lo, n_x, n_c)
    for copy in copies:
        copy.wait()
    out[0] = held[0]
    out[1] = spread(held[1], by_owner)


def arrange_bases(y_lo, n_x, n_c, act, grad):
    return pl.pallas_call(
        lambda *refs: bases_kernel(y_lo, n_x, n_c, *refs),
        out_shape=jax.ShapeDtypeStruct((2, *act.shape), BF16),
        in_specs=[pl.BlockSpec(memory_space=pl.ANY)] * 2,
        out_specs=VMEM,
        scratch_shapes=[pltpu.VMEM((2, *act.shape), BF16), pltpu.SemaphoreType.DMA((2,))],
        compiler_params=pltpu.CompilerParams(vmem_limit_bytes=60 * 2**20),
        cost_estimate=pl.CostEstimate(
            flops=2 * act.shape[0] * act.shape[1] ** 2, bytes_accessed=2**17, transcendentals=0
        ),
        name="arrange_bases",
    )(act, grad)


def tokens_kernel(y_lo, n_c, act, grad, act_out, grad_out, held, in_sems, moved, out_sems):
    copies = [
        pltpu.make_async_copy(ref, held.at[i], in_sems.at[i]) for i, ref in enumerate((act, grad))
    ]
    for copy in copies:
        copy.start()
    n_x, n_zh, toks, width = act_out.shape
    by_x = sorting(n_x * width, y_lo, n_x, n_c)
    sent = []
    for which, out in enumerate((act_out, grad_out)):
        copies[which].wait()
        part = spread(held[which], by_x)
        for x in range(n_x):
            moved[which, x] = part[:, x * width : (x + 1) * width]
            for zh in range(n_zh):
                sent.append(
                    pltpu.make_async_copy(
                        moved.at[which, x], out.at[x, zh], out_sems.at[which, x, zh]
                    )
                )
                sent[-1].start()
    for copy in sent:
        copy.wait()


def arrange_tokens(y_lo, n_x, n_c, n_zh, act, grad):
    toks, feats = act.shape
    out = jax.ShapeDtypeStruct((n_x, n_zh, toks, feats // n_x), BF16)
    hbm = pl.BlockSpec(memory_space=pl.ANY)
    return pl.pallas_call(
        lambda *refs: tokens_kernel(y_lo, n_c, *refs),
        out_shape=(out, out),
        in_specs=[hbm, hbm],
        out_specs=(hbm, hbm),
        scratch_shapes=[
            pltpu.VMEM((2, toks, feats), BF16),
            pltpu.SemaphoreType.DMA((2,)),
            pltpu.VMEM((2, n_x, toks, feats // n_x), BF16),
            pltpu.SemaphoreType.DMA((2, n_x, n_zh)),
        ],
        compiler_params=pltpu.CompilerParams(vmem_limit_bytes=60 * 2**20),
        cost_estimate=pl.CostEstimate(
            flops=4 * toks * feats * feats, bytes_accessed=2**20, transcendentals=0
        ),
        name="arrange_tokens",
    )(act, grad)


def rotate_kernel(which, place, lengths, tokens, low, high, core_low, core_high, out, whole):
    n_x, n_zh, toks, width = tokens.shape
    rows, cols = low.shape[4], low.shape[5]
    group, part = n_x * toks, cols // n_x
    zl, y, c, own_x = (place[i] for i in range(4))
    for one, pair in enumerate(((low, core_low), (high, core_high))):
        for two in range(2):
            for four in range(2):
                from_y = y ^ (four * 4 + two * 2 + one)
                for far in range(2):
                    owner = (zl ^ far) * 2 + from_y // 4
                    for ref, core in zip(pair, (c, 1 - c)):
                        at = pl.multiple_of((core * 4 + from_y % 4) * rows, rows)
                        whole[owner, pl.ds(at, rows)] = ref[two, four, far, which]
    total = None
    for owner in range(n_zh):
        left = tokens[:, owner].reshape(group, width)
        product = jnp.dot(left, whole[owner], preferred_element_type=F32)
        total = product if total is None else total + product
    if which == 0:
        index = lax.broadcasted_iota(jnp.int32, (group, 1), 0)
        position = ((y * n_x + index // toks) * 2 + c) * toks + index % toks
        total = jnp.where(position < lengths[zl], total, 0.0)
    largest = jnp.max(jnp.max(jnp.abs(total), axis=0, keepdims=True), axis=1, keepdims=True)
    level = jnp.clip(jnp.ceil(jnp.log2(jnp.maximum(largest, 1e-30))), -100.0, 100.0)
    total = total * jnp.exp2(F32(TOP) - level)
    for i in range(out.shape[0]):
        if which == 0:
            to = own_x ^ i
            value = total[:, i * part : (i + 1) * part]
        else:
            value = total[:, i * part // 2 : (i + 1) * part // 2]
            to = i
            value = jnp.concatenate([value[: group // 2], value[group // 2 :]], axis=1)
        out[to, pl.ds(0, value.shape[0])] = value
        out[to, pl.ds(value.shape[0], TILE)] = jnp.broadcast_to(level, (TILE, part))


def rotate(which, place, lengths, *arrays):
    n_x, n_zh, toks, width = arrays[0].shape
    cols = arrays[1].shape[5]
    pieces = n_x * (1 + which)
    depth = n_x * toks // (1 + which) + TILE
    return pl.pallas_call(
        lambda *refs: rotate_kernel(which, *refs),
        out_shape=jax.ShapeDtypeStruct((pieces, depth, cols // n_x), F32),
        in_specs=[SMEM] * 2 + [VMEM] * len(arrays),
        out_specs=VMEM,
        scratch_shapes=[pltpu.VMEM((n_zh, width, cols), BF16)],
        compiler_params=pltpu.CompilerParams(vmem_limit_bytes=40 * 2**20),
        cost_estimate=pl.CostEstimate(
            flops=2 * n_x * n_zh * toks * width * cols, bytes_accessed=4 * 2**20, transcendentals=0
        ),
        name="rotate",
    )(place, lengths, *arrays)


def share_kernel(place, grad, act, core_act, out):
    n_k, _, depth, part = grad.shape
    n_x, half = act.shape[0], part // 2
    c = place[2]
    total = None
    for core, tokens in ((c, act), (1 - c, core_act)):
        turned = [grad[k, core].T for k in range(n_k)]
        for side in range(2):
            left = jnp.concatenate([t[side * half : (side + 1) * half] for t in turned], axis=0)
            right = jnp.concatenate(
                [tokens[x, side * depth : (side + 1) * depth] for x in range(n_x)], axis=1
            )
            product = jnp.dot(left, right, preferred_element_type=F32)
            total = product if total is None else total + product
    out[...] = total.astype(BF16)


def share_of(place, grad, act, core_act):
    n_k, n_c, depth, part = grad.shape
    rows, cols = n_k * part // 2, act.shape[0] * part
    return pl.pallas_call(
        share_kernel,
        out_shape=jax.ShapeDtypeStruct((rows, cols), BF16),
        in_specs=[SMEM] + [VMEM] * 3,
        out_specs=VMEM,
        compiler_params=pltpu.CompilerParams(vmem_limit_bytes=32 * 2**20),
        cost_estimate=pl.CostEstimate(
            flops=4 * n_c * rows * cols * depth, bytes_accessed=2 * 2**20, transcendentals=0
        ),
        name="share",
    )(place, grad, act, core_act)


def on_device(activations, gradients, basis_act, basis_grad, lengths):
    n_zl, n_y, n_x, n_c, n_zh = (lax.axis_size(a) for a in ("zl", "y", "x", "c", "zh"))
    zl, y, x, c = (lax.axis_index(a) for a in ("zl", "y", "x", "c"))
    cols, group = basis_act.shape[1], n_x * activations.shape[0]

    def partner(value, axis, step):
        return lax.ppermute(value, axis, [(i, i ^ step) for i in range(lax.axis_size(axis))])

    bases = arrange_bases(n_y // 2, n_x, n_c, basis_act, basis_grad)
    act, grad = arrange_tokens(n_y // 2, n_x, n_c, n_zh, activations, gradients)
    far_bases, act = lax.optimization_barrier((partner(bases, "zl", 1), act))
    low = jnp.stack([bases, far_bases])
    low = jnp.stack([low, partner(low, "y", 4)])
    low = jnp.stack([low, partner(low, "y", 2)])
    high = partner(low, "y", 1)
    arrays = (low, high, partner(low, "c", 1), partner(high, "c", 1))

    def to_owners(tokens):
        flat = tokens.reshape(n_x * n_zh, *tokens.shape[2:])
        return lax.all_to_all(flat, ("x", "zh"), 0, 0, tiled=True).reshape(tokens.shape)

    act, grad = lax.optimization_barrier((to_owners(act), grad))
    grad = to_owners(grad)

    def unscaled(partial):
        factors = jnp.exp2(partial[..., None, -TILE:, :].astype(F32) - F32(TOP))
        partial = partial[..., :-TILE, :]
        tiles = partial.reshape(*partial.shape[:-2], -1, TILE, partial.shape[-1])
        return tiles.astype(F32) * factors

    place = jnp.stack([zl, y, c, x]).astype(jnp.int32)
    partial = rotate(0, place, lengths, act, *arrays).astype(F16)
    rot_act = unscaled(partial[0])
    for step in range(1, n_x):
        rot_act += unscaled(partner(partial[step], "x", step))
    rot_act = rot_act.astype(BF16).reshape(group, -1)

    partial = rotate(1, place, lengths, grad, *arrays).astype(F16)
    partial = unscaled(lax.all_to_all(partial, ("x", "c"), 0, 0, tiled=True))
    rot_grad = jnp.sum(partial.reshape(n_x, n_c, *partial.shape[1:]), axis=0)
    rot_grad = rot_grad.astype(BF16).reshape(n_c, group // 2, -1)
    wide_act = lax.all_gather(rot_act, "x", axis=0)
    wide_act, rot_grad = lax.optimization_barrier((wide_act, rot_grad))
    core_act = partner(wide_act, "c", 1)
    wide_grad = lax.all_gather(rot_grad, "zh", axis=0)
    share = share_of(place, wide_grad, wide_act, core_act).reshape(n_zl * n_y, -1, cols)
    received = lax.all_to_all(share, ("zl", "y"), 0, 0, tiled=True)
    received = received.astype(F32).reshape(SEQS, n_y, -1, cols)
    per_seq = jnp.sum(received, axis=1)
    scale = lengths.astype(F32)[:, None, None]
    return jnp.sum(per_seq * per_seq / scale, axis=0) / F32(SEQS)


def solution(mesh):
    split = Mesh(mesh.devices.reshape(2, 8, 4, 2, 4), ("zl", "y", "x", "c", "zh"))
    spec = P(("zl", "y", "x", "c"), "zh")
    return jax.shard_map(
        on_device, mesh=split, in_specs=(spec, spec, spec, spec, P()), out_specs=spec, check_vma=False
    )
```

time: 144 us -> 155 us (1.076)
  blocking collectives: 17.9 us -> 34 us
  waiting for transfers between devices: 53.7 us -> 41.3 us
  starting transfers between devices: 55.6 us -> 62.2 us
    all_gather x0 -> x1, blocking collectives: none -> 15.9 us  [on_device(): wide_act = lax.all_gather(rot_act, 'x', axis=0)]
    ppermute x7 -> x10, starting transfers between devices: 24.7 us -> 33.2 us  [partner(): lax.ppermute(value, axis, [(i, i ^ step) for i in range(lax.axis_size(axi...]
    ppermute x7 -> x10, waiting for transfers between devices: 27.5 us -> 20.3 us  [partner(): lax.ppermute(value, axis, [(i, i ^ step) for i in range(lax.axis_size(axi...]
    all_to_all x4 -> x3, waiting for transfers between devices: 16.7 us -> 12 us  [the longest x2 12 us: to_owners(): lax.all_to_all(flat, ('x', 'zh'), 0, 0, tiled=True).reshape(tokens.shape)]
    all_to_all x4 -> x3, starting transfers between devices: 23.3 us -> 21.5 us  [the longest x2 16.4 us: to_owners(): lax.all_to_all(flat, ('x', 'zh'), 0, 0, tiled=True).reshape(tokens.shape)]
  transfers between devices with their start and end apart: 12 -> 14, of which waited for: 9 -> 6; matrix products, arithmetic and copies ran while one was open for 2% -> 2% of each run, Pallas kernels for 4% -> 5%
where the time goes in v13:
time: 155 us; the launch traced here: 154 us
  starting transfers between devices  62.2 us (40%)
  waiting for transfers between devices  41.3 us (27%)
  blocking collectives  34 us (22%)
  Pallas kernels  11.1 us (7%)
  other arithmetic  4.57 us (3%)
    ppermute x10, starting transfers between devices, partner(): lax.ppermute(value, axis, [(i, i ^ step) for i in range(lax.axis_size(axi...  33.2 us
    ppermute x10, waiting for transfers between devices, partner(): lax.ppermute(value, axis, [(i, i ^ step) for i in range(lax.axis_size(axi...  20.3 us
    all_gather x1, blocking collectives, on_device(): wide_grad = lax.all_gather(rot_grad, 'zh', axis=0)  18.1 us
    all_to_all x2, starting transfers between devices, to_owners(): lax.all_to_all(flat, ('x', 'zh'), 0, 0, tiled=True).reshape(tokens.shape)  16.4 us
    all_gather x1, blocking collectives, on_device(): wide_act = lax.all_gather(rot_act, 'x', axis=0)  15.9 us
    all_to_all x2, waiting for transfers between devices, to_owners(): lax.all_to_all(flat, ('x', 'zh'), 0, 0, tiled=True).reshape(tokens.shape)  12 us
    all_to_all x1, waiting for transfers between devices, on_device(): received = lax.all_to_all(share, ('zl', 'y'), 0, 0, tiled=True)  9.04 us
    all_to_all x1, starting transfers between devices, on_device(): received = lax.all_to_all(share, ('zl', 'y'), 0, 0, tiled=True)  7.48 us
  transfers between devices with their start and end apart: 14, of which 6 were waited for; matrix products, arithmetic and copies ran while one was open for 2% of the time, Pallas kernels for 5%

profile of v13, /device:TPU:8, one launch (start us, length us, event | category | flops | bytes accessed | tf_op | source)
XLA Modules:
  0.0 153.7 jit_solution(7222995644383951457)
XLA Ops:
  0.0 1.6 %arrange_bases.1 = bf16[2,32,512]{2,1,0:T(8,128)(2,1)} custom-call(bf16[32,512]{1,0:T(8,128)(2,1)} %refs_0_.2, bf16[32,512]{1,0:T(8,128)(2,1)} %refs_1_.4), custom_call_target="tpu_custom_call" | custom-call | flops 16777216 | bytes 131072 | tf_op jit(solution)/shard_map/arrange_bases/pallas_call | solution.py:47
  1.6 4.3 %collective-permute-start = (bf16[2,32,512]{2,1,0:T(8,128)(2,1)}, bf16[2,32,512]{2,1,0:T(8,128)(2,1)S(1)}, u32[]{:S(2)}, u32[]{:S(2)}) collective-permute-start(bf16[2,32,512]{2,1,0:T(8,128)(2,1)} %arrange_bases.1), channel_id=1, source_target_pairs={{0,256},{256,0},{1,257},{257,1},{2,258},{258,2},{3,259},{259,3},{4... | collective-permute-start | bytes 196616 | tf_op jit(solution)/shard_map/ppermute | solution.py:205
  5.9 3.0 %arrange_tokens.1 = (bf16[4,4,128,256]{3,2,1,0:T(8,128)(2,1)}, bf16[4,4,128,256]{3,2,1,0:T(8,128)(2,1)}) custom-call(bf16[128,1024]{1,0:T(8,128)(2,1)} %refs_0_.3, bf16[128,1024]{1,0:T(8,128)(2,1)} %refs_1_.5), custom_call_target="tpu_custom_call" | custom-call | flops 536870912 | bytes 1048576 | tf_op jit(solution)/shard_map/arrange_tokens/pallas_call | solution.py:90
  8.9 12.0 %all-to-all-start = ((bf16[16,128,256]{2,1,0:T(8,128)(2,1)}), bf16[16,128,256]{2,1,0:T(8,128)(2,1)S(1)}, u32[]{:S(2)}, u32[]{:S(2)}) async-start(bf16[16,128,256]{2,1,0:T(8,128)(2,1)} %bitcast.67), calls=%async_computation | async-start | bytes 2097152 | tf_op jit(solution)/shard_map/all_to_all | solution.py:218
  20.9 6.8 %collective-permute-start.1 = (bf16[2,2,32,512]{3,2,1,0:T(8,128)(2,1)S(1)}, bf16[2,2,32,512]{3,2,1,0:T(8,128)(2,1)S(1)}, u32[]{:S(2)}, u32[]{:S(2)}) collective-permute-start(bf16[2,2,32,512]{3,2,1,0:T(8,128)(2,1)S(1)} %get-tuple-element.27), channel_id=1, source_target_pairs={{0,128},{32,160},{64,192},{96,224},{128,0},{160,32},{192,64},{224,... | collective-permute-start | bytes 393224 | tf_op jit(solution)/shard_map/ppermute | solution.py:205
  27.8 6.3 %collective-permute-done.1 = bf16[2,2,32,512]{3,2,1,0:T(8,128)(2,1)S(1)} collective-permute-done((bf16[2,2,32,512]{3,2,1,0:T(8,128)(2,1)S(1)}, bf16[2,2,32,512]{3,2,1,0:T(8,128)(2,1)S(1)}, u32[]{:S(2)}, u32[]{:S(2)}) %collective-permute-start.1) | collective-permute-done | bytes 131104 | tf_op jit(solution)/shard_map/ppermute | solution.py:205
  34.1 4.2 %collective-permute-start.2 = (bf16[2,2,2,32,512]{4,3,2,1,0:T(8,128)(2,1)S(1)}, bf16[2,2,2,32,512]{4,3,2,1,0:T(8,128)(2,1)S(1)}, u32[]{:S(2)}, u32[]{:S(2)}) collective-permute-start(bf16[2,2,2,32,512]{4,3,2,1,0:T(8,128)(2,1)S(1)} %get-tuple-element.25), channel_id=1, source_target_pairs={{0,64},{32,96},{64,0},{96,32},{128,192},{160,224},{192,128},{224,1... | collective-permute-start | bytes 786440 | tf_op jit(solution)/shard_map/ppermute | solution.py:205
  38.3 12.0 %all-to-all-done = bf16[16,128,256]{2,1,0:T(8,128)(2,1)S(1)} async-done(((bf16[16,128,256]{2,1,0:T(8,128)(2,1)}), bf16[16,128,256]{2,1,0:T(8,128)(2,1)S(1)}, u32[]{:S(2)}, u32[]{:S(2)}) %all-to-all-start) | async-done | bytes 1048608 | tf_op jit(solution)/shard_map/all_to_all | solution.py:218
  50.3 4.4 %all-to-all-start.1 = ((bf16[16,128,256]{2,1,0:T(8,128)(2,1)}), bf16[16,128,256]{2,1,0:T(8,128)(2,1)S(1)}, u32[]{:S(2)}, u32[]{:S(2)}) async-start(bf16[16,128,256]{2,1,0:T(8,128)(2,1)} %bitcast.23), calls=%async_computation.1 | async-start | bytes 2097152 | tf_op jit(solution)/shard_map/all_to_all | solution.py:218
  54.8 2.4 %collective-permute-start.3 = (bf16[2,2,2,2,32,512]{5,4,3,2,1,0:T(8,128)(2,1)S(1)}, bf16[2,2,2,2,32,512]{5,4,3,2,1,0:T(8,128)(2,1)S(1)}, u32[]{:S(2)}, u32[]{:S(2)}) collective-permute-start(bf16[2,2,2,2,32,512]{5,4,3,2,1,0:T(8,128)(2,1)S(1)} %pad_maximum_fusion.refs_3_), channel_id=1, source_target_pairs={{0,32},{32,0},{64,96},{96,64},{128,160},{160,128},{192,224},{224,1... | collective-permute-start | bytes 1572872 | tf_op jit(solution)/shard_map/ppermute | solution.py:205
  57.2 1.9 %collective-permute-start.4 = (bf16[2,2,2,2,32,512]{5,4,3,2,1,0:T(8,128)(2,1)S(1)}, bf16[2,2,2,2,32,512]{5,4,3,2,1,0:T(8,128)(2,1)}, u32[]{:S(2)}, u32[]{:S(2)}) collective-permute-start(bf16[2,2,2,2,32,512]{5,4,3,2,1,0:T(8,128)(2,1)S(1)} %pad_maximum_fusion.refs_3_), channel_id=1, source_target_pairs={{0,4},{4,0},{1,5},{5,1},{2,6},{6,2},{3,7},{7,3},{8,12},{12,8},{9,1... | collective-permute-start | bytes 1572872 | tf_op jit(solution)/shard_map/ppermute | solution.py:205
  59.1 11.1 %collective-permute-done.3.refs_4_ = bf16[2,2,2,2,32,512]{5,4,3,2,1,0:T(8,128)(2,1)S(1)} collective-permute-done((bf16[2,2,2,2,32,512]{5,4,3,2,1,0:T(8,128)(2,1)S(1)}, bf16[2,2,2,2,32,512]{5,4,3,2,1,0:T(8,128)(2,1)S(1)}, u32[]{:S(2)}, u32[]{:S(2)}) %collective-permute-start.3) | collective-permute-done | bytes 524320 | tf_op jit(solution)/shard_map/ppermute | solution.py:205
  70.2 1.9 %collective-permute-start.5 = (bf16[2,2,2,2,32,512]{5,4,3,2,1,0:T(8,128)(2,1)S(1)}, bf16[2,2,2,2,32,512]{5,4,3,2,1,0:T(8,128)(2,1)}, u32[]{:S(2)}, u32[]{:S(2)}) collective-permute-start(bf16[2,2,2,2,32,512]{5,4,3,2,1,0:T(8,128)(2,1)S(1)} %collective-permute-done.3.refs_4_), channel_id=1, source_target_pairs={{0,4},{4,0},{1,5},{5,1},{2,6},{6,2},{3,7},{7,3},{8,12},{12,8},{9,1... | collective-permute-start | bytes 1572872 | tf_op jit(solution)/shard_map/ppermute | solution.py:205
  72.2 1.9 %collective-permute-done.5.refs_6_ = bf16[2,2,2,2,32,512]{5,4,3,2,1,0:T(8,128)(2,1)} collective-permute-done((bf16[2,2,2,2,32,512]{5,4,3,2,1,0:T(8,128)(2,1)S(1)}, bf16[2,2,2,2,32,512]{5,4,3,2,1,0:T(8,128)(2,1)}, u32[]{:S(2)}, u32[]{:S(2)}) %collective-permute-start.5) | collective-permute-done | bytes 524320 | tf_op jit(solution)/shard_map/ppermute | solution.py:205
  74.1 2.2 %rotate.2 = f32[4,528,128]{2,1,0:T(8,128)S(1)} custom-call(s32[4]{0:T(128)S(1)} %pad_add_fusion.refs_0_.place, s32[2]{0:T(128)S(1)} %copy-done, bf16[4,4,128,256]{3,2,1,0:T(8,128)(2,1)S(1)} %bitcast.62, bf16[2,2,2,2,32,512]{5,4,3,2,1,0:T(8,128)(2,1)S(1)} %pad_maximum_fusion.refs_3_, bf16[2,2,2,2,32,512]{5,4,3,2,1,0:T(8,128)(2,1)S(1)} %collective-permute-done.3.refs_4_, ...), custom_call_target="tpu_custom_call" | custom-call | flops 536870912 | bytes 4194304 | tf_op jit(solution)/shard_map/rotate/pallas_call | solution.py:152
  76.5 4.8 %collective-permute-start.8 = (f16[528,128]{1,0:T(8,128)(2,1)S(1)}, f16[528,128]{1,0:T(8,128)(2,1)S(1)}, u32[]{:S(2)}, u32[]{:S(2)}) collective-permute-start(f16[528,128]{1,0:T(8,128)(2,1)S(1)} %get-tuple-element.22), channel_id=1, source_target_pairs={{0,24},{8,16},{16,8},{24,0},{1,25},{9,17},{17,9},{25,1},{2,26},{10... | collective-permute-start | bytes 405512 | tf_op jit(solution)/shard_map/ppermute | solution.py:205
  81.3 2.8 %collective-permute-start.7 = (f16[528,128]{1,0:T(8,128)(2,1)S(1)}, f16[528,128]{1,0:T(8,128)(2,1)}, u32[]{:S(2)}, u32[]{:S(2)}) collective-permute-start(f16[528,128]{1,0:T(8,128)(2,1)S(1)} %get-tuple-element.23), channel_id=1, source_target_pairs={{0,16},{8,24},{16,0},{24,8},{1,17},{9,25},{17,1},{25,9},{2,18},{10... | collective-permute-start | bytes 405512 | tf_op jit(solution)/shard_map/ppermute | solution.py:205
  84.1 2.3 %collective-permute-start.6 = (f16[528,128]{1,0:T(8,128)(2,1)S(1)}, f16[528,128]{1,0:T(8,128)(2,1)}, u32[]{:S(2)}, u32[]{:S(2)}) collective-permute-start(f16[528,128]{1,0:T(8,128)(2,1)S(1)} %get-tuple-element.21), channel_id=1, source_target_pairs={{0,8},{8,0},{16,24},{24,16},{1,9},{9,1},{17,25},{25,17},{2,10},{10... | collective-permute-start | bytes 405512 | tf_op jit(solution)/shard_map/ppermute | solution.py:205
  86.4 1.0 collective-permute-done.8
  87.4 2.6 %rotate.3 = f32[8,272,128]{2,1,0:T(8,128)S(1)} custom-call(s32[4]{0:T(128)S(1)} %pad_add_fusion.refs_0_.place, s32[2]{0:T(128)S(1)} %copy-done, bf16[4,4,128,256]{3,2,1,0:T(8,128)(2,1)S(1)} %bitcast.63, bf16[2,2,2,2,32,512]{5,4,3,2,1,0:T(8,128)(2,1)S(1)} %pad_maximum_fusion.refs_3_, bf16[2,2,2,2,32,512]{5,4,3,2,1,0:T(8,128)(2,1)S(1)} %collective-permute-done.3.refs_4_, ...), custom_call_target="tpu_custom_call" | custom-call | flops 536870912 | bytes 4194304 | tf_op jit(solution)/shard_map/rotate/pallas_call | solution.py:152
  90.0 0.9 convert_element_type.78
  90.9 5.1 %all-to-all-start.2 = ((f16[8,272,128]{2,1,0:T(8,128)(2,1)}), f16[8,272,128]{2,1,0:T(8,128)(2,1)S(1)}, u32[]{:S(2)}, u32[]{:S(2)}) async-start(f16[8,272,128]{2,1,0:T(8,128)(2,1)} %convert_element_type.78), calls=%async_computation.2 | async-start | bytes 1114112 | tf_op jit(solution)/shard_map/all_to_all | solution.py:237
  95.9 0.7 multiply_exponential_fusion.2
  96.6 0.7 multiply_exponential_fusion.3
  97.3 1.2 fusion.1
  98.5 15.9 %all_gather.9.act = bf16[4,512,128]{2,1,0:T(8,128)(2,1)S(1)} all-gather(bf16[1,512,128]{2,1,0:T(8,128)(2,1)S(1)} %fusion.1), channel_id=1, replica_groups=mesh['zl'=2,'y'=8,'x'=4,'c'=2,'zh'=4] {'x'}, dimensions={0}, use_global_device_ids=true | all-gather | bytes 655360 | tf_op jit(solution)/shard_map/all_gather | solution.py:240
  114.7 1.9 %collective-permute-start.9 = (bf16[4,512,128]{2,1,0:T(8,128)(2,1)S(1)}, bf16[4,512,128]{2,1,0:T(8,128)(2,1)S(1)}, u32[]{:S(2)}, u32[]{:S(2)}) collective-permute-start(bf16[4,512,128]{2,1,0:T(8,128)(2,1)S(1)} %all_gather.9.act), channel_id=1, source_target_pairs={{0,4},{4,0},{1,5},{5,1},{2,6},{6,2},{3,7},{7,3},{8,12},{12,8},{9,1... | collective-permute-start | bytes 1572872 | tf_op jit(solution)/shard_map/ppermute | solution.py:205
  116.6 18.1 %all-gather = bf16[8,256,128]{2,1,0:T(8,128)(2,1)S(1)} all-gather(bf16[2,256,128]{2,1,0:T(8,128)(2,1)S(1)} %bitcast.68), channel_id=2, replica_groups=mesh['zl'=2,'y'=8,'x'=4,'c'=2,'zh'=4] {'zh'}, dimensions={0}, use_global_device_ids=true | all-gather | bytes 655360 | tf_op jit(solution)/shard_map/all_gather | solution.py:243
  134.7 1.7 %share.1 = bf16[256,512]{1,0:T(8,128)(2,1)} custom-call(s32[4]{0:T(128)S(1)} %pad_add_fusion.refs_0_.place, bf16[4,2,256,128]{3,2,1,0:T(8,128)(2,1)S(1)} %bitcast.64, bf16[4,512,128]{2,1,0:T(8,128)(2,1)S(1)} %all_gather.9.act, bf16[4,512,128]{2,1,0:T(8,128)(2,1)S(1)} %collective-permute-done.9.core_act), custom_call_target="tpu_custom_call" | custom-call | flops 268435456 | bytes 2097152 | tf_op jit(solution)/shard_map/share/pallas_call | solution.py:186
  136.4 7.5 %all-to-all-start.3 = ((bf16[16,16,512]{2,1,0:T(8,128)(2,1)}), bf16[16,16,512]{2,1,0:T(8,128)(2,1)S(1)}, u32[]{:S(2)}, u32[]{:S(2)}) async-start(bf16[16,16,512]{2,1,0:T(8,128)(2,1)} %bitcast.29), calls=%async_computation.3 | async-start | bytes 524288 | tf_op jit(solution)/shard_map/all_to_all | solution.py:245
  143.9 9.0 %all-to-all-done.3 = bf16[16,16,512]{2,1,0:T(8,128)(2,1)S(1)} async-done(((bf16[16,16,512]{2,1,0:T(8,128)(2,1)}), bf16[16,16,512]{2,1,0:T(8,128)(2,1)S(1)}, u32[]{:S(2)}, u32[]{:S(2)}) %all-to-all-start.3) | async-done | bytes 262176 | tf_op jit(solution)/shard_map/all_to_all | solution.py:245
  153.0 0.6 broadcast_multiply_fusion
  (33 shorter events, 0.8 us)
Async XLA Ops:
  1.6 7.3 %collective-permute-start = (bf16[2,32,512]{2,1,0:T(8,128)(2,1)}, bf16[2,32,512]{2,1,0:T(8,128)(2,1)S(1)}, u32[]{:S(2)}, u32[]{:S(2)}) collective-permute-start(bf16[2,32,512]{2,1,0:T(8,128)(2,1)} %arrange_bases.1), channel_id=1, source_target_pairs={{0,256},{256,0},{1,257},{257,1},{2,258},{258,2},{3,259},{259,3},{4... | collective-permute-start | bytes 196616 | tf_op jit(solution)/shard_map/ppermute | solution.py:205
  8.9 12.0 %copy-start.2 = (bf16[2,32,512]{2,1,0:T(8,128)(2,1)S(1)}, bf16[2,32,512]{2,1,0:T(8,128)(2,1)}, u32[]{:S(2)}) copy-start(bf16[2,32,512]{2,1,0:T(8,128)(2,1)} %arrange_bases.1) | copy-start | bytes 196612
  8.9 41.4 %all-to-all-start = ((bf16[16,128,256]{2,1,0:T(8,128)(2,1)}), bf16[16,128,256]{2,1,0:T(8,128)(2,1)S(1)}, u32[]{:S(2)}, u32[]{:S(2)}) async-start(bf16[16,128,256]{2,1,0:T(8,128)(2,1)} %bitcast.67), calls=%async_computation | async-start | bytes 2097152 | tf_op jit(solution)/shard_map/all_to_all | solution.py:218
  20.9 13.1 %collective-permute-start.1 = (bf16[2,2,32,512]{3,2,1,0:T(8,128)(2,1)S(1)}, bf16[2,2,32,512]{3,2,1,0:T(8,128)(2,1)S(1)}, u32[]{:S(2)}, u32[]{:S(2)}) collective-permute-start(bf16[2,2,32,512]{3,2,1,0:T(8,128)(2,1)S(1)} %get-tuple-element.27), channel_id=1, source_target_pairs={{0,128},{32,160},{64,192},{96,224},{128,0},{160,32},{192,64},{224,... | collective-permute-start | bytes 393224 | tf_op jit(solution)/shard_map/ppermute | solution.py:205
  34.1 20.6 %collective-permute-start.2 = (bf16[2,2,2,32,512]{4,3,2,1,0:T(8,128)(2,1)S(1)}, bf16[2,2,2,32,512]{4,3,2,1,0:T(8,128)(2,1)S(1)}, u32[]{:S(2)}, u32[]{:S(2)}) collective-permute-start(bf16[2,2,2,32,512]{4,3,2,1,0:T(8,128)(2,1)S(1)} %get-tuple-element.25), channel_id=1, source_target_pairs={{0,64},{32,96},{64,0},{96,32},{128,192},{160,224},{192,128},{224,1... | collective-permute-start | bytes 786440 | tf_op jit(solution)/shard_map/ppermute | solution.py:205
  50.3 23.8 %copy-start = (s32[2]{0:T(128)S(1)}, s32[2]{0:T(128)}, u32[]{:S(2)}) copy-start(s32[2]{0:T(128)} %refs_1_.7) | copy-start | bytes 28
  50.3 37.1 %all-to-all-start.1 = ((bf16[16,128,256]{2,1,0:T(8,128)(2,1)}), bf16[16,128,256]{2,1,0:T(8,128)(2,1)S(1)}, u32[]{:S(2)}, u32[]{:S(2)}) async-start(bf16[16,128,256]{2,1,0:T(8,128)(2,1)} %bitcast.23), calls=%async_computation.1 | async-start | bytes 2097152 | tf_op jit(solution)/shard_map/all_to_all | solution.py:218
  54.8 15.4 %collective-permute-start.3 = (bf16[2,2,2,2,32,512]{5,4,3,2,1,0:T(8,128)(2,1)S(1)}, bf16[2,2,2,2,32,512]{5,4,3,2,1,0:T(8,128)(2,1)S(1)}, u32[]{:S(2)}, u32[]{:S(2)}) collective-permute-start(bf16[2,2,2,2,32,512]{5,4,3,2,1,0:T(8,128)(2,1)S(1)} %pad_maximum_fusion.refs_3_), channel_id=1, source_target_pairs={{0,32},{32,0},{64,96},{96,64},{128,160},{160,128},{192,224},{224,1... | collective-permute-start | bytes 1572872 | tf_op jit(solution)/shard_map/ppermute | solution.py:205
  57.2 15.0 %collective-permute-start.4 = (bf16[2,2,2,2,32,512]{5,4,3,2,1,0:T(8,128)(2,1)S(1)}, bf16[2,2,2,2,32,512]{5,4,3,2,1,0:T(8,128)(2,1)}, u32[]{:S(2)}, u32[]{:S(2)}) collective-permute-start(bf16[2,2,2,2,32,512]{5,4,3,2,1,0:T(8,128)(2,1)S(1)} %pad_maximum_fusion.refs_3_), channel_id=1, source_target_pairs={{0,4},{4,0},{1,5},{5,1},{2,6},{6,2},{3,7},{7,3},{8,12},{12,8},{9,1... | collective-permute-start | bytes 1572872 | tf_op jit(solution)/shard_map/ppermute | solution.py:205
  70.2 3.9 %collective-permute-start.5 = (bf16[2,2,2,2,32,512]{5,4,3,2,1,0:T(8,128)(2,1)S(1)}, bf16[2,2,2,2,32,512]{5,4,3,2,1,0:T(8,128)(2,1)}, u32[]{:S(2)}, u32[]{:S(2)}) collective-permute-start(bf16[2,2,2,2,32,512]{5,4,3,2,1,0:T(8,128)(2,1)S(1)} %collective-permute-done.3.refs_4_), channel_id=1, source_target_pairs={{0,4},{4,0},{1,5},{5,1},{2,6},{6,2},{3,7},{7,3},{8,12},{12,8},{9,1... | collective-permute-start | bytes 1572872 | tf_op jit(solution)/shard_map/ppermute | solution.py:205
  76.4 13.5 %copy-start.1 = (f16[4,528,128]{2,1,0:T(8,128)(2,1)}, f16[4,528,128]{2,1,0:T(8,128)(2,1)S(1)}, u32[]{:S(2)}) copy-start(f16[4,528,128]{2,1,0:T(8,128)(2,1)S(1)} %convert_element_type.68) | copy-start | bytes 1622020
  76.5 10.8 %collective-permute-start.8 = (f16[528,128]{1,0:T(8,128)(2,1)S(1)}, f16[528,128]{1,0:T(8,128)(2,1)S(1)}, u32[]{:S(2)}, u32[]{:S(2)}) collective-permute-start(f16[528,128]{1,0:T(8,128)(2,1)S(1)} %get-tuple-element.22), channel_id=1, source_target_pairs={{0,24},{8,16},{16,8},{24,0},{1,25},{9,17},{17,9},{25,1},{2,26},{10... | collective-permute-start | bytes 405512 | tf_op jit(solution)/shard_map/ppermute | solution.py:205
  81.3 14.6 %collective-permute-start.7 = (f16[528,128]{1,0:T(8,128)(2,1)S(1)}, f16[528,128]{1,0:T(8,128)(2,1)}, u32[]{:S(2)}, u32[]{:S(2)}) collective-permute-start(f16[528,128]{1,0:T(8,128)(2,1)S(1)} %get-tuple-element.23), channel_id=1, source_target_pairs={{0,16},{8,24},{16,0},{24,8},{1,17},{9,25},{17,1},{25,9},{2,18},{10... | collective-permute-start | bytes 405512 | tf_op jit(solution)/shard_map/ppermute | solution.py:205
  84.1 12.5 %collective-permute-start.6 = (f16[528,128]{1,0:T(8,128)(2,1)S(1)}, f16[528,128]{1,0:T(8,128)(2,1)}, u32[]{:S(2)}, u32[]{:S(2)}) collective-permute-start(f16[528,128]{1,0:T(8,128)(2,1)S(1)} %get-tuple-element.21), channel_id=1, source_target_pairs={{0,8},{8,0},{16,24},{24,16},{1,9},{9,1},{17,25},{25,17},{2,10},{10... | collective-permute-start | bytes 405512 | tf_op jit(solution)/shard_map/ppermute | solution.py:205
  87.4 2.6 %copy-start.3 = (f16[528,128]{1,0:T(8,128)(2,1)}, f16[528,128]{1,0:T(8,128)(2,1)S(1)}, u32[]{:S(2)}) copy-start(f16[528,128]{1,0:T(8,128)(2,1)S(1)} %collective-permute-done.8) | copy-start | bytes 405508
  90.9 6.5 %copy-start.4 = (f16[528,128]{1,0:T(8,128)(2,1)S(1)}, f16[528,128]{1,0:T(8,128)(2,1)}, u32[]{:S(2)}) copy-start(f16[528,128]{1,0:T(8,128)(2,1)} %copy-done.3) | copy-start | bytes 405508
  90.9 23.5 %all-to-all-start.2 = ((f16[8,272,128]{2,1,0:T(8,128)(2,1)}), f16[8,272,128]{2,1,0:T(8,128)(2,1)S(1)}, u32[]{:S(2)}, u32[]{:S(2)}) async-start(f16[8,272,128]{2,1,0:T(8,128)(2,1)} %convert_element_type.78), calls=%async_computation.2 | async-start | bytes 1114112 | tf_op jit(solution)/shard_map/all_to_all | solution.py:237
  114.7 20.0 %collective-permute-start.9 = (bf16[4,512,128]{2,1,0:T(8,128)(2,1)S(1)}, bf16[4,512,128]{2,1,0:T(8,128)(2,1)S(1)}, u32[]{:S(2)}, u32[]{:S(2)}) collective-permute-start(bf16[4,512,128]{2,1,0:T(8,128)(2,1)S(1)} %all_gather.9.act), channel_id=1, source_target_pairs={{0,4},{4,0},{1,5},{5,1},{2,6},{6,2},{3,7},{7,3},{8,12},{12,8},{9,1... | collective-permute-start | bytes 1572872 | tf_op jit(solution)/shard_map/ppermute | solution.py:205
  136.4 16.5 %all-to-all-start.3 = ((bf16[16,16,512]{2,1,0:T(8,128)(2,1)}), bf16[16,16,512]{2,1,0:T(8,128)(2,1)S(1)}, u32[]{:S(2)}, u32[]{:S(2)}) async-start(bf16[16,16,512]{2,1,0:T(8,128)(2,1)} %bitcast.29), calls=%async_computation.3 | async-start | bytes 524288 | tf_op jit(solution)/shard_map/all_to_all | solution.py:245

commit v14 on v11

--- a/solution.py
+++ b/solution.py
@@ -63,21 +63,23 @@
     )(act, grad)
 
 
-def tokens_kernel(y_lo, n_c, act, grad, tokens, held, in_sems, moved, out_sems):
+def tokens_kernel(y_lo, act, grad, tokens, held, in_sems, moved, out_sems):
     copies = [
         pltpu.make_async_copy(ref, held.at[i], in_sems.at[i]) for i, ref in enumerate((act, grad))
     ]
     for copy in copies:
         copy.start()
     n_x, n_zh, _, toks, width = tokens.shape
-    by_x = sorting(n_x * width, y_lo, n_x, n_c)
+    run = width // y_lo
     for copy in copies:
         copy.wait()
-    both = held[...].reshape(2 * toks, n_x * width)
     sent = []
     for x in range(n_x):
-        part = spread(both, by_x[:, x * width : (x + 1) * width])
-        moved[x] = part.reshape(2, toks, width)
+        for which in range(2):
+            runs = [
+                held[which, :, (y * n_x + x) * run : (y * n_x + x + 1) * run] for y in range(y_lo)
+            ]
+            moved[x, which] = jnp.concatenate(runs, axis=1)
         for zh in range(n_zh):
             sent.append(pltpu.make_async_copy(moved.at[x], tokens.at[x, zh], out_sems.at[x, zh]))
             sent[-1].start()
@@ -85,10 +87,10 @@
         copy.wait()
 
 
-def arrange_tokens(y_lo, n_x, n_c, n_zh, act, grad):
+def arrange_tokens(y_lo, n_x, n_zh, act, grad):
     toks, feats = act.shape
     return pl.pallas_call(
-        lambda *refs: tokens_kernel(y_lo, n_c, *refs),
+        lambda *refs: tokens_kernel(y_lo, *refs),
         out_shape=jax.ShapeDtypeStruct((n_x, n_zh, 2, toks, feats // n_x), BF16),
         in_specs=[pl.BlockSpec(memory_space=pl.ANY)] * 2,
         out_specs=pl.BlockSpec(memory_space=pl.ANY),
@@ -100,7 +102,7 @@
         ],
         compiler_params=pltpu.CompilerParams(vmem_limit_bytes=60 * 2**20),
         cost_estimate=pl.CostEstimate(
-            flops=4 * toks * feats * feats, bytes_accessed=2**20, transcendentals=0
+            flops=toks * feats, bytes_accessed=2**20, transcendentals=0
         ),
         name="arrange_tokens",
     )(act, grad)
@@ -120,7 +122,7 @@
                     for far in range(2):
                         owner = (zl ^ far) * 2 + from_y // 4
                         for ref, core in zip(pair, (c, 1 - c)):
-                            at = pl.multiple_of((core * 4 + from_y % 4) * rows, rows)
+                            at = pl.multiple_of((from_y % 4 * 2 + core) * rows, rows)
                             whole[which, owner, pl.ds(at, rows)] = ref[two, four, far, which]
         total = None
         for owner in range(n_zh):
@@ -184,7 +186,7 @@
         out_shape=jax.ShapeDtypeStruct((rows, cols), BF16),
         in_specs=[VMEM, VMEM],
         out_specs=VMEM,
-        compiler_params=pltpu.CompilerParams(vmem_limit_bytes=32 * 2**20),
+        compiler_params=pltpu.CompilerParams(vmem_limit_bytes=16 * 2**20),
         cost_estimate=pl.CostEstimate(
             flops=4 * n_c * rows * cols * depth, bytes_accessed=2 * 2**20, transcendentals=0
         ),
@@ -201,7 +203,7 @@
         return lax.ppermute(value, "y", [(i, i ^ step) for i in range(n_y)])
 
     bases = arrange_bases(n_y // 2, n_x, n_c, basis_act, basis_grad)
-    tokens = arrange_tokens(n_y // 2, n_x, n_c, n_zh, activations, gradients)
+    tokens = arrange_tokens(n_y // 2, n_x, n_zh, activations, gradients)
     far_bases, tokens = lax.optimization_barrier((shift(bases, "zl", 1), tokens))
     low = jnp.stack([bases, far_bases])
     low = jnp.stack([low, partner(low, 4)])

time: 138 us -> 137 us (level)
  blocking collectives: 38.3 us -> 33.7 us
  waiting for transfers between devices: 41.2 us -> 45.3 us
    all_gather x1, blocking collectives: 18.7 us -> 14.8 us  [on_device(): wide_grad = lax.all_gather(rot_grad, 'zh', axis=0)]
    all_to_all x1, waiting for transfers between devices: 4.74 us -> 8.56 us  [on_device(): lax.all_to_all(tokens.reshape(n_x * n_zh, *tokens.shape[2:]), ('x', 'zh')...]
  transfers between devices with their start and end apart: 9 -> 9, of which waited for: 6 -> 7; matrix products, arithmetic and copies ran while one was open for 0% -> 0% of each run, Pallas kernels for 2% -> 2%
where the time goes in v14:
time: 137 us; the launch traced here: 136 us
  starting transfers between devices  45.6 us (33%)
  waiting for transfers between devices  45.3 us (33%)
  blocking collectives  33.7 us (25%)
  Pallas kernels  8.52 us (6%)
  local copies, waits for them, and re-layouts  1.41 us (1%)
    ppermute x3, waiting for transfers between devices, partner(): return lax.ppermute(value, 'y', [(i, i ^ step) for i in range(n_y)])  23.8 us
    all_to_all x1, blocking collectives, on_device(): partial = lax.all_to_all(partial, ('x', 'c'), 0, 0, tiled=True)  18.8 us
    all_gather x1, blocking collectives, on_device(): wide_grad = lax.all_gather(rot_grad, 'zh', axis=0)  14.8 us
    ppermute x3, starting transfers between devices, partner(): return lax.ppermute(value, 'y', [(i, i ^ step) for i in range(n_y)])  13.9 us
    all_to_all x1, starting transfers between devices, on_device(): lax.all_to_all(tokens.reshape(n_x * n_zh, *tokens.shape[2:]), ('x', 'zh')...  12.4 us
    all_to_all x1, waiting for transfers between devices, on_device(): received = lax.all_to_all(share, ('zl', 'y'), 0, 0, tiled=True)  9.93 us
    all_to_all x1, waiting for transfers between devices, on_device(): lax.all_to_all(tokens.reshape(n_x * n_zh, *tokens.shape[2:]), ('x', 'zh')...  8.56 us
    ppermute x3, starting transfers between devices, shift(): return lax.ppermute(value, axis, [(i, (i + step) % n) for i in range(n)])  8.11 us
  transfers between devices with their start and end apart: 9, of which 7 were waited for; matrix products, arithmetic and copies ran while one was open for 0% of the time, Pallas kernels for 2%

profile of v14, /device:TPU:8, one launch (start us, length us, event | category | flops | bytes accessed | tf_op | source)
XLA Modules:
  0.0 136.0 jit_solution(6459140582663711830)
XLA Ops:
  0.0 1.6 %arrange_bases.1 = bf16[2,32,512]{2,1,0:T(8,128)(2,1)} custom-call(bf16[32,512]{1,0:T(8,128)(2,1)} %refs_0_.2, bf16[32,512]{1,0:T(8,128)(2,1)} %refs_1_.2), custom_call_target="tpu_custom_call" | custom-call | flops 16777216 | bytes 131072 | tf_op jit(solution)/shard_map/arrange_bases/pallas_call | solution.py:52
  1.6 4.3 %collective-permute-start = (bf16[2,32,512]{2,1,0:T(8,128)(2,1)}, bf16[2,32,512]{2,1,0:T(8,128)(2,1)S(1)}, u32[]{:S(2)}, u32[]{:S(2)}) collective-permute-start(bf16[2,32,512]{2,1,0:T(8,128)(2,1)} %arrange_bases.1), channel_id=1, source_target_pairs={{0,256},{256,0},{1,257},{257,1},{2,258},{258,2},{3,259},{259,3},{4... | collective-permute-start | bytes 196616 | tf_op jit(solution)/shard_map/ppermute | solution.py:21
  5.9 2.6 %arrange_tokens.1 = bf16[4,4,2,128,256]{4,3,2,1,0:T(8,128)(2,1)} custom-call(bf16[128,1024]{1,0:T(8,128)(2,1)} %refs_0_.3, bf16[128,1024]{1,0:T(8,128)(2,1)} %refs_1_.3), custom_call_target="tpu_custom_call" | custom-call | flops 131072 | bytes 1048576 | tf_op jit(solution)/shard_map/arrange_tokens/pallas_call | solution.py:92
  8.5 0.0 collective-permute-done
  8.6 12.4 %all-to-all-start = ((bf16[16,2,128,256]{3,2,1,0:T(8,128)(2,1)}), bf16[16,2,128,256]{3,2,1,0:T(8,128)(2,1)S(1)}, u32[]{:S(2)}, u32[]{:S(2)}) async-start(bf16[16,2,128,256]{3,2,1,0:T(8,128)(2,1)} %bitcast.26), calls=%async_computation | async-start | bytes 4194304 | tf_op jit(solution)/shard_map/all_to_all | solution.py:214
  21.0 0.0 copy-start
  21.0 6.8 %collective-permute-start.1 = (bf16[2,2,32,512]{3,2,1,0:T(8,128)(2,1)S(1)}, bf16[2,2,32,512]{3,2,1,0:T(8,128)(2,1)S(1)}, u32[]{:S(2)}, u32[]{:S(2)}) collective-permute-start(bf16[2,2,32,512]{3,2,1,0:T(8,128)(2,1)S(1)} %get-tuple-element.14), channel_id=1, source_target_pairs={{0,128},{32,160},{64,192},{96,224},{128,0},{160,32},{192,64},{224,... | collective-permute-start | bytes 393224 | tf_op jit(solution)/shard_map/ppermute | solution.py:203
  27.9 6.0 %collective-permute-done.1 = bf16[2,2,32,512]{3,2,1,0:T(8,128)(2,1)S(1)} collective-permute-done((bf16[2,2,32,512]{3,2,1,0:T(8,128)(2,1)S(1)}, bf16[2,2,32,512]{3,2,1,0:T(8,128)(2,1)S(1)}, u32[]{:S(2)}, u32[]{:S(2)}) %collective-permute-start.1) | collective-permute-done | bytes 131104 | tf_op jit(solution)/shard_map/ppermute | solution.py:203
  33.9 3.9 %collective-permute-start.2 = (bf16[2,2,2,32,512]{4,3,2,1,0:T(8,128)(2,1)S(1)}, bf16[2,2,2,32,512]{4,3,2,1,0:T(8,128)(2,1)S(1)}, u32[]{:S(2)}, u32[]{:S(2)}) collective-permute-start(bf16[2,2,2,32,512]{4,3,2,1,0:T(8,128)(2,1)S(1)} %get-tuple-element.12), channel_id=1, source_target_pairs={{0,64},{32,96},{64,0},{96,32},{128,192},{160,224},{192,128},{224,1... | collective-permute-start | bytes 786440 | tf_op jit(solution)/shard_map/ppermute | solution.py:203
  37.8 8.8 %collective-permute-done.2 = bf16[2,2,2,32,512]{4,3,2,1,0:T(8,128)(2,1)S(1)} collective-permute-done((bf16[2,2,2,32,512]{4,3,2,1,0:T(8,128)(2,1)S(1)}, bf16[2,2,2,32,512]{4,3,2,1,0:T(8,128)(2,1)S(1)}, u32[]{:S(2)}, u32[]{:S(2)}) %collective-permute-start.2) | collective-permute-done | bytes 262176 | tf_op jit(solution)/shard_map/ppermute | solution.py:203
  46.6 0.1 pad_maximum_fusion.low
  46.6 3.2 %collective-permute-start.3 = (bf16[2,2,2,2,32,512]{5,4,3,2,1,0:T(8,128)(2,1)S(1)}, bf16[2,2,2,2,32,512]{5,4,3,2,1,0:T(8,128)(2,1)S(1)}, u32[]{:S(2)}, u32[]{:S(2)}) collective-permute-start(bf16[2,2,2,2,32,512]{5,4,3,2,1,0:T(8,128)(2,1)S(1)} %pad_maximum_fusion.low), channel_id=1, source_target_pairs={{0,32},{32,0},{64,96},{96,64},{128,160},{160,128},{192,224},{224,1... | collective-permute-start | bytes 1572872 | tf_op jit(solution)/shard_map/ppermute | solution.py:203
  49.8 1.9 %collective-permute-start.4 = (bf16[2,2,2,2,32,512]{5,4,3,2,1,0:T(8,128)(2,1)S(1)}, bf16[2,2,2,2,32,512]{5,4,3,2,1,0:T(8,128)(2,1)}, u32[]{:S(2)}, u32[]{:S(2)}) collective-permute-start(bf16[2,2,2,2,32,512]{5,4,3,2,1,0:T(8,128)(2,1)S(1)} %pad_maximum_fusion.low), channel_id=1, source_target_pairs={{0,4},{4,0},{1,5},{5,1},{2,6},{6,2},{3,7},{7,3},{8,12},{12,8},{9,1... | collective-permute-start | bytes 1572872 | tf_op jit(solution)/shard_map/ppermute | solution.py:21
  51.8 9.1 %collective-permute-done.3.high = bf16[2,2,2,2,32,512]{5,4,3,2,1,0:T(8,128)(2,1)S(1)} collective-permute-done((bf16[2,2,2,2,32,512]{5,4,3,2,1,0:T(8,128)(2,1)S(1)}, bf16[2,2,2,2,32,512]{5,4,3,2,1,0:T(8,128)(2,1)S(1)}, u32[]{:S(2)}, u32[]{:S(2)}) %collective-permute-start.3) | collective-permute-done | bytes 524320 | tf_op jit(solution)/shard_map/ppermute | solution.py:203
  60.8 1.9 %collective-permute-start.5 = (bf16[2,2,2,2,32,512]{5,4,3,2,1,0:T(8,128)(2,1)S(1)}, bf16[2,2,2,2,32,512]{5,4,3,2,1,0:T(8,128)(2,1)}, u32[]{:S(2)}, u32[]{:S(2)}) collective-permute-start(bf16[2,2,2,2,32,512]{5,4,3,2,1,0:T(8,128)(2,1)S(1)} %collective-permute-done.3.high), channel_id=1, source_target_pairs={{0,4},{4,0},{1,5},{5,1},{2,6},{6,2},{3,7},{7,3},{8,12},{12,8},{9,1... | collective-permute-start | bytes 1572872 | tf_op jit(solution)/shard_map/ppermute | solution.py:21
  62.8 0.1 pad_add_fusion.place
  62.9 1.9 %collective-permute-done.5.core_high = bf16[2,2,2,2,32,512]{5,4,3,2,1,0:T(8,128)(2,1)} collective-permute-done((bf16[2,2,2,2,32,512]{5,4,3,2,1,0:T(8,128)(2,1)S(1)}, bf16[2,2,2,2,32,512]{5,4,3,2,1,0:T(8,128)(2,1)}, u32[]{:S(2)}, u32[]{:S(2)}) %collective-permute-start.5) | collective-permute-done | bytes 524320 | tf_op jit(solution)/shard_map/ppermute | solution.py:21
  64.8 8.6 %all-to-all-done = bf16[16,2,128,256]{3,2,1,0:T(8,128)(2,1)S(1)} async-done(((bf16[16,2,128,256]{3,2,1,0:T(8,128)(2,1)}), bf16[16,2,128,256]{3,2,1,0:T(8,128)(2,1)S(1)}, u32[]{:S(2)}, u32[]{:S(2)}) %all-to-all-start) | async-done | bytes 2097184 | tf_op jit(solution)/shard_map/all_to_all | solution.py:214
  73.3 3.1 %rotate.1 = f32[8,528,128]{2,1,0:T(8,128)S(1)} custom-call(s32[3]{0:T(128)S(1)} %pad_add_fusion.place, s32[2]{0:T(128)S(1)} %copy-done, bf16[4,4,2,128,256]{4,3,2,1,0:T(8,128)(2,1)S(1)} %bitcast.23, bf16[2,2,2,2,32,512]{5,4,3,2,1,0:T(8,128)(2,1)S(1)} %pad_maximum_fusion.low, bf16[2,2,2,2,32,512]{5,4,3,2,1,0:T(8,128)(2,1)S(1)} %collective-permute-done.3.high, ...), custom_call_target="tpu_custom_call" | custom-call | flops 1073741824 | bytes 8388608 | tf_op jit(solution)/shard_map/rotate/pallas_call | solution.py:153
  76.4 0.1 convert_element_type.25
  76.6 18.8 %all_to_all.20 = f16[8,528,128]{2,1,0:T(8,128)(2,1)S(1)} all-to-all(f16[8,528,128]{2,1,0:T(8,128)(2,1)S(1)} %convert_element_type.25), channel_id=1, replica_groups=mesh['zl'=2,'y'=8,'x'=4,'c'=2,'zh'=4] {'x','c'}, dimensions={0} | all-to-all | bytes 2162688 | tf_op jit(solution)/shard_map/all_to_all | solution.py:221
  95.4 0.2 slice.16
  95.7 0.2 fusion
  95.9 1.2 broadcast_in_dim.2
  97.1 3.6 %all-to-all-start.2 = ((bf16[8,2,256,128]{3,2,1,0:T(8,128)(2,1)}), bf16[8,2,256,128]{3,2,1,0:T(8,128)(2,1)S(1)}, u32[]{:S(2)}, u32[]{:S(2)}) async-start(bf16[8,2,256,128]{3,2,1,0:T(8,128)(2,1)} %broadcast_in_dim.2), calls=%async_computation.2 | async-start | bytes 2097152 | tf_op jit(solution)/shard_map/all_to_all | solution.py:228
  100.7 14.8 %all-gather = bf16[8,256,128]{2,1,0:T(8,128)(2,1)S(1)} all-gather(bf16[2,256,128]{2,1,0:T(8,128)(2,1)S(1)} %get-tuple-element.10), channel_id=2, replica_groups=mesh['zl'=2,'y'=8,'x'=4,'c'=2,'zh'=4] {'zh'}, dimensions={0}, use_global_device_ids=true | all-gather | bytes 655360 | tf_op jit(solution)/shard_map/all_gather | solution.py:231
  115.5 1.1 all-to-all-done.2
  116.5 1.2 share.1
  117.7 7.6 %all-to-all-start.3 = ((bf16[16,16,512]{2,1,0:T(8,128)(2,1)}), bf16[16,16,512]{2,1,0:T(8,128)(2,1)S(1)}, u32[]{:S(2)}, u32[]{:S(2)}) async-start(bf16[16,16,512]{2,1,0:T(8,128)(2,1)} %bitcast.16), calls=%async_computation.3 | async-start | bytes 524288 | tf_op jit(solution)/shard_map/all_to_all | solution.py:233
  125.3 9.9 %all-to-all-done.3 = bf16[16,16,512]{2,1,0:T(8,128)(2,1)S(1)} async-done(((bf16[16,16,512]{2,1,0:T(8,128)(2,1)}), bf16[16,16,512]{2,1,0:T(8,128)(2,1)S(1)}, u32[]{:S(2)}, u32[]{:S(2)}) %all-to-all-start.3) | async-done | bytes 262176 | tf_op jit(solution)/shard_map/all_to_all | solution.py:233
  135.3 0.1 divide_reduce_fusion
  135.3 0.6 broadcast_multiply_fusion
  (10 shorter events, 0.1 us)
Async XLA Ops:
  1.6 6.9 %collective-permute-start = (bf16[2,32,512]{2,1,0:T(8,128)(2,1)}, bf16[2,32,512]{2,1,0:T(8,128)(2,1)S(1)}, u32[]{:S(2)}, u32[]{:S(2)}) collective-permute-start(bf16[2,32,512]{2,1,0:T(8,128)(2,1)} %arrange_bases.1), channel_id=1, source_target_pairs={{0,256},{256,0},{1,257},{257,1},{2,258},{258,2},{3,259},{259,3},{4... | collective-permute-start | bytes 196616 | tf_op jit(solution)/shard_map/ppermute | solution.py:21
  8.6 12.5 %copy-start.1 = (bf16[2,32,512]{2,1,0:T(8,128)(2,1)S(1)}, bf16[2,32,512]{2,1,0:T(8,128)(2,1)}, u32[]{:S(2)}) copy-start(bf16[2,32,512]{2,1,0:T(8,128)(2,1)} %arrange_bases.1) | copy-start | bytes 196612
  8.6 64.8 %all-to-all-start = ((bf16[16,2,128,256]{3,2,1,0:T(8,128)(2,1)}), bf16[16,2,128,256]{3,2,1,0:T(8,128)(2,1)S(1)}, u32[]{:S(2)}, u32[]{:S(2)}) async-start(bf16[16,2,128,256]{3,2,1,0:T(8,128)(2,1)} %bitcast.26), calls=%async_computation | async-start | bytes 4194304 | tf_op jit(solution)/shard_map/all_to_all | solution.py:214
  21.0 52.3 %copy-start = (s32[2]{0:T(128)S(1)}, s32[2]{0:T(128)}, u32[]{:S(2)}) copy-start(s32[2]{0:T(128)} %lengths.1) | copy-start | bytes 28
  21.0 12.8 %collective-permute-start.1 = (bf16[2,2,32,512]{3,2,1,0:T(8,128)(2,1)S(1)}, bf16[2,2,32,512]{3,2,1,0:T(8,128)(2,1)S(1)}, u32[]{:S(2)}, u32[]{:S(2)}) collective-permute-start(bf16[2,2,32,512]{3,2,1,0:T(8,128)(2,1)S(1)} %get-tuple-element.14), channel_id=1, source_target_pairs={{0,128},{32,160},{64,192},{96,224},{128,0},{160,32},{192,64},{224,... | collective-permute-start | bytes 393224 | tf_op jit(solution)/shard_map/ppermute | solution.py:203
  33.9 12.6 %collective-permute-start.2 = (bf16[2,2,2,32,512]{4,3,2,1,0:T(8,128)(2,1)S(1)}, bf16[2,2,2,32,512]{4,3,2,1,0:T(8,128)(2,1)S(1)}, u32[]{:S(2)}, u32[]{:S(2)}) collective-permute-start(bf16[2,2,2,32,512]{4,3,2,1,0:T(8,128)(2,1)S(1)} %get-tuple-element.12), channel_id=1, source_target_pairs={{0,64},{32,96},{64,0},{96,32},{128,192},{160,224},{192,128},{224,1... | collective-permute-start | bytes 786440 | tf_op jit(solution)/shard_map/ppermute | solution.py:203
  46.6 14.2 %collective-permute-start.3 = (bf16[2,2,2,2,32,512]{5,4,3,2,1,0:T(8,128)(2,1)S(1)}, bf16[2,2,2,2,32,512]{5,4,3,2,1,0:T(8,128)(2,1)S(1)}, u32[]{:S(2)}, u32[]{:S(2)}) collective-permute-start(bf16[2,2,2,2,32,512]{5,4,3,2,1,0:T(8,128)(2,1)S(1)} %pad_maximum_fusion.low), channel_id=1, source_target_pairs={{0,32},{32,0},{64,96},{96,64},{128,160},{160,128},{192,224},{224,1... | collective-permute-start | bytes 1572872 | tf_op jit(solution)/shard_map/ppermute | solution.py:203
  49.8 13.0 %collective-permute-start.4 = (bf16[2,2,2,2,32,512]{5,4,3,2,1,0:T(8,128)(2,1)S(1)}, bf16[2,2,2,2,32,512]{5,4,3,2,1,0:T(8,128)(2,1)}, u32[]{:S(2)}, u32[]{:S(2)}) collective-permute-start(bf16[2,2,2,2,32,512]{5,4,3,2,1,0:T(8,128)(2,1)S(1)} %pad_maximum_fusion.low), channel_id=1, source_target_pairs={{0,4},{4,0},{1,5},{5,1},{2,6},{6,2},{3,7},{7,3},{8,12},{12,8},{9,1... | collective-permute-start | bytes 1572872 | tf_op jit(solution)/shard_map/ppermute | solution.py:21
  60.8 3.9 %collective-permute-start.5 = (bf16[2,2,2,2,32,512]{5,4,3,2,1,0:T(8,128)(2,1)S(1)}, bf16[2,2,2,2,32,512]{5,4,3,2,1,0:T(8,128)(2,1)}, u32[]{:S(2)}, u32[]{:S(2)}) collective-permute-start(bf16[2,2,2,2,32,512]{5,4,3,2,1,0:T(8,128)(2,1)S(1)} %collective-permute-done.3.high), channel_id=1, source_target_pairs={{0,4},{4,0},{1,5},{5,1},{2,6},{6,2},{3,7},{7,3},{8,12},{12,8},{9,1... | collective-permute-start | bytes 1572872 | tf_op jit(solution)/shard_map/ppermute | solution.py:21
  97.1 19.4 %all-to-all-start.2 = ((bf16[8,2,256,128]{3,2,1,0:T(8,128)(2,1)}), bf16[8,2,256,128]{3,2,1,0:T(8,128)(2,1)S(1)}, u32[]{:S(2)}, u32[]{:S(2)}) async-start(bf16[8,2,256,128]{3,2,1,0:T(8,128)(2,1)} %broadcast_in_dim.2), calls=%async_computation.2 | async-start | bytes 2097152 | tf_op jit(solution)/shard_map/all_to_all | solution.py:228
  117.7 17.5 %all-to-all-start.3 = ((bf16[16,16,512]{2,1,0:T(8,128)(2,1)}), bf16[16,16,512]{2,1,0:T(8,128)(2,1)S(1)}, u32[]{:S(2)}, u32[]{:S(2)}) async-start(bf16[16,16,512]{2,1,0:T(8,128)(2,1)} %bitcast.16), calls=%async_computation.3 | async-start | bytes 524288 | tf_op jit(solution)/shard_map/all_to_all | solution.py:233

commit v15 on v14

--- a/solution.py
+++ b/solution.py
@@ -35,32 +35,25 @@
     return jnp.dot(value, ones, preferred_element_type=F32).astype(BF16)
 
 
-def bases_kernel(y_lo, n_x, n_c, act, grad, out, held, sems):
-    copies = [
-        pltpu.make_async_copy(ref, held.at[i], sems.at[i]) for i, ref in enumerate((act, grad))
-    ]
-    for copy in copies:
-        copy.start()
-    by_owner = sorting(held.shape[2], y_lo, n_x, n_c)
-    for copy in copies:
-        copy.wait()
-    out[0] = held[0]
-    out[1] = spread(held[1], by_owner)
-
-
-def arrange_bases(y_lo, n_x, n_c, act, grad):
+def bases_kernel(y_lo, n_x, n_c, own, far, out):
+    by_owner = sorting(own.shape[2], y_lo, n_x, n_c)
+    for i, ref in enumerate((own, far)):
+        out[i, 0] = ref[0]
+        out[i, 1] = spread(ref[1], by_owner)
+
+
+def arrange_bases(y_lo, n_x, n_c, own, far):
     return pl.pallas_call(
         lambda *refs: bases_kernel(y_lo, n_x, n_c, *refs),
-        out_shape=jax.ShapeDtypeStruct((2, *act.shape), BF16),
-        in_specs=[pl.BlockSpec(memory_space=pl.ANY)] * 2,
+        out_shape=jax.ShapeDtypeStruct((2, *own.shape), BF16),
+        in_specs=[VMEM] * 2,
         out_specs=VMEM,
-        scratch_shapes=[pltpu.VMEM((2, *act.shape), BF16), pltpu.SemaphoreType.DMA((2,))],
-        compiler_params=pltpu.CompilerParams(vmem_limit_bytes=60 * 2**20),
-        cost_estimate=pl.CostEstimate(
-            flops=2 * act.shape[0] * act.shape[1] ** 2, bytes_accessed=2**17, transcendentals=0
+        compiler_params=pltpu.CompilerParams(vmem_limit_bytes=16 * 2**20),
+        cost_estimate=pl.CostEstimate(
+            flops=4 * own.shape[1] * own.shape[2] ** 2, bytes_accessed=2**18, transcendentals=0
         ),
         name="arrange_bases",
-    )(act, grad)
+    )(own, far)
 
 
 def tokens_kernel(y_lo, act, grad, tokens, held, in_sems, moved, out_sems):
@@ -71,18 +64,21 @@
         copy.start()
     n_x, n_zh, _, toks, width = tokens.shape
     run = width // y_lo
-    for copy in copies:
-        copy.wait()
     sent = []
-    for x in range(n_x):
-        for which in range(2):
+    for which in range(2):
+        copies[which].wait()
+        for x in range(n_x):
             runs = [
                 held[which, :, (y * n_x + x) * run : (y * n_x + x + 1) * run] for y in range(y_lo)
             ]
-            moved[x, which] = jnp.concatenate(runs, axis=1)
-        for zh in range(n_zh):
-            sent.append(pltpu.make_async_copy(moved.at[x], tokens.at[x, zh], out_sems.at[x, zh]))
-            sent[-1].start()
+            moved[which, x] = jnp.concatenate(runs, axis=1)
+            for zh in range(n_zh):
+                sent.append(
+                    pltpu.make_async_copy(
+                        moved.at[which, x], tokens.at[x, zh, which], out_sems.at[which, x, zh]
+                    )
+                )
+                sent[-1].start()
     for copy in sent:
         copy.wait()
 
@@ -97,8 +93,8 @@
         scratch_shapes=[
             pltpu.VMEM((2, toks, feats), BF16),
             pltpu.SemaphoreType.DMA((2,)),
-            pltpu.VMEM((n_x, 2, toks, feats // n_x), BF16),
-            pltpu.SemaphoreType.DMA((n_x, n_zh)),
+            pltpu.VMEM((2, n_x, toks, feats // n_x), BF16),
+            pltpu.SemaphoreType.DMA((2, n_x, n_zh)),
         ],
         compiler_params=pltpu.CompilerParams(vmem_limit_bytes=60 * 2**20),
         cost_estimate=pl.CostEstimate(
@@ -202,10 +198,12 @@
     def partner(value, step):
         return lax.ppermute(value, "y", [(i, i ^ step) for i in range(n_y)])
 
-    bases = arrange_bases(n_y // 2, n_x, n_c, basis_act, basis_grad)
+    raw = jnp.stack([basis_act, basis_grad])
+    raw, activations = lax.optimization_barrier((raw, activations))
+    far = shift(raw, "zl", 1)
     tokens = arrange_tokens(n_y // 2, n_x, n_zh, activations, gradients)
-    far_bases, tokens = lax.optimization_barrier((shift(bases, "zl", 1), tokens))
-    low = jnp.stack([bases, far_bases])
+    far, tokens = lax.optimization_barrier((far, tokens))
+    low = arrange_bases(n_y // 2, n_x, n_c, raw, far)
     low = jnp.stack([low, partner(low, 4)])
     low = jnp.stack([low, partner(low, 2)])
     high = partner(low, 1)

time: 137 us -> 136 us (level)
  the two profiles are of different devices: /device:TPU:8 before, /device:TPU:10 now
where the time goes in v15:
time: 136 us; the launch traced here: 135 us
  starting transfers between devices  47.2 us (35%)
  waiting for transfers between devices  38.6 us (28%)
  blocking collectives  38.6 us (28%)
  Pallas kernels  7.44 us (5%)
  other arithmetic  2.06 us (2%)
  local copies, waits for them, and re-layouts  1.4 us (1%)
    ppermute x3, waiting for transfers between devices, partner(): return lax.ppermute(value, 'y', [(i, i ^ step) for i in range(n_y)])  23.9 us
    all_to_all x1, blocking collectives, on_device(): partial = lax.all_to_all(partial, ('x', 'c'), 0, 0, tiled=True)  19.7 us
    all_gather x1, blocking collectives, on_device(): wide_grad = lax.all_gather(rot_grad, 'zh', axis=0)  18.9 us
    ppermute x3, starting transfers between devices, partner(): return lax.ppermute(value, 'y', [(i, i ^ step) for i in range(n_y)])  14.2 us
    all_to_all x1, starting transfers between devices, on_device(): lax.all_to_all(tokens.reshape(n_x * n_zh, *tokens.shape[2:]), ('x', 'zh')...  12.5 us
    all_to_all x1, waiting for transfers between devices, on_device(): received = lax.all_to_all(share, ('zl', 'y'), 0, 0, tiled=True)  9.03 us
    ppermute x3, starting transfers between devices, shift(): return lax.ppermute(value, axis, [(i, (i + step) % n) for i in range(n)])  8.1 us
    all_to_all x1, starting transfers between devices, on_device(): received = lax.all_to_all(share, ('zl', 'y'), 0, 0, tiled=True)  7.56 us
  transfers between devices with their start and end apart: 9, of which 6 were waited for; matrix products, arithmetic and copies ran while one was open for 0% of the time, Pallas kernels for 2%

profile of v15, /device:TPU:10, one launch (start us, length us, event | category | flops | bytes accessed | tf_op | source)
XLA Modules:
  0.0 135.4 jit_solution(5890022492290536391)
XLA Ops:
  0.0 0.8 pad_maximum_fusion.2.refs_0_
  0.8 4.3 %collective-permute-start = (bf16[2,32,512]{2,1,0:T(8,128)(2,1)S(1)}, bf16[2,32,512]{2,1,0:T(8,128)(2,1)S(1)}, u32[]{:S(2)}, u32[]{:S(2)}) collective-permute-start(bf16[2,32,512]{2,1,0:T(8,128)(2,1)S(1)} %pad_maximum_fusion.2.refs_0_), channel_id=1, source_target_pairs={{0,256},{256,0},{1,257},{257,1},{2,258},{258,2},{3,259},{259,3},{4... | collective-permute-start | bytes 196616 | tf_op jit(solution)/shard_map/ppermute | solution.py:21
  5.1 2.7 %arrange_tokens.1 = bf16[4,4,2,128,256]{4,3,2,1,0:T(8,128)(2,1)} custom-call(bf16[128,1024]{1,0:T(8,128)(2,1)} %refs_0_, bf16[128,1024]{1,0:T(8,128)(2,1)} %refs_1_.1), custom_call_target="tpu_custom_call" | custom-call | flops 131072 | bytes 1048576 | tf_op jit(solution)/shard_map/arrange_tokens/pallas_call | solution.py:88
  7.8 0.0 collective-permute-done.refs_1_
  7.8 12.5 %all-to-all-start = ((bf16[16,2,128,256]{3,2,1,0:T(8,128)(2,1)}), bf16[16,2,128,256]{3,2,1,0:T(8,128)(2,1)S(1)}, u32[]{:S(2)}, u32[]{:S(2)}) async-start(bf16[16,2,128,256]{3,2,1,0:T(8,128)(2,1)} %bitcast.26), calls=%async_computation | async-start | bytes 4194304 | tf_op jit(solution)/shard_map/all_to_all | solution.py:212
  20.3 0.5 arrange_bases.1
  20.7 6.8 %collective-permute-start.1 = (bf16[2,2,32,512]{3,2,1,0:T(8,128)(2,1)S(1)}, bf16[2,2,32,512]{3,2,1,0:T(8,128)(2,1)S(1)}, u32[]{:S(2)}, u32[]{:S(2)}) collective-permute-start(bf16[2,2,32,512]{3,2,1,0:T(8,128)(2,1)S(1)} %arrange_bases.1), channel_id=1, source_target_pairs={{0,128},{32,160},{64,192},{96,224},{128,0},{160,32},{192,64},{224,... | collective-permute-start | bytes 393224 | tf_op jit(solution)/shard_map/ppermute | solution.py:199
  27.6 6.0 %collective-permute-done.1 = bf16[2,2,32,512]{3,2,1,0:T(8,128)(2,1)S(1)} collective-permute-done((bf16[2,2,32,512]{3,2,1,0:T(8,128)(2,1)S(1)}, bf16[2,2,32,512]{3,2,1,0:T(8,128)(2,1)S(1)}, u32[]{:S(2)}, u32[]{:S(2)}) %collective-permute-start.1) | collective-permute-done | bytes 131104 | tf_op jit(solution)/shard_map/ppermute | solution.py:199
  33.6 3.9 %collective-permute-start.2 = (bf16[2,2,2,32,512]{4,3,2,1,0:T(8,128)(2,1)S(1)}, bf16[2,2,2,32,512]{4,3,2,1,0:T(8,128)(2,1)S(1)}, u32[]{:S(2)}, u32[]{:S(2)}) collective-permute-start(bf16[2,2,2,32,512]{4,3,2,1,0:T(8,128)(2,1)S(1)} %get-tuple-element.16), channel_id=1, source_target_pairs={{0,64},{32,96},{64,0},{96,32},{128,192},{160,224},{192,128},{224,1... | collective-permute-start | bytes 786440 | tf_op jit(solution)/shard_map/ppermute | solution.py:199
  37.5 8.7 %collective-permute-done.2 = bf16[2,2,2,32,512]{4,3,2,1,0:T(8,128)(2,1)S(1)} collective-permute-done((bf16[2,2,2,32,512]{4,3,2,1,0:T(8,128)(2,1)S(1)}, bf16[2,2,2,32,512]{4,3,2,1,0:T(8,128)(2,1)S(1)}, u32[]{:S(2)}, u32[]{:S(2)}) %collective-permute-start.2) | collective-permute-done | bytes 262176 | tf_op jit(solution)/shard_map/ppermute | solution.py:199
  46.2 0.1 pad_maximum_fusion.low
  46.2 3.4 %collective-permute-start.3 = (bf16[2,2,2,2,32,512]{5,4,3,2,1,0:T(8,128)(2,1)S(1)}, bf16[2,2,2,2,32,512]{5,4,3,2,1,0:T(8,128)(2,1)S(1)}, u32[]{:S(2)}, u32[]{:S(2)}) collective-permute-start(bf16[2,2,2,2,32,512]{5,4,3,2,1,0:T(8,128)(2,1)S(1)} %pad_maximum_fusion.low), channel_id=1, source_target_pairs={{0,32},{32,0},{64,96},{96,64},{128,160},{160,128},{192,224},{224,1... | collective-permute-start | bytes 1572872 | tf_op jit(solution)/shard_map/ppermute | solution.py:199
  49.7 1.9 %collective-permute-start.4 = (bf16[2,2,2,2,32,512]{5,4,3,2,1,0:T(8,128)(2,1)S(1)}, bf16[2,2,2,2,32,512]{5,4,3,2,1,0:T(8,128)(2,1)}, u32[]{:S(2)}, u32[]{:S(2)}) collective-permute-start(bf16[2,2,2,2,32,512]{5,4,3,2,1,0:T(8,128)(2,1)S(1)} %pad_maximum_fusion.low), channel_id=1, source_target_pairs={{0,4},{4,0},{1,5},{5,1},{2,6},{6,2},{3,7},{7,3},{8,12},{12,8},{9,1... | collective-permute-start | bytes 1572872 | tf_op jit(solution)/shard_map/ppermute | solution.py:21
  51.6 9.3 %collective-permute-done.3.high = bf16[2,2,2,2,32,512]{5,4,3,2,1,0:T(8,128)(2,1)S(1)} collective-permute-done((bf16[2,2,2,2,32,512]{5,4,3,2,1,0:T(8,128)(2,1)S(1)}, bf16[2,2,2,2,32,512]{5,4,3,2,1,0:T(8,128)(2,1)S(1)}, u32[]{:S(2)}, u32[]{:S(2)}) %collective-permute-start.3) | collective-permute-done | bytes 524320 | tf_op jit(solution)/shard_map/ppermute | solution.py:199
  60.9 1.9 %collective-permute-start.5 = (bf16[2,2,2,2,32,512]{5,4,3,2,1,0:T(8,128)(2,1)S(1)}, bf16[2,2,2,2,32,512]{5,4,3,2,1,0:T(8,128)(2,1)}, u32[]{:S(2)}, u32[]{:S(2)}) collective-permute-start(bf16[2,2,2,2,32,512]{5,4,3,2,1,0:T(8,128)(2,1)S(1)} %collective-permute-done.3.high), channel_id=1, source_target_pairs={{0,4},{4,0},{1,5},{5,1},{2,6},{6,2},{3,7},{7,3},{8,12},{12,8},{9,1... | collective-permute-start | bytes 1572872 | tf_op jit(solution)/shard_map/ppermute | solution.py:21
  62.8 0.1 pad_add_fusion.place
  62.9 1.9 %collective-permute-done.5.core_high = bf16[2,2,2,2,32,512]{5,4,3,2,1,0:T(8,128)(2,1)} collective-permute-done((bf16[2,2,2,2,32,512]{5,4,3,2,1,0:T(8,128)(2,1)S(1)}, bf16[2,2,2,2,32,512]{5,4,3,2,1,0:T(8,128)(2,1)}, u32[]{:S(2)}, u32[]{:S(2)}) %collective-permute-start.5) | collective-permute-done | bytes 524320 | tf_op jit(solution)/shard_map/ppermute | solution.py:21
  64.8 3.7 %all-to-all-done = bf16[16,2,128,256]{3,2,1,0:T(8,128)(2,1)S(1)} async-done(((bf16[16,2,128,256]{3,2,1,0:T(8,128)(2,1)}), bf16[16,2,128,256]{3,2,1,0:T(8,128)(2,1)S(1)}, u32[]{:S(2)}, u32[]{:S(2)}) %all-to-all-start) | async-done | bytes 2097184 | tf_op jit(solution)/shard_map/all_to_all | solution.py:212
  68.4 3.1 %rotate.1 = f32[8,528,128]{2,1,0:T(8,128)S(1)} custom-call(s32[3]{0:T(128)S(1)} %pad_add_fusion.place, s32[2]{0:T(128)S(1)} %copy-done, bf16[4,4,2,128,256]{4,3,2,1,0:T(8,128)(2,1)S(1)} %bitcast.22, bf16[2,2,2,2,32,512]{5,4,3,2,1,0:T(8,128)(2,1)S(1)} %pad_maximum_fusion.low, bf16[2,2,2,2,32,512]{5,4,3,2,1,0:T(8,128)(2,1)S(1)} %collective-permute-done.3.high, ...), custom_call_target="tpu_custom_call" | custom-call | flops 1073741824 | bytes 8388608 | tf_op jit(solution)/shard_map/rotate/pallas_call | solution.py:149
  71.6 0.1 convert_element_type.25
  71.7 19.7 %all_to_all.20 = f16[8,528,128]{2,1,0:T(8,128)(2,1)S(1)} all-to-all(f16[8,528,128]{2,1,0:T(8,128)(2,1)S(1)} %convert_element_type.25), channel_id=1, replica_groups=mesh['zl'=2,'y'=8,'x'=4,'c'=2,'zh'=4] {'x','c'}, dimensions={0} | all-to-all | bytes 2162688 | tf_op jit(solution)/shard_map/all_to_all | solution.py:219
  91.4 0.2 slice.16
  91.7 0.2 fusion
  91.9 1.2 broadcast_in_dim.2
  93.1 4.9 %all-to-all-start.2 = ((bf16[8,2,256,128]{3,2,1,0:T(8,128)(2,1)}), bf16[8,2,256,128]{3,2,1,0:T(8,128)(2,1)S(1)}, u32[]{:S(2)}, u32[]{:S(2)}) async-start(bf16[8,2,256,128]{3,2,1,0:T(8,128)(2,1)} %broadcast_in_dim.2), calls=%async_computation.2 | async-start | bytes 2097152 | tf_op jit(solution)/shard_map/all_to_all | solution.py:226
  98.0 18.9 %all-gather = bf16[8,256,128]{2,1,0:T(8,128)(2,1)S(1)} all-gather(bf16[2,256,128]{2,1,0:T(8,128)(2,1)S(1)} %get-tuple-element.14), channel_id=2, replica_groups=mesh['zl'=2,'y'=8,'x'=4,'c'=2,'zh'=4] {'zh'}, dimensions={0}, use_global_device_ids=true | all-gather | bytes 655360 | tf_op jit(solution)/shard_map/all_gather | solution.py:229
  116.9 0.0 all-to-all-done.2
  116.9 1.2 share.1
  118.1 7.6 %all-to-all-start.3 = ((bf16[16,16,512]{2,1,0:T(8,128)(2,1)}), bf16[16,16,512]{2,1,0:T(8,128)(2,1)S(1)}, u32[]{:S(2)}, u32[]{:S(2)}) async-start(bf16[16,16,512]{2,1,0:T(8,128)(2,1)} %bitcast.16), calls=%async_computation.3 | async-start | bytes 524288 | tf_op jit(solution)/shard_map/all_to_all | solution.py:231
  125.7 9.0 %all-to-all-done.3 = bf16[16,16,512]{2,1,0:T(8,128)(2,1)S(1)} async-done(((bf16[16,16,512]{2,1,0:T(8,128)(2,1)}), bf16[16,16,512]{2,1,0:T(8,128)(2,1)S(1)}, u32[]{:S(2)}, u32[]{:S(2)}) %all-to-all-start.3) | async-done | bytes 262176 | tf_op jit(solution)/shard_map/all_to_all | solution.py:231
  134.7 0.1 divide_reduce_fusion
  134.8 0.6 broadcast_multiply_fusion
  (8 shorter events, 0.1 us)
Async XLA Ops:
  0.8 7.0 %collective-permute-start = (bf16[2,32,512]{2,1,0:T(8,128)(2,1)S(1)}, bf16[2,32,512]{2,1,0:T(8,128)(2,1)S(1)}, u32[]{:S(2)}, u32[]{:S(2)}) collective-permute-start(bf16[2,32,512]{2,1,0:T(8,128)(2,1)S(1)} %pad_maximum_fusion.2.refs_0_), channel_id=1, source_target_pairs={{0,256},{256,0},{1,257},{257,1},{2,258},{258,2},{3,259},{259,3},{4... | collective-permute-start | bytes 196616 | tf_op jit(solution)/shard_map/ppermute | solution.py:21
  7.8 60.7 %all-to-all-start = ((bf16[16,2,128,256]{3,2,1,0:T(8,128)(2,1)}), bf16[16,2,128,256]{3,2,1,0:T(8,128)(2,1)S(1)}, u32[]{:S(2)}, u32[]{:S(2)}) async-start(bf16[16,2,128,256]{3,2,1,0:T(8,128)(2,1)} %bitcast.26), calls=%async_computation | async-start | bytes 4194304 | tf_op jit(solution)/shard_map/all_to_all | solution.py:212
  20.2 48.2 %copy-start = (s32[2]{0:T(128)S(1)}, s32[2]{0:T(128)}, u32[]{:S(2)}) copy-start(s32[2]{0:T(128)} %lengths.1) | copy-start | bytes 28
  20.7 12.8 %collective-permute-start.1 = (bf16[2,2,32,512]{3,2,1,0:T(8,128)(2,1)S(1)}, bf16[2,2,32,512]{3,2,1,0:T(8,128)(2,1)S(1)}, u32[]{:S(2)}, u32[]{:S(2)}) collective-permute-start(bf16[2,2,32,512]{3,2,1,0:T(8,128)(2,1)S(1)} %arrange_bases.1), channel_id=1, source_target_pairs={{0,128},{32,160},{64,192},{96,224},{128,0},{160,32},{192,64},{224,... | collective-permute-start | bytes 393224 | tf_op jit(solution)/shard_map/ppermute | solution.py:199
  33.6 12.6 %collective-permute-start.2 = (bf16[2,2,2,32,512]{4,3,2,1,0:T(8,128)(2,1)S(1)}, bf16[2,2,2,32,512]{4,3,2,1,0:T(8,128)(2,1)S(1)}, u32[]{:S(2)}, u32[]{:S(2)}) collective-permute-start(bf16[2,2,2,32,512]{4,3,2,1,0:T(8,128)(2,1)S(1)} %get-tuple-element.16), channel_id=1, source_target_pairs={{0,64},{32,96},{64,0},{96,32},{128,192},{160,224},{192,128},{224,1... | collective-permute-start | bytes 786440 | tf_op jit(solution)/shard_map/ppermute | solution.py:199
  46.2 14.6 %collective-permute-start.3 = (bf16[2,2,2,2,32,512]{5,4,3,2,1,0:T(8,128)(2,1)S(1)}, bf16[2,2,2,2,32,512]{5,4,3,2,1,0:T(8,128)(2,1)S(1)}, u32[]{:S(2)}, u32[]{:S(2)}) collective-permute-start(bf16[2,2,2,2,32,512]{5,4,3,2,1,0:T(8,128)(2,1)S(1)} %pad_maximum_fusion.low), channel_id=1, source_target_pairs={{0,32},{32,0},{64,96},{96,64},{128,160},{160,128},{192,224},{224,1... | collective-permute-start | bytes 1572872 | tf_op jit(solution)/shard_map/ppermute | solution.py:199
  49.7 13.2 %collective-permute-start.4 = (bf16[2,2,2,2,32,512]{5,4,3,2,1,0:T(8,128)(2,1)S(1)}, bf16[2,2,2,2,32,512]{5,4,3,2,1,0:T(8,128)(2,1)}, u32[]{:S(2)}, u32[]{:S(2)}) collective-permute-start(bf16[2,2,2,2,32,512]{5,4,3,2,1,0:T(8,128)(2,1)S(1)} %pad_maximum_fusion.low), channel_id=1, source_target_pairs={{0,4},{4,0},{1,5},{5,1},{2,6},{6,2},{3,7},{7,3},{8,12},{12,8},{9,1... | collective-permute-start | bytes 1572872 | tf_op jit(solution)/shard_map/ppermute | solution.py:21
  60.9 3.9 %collective-permute-start.5 = (bf16[2,2,2,2,32,512]{5,4,3,2,1,0:T(8,128)(2,1)S(1)}, bf16[2,2,2,2,32,512]{5,4,3,2,1,0:T(8,128)(2,1)}, u32[]{:S(2)}, u32[]{:S(2)}) collective-permute-start(bf16[2,2,2,2,32,512]{5,4,3,2,1,0:T(8,128)(2,1)S(1)} %collective-permute-done.3.high), channel_id=1, source_target_pairs={{0,4},{4,0},{1,5},{5,1},{2,6},{6,2},{3,7},{7,3},{8,12},{12,8},{9,1... | collective-permute-start | bytes 1572872 | tf_op jit(solution)/shard_map/ppermute | solution.py:21
  93.1 23.8 %all-to-all-start.2 = ((bf16[8,2,256,128]{3,2,1,0:T(8,128)(2,1)}), bf16[8,2,256,128]{3,2,1,0:T(8,128)(2,1)S(1)}, u32[]{:S(2)}, u32[]{:S(2)}) async-start(bf16[8,2,256,128]{3,2,1,0:T(8,128)(2,1)} %broadcast_in_dim.2), calls=%async_computation.2 | async-start | bytes 2097152 | tf_op jit(solution)/shard_map/all_to_all | solution.py:226
  118.1 16.6 %all-to-all-start.3 = ((bf16[16,16,512]{2,1,0:T(8,128)(2,1)}), bf16[16,16,512]{2,1,0:T(8,128)(2,1)S(1)}, u32[]{:S(2)}, u32[]{:S(2)}) async-start(bf16[16,16,512]{2,1,0:T(8,128)(2,1)} %bitcast.16), calls=%async_computation.3 | async-start | bytes 524288 | tf_op jit(solution)/shard_map/all_to_all | solution.py:231

commit v16 on v15

--- a/solution.py
+++ b/solution.py
@@ -62,7 +62,7 @@
     ]
     for copy in copies:
         copy.start()
-    n_x, n_zh, _, toks, width = tokens.shape
+    n_zh, n_x, _, toks, width = tokens.shape
     run = width // y_lo
     sent = []
     for which in range(2):
@@ -75,7 +75,7 @@
             for zh in range(n_zh):
                 sent.append(
                     pltpu.make_async_copy(
-                        moved.at[which, x], tokens.at[x, zh, which], out_sems.at[which, x, zh]
+                        moved.at[which, x], tokens.at[zh, x, which], out_sems.at[which, x, zh]
                     )
                 )
                 sent[-1].start()
@@ -87,7 +87,7 @@
     toks, feats = act.shape
     return pl.pallas_call(
         lambda *refs: tokens_kernel(y_lo, *refs),
-        out_shape=jax.ShapeDtypeStruct((n_x, n_zh, 2, toks, feats // n_x), BF16),
+        out_shape=jax.ShapeDtypeStruct((n_zh, n_x, 2, toks, feats // n_x), BF16),
         in_specs=[pl.BlockSpec(memory_space=pl.ANY)] * 2,
         out_specs=pl.BlockSpec(memory_space=pl.ANY),
         scratch_shapes=[
@@ -105,7 +105,7 @@
 
 
 def rotate_kernel(place, lengths, tokens, low, high, core_low, core_high, out, whole):
-    n_x, n_zh, _, toks, width = tokens.shape
+    n_zh, n_x, _, toks, width = tokens.shape
     rows, cols = low.shape[4], low.shape[5]
     group, part = n_x * toks, cols // n_x
     zl, y, c = place[0], place[1], place[2]
@@ -122,7 +122,7 @@
                             whole[which, owner, pl.ds(at, rows)] = ref[two, four, far, which]
         total = None
         for owner in range(n_zh):
-            left = tokens[:, owner, which].reshape(group, width)
+            left = tokens[owner, :, which].reshape(group, width)
             product = jnp.dot(left, whole[which, owner], preferred_element_type=F32)
             total = product if total is None else total + product
         sums.append(total)
@@ -136,15 +136,15 @@
     half = group // 2
     for x in range(n_x):
         for core in range(2):
-            piece = 2 * x + core
-            out[piece, pl.ds(0, half)] = act[core * half : (core + 1) * half, x * part : (x + 1) * part]
+            piece, to = 2 * x + core, core * n_x + x
+            out[to, pl.ds(0, half)] = act[core * half : (core + 1) * half, x * part : (x + 1) * part]
             value = grad[:, piece * part // 2 : (piece + 1) * part // 2]
-            out[piece, pl.ds(half, half)] = jnp.concatenate([value[:half], value[half:]], axis=1)
-            out[piece, pl.ds(group, TILE)] = jnp.broadcast_to(level, (TILE, part))
+            out[to, pl.ds(half, half)] = jnp.concatenate([value[:half], value[half:]], axis=1)
+            out[to, pl.ds(group, TILE)] = jnp.broadcast_to(level, (TILE, part))
 
 
 def rotate(place, lengths, *arrays):
-    n_x, n_zh, _, toks, width = arrays[0].shape
+    n_zh, n_x, _, toks, width = arrays[0].shape
     cols = arrays[1].shape[5]
     return pl.pallas_call(
         rotate_kernel,
@@ -162,24 +162,28 @@
 
 def share_kernel(grad, act, out):
     n_k, n_c, depth, part = grad.shape
-    n_x, half = act.shape[0], part // 2
+    n_x, half = act.shape[1], part // 2
     total = None
     for core in range(n_c):
         turned = [grad[k, core].T for k in range(n_k)]
         for side in range(2):
             left = jnp.concatenate([t[side * half : (side + 1) * half] for t in turned], axis=0)
-            right = jnp.concatenate([act[x, side, core] for x in range(n_x)], axis=1)
+            right = jnp.concatenate([act[side, x, core] for x in range(n_x)], axis=1)
             product = jnp.dot(left, right, preferred_element_type=F32)
             total = product if total is None else total + product
-    out[...] = total.astype(BF16)
-
-
-def share_of(grad, act):
+    rows = out.shape[2]
+    for z in range(2):
+        for y in range(out.shape[0]):
+            at = (z * out.shape[0] + y) * rows
+            out[y, z] = total[at : at + rows].astype(BF16)
+
+
+def share_of(n_y, grad, act):
     n_k, n_c, depth, part = grad.shape
-    rows, cols = n_k * part // 2, act.shape[0] * part
+    rows, cols = n_k * part // 2, act.shape[1] * part
     return pl.pallas_call(
         share_kernel,
-        out_shape=jax.ShapeDtypeStruct((rows, cols), BF16),
+        out_shape=jax.ShapeDtypeStruct((n_y, 2, rows // n_y // 2, cols), BF16),
         in_specs=[VMEM, VMEM],
         out_specs=VMEM,
         compiler_params=pltpu.CompilerParams(vmem_limit_bytes=16 * 2**20),
@@ -210,27 +214,27 @@
     core_low, core_high = shift(low, "c", 1), shift(high, "c", 1)
 
     tokens = lax.all_to_all(
-        tokens.reshape(n_x * n_zh, *tokens.shape[2:]), ("x", "zh"), 0, 0, tiled=True
+        tokens.reshape(n_x * n_zh, *tokens.shape[2:]), ("zh", "x"), 0, 0, tiled=True
     ).reshape(tokens.shape)
 
     place = jnp.stack([zl, y, c]).astype(jnp.int32)
     arrays = (lengths, tokens, low, high, core_low, core_high)
     partial = rotate(place, *arrays).astype(F16)
-    partial = lax.all_to_all(partial, ("x", "c"), 0, 0, tiled=True)
+    partial = lax.all_to_all(partial, ("c", "x"), 0, 0, tiled=True)
     factors = jnp.exp2(partial[:, None, -TILE:].astype(F32) - F32(TOP))
     partial = partial[:, :-TILE].reshape(n_x * n_c, -1, TILE, partial.shape[2]).astype(F32)
-    partial = (partial * factors).reshape(n_x, n_c, *partial.shape[1:])
-    rotated = jnp.sum(partial, axis=0).astype(BF16).reshape(n_c, group, -1)
+    partial = (partial * factors).reshape(n_c, n_x, *partial.shape[1:])
+    rotated = jnp.sum(partial, axis=1).astype(BF16).reshape(n_c, group, -1)
     rot_act, rot_grad = rotated[:, : group // 2], rotated[:, group // 2 :]
 
     wide_act = lax.all_to_all(
-        jnp.broadcast_to(rot_act[None], (n_x * n_c, *rot_act.shape)), ("x", "c"), 0, 0, tiled=True
-    ).reshape(n_x, n_c, *rot_act.shape)
+        jnp.broadcast_to(rot_act[None], (n_c * n_x, *rot_act.shape)), ("c", "x"), 0, 0, tiled=True
+    ).reshape(n_c, n_x, *rot_act.shape)
     wide_grad = lax.all_gather(rot_grad, "zh", axis=0)
-    share = share_of(wide_grad, wide_act).reshape(n_zl * n_y, -1, cols)
-    received = lax.all_to_all(share, ("zl", "y"), 0, 0, tiled=True)
-    received = received.astype(F32).reshape(SEQS, n_y, -1, cols)
-    per_seq = jnp.sum(received, axis=1)
+    share = share_of(n_y, wide_grad, wide_act).reshape(n_y * n_zl, -1, cols)
+    received = lax.all_to_all(share, ("y", "zl"), 0, 0, tiled=True)
+    received = received.astype(F32).reshape(n_y, SEQS, -1, cols)
+    per_seq = jnp.sum(received, axis=0)
     scale = lengths.astype(F32)[:, None, None]
     return jnp.sum(per_seq * per_seq / scale, axis=0) / F32(SEQS)
 

time: 136 us -> 138 us (1.015)
  the two profiles are of different devices: /device:TPU:10 before, /device:TPU:1 now
where the time goes in v16:
time: 138 us; the launch traced here: 137 us
  starting transfers between devices  52.6 us (38%)
  waiting for transfers between devices  37.5 us (27%)
  blocking collectives  35.7 us (26%)
  Pallas kernels  7.42 us (5%)
  other arithmetic  2.06 us (1%)
  local copies, waits for them, and re-layouts  1.41 us (1%)
    all_to_all x1, blocking collectives, on_device(): partial = lax.all_to_all(partial, ('c', 'x'), 0, 0, tiled=True)  21 us
    ppermute x3, waiting for transfers between devices, partner(): return lax.ppermute(value, 'y', [(i, i ^ step) for i in range(n_y)])  19.8 us
    ppermute x3, starting transfers between devices, partner(): return lax.ppermute(value, 'y', [(i, i ^ step) for i in range(n_y)])  17.4 us
    all_gather x1, blocking collectives, on_device(): wide_grad = lax.all_gather(rot_grad, 'zh', axis=0)  14.7 us
    ppermute x3, starting transfers between devices, shift(): return lax.ppermute(value, axis, [(i, (i + step) % n) for i in range(n)])  12.7 us
    all_to_all x1, starting transfers between devices, on_device(): lax.all_to_all(tokens.reshape(n_x * n_zh, *tokens.shape[2:]), ('zh', 'x')...  11.7 us
    all_to_all x1, waiting for transfers between devices, on_device(): received = lax.all_to_all(share, ('y', 'zl'), 0, 0, tiled=True)  10.8 us
    all_to_all x1, starting transfers between devices, on_device(): received = lax.all_to_all(share, ('y', 'zl'), 0, 0, tiled=True)  6.93 us
  transfers between devices with their start and end apart: 9, of which 7 were waited for; matrix products, arithmetic and copies ran while one was open for 0% of the time, Pallas kernels for 2%

profile of v16, /device:TPU:1, one launch (start us, length us, event | category | flops | bytes accessed | tf_op | source)
XLA Modules:
  0.0 136.8 jit_solution(6318663349817281261)
XLA Ops:
  0.0 0.8 pad_maximum_fusion.2.refs_0_
  0.8 4.8 %collective-permute-start = (bf16[2,32,512]{2,1,0:T(8,128)(2,1)S(1)}, bf16[2,32,512]{2,1,0:T(8,128)(2,1)S(1)}, u32[]{:S(2)}, u32[]{:S(2)}) collective-permute-start(bf16[2,32,512]{2,1,0:T(8,128)(2,1)S(1)} %pad_maximum_fusion.2.refs_0_), channel_id=1, source_target_pairs={{0,256},{256,0},{1,257},{257,1},{2,258},{258,2},{3,259},{259,3},{4... | collective-permute-start | bytes 196616 | tf_op jit(solution)/shard_map/ppermute | solution.py:21
  5.6 2.7 %arrange_tokens.1 = bf16[4,4,2,128,256]{4,3,2,1,0:T(8,128)(2,1)} custom-call(bf16[128,1024]{1,0:T(8,128)(2,1)} %refs_0_, bf16[128,1024]{1,0:T(8,128)(2,1)} %refs_1_.1), custom_call_target="tpu_custom_call" | custom-call | flops 131072 | bytes 1048576 | tf_op jit(solution)/shard_map/arrange_tokens/pallas_call | solution.py:88
  8.3 11.7 %all-to-all-start = ((bf16[16,2,128,256]{3,2,1,0:T(8,128)(2,1)}), bf16[16,2,128,256]{3,2,1,0:T(8,128)(2,1)S(1)}, u32[]{:S(2)}, u32[]{:S(2)}) async-start(bf16[16,2,128,256]{3,2,1,0:T(8,128)(2,1)} %bitcast.25), calls=%async_computation | async-start | bytes 4194304 | tf_op jit(solution)/shard_map/all_to_all | solution.py:216
  20.0 0.0 copy-start
  20.0 0.5 arrange_bases.1
  20.5 7.5 %collective-permute-start.1 = (bf16[2,2,32,512]{3,2,1,0:T(8,128)(2,1)S(1)}, bf16[2,2,32,512]{3,2,1,0:T(8,128)(2,1)S(1)}, u32[]{:S(2)}, u32[]{:S(2)}) collective-permute-start(bf16[2,2,32,512]{3,2,1,0:T(8,128)(2,1)S(1)} %arrange_bases.1), channel_id=1, source_target_pairs={{0,128},{32,160},{64,192},{96,224},{128,0},{160,32},{192,64},{224,... | collective-permute-start | bytes 393224 | tf_op jit(solution)/shard_map/ppermute | solution.py:203
  27.9 2.6 %collective-permute-done.1 = bf16[2,2,32,512]{3,2,1,0:T(8,128)(2,1)S(1)} collective-permute-done((bf16[2,2,32,512]{3,2,1,0:T(8,128)(2,1)S(1)}, bf16[2,2,32,512]{3,2,1,0:T(8,128)(2,1)S(1)}, u32[]{:S(2)}, u32[]{:S(2)}) %collective-permute-start.1) | collective-permute-done | bytes 131104 | tf_op jit(solution)/shard_map/ppermute | solution.py:203
  30.6 8.0 %collective-permute-start.2 = (bf16[2,2,2,32,512]{4,3,2,1,0:T(8,128)(2,1)S(1)}, bf16[2,2,2,32,512]{4,3,2,1,0:T(8,128)(2,1)S(1)}, u32[]{:S(2)}, u32[]{:S(2)}) collective-permute-start(bf16[2,2,2,32,512]{4,3,2,1,0:T(8,128)(2,1)S(1)} %get-tuple-element.16), channel_id=1, source_target_pairs={{0,64},{32,96},{64,0},{96,32},{128,192},{160,224},{192,128},{224,1... | collective-permute-start | bytes 786440 | tf_op jit(solution)/shard_map/ppermute | solution.py:203
  38.7 8.8 %collective-permute-done.2 = bf16[2,2,2,32,512]{4,3,2,1,0:T(8,128)(2,1)S(1)} collective-permute-done((bf16[2,2,2,32,512]{4,3,2,1,0:T(8,128)(2,1)S(1)}, bf16[2,2,2,32,512]{4,3,2,1,0:T(8,128)(2,1)S(1)}, u32[]{:S(2)}, u32[]{:S(2)}) %collective-permute-start.2) | collective-permute-done | bytes 262176 | tf_op jit(solution)/shard_map/ppermute | solution.py:203
  47.5 0.1 pad_maximum_fusion.low
  47.5 1.9 %collective-permute-start.3 = (bf16[2,2,2,2,32,512]{5,4,3,2,1,0:T(8,128)(2,1)S(1)}, bf16[2,2,2,2,32,512]{5,4,3,2,1,0:T(8,128)(2,1)S(1)}, u32[]{:S(2)}, u32[]{:S(2)}) collective-permute-start(bf16[2,2,2,2,32,512]{5,4,3,2,1,0:T(8,128)(2,1)S(1)} %pad_maximum_fusion.low), channel_id=1, source_target_pairs={{0,32},{32,0},{64,96},{96,64},{128,160},{160,128},{192,224},{224,1... | collective-permute-start | bytes 1572872 | tf_op jit(solution)/shard_map/ppermute | solution.py:203
  49.5 3.8 %collective-permute-start.4 = (bf16[2,2,2,2,32,512]{5,4,3,2,1,0:T(8,128)(2,1)S(1)}, bf16[2,2,2,2,32,512]{5,4,3,2,1,0:T(8,128)(2,1)}, u32[]{:S(2)}, u32[]{:S(2)}) collective-permute-start(bf16[2,2,2,2,32,512]{5,4,3,2,1,0:T(8,128)(2,1)S(1)} %pad_maximum_fusion.low), channel_id=1, source_target_pairs={{0,4},{4,0},{1,5},{5,1},{2,6},{6,2},{3,7},{7,3},{8,12},{12,8},{9,1... | collective-permute-start | bytes 1572872 | tf_op jit(solution)/shard_map/ppermute | solution.py:21
  53.3 8.3 %collective-permute-done.3.high = bf16[2,2,2,2,32,512]{5,4,3,2,1,0:T(8,128)(2,1)S(1)} collective-permute-done((bf16[2,2,2,2,32,512]{5,4,3,2,1,0:T(8,128)(2,1)S(1)}, bf16[2,2,2,2,32,512]{5,4,3,2,1,0:T(8,128)(2,1)S(1)}, u32[]{:S(2)}, u32[]{:S(2)}) %collective-permute-start.3) | collective-permute-done | bytes 524320 | tf_op jit(solution)/shard_map/ppermute | solution.py:203
  61.6 4.0 %collective-permute-start.5 = (bf16[2,2,2,2,32,512]{5,4,3,2,1,0:T(8,128)(2,1)S(1)}, bf16[2,2,2,2,32,512]{5,4,3,2,1,0:T(8,128)(2,1)}, u32[]{:S(2)}, u32[]{:S(2)}) collective-permute-start(bf16[2,2,2,2,32,512]{5,4,3,2,1,0:T(8,128)(2,1)S(1)} %collective-permute-done.3.high), channel_id=1, source_target_pairs={{0,4},{4,0},{1,5},{5,1},{2,6},{6,2},{3,7},{7,3},{8,12},{12,8},{9,1... | collective-permute-start | bytes 1572872 | tf_op jit(solution)/shard_map/ppermute | solution.py:21
  65.7 0.1 pad_add_fusion.place
  65.8 1.6 %collective-permute-done.5.core_high = bf16[2,2,2,2,32,512]{5,4,3,2,1,0:T(8,128)(2,1)} collective-permute-done((bf16[2,2,2,2,32,512]{5,4,3,2,1,0:T(8,128)(2,1)S(1)}, bf16[2,2,2,2,32,512]{5,4,3,2,1,0:T(8,128)(2,1)}, u32[]{:S(2)}, u32[]{:S(2)}) %collective-permute-start.5) | collective-permute-done | bytes 524320 | tf_op jit(solution)/shard_map/ppermute | solution.py:21
  67.3 4.8 %all-to-all-done = bf16[16,2,128,256]{3,2,1,0:T(8,128)(2,1)S(1)} async-done(((bf16[16,2,128,256]{3,2,1,0:T(8,128)(2,1)}), bf16[16,2,128,256]{3,2,1,0:T(8,128)(2,1)S(1)}, u32[]{:S(2)}, u32[]{:S(2)}) %all-to-all-start) | async-done | bytes 2097184 | tf_op jit(solution)/shard_map/all_to_all | solution.py:216
  72.1 3.1 %rotate.1 = f32[8,528,128]{2,1,0:T(8,128)S(1)} custom-call(s32[3]{0:T(128)S(1)} %pad_add_fusion.place, s32[2]{0:T(128)S(1)} %copy-done, bf16[4,4,2,128,256]{4,3,2,1,0:T(8,128)(2,1)S(1)} %bitcast.21, bf16[2,2,2,2,32,512]{5,4,3,2,1,0:T(8,128)(2,1)S(1)} %pad_maximum_fusion.low, bf16[2,2,2,2,32,512]{5,4,3,2,1,0:T(8,128)(2,1)S(1)} %collective-permute-done.3.high, ...), custom_call_target="tpu_custom_call" | custom-call | flops 1073741824 | bytes 8388608 | tf_op jit(solution)/shard_map/rotate/pallas_call | solution.py:149
  75.2 0.1 convert_element_type.25
  75.4 21.0 %all_to_all.20 = f16[8,528,128]{2,1,0:T(8,128)(2,1)S(1)} all-to-all(f16[8,528,128]{2,1,0:T(8,128)(2,1)S(1)} %convert_element_type.25), channel_id=1, replica_groups=mesh['zl'=2,'y'=8,'x'=4,'c'=2,'zh'=4] {'c','x'}, dimensions={0} | all-to-all | bytes 2162688 | tf_op jit(solution)/shard_map/all_to_all | solution.py:223
  96.3 0.2 slice.16
  96.6 0.2 fusion
  96.8 1.2 broadcast_in_dim.2
  98.0 3.9 %all-to-all-start.2 = ((bf16[8,2,256,128]{3,2,1,0:T(8,128)(2,1)}), bf16[8,2,256,128]{3,2,1,0:T(8,128)(2,1)S(1)}, u32[]{:S(2)}, u32[]{:S(2)}) async-start(bf16[8,2,256,128]{3,2,1,0:T(8,128)(2,1)} %broadcast_in_dim.2), calls=%async_computation.2 | async-start | bytes 2097152 | tf_op jit(solution)/shard_map/all_to_all | solution.py:230
  101.9 14.7 %all-gather = bf16[8,256,128]{2,1,0:T(8,128)(2,1)S(1)} all-gather(bf16[2,256,128]{2,1,0:T(8,128)(2,1)S(1)} %get-tuple-element.14), channel_id=2, replica_groups=mesh['zl'=2,'y'=8,'x'=4,'c'=2,'zh'=4] {'zh'}, dimensions={0}, use_global_device_ids=true | all-gather | bytes 655360 | tf_op jit(solution)/shard_map/all_gather | solution.py:233
  116.6 0.6 all-to-all-done.2
  117.2 1.2 share.1
  118.3 6.9 %all-to-all-start.3 = ((bf16[16,16,512]{2,1,0:T(8,128)(2,1)}), bf16[16,16,512]{2,1,0:T(8,128)(2,1)S(1)}, u32[]{:S(2)}, u32[]{:S(2)}) async-start(bf16[16,16,512]{2,1,0:T(8,128)(2,1)} %bitcast.16), calls=%async_computation.3 | async-start | bytes 524288 | tf_op jit(solution)/shard_map/all_to_all | solution.py:235
  125.3 10.8 %all-to-all-done.3 = bf16[16,16,512]{2,1,0:T(8,128)(2,1)S(1)} async-done(((bf16[16,16,512]{2,1,0:T(8,128)(2,1)}), bf16[16,16,512]{2,1,0:T(8,128)(2,1)S(1)}, u32[]{:S(2)}, u32[]{:S(2)}) %all-to-all-start.3) | async-done | bytes 262176 | tf_op jit(solution)/shard_map/all_to_all | solution.py:235
  136.1 0.1 divide_reduce_fusion
  136.2 0.6 broadcast_multiply_fusion
  (8 shorter events, 0.1 us)
Async XLA Ops:
  0.8 7.5 %collective-permute-start = (bf16[2,32,512]{2,1,0:T(8,128)(2,1)S(1)}, bf16[2,32,512]{2,1,0:T(8,128)(2,1)S(1)}, u32[]{:S(2)}, u32[]{:S(2)}) collective-permute-start(bf16[2,32,512]{2,1,0:T(8,128)(2,1)S(1)} %pad_maximum_fusion.2.refs_0_), channel_id=1, source_target_pairs={{0,256},{256,0},{1,257},{257,1},{2,258},{258,2},{3,259},{259,3},{4... | collective-permute-start | bytes 196616 | tf_op jit(solution)/shard_map/ppermute | solution.py:21
  8.3 63.8 %all-to-all-start = ((bf16[16,2,128,256]{3,2,1,0:T(8,128)(2,1)}), bf16[16,2,128,256]{3,2,1,0:T(8,128)(2,1)S(1)}, u32[]{:S(2)}, u32[]{:S(2)}) async-start(bf16[16,2,128,256]{3,2,1,0:T(8,128)(2,1)} %bitcast.25), calls=%async_computation | async-start | bytes 4194304 | tf_op jit(solution)/shard_map/all_to_all | solution.py:216
  20.0 52.1 %copy-start = (s32[2]{0:T(128)S(1)}, s32[2]{0:T(128)}, u32[]{:S(2)}) copy-start(s32[2]{0:T(128)} %lengths.1) | copy-start | bytes 28
  20.5 10.1 %collective-permute-start.1 = (bf16[2,2,32,512]{3,2,1,0:T(8,128)(2,1)S(1)}, bf16[2,2,32,512]{3,2,1,0:T(8,128)(2,1)S(1)}, u32[]{:S(2)}, u32[]{:S(2)}) collective-permute-start(bf16[2,2,32,512]{3,2,1,0:T(8,128)(2,1)S(1)} %arrange_bases.1), channel_id=1, source_target_pairs={{0,128},{32,160},{64,192},{96,224},{128,0},{160,32},{192,64},{224,... | collective-permute-start | bytes 393224 | tf_op jit(solution)/shard_map/ppermute | solution.py:203
  30.6 16.9 %collective-permute-start.2 = (bf16[2,2,2,32,512]{4,3,2,1,0:T(8,128)(2,1)S(1)}, bf16[2,2,2,32,512]{4,3,2,1,0:T(8,128)(2,1)S(1)}, u32[]{:S(2)}, u32[]{:S(2)}) collective-permute-start(bf16[2,2,2,32,512]{4,3,2,1,0:T(8,128)(2,1)S(1)} %get-tuple-element.16), channel_id=1, source_target_pairs={{0,64},{32,96},{64,0},{96,32},{128,192},{160,224},{192,128},{224,1... | collective-permute-start | bytes 786440 | tf_op jit(solution)/shard_map/ppermute | solution.py:203
  47.5 14.1 %collective-permute-start.3 = (bf16[2,2,2,2,32,512]{5,4,3,2,1,0:T(8,128)(2,1)S(1)}, bf16[2,2,2,2,32,512]{5,4,3,2,1,0:T(8,128)(2,1)S(1)}, u32[]{:S(2)}, u32[]{:S(2)}) collective-permute-start(bf16[2,2,2,2,32,512]{5,4,3,2,1,0:T(8,128)(2,1)S(1)} %pad_maximum_fusion.low), channel_id=1, source_target_pairs={{0,32},{32,0},{64,96},{96,64},{128,160},{160,128},{192,224},{224,1... | collective-permute-start | bytes 1572872 | tf_op jit(solution)/shard_map/ppermute | solution.py:203
  49.5 16.3 %collective-permute-start.4 = (bf16[2,2,2,2,32,512]{5,4,3,2,1,0:T(8,128)(2,1)S(1)}, bf16[2,2,2,2,32,512]{5,4,3,2,1,0:T(8,128)(2,1)}, u32[]{:S(2)}, u32[]{:S(2)}) collective-permute-start(bf16[2,2,2,2,32,512]{5,4,3,2,1,0:T(8,128)(2,1)S(1)} %pad_maximum_fusion.low), channel_id=1, source_target_pairs={{0,4},{4,0},{1,5},{5,1},{2,6},{6,2},{3,7},{7,3},{8,12},{12,8},{9,1... | collective-permute-start | bytes 1572872 | tf_op jit(solution)/shard_map/ppermute | solution.py:21
  61.6 5.7 %collective-permute-start.5 = (bf16[2,2,2,2,32,512]{5,4,3,2,1,0:T(8,128)(2,1)S(1)}, bf16[2,2,2,2,32,512]{5,4,3,2,1,0:T(8,128)(2,1)}, u32[]{:S(2)}, u32[]{:S(2)}) collective-permute-start(bf16[2,2,2,2,32,512]{5,4,3,2,1,0:T(8,128)(2,1)S(1)} %collective-permute-done.3.high), channel_id=1, source_target_pairs={{0,4},{4,0},{1,5},{5,1},{2,6},{6,2},{3,7},{7,3},{8,12},{12,8},{9,1... | collective-permute-start | bytes 1572872 | tf_op jit(solution)/shard_map/ppermute | solution.py:21
  98.0 19.2 %all-to-all-start.2 = ((bf16[8,2,256,128]{3,2,1,0:T(8,128)(2,1)}), bf16[8,2,256,128]{3,2,1,0:T(8,128)(2,1)S(1)}, u32[]{:S(2)}, u32[]{:S(2)}) async-start(bf16[8,2,256,128]{3,2,1,0:T(8,128)(2,1)} %broadcast_in_dim.2), calls=%async_computation.2 | async-start | bytes 2097152 | tf_op jit(solution)/shard_map/all_to_all | solution.py:230
  118.3 17.7 %all-to-all-start.3 = ((bf16[16,16,512]{2,1,0:T(8,128)(2,1)}), bf16[16,16,512]{2,1,0:T(8,128)(2,1)S(1)}, u32[]{:S(2)}, u32[]{:S(2)}) async-start(bf16[16,16,512]{2,1,0:T(8,128)(2,1)} %bitcast.16), calls=%async_computation.3 | async-start | bytes 524288 | tf_op jit(solution)/shard_map/all_to_all | solution.py:235

commit v17 on v16

--- a/solution.py
+++ b/solution.py
@@ -171,19 +171,15 @@
             right = jnp.concatenate([act[side, x, core] for x in range(n_x)], axis=1)
             product = jnp.dot(left, right, preferred_element_type=F32)
             total = product if total is None else total + product
-    rows = out.shape[2]
-    for z in range(2):
-        for y in range(out.shape[0]):
-            at = (z * out.shape[0] + y) * rows
-            out[y, z] = total[at : at + rows].astype(BF16)
-
-
-def share_of(n_y, grad, act):
+    out[...] = total.astype(BF16)
+
+
+def share_of(grad, act):
     n_k, n_c, depth, part = grad.shape
     rows, cols = n_k * part // 2, act.shape[1] * part
     return pl.pallas_call(
         share_kernel,
-        out_shape=jax.ShapeDtypeStruct((n_y, 2, rows // n_y // 2, cols), BF16),
+        out_shape=jax.ShapeDtypeStruct((rows, cols), BF16),
         in_specs=[VMEM, VMEM],
         out_specs=VMEM,
         compiler_params=pltpu.CompilerParams(vmem_limit_bytes=16 * 2**20),
@@ -231,10 +227,10 @@
         jnp.broadcast_to(rot_act[None], (n_c * n_x, *rot_act.shape)), ("c", "x"), 0, 0, tiled=True
     ).reshape(n_c, n_x, *rot_act.shape)
     wide_grad = lax.all_gather(rot_grad, "zh", axis=0)
-    share = share_of(n_y, wide_grad, wide_act).reshape(n_y * n_zl, -1, cols)
-    received = lax.all_to_all(share, ("y", "zl"), 0, 0, tiled=True)
-    received = received.astype(F32).reshape(n_y, SEQS, -1, cols)
-    per_seq = jnp.sum(received, axis=0)
+    share = share_of(wide_grad, wide_act).reshape(n_zl * n_y, -1, cols)
+    received = lax.all_to_all(share, ("zl", "y"), 0, 0, tiled=True)
+    received = received.astype(F32).reshape(SEQS, n_y, -1, cols)
+    per_seq = jnp.sum(received, axis=1)
     scale = lengths.astype(F32)[:, None, None]
     return jnp.sum(per_seq * per_seq / scale, axis=0) / F32(SEQS)
 

time: 138 us -> 136 us (0.986)
  waiting for transfers between devices: 37.5 us -> 35.5 us
    all_to_all x1, waiting for transfers between devices: 10.8 us -> 8.78 us  [on_device(): received = lax.all_to_all(share, ('zl', 'y'), 0, 0, tiled=True)]
where the time goes in v17:
time: 136 us; the launch traced here: 135 us
  starting transfers between devices  52.6 us (39%)
  blocking collectives  35.7 us (26%)
  waiting for transfers between devices  35.5 us (26%)
  Pallas kernels  7.42 us (5%)
  other arithmetic  2.06 us (2%)
  local copies, waits for them, and re-layouts  1.41 us (1%)
    all_to_all x1, blocking collectives, on_device(): partial = lax.all_to_all(partial, ('c', 'x'), 0, 0, tiled=True)  21 us
    ppermute x3, waiting for transfers between devices, partner(): return lax.ppermute(value, 'y', [(i, i ^ step) for i in range(n_y)])  19.8 us
    ppermute x3, starting transfers between devices, partner(): return lax.ppermute(value, 'y', [(i, i ^ step) for i in range(n_y)])  17.4 us
    all_gather x1, blocking collectives, on_device(): wide_grad = lax.all_gather(rot_grad, 'zh', axis=0)  14.7 us
    ppermute x3, starting transfers between devices, shift(): return lax.ppermute(value, axis, [(i, (i + step) % n) for i in range(n)])  12.7 us
    all_to_all x1, starting transfers between devices, on_device(): lax.all_to_all(tokens.reshape(n_x * n_zh, *tokens.shape[2:]), ('zh', 'x')...  11.7 us
    all_to_all x1, waiting for transfers between devices, on_device(): received = lax.all_to_all(share, ('zl', 'y'), 0, 0, tiled=True)  8.78 us
    all_to_all x1, starting transfers between devices, on_device(): received = lax.all_to_all(share, ('zl', 'y'), 0, 0, tiled=True)  6.93 us
  transfers between devices with their start and end apart: 9, of which 7 were waited for; matrix products, arithmetic and copies ran while one was open for 0% of the time, Pallas kernels for 2%

profile of v17, /device:TPU:1, one launch (start us, length us, event | category | flops | bytes accessed | tf_op | source)
XLA Modules:
  0.0 134.8 jit_solution(3987242813500765842)
XLA Ops:
  0.0 0.8 pad_maximum_fusion.2.refs_0_
  0.8 4.8 %collective-permute-start = (bf16[2,32,512]{2,1,0:T(8,128)(2,1)S(1)}, bf16[2,32,512]{2,1,0:T(8,128)(2,1)S(1)}, u32[]{:S(2)}, u32[]{:S(2)}) collective-permute-start(bf16[2,32,512]{2,1,0:T(8,128)(2,1)S(1)} %pad_maximum_fusion.2.refs_0_), channel_id=1, source_target_pairs={{0,256},{256,0},{1,257},{257,1},{2,258},{258,2},{3,259},{259,3},{4... | collective-permute-start | bytes 196616 | tf_op jit(solution)/shard_map/ppermute | solution.py:21
  5.6 2.7 %arrange_tokens.1 = bf16[4,4,2,128,256]{4,3,2,1,0:T(8,128)(2,1)} custom-call(bf16[128,1024]{1,0:T(8,128)(2,1)} %refs_0_, bf16[128,1024]{1,0:T(8,128)(2,1)} %refs_1_.1), custom_call_target="tpu_custom_call" | custom-call | flops 131072 | bytes 1048576 | tf_op jit(solution)/shard_map/arrange_tokens/pallas_call | solution.py:88
  8.3 11.7 %all-to-all-start = ((bf16[16,2,128,256]{3,2,1,0:T(8,128)(2,1)}), bf16[16,2,128,256]{3,2,1,0:T(8,128)(2,1)S(1)}, u32[]{:S(2)}, u32[]{:S(2)}) async-start(bf16[16,2,128,256]{3,2,1,0:T(8,128)(2,1)} %bitcast.26), calls=%async_computation | async-start | bytes 4194304 | tf_op jit(solution)/shard_map/all_to_all | solution.py:212
  20.0 0.0 copy-start
  20.0 0.5 arrange_bases.1
  20.5 7.5 %collective-permute-start.1 = (bf16[2,2,32,512]{3,2,1,0:T(8,128)(2,1)S(1)}, bf16[2,2,32,512]{3,2,1,0:T(8,128)(2,1)S(1)}, u32[]{:S(2)}, u32[]{:S(2)}) collective-permute-start(bf16[2,2,32,512]{3,2,1,0:T(8,128)(2,1)S(1)} %arrange_bases.1), channel_id=1, source_target_pairs={{0,128},{32,160},{64,192},{96,224},{128,0},{160,32},{192,64},{224,... | collective-permute-start | bytes 393224 | tf_op jit(solution)/shard_map/ppermute | solution.py:199
  27.9 2.6 %collective-permute-done.1 = bf16[2,2,32,512]{3,2,1,0:T(8,128)(2,1)S(1)} collective-permute-done((bf16[2,2,32,512]{3,2,1,0:T(8,128)(2,1)S(1)}, bf16[2,2,32,512]{3,2,1,0:T(8,128)(2,1)S(1)}, u32[]{:S(2)}, u32[]{:S(2)}) %collective-permute-start.1) | collective-permute-done | bytes 131104 | tf_op jit(solution)/shard_map/ppermute | solution.py:199
  30.6 8.0 %collective-permute-start.2 = (bf16[2,2,2,32,512]{4,3,2,1,0:T(8,128)(2,1)S(1)}, bf16[2,2,2,32,512]{4,3,2,1,0:T(8,128)(2,1)S(1)}, u32[]{:S(2)}, u32[]{:S(2)}) collective-permute-start(bf16[2,2,2,32,512]{4,3,2,1,0:T(8,128)(2,1)S(1)} %get-tuple-element.16), channel_id=1, source_target_pairs={{0,64},{32,96},{64,0},{96,32},{128,192},{160,224},{192,128},{224,1... | collective-permute-start | bytes 786440 | tf_op jit(solution)/shard_map/ppermute | solution.py:199
  38.7 8.8 %collective-permute-done.2 = bf16[2,2,2,32,512]{4,3,2,1,0:T(8,128)(2,1)S(1)} collective-permute-done((bf16[2,2,2,32,512]{4,3,2,1,0:T(8,128)(2,1)S(1)}, bf16[2,2,2,32,512]{4,3,2,1,0:T(8,128)(2,1)S(1)}, u32[]{:S(2)}, u32[]{:S(2)}) %collective-permute-start.2) | collective-permute-done | bytes 262176 | tf_op jit(solution)/shard_map/ppermute | solution.py:199
  47.5 0.1 pad_maximum_fusion.low
  47.5 1.9 %collective-permute-start.3 = (bf16[2,2,2,2,32,512]{5,4,3,2,1,0:T(8,128)(2,1)S(1)}, bf16[2,2,2,2,32,512]{5,4,3,2,1,0:T(8,128)(2,1)S(1)}, u32[]{:S(2)}, u32[]{:S(2)}) collective-permute-start(bf16[2,2,2,2,32,512]{5,4,3,2,1,0:T(8,128)(2,1)S(1)} %pad_maximum_fusion.low), channel_id=1, source_target_pairs={{0,32},{32,0},{64,96},{96,64},{128,160},{160,128},{192,224},{224,1... | collective-permute-start | bytes 1572872 | tf_op jit(solution)/shard_map/ppermute | solution.py:199
  49.5 3.8 %collective-permute-start.4 = (bf16[2,2,2,2,32,512]{5,4,3,2,1,0:T(8,128)(2,1)S(1)}, bf16[2,2,2,2,32,512]{5,4,3,2,1,0:T(8,128)(2,1)}, u32[]{:S(2)}, u32[]{:S(2)}) collective-permute-start(bf16[2,2,2,2,32,512]{5,4,3,2,1,0:T(8,128)(2,1)S(1)} %pad_maximum_fusion.low), channel_id=1, source_target_pairs={{0,4},{4,0},{1,5},{5,1},{2,6},{6,2},{3,7},{7,3},{8,12},{12,8},{9,1... | collective-permute-start | bytes 1572872 | tf_op jit(solution)/shard_map/ppermute | solution.py:21
  53.3 8.3 %collective-permute-done.3.high = bf16[2,2,2,2,32,512]{5,4,3,2,1,0:T(8,128)(2,1)S(1)} collective-permute-done((bf16[2,2,2,2,32,512]{5,4,3,2,1,0:T(8,128)(2,1)S(1)}, bf16[2,2,2,2,32,512]{5,4,3,2,1,0:T(8,128)(2,1)S(1)}, u32[]{:S(2)}, u32[]{:S(2)}) %collective-permute-start.3) | collective-permute-done | bytes 524320 | tf_op jit(solution)/shard_map/ppermute | solution.py:199
  61.6 4.0 %collective-permute-start.5 = (bf16[2,2,2,2,32,512]{5,4,3,2,1,0:T(8,128)(2,1)S(1)}, bf16[2,2,2,2,32,512]{5,4,3,2,1,0:T(8,128)(2,1)}, u32[]{:S(2)}, u32[]{:S(2)}) collective-permute-start(bf16[2,2,2,2,32,512]{5,4,3,2,1,0:T(8,128)(2,1)S(1)} %collective-permute-done.3.high), channel_id=1, source_target_pairs={{0,4},{4,0},{1,5},{5,1},{2,6},{6,2},{3,7},{7,3},{8,12},{12,8},{9,1... | collective-permute-start | bytes 1572872 | tf_op jit(solution)/shard_map/ppermute | solution.py:21
  65.7 0.1 pad_add_fusion.place
  65.8 1.6 %collective-permute-done.5.core_high = bf16[2,2,2,2,32,512]{5,4,3,2,1,0:T(8,128)(2,1)} collective-permute-done((bf16[2,2,2,2,32,512]{5,4,3,2,1,0:T(8,128)(2,1)S(1)}, bf16[2,2,2,2,32,512]{5,4,3,2,1,0:T(8,128)(2,1)}, u32[]{:S(2)}, u32[]{:S(2)}) %collective-permute-start.5) | collective-permute-done | bytes 524320 | tf_op jit(solution)/shard_map/ppermute | solution.py:21
  67.3 4.8 %all-to-all-done = bf16[16,2,128,256]{3,2,1,0:T(8,128)(2,1)S(1)} async-done(((bf16[16,2,128,256]{3,2,1,0:T(8,128)(2,1)}), bf16[16,2,128,256]{3,2,1,0:T(8,128)(2,1)S(1)}, u32[]{:S(2)}, u32[]{:S(2)}) %all-to-all-start) | async-done | bytes 2097184 | tf_op jit(solution)/shard_map/all_to_all | solution.py:212
  72.1 3.1 %rotate.1 = f32[8,528,128]{2,1,0:T(8,128)S(1)} custom-call(s32[3]{0:T(128)S(1)} %pad_add_fusion.place, s32[2]{0:T(128)S(1)} %copy-done, bf16[4,4,2,128,256]{4,3,2,1,0:T(8,128)(2,1)S(1)} %bitcast.22, bf16[2,2,2,2,32,512]{5,4,3,2,1,0:T(8,128)(2,1)S(1)} %pad_maximum_fusion.low, bf16[2,2,2,2,32,512]{5,4,3,2,1,0:T(8,128)(2,1)S(1)} %collective-permute-done.3.high, ...), custom_call_target="tpu_custom_call" | custom-call | flops 1073741824 | bytes 8388608 | tf_op jit(solution)/shard_map/rotate/pallas_call | solution.py:149
  75.2 0.1 convert_element_type.25
  75.4 21.0 %all_to_all.20 = f16[8,528,128]{2,1,0:T(8,128)(2,1)S(1)} all-to-all(f16[8,528,128]{2,1,0:T(8,128)(2,1)S(1)} %convert_element_type.25), channel_id=1, replica_groups=mesh['zl'=2,'y'=8,'x'=4,'c'=2,'zh'=4] {'c','x'}, dimensions={0} | all-to-all | bytes 2162688 | tf_op jit(solution)/shard_map/all_to_all | solution.py:219
  96.3 0.2 slice.16
  96.6 0.2 fusion
  96.8 1.2 broadcast_in_dim.2
  98.0 3.9 %all-to-all-start.2 = ((bf16[8,2,256,128]{3,2,1,0:T(8,128)(2,1)}), bf16[8,2,256,128]{3,2,1,0:T(8,128)(2,1)S(1)}, u32[]{:S(2)}, u32[]{:S(2)}) async-start(bf16[8,2,256,128]{3,2,1,0:T(8,128)(2,1)} %broadcast_in_dim.2), calls=%async_computation.2 | async-start | bytes 2097152 | tf_op jit(solution)/shard_map/all_to_all | solution.py:226
  101.9 14.7 %all-gather = bf16[8,256,128]{2,1,0:T(8,128)(2,1)S(1)} all-gather(bf16[2,256,128]{2,1,0:T(8,128)(2,1)S(1)} %get-tuple-element.14), channel_id=2, replica_groups=mesh['zl'=2,'y'=8,'x'=4,'c'=2,'zh'=4] {'zh'}, dimensions={0}, use_global_device_ids=true | all-gather | bytes 655360 | tf_op jit(solution)/shard_map/all_gather | solution.py:229
  116.6 0.6 all-to-all-done.2
  117.2 1.2 share.1
  118.3 6.9 %all-to-all-start.3 = ((bf16[16,16,512]{2,1,0:T(8,128)(2,1)}), bf16[16,16,512]{2,1,0:T(8,128)(2,1)S(1)}, u32[]{:S(2)}, u32[]{:S(2)}) async-start(bf16[16,16,512]{2,1,0:T(8,128)(2,1)} %bitcast.16), calls=%async_computation.3 | async-start | bytes 524288 | tf_op jit(solution)/shard_map/all_to_all | solution.py:231
  125.3 8.8 %all-to-all-done.3 = bf16[16,16,512]{2,1,0:T(8,128)(2,1)S(1)} async-done(((bf16[16,16,512]{2,1,0:T(8,128)(2,1)}), bf16[16,16,512]{2,1,0:T(8,128)(2,1)S(1)}, u32[]{:S(2)}, u32[]{:S(2)}) %all-to-all-start.3) | async-done | bytes 262176 | tf_op jit(solution)/shard_map/all_to_all | solution.py:231
  134.1 0.1 divide_reduce_fusion
  134.2 0.6 broadcast_multiply_fusion
  (8 shorter events, 0.1 us)
Async XLA Ops:
  0.8 7.5 %collective-permute-start = (bf16[2,32,512]{2,1,0:T(8,128)(2,1)S(1)}, bf16[2,32,512]{2,1,0:T(8,128)(2,1)S(1)}, u32[]{:S(2)}, u32[]{:S(2)}) collective-permute-start(bf16[2,32,512]{2,1,0:T(8,128)(2,1)S(1)} %pad_maximum_fusion.2.refs_0_), channel_id=1, source_target_pairs={{0,256},{256,0},{1,257},{257,1},{2,258},{258,2},{3,259},{259,3},{4... | collective-permute-start | bytes 196616 | tf_op jit(solution)/shard_map/ppermute | solution.py:21
  8.3 63.8 %all-to-all-start = ((bf16[16,2,128,256]{3,2,1,0:T(8,128)(2,1)}), bf16[16,2,128,256]{3,2,1,0:T(8,128)(2,1)S(1)}, u32[]{:S(2)}, u32[]{:S(2)}) async-start(bf16[16,2,128,256]{3,2,1,0:T(8,128)(2,1)} %bitcast.26), calls=%async_computation | async-start | bytes 4194304 | tf_op jit(solution)/shard_map/all_to_all | solution.py:212
  20.0 52.1 %copy-start = (s32[2]{0:T(128)S(1)}, s32[2]{0:T(128)}, u32[]{:S(2)}) copy-start(s32[2]{0:T(128)} %lengths.1) | copy-start | bytes 28
  20.5 10.1 %collective-permute-start.1 = (bf16[2,2,32,512]{3,2,1,0:T(8,128)(2,1)S(1)}, bf16[2,2,32,512]{3,2,1,0:T(8,128)(2,1)S(1)}, u32[]{:S(2)}, u32[]{:S(2)}) collective-permute-start(bf16[2,2,32,512]{3,2,1,0:T(8,128)(2,1)S(1)} %arrange_bases.1), channel_id=1, source_target_pairs={{0,128},{32,160},{64,192},{96,224},{128,0},{160,32},{192,64},{224,... | collective-permute-start | bytes 393224 | tf_op jit(solution)/shard_map/ppermute | solution.py:199
  30.6 16.9 %collective-permute-start.2 = (bf16[2,2,2,32,512]{4,3,2,1,0:T(8,128)(2,1)S(1)}, bf16[2,2,2,32,512]{4,3,2,1,0:T(8,128)(2,1)S(1)}, u32[]{:S(2)}, u32[]{:S(2)}) collective-permute-start(bf16[2,2,2,32,512]{4,3,2,1,0:T(8,128)(2,1)S(1)} %get-tuple-element.16), channel_id=1, source_target_pairs={{0,64},{32,96},{64,0},{96,32},{128,192},{160,224},{192,128},{224,1... | collective-permute-start | bytes 786440 | tf_op jit(solution)/shard_map/ppermute | solution.py:199
  47.5 14.1 %collective-permute-start.3 = (bf16[2,2,2,2,32,512]{5,4,3,2,1,0:T(8,128)(2,1)S(1)}, bf16[2,2,2,2,32,512]{5,4,3,2,1,0:T(8,128)(2,1)S(1)}, u32[]{:S(2)}, u32[]{:S(2)}) collective-permute-start(bf16[2,2,2,2,32,512]{5,4,3,2,1,0:T(8,128)(2,1)S(1)} %pad_maximum_fusion.low), channel_id=1, source_target_pairs={{0,32},{32,0},{64,96},{96,64},{128,160},{160,128},{192,224},{224,1... | collective-permute-start | bytes 1572872 | tf_op jit(solution)/shard_map/ppermute | solution.py:199
  49.5 16.3 %collective-permute-start.4 = (bf16[2,2,2,2,32,512]{5,4,3,2,1,0:T(8,128)(2,1)S(1)}, bf16[2,2,2,2,32,512]{5,4,3,2,1,0:T(8,128)(2,1)}, u32[]{:S(2)}, u32[]{:S(2)}) collective-permute-start(bf16[2,2,2,2,32,512]{5,4,3,2,1,0:T(8,128)(2,1)S(1)} %pad_maximum_fusion.low), channel_id=1, source_target_pairs={{0,4},{4,0},{1,5},{5,1},{2,6},{6,2},{3,7},{7,3},{8,12},{12,8},{9,1... | collective-permute-start | bytes 1572872 | tf_op jit(solution)/shard_map/ppermute | solution.py:21
  61.6 5.7 %collective-permute-start.5 = (bf16[2,2,2,2,32,512]{5,4,3,2,1,0:T(8,128)(2,1)S(1)}, bf16[2,2,2,2,32,512]{5,4,3,2,1,0:T(8,128)(2,1)}, u32[]{:S(2)}, u32[]{:S(2)}) collective-permute-start(bf16[2,2,2,2,32,512]{5,4,3,2,1,0:T(8,128)(2,1)S(1)} %collective-permute-done.3.high), channel_id=1, source_target_pairs={{0,4},{4,0},{1,5},{5,1},{2,6},{6,2},{3,7},{7,3},{8,12},{12,8},{9,1... | collective-permute-start | bytes 1572872 | tf_op jit(solution)/shard_map/ppermute | solution.py:21
  98.0 19.2 %all-to-all-start.2 = ((bf16[8,2,256,128]{3,2,1,0:T(8,128)(2,1)}), bf16[8,2,256,128]{3,2,1,0:T(8,128)(2,1)S(1)}, u32[]{:S(2)}, u32[]{:S(2)}) async-start(bf16[8,2,256,128]{3,2,1,0:T(8,128)(2,1)} %broadcast_in_dim.2), calls=%async_computation.2 | async-start | bytes 2097152 | tf_op jit(solution)/shard_map/all_to_all | solution.py:226
  118.3 15.7 %all-to-all-start.3 = ((bf16[16,16,512]{2,1,0:T(8,128)(2,1)}), bf16[16,16,512]{2,1,0:T(8,128)(2,1)S(1)}, u32[]{:S(2)}, u32[]{:S(2)}) async-start(bf16[16,16,512]{2,1,0:T(8,128)(2,1)} %bitcast.16), calls=%async_computation.3 | async-start | bytes 524288 | tf_op jit(solution)/shard_map/all_to_all | solution.py:231

commit v18 on v17

--- a/solution.py
+++ b/solution.py
@@ -62,7 +62,7 @@
     ]
     for copy in copies:
         copy.start()
-    n_zh, n_x, _, toks, width = tokens.shape
+    n_x, n_zh, _, toks, width = tokens.shape
     run = width // y_lo
     sent = []
     for which in range(2):
@@ -75,7 +75,7 @@
             for zh in range(n_zh):
                 sent.append(
                     pltpu.make_async_copy(
-                        moved.at[which, x], tokens.at[zh, x, which], out_sems.at[which, x, zh]
+                        moved.at[which, x], tokens.at[x, zh, which], out_sems.at[which, x, zh]
                     )
                 )
                 sent[-1].start()
@@ -87,7 +87,7 @@
     toks, feats = act.shape
     return pl.pallas_call(
         lambda *refs: tokens_kernel(y_lo, *refs),
-        out_shape=jax.ShapeDtypeStruct((n_zh, n_x, 2, toks, feats // n_x), BF16),
+        out_shape=jax.ShapeDtypeStruct((n_x, n_zh, 2, toks, feats // n_x), BF16),
         in_specs=[pl.BlockSpec(memory_space=pl.ANY)] * 2,
         out_specs=pl.BlockSpec(memory_space=pl.ANY),
         scratch_shapes=[
@@ -105,7 +105,7 @@
 
 
 def rotate_kernel(place, lengths, tokens, low, high, core_low, core_high, out, whole):
-    n_zh, n_x, _, toks, width = tokens.shape
+    n_x, n_zh, _, toks, width = tokens.shape
     rows, cols = low.shape[4], low.shape[5]
     group, part = n_x * toks, cols // n_x
     zl, y, c = place[0], place[1], place[2]
@@ -122,7 +122,7 @@
                             whole[which, owner, pl.ds(at, rows)] = ref[two, four, far, which]
         total = None
         for owner in range(n_zh):
-            left = tokens[owner, :, which].reshape(group, width)
+            left = tokens[:, owner, which].reshape(group, width)
             product = jnp.dot(left, whole[which, owner], preferred_element_type=F32)
             total = product if total is None else total + product
         sums.append(total)
@@ -144,7 +144,7 @@
 
 
 def rotate(place, lengths, *arrays):
-    n_zh, n_x, _, toks, width = arrays[0].shape
+    n_x, n_zh, _, toks, width = arrays[0].shape
     cols = arrays[1].shape[5]
     return pl.pallas_call(
         rotate_kernel,
@@ -210,7 +210,7 @@
     core_low, core_high = shift(low, "c", 1), shift(high, "c", 1)
 
     tokens = lax.all_to_all(
-        tokens.reshape(n_x * n_zh, *tokens.shape[2:]), ("zh", "x"), 0, 0, tiled=True
+        tokens.reshape(n_x * n_zh, *tokens.shape[2:]), ("x", "zh"), 0, 0, tiled=True
     ).reshape(tokens.shape)
 
     place = jnp.stack([zl, y, c]).astype(jnp.int32)

time: 136 us -> 136 us (level)
  the two profiles are of different devices: /device:TPU:1 before, /device:TPU:10 now
where the time goes in v18:
time: 136 us; the launch traced here: 135 us
  starting transfers between devices  47.1 us (35%)
  waiting for transfers between devices  38.5 us (28%)
  blocking collectives  38.4 us (28%)
  Pallas kernels  7.44 us (5%)
  other arithmetic  2.06 us (2%)
  local copies, waits for them, and re-layouts  1.4 us (1%)
    ppermute x3, waiting for transfers between devices, partner(): return lax.ppermute(value, 'y', [(i, i ^ step) for i in range(n_y)])  23.9 us
    all_to_all x1, blocking collectives, on_device(): partial = lax.all_to_all(partial, ('c', 'x'), 0, 0, tiled=True)  19.5 us
    all_gather x1, blocking collectives, on_device(): wide_grad = lax.all_gather(rot_grad, 'zh', axis=0)  18.9 us
    ppermute x3, starting transfers between devices, partner(): return lax.ppermute(value, 'y', [(i, i ^ step) for i in range(n_y)])  14.2 us
    all_to_all x1, starting transfers between devices, on_device(): lax.all_to_all(tokens.reshape(n_x * n_zh, *tokens.shape[2:]), ('x', 'zh')...  12.5 us
    all_to_all x1, waiting for transfers between devices, on_device(): received = lax.all_to_all(share, ('zl', 'y'), 0, 0, tiled=True)  8.93 us
    ppermute x3, starting transfers between devices, shift(): return lax.ppermute(value, axis, [(i, (i + step) % n) for i in range(n)])  8.1 us
    all_to_all x1, starting transfers between devices, on_device(): received = lax.all_to_all(share, ('zl', 'y'), 0, 0, tiled=True)  7.56 us
  transfers between devices with their start and end apart: 9, of which 6 were waited for; matrix products, arithmetic and copies ran while one was open for 0% of the time, Pallas kernels for 2%

profile of v18, /device:TPU:10, one launch (start us, length us, event | category | flops | bytes accessed | tf_op | source)
XLA Modules:
  0.0 135.1 jit_solution(4266823457416159919)
XLA Ops:
  0.0 0.8 pad_maximum_fusion.2.refs_0_
  0.8 4.3 %collective-permute-start = (bf16[2,32,512]{2,1,0:T(8,128)(2,1)S(1)}, bf16[2,32,512]{2,1,0:T(8,128)(2,1)S(1)}, u32[]{:S(2)}, u32[]{:S(2)}) collective-permute-start(bf16[2,32,512]{2,1,0:T(8,128)(2,1)S(1)} %pad_maximum_fusion.2.refs_0_), channel_id=1, source_target_pairs={{0,256},{256,0},{1,257},{257,1},{2,258},{258,2},{3,259},{259,3},{4... | collective-permute-start | bytes 196616 | tf_op jit(solution)/shard_map/ppermute | solution.py:21
  5.1 2.7 %arrange_tokens.1 = bf16[4,4,2,128,256]{4,3,2,1,0:T(8,128)(2,1)} custom-call(bf16[128,1024]{1,0:T(8,128)(2,1)} %refs_0_, bf16[128,1024]{1,0:T(8,128)(2,1)} %refs_1_.1), custom_call_target="tpu_custom_call" | custom-call | flops 131072 | bytes 1048576 | tf_op jit(solution)/shard_map/arrange_tokens/pallas_call | solution.py:88
  7.8 0.0 collective-permute-done.refs_1_
  7.8 12.5 %all-to-all-start = ((bf16[16,2,128,256]{3,2,1,0:T(8,128)(2,1)}), bf16[16,2,128,256]{3,2,1,0:T(8,128)(2,1)S(1)}, u32[]{:S(2)}, u32[]{:S(2)}) async-start(bf16[16,2,128,256]{3,2,1,0:T(8,128)(2,1)} %bitcast.26), calls=%async_computation | async-start | bytes 4194304 | tf_op jit(solution)/shard_map/all_to_all | solution.py:212
  20.3 0.5 arrange_bases.1
  20.7 6.8 %collective-permute-start.1 = (bf16[2,2,32,512]{3,2,1,0:T(8,128)(2,1)S(1)}, bf16[2,2,32,512]{3,2,1,0:T(8,128)(2,1)S(1)}, u32[]{:S(2)}, u32[]{:S(2)}) collective-permute-start(bf16[2,2,32,512]{3,2,1,0:T(8,128)(2,1)S(1)} %arrange_bases.1), channel_id=1, source_target_pairs={{0,128},{32,160},{64,192},{96,224},{128,0},{160,32},{192,64},{224,... | collective-permute-start | bytes 393224 | tf_op jit(solution)/shard_map/ppermute | solution.py:199
  27.6 6.0 %collective-permute-done.1 = bf16[2,2,32,512]{3,2,1,0:T(8,128)(2,1)S(1)} collective-permute-done((bf16[2,2,32,512]{3,2,1,0:T(8,128)(2,1)S(1)}, bf16[2,2,32,512]{3,2,1,0:T(8,128)(2,1)S(1)}, u32[]{:S(2)}, u32[]{:S(2)}) %collective-permute-start.1) | collective-permute-done | bytes 131104 | tf_op jit(solution)/shard_map/ppermute | solution.py:199
  33.6 3.9 %collective-permute-start.2 = (bf16[2,2,2,32,512]{4,3,2,1,0:T(8,128)(2,1)S(1)}, bf16[2,2,2,32,512]{4,3,2,1,0:T(8,128)(2,1)S(1)}, u32[]{:S(2)}, u32[]{:S(2)}) collective-permute-start(bf16[2,2,2,32,512]{4,3,2,1,0:T(8,128)(2,1)S(1)} %get-tuple-element.16), channel_id=1, source_target_pairs={{0,64},{32,96},{64,0},{96,32},{128,192},{160,224},{192,128},{224,1... | collective-permute-start | bytes 786440 | tf_op jit(solution)/shard_map/ppermute | solution.py:199
  37.5 8.7 %collective-permute-done.2 = bf16[2,2,2,32,512]{4,3,2,1,0:T(8,128)(2,1)S(1)} collective-permute-done((bf16[2,2,2,32,512]{4,3,2,1,0:T(8,128)(2,1)S(1)}, bf16[2,2,2,32,512]{4,3,2,1,0:T(8,128)(2,1)S(1)}, u32[]{:S(2)}, u32[]{:S(2)}) %collective-permute-start.2) | collective-permute-done | bytes 262176 | tf_op jit(solution)/shard_map/ppermute | solution.py:199
  46.2 0.1 pad_maximum_fusion.low
  46.2 3.4 %collective-permute-start.3 = (bf16[2,2,2,2,32,512]{5,4,3,2,1,0:T(8,128)(2,1)S(1)}, bf16[2,2,2,2,32,512]{5,4,3,2,1,0:T(8,128)(2,1)S(1)}, u32[]{:S(2)}, u32[]{:S(2)}) collective-permute-start(bf16[2,2,2,2,32,512]{5,4,3,2,1,0:T(8,128)(2,1)S(1)} %pad_maximum_fusion.low), channel_id=1, source_target_pairs={{0,32},{32,0},{64,96},{96,64},{128,160},{160,128},{192,224},{224,1... | collective-permute-start | bytes 1572872 | tf_op jit(solution)/shard_map/ppermute | solution.py:199
  49.7 1.9 %collective-permute-start.4 = (bf16[2,2,2,2,32,512]{5,4,3,2,1,0:T(8,128)(2,1)S(1)}, bf16[2,2,2,2,32,512]{5,4,3,2,1,0:T(8,128)(2,1)}, u32[]{:S(2)}, u32[]{:S(2)}) collective-permute-start(bf16[2,2,2,2,32,512]{5,4,3,2,1,0:T(8,128)(2,1)S(1)} %pad_maximum_fusion.low), channel_id=1, source_target_pairs={{0,4},{4,0},{1,5},{5,1},{2,6},{6,2},{3,7},{7,3},{8,12},{12,8},{9,1... | collective-permute-start | bytes 1572872 | tf_op jit(solution)/shard_map/ppermute | solution.py:21
  51.6 9.3 %collective-permute-done.3.high = bf16[2,2,2,2,32,512]{5,4,3,2,1,0:T(8,128)(2,1)S(1)} collective-permute-done((bf16[2,2,2,2,32,512]{5,4,3,2,1,0:T(8,128)(2,1)S(1)}, bf16[2,2,2,2,32,512]{5,4,3,2,1,0:T(8,128)(2,1)S(1)}, u32[]{:S(2)}, u32[]{:S(2)}) %collective-permute-start.3) | collective-permute-done | bytes 524320 | tf_op jit(solution)/shard_map/ppermute | solution.py:199
  60.9 1.9 %collective-permute-start.5 = (bf16[2,2,2,2,32,512]{5,4,3,2,1,0:T(8,128)(2,1)S(1)}, bf16[2,2,2,2,32,512]{5,4,3,2,1,0:T(8,128)(2,1)}, u32[]{:S(2)}, u32[]{:S(2)}) collective-permute-start(bf16[2,2,2,2,32,512]{5,4,3,2,1,0:T(8,128)(2,1)S(1)} %collective-permute-done.3.high), channel_id=1, source_target_pairs={{0,4},{4,0},{1,5},{5,1},{2,6},{6,2},{3,7},{7,3},{8,12},{12,8},{9,1... | collective-permute-start | bytes 1572872 | tf_op jit(solution)/shard_map/ppermute | solution.py:21
  62.8 0.1 pad_add_fusion.place
  62.9 0.0 collective-permute-done.4.core_low
  62.9 1.9 %collective-permute-done.5.core_high = bf16[2,2,2,2,32,512]{5,4,3,2,1,0:T(8,128)(2,1)} collective-permute-done((bf16[2,2,2,2,32,512]{5,4,3,2,1,0:T(8,128)(2,1)S(1)}, bf16[2,2,2,2,32,512]{5,4,3,2,1,0:T(8,128)(2,1)}, u32[]{:S(2)}, u32[]{:S(2)}) %collective-permute-start.5) | collective-permute-done | bytes 524320 | tf_op jit(solution)/shard_map/ppermute | solution.py:21
  64.8 3.7 %all-to-all-done = bf16[16,2,128,256]{3,2,1,0:T(8,128)(2,1)S(1)} async-done(((bf16[16,2,128,256]{3,2,1,0:T(8,128)(2,1)}), bf16[16,2,128,256]{3,2,1,0:T(8,128)(2,1)S(1)}, u32[]{:S(2)}, u32[]{:S(2)}) %all-to-all-start) | async-done | bytes 2097184 | tf_op jit(solution)/shard_map/all_to_all | solution.py:212
  68.4 3.1 %rotate.1 = f32[8,528,128]{2,1,0:T(8,128)S(1)} custom-call(s32[3]{0:T(128)S(1)} %pad_add_fusion.place, s32[2]{0:T(128)S(1)} %copy-done, bf16[4,4,2,128,256]{4,3,2,1,0:T(8,128)(2,1)S(1)} %bitcast.22, bf16[2,2,2,2,32,512]{5,4,3,2,1,0:T(8,128)(2,1)S(1)} %pad_maximum_fusion.low, bf16[2,2,2,2,32,512]{5,4,3,2,1,0:T(8,128)(2,1)S(1)} %collective-permute-done.3.high, ...), custom_call_target="tpu_custom_call" | custom-call | flops 1073741824 | bytes 8388608 | tf_op jit(solution)/shard_map/rotate/pallas_call | solution.py:149
  71.6 0.1 convert_element_type.25
  71.7 19.5 %all_to_all.20 = f16[8,528,128]{2,1,0:T(8,128)(2,1)S(1)} all-to-all(f16[8,528,128]{2,1,0:T(8,128)(2,1)S(1)} %convert_element_type.25), channel_id=1, replica_groups=mesh['zl'=2,'y'=8,'x'=4,'c'=2,'zh'=4] {'c','x'}, dimensions={0} | all-to-all | bytes 2162688 | tf_op jit(solution)/shard_map/all_to_all | solution.py:219
  91.2 0.2 slice.16
  91.5 0.2 fusion
  91.7 1.2 broadcast_in_dim.2
  92.9 4.8 %all-to-all-start.2 = ((bf16[8,2,256,128]{3,2,1,0:T(8,128)(2,1)}), bf16[8,2,256,128]{3,2,1,0:T(8,128)(2,1)S(1)}, u32[]{:S(2)}, u32[]{:S(2)}) async-start(bf16[8,2,256,128]{3,2,1,0:T(8,128)(2,1)} %broadcast_in_dim.2), calls=%async_computation.2 | async-start | bytes 2097152 | tf_op jit(solution)/shard_map/all_to_all | solution.py:226
  97.7 18.9 %all-gather = bf16[8,256,128]{2,1,0:T(8,128)(2,1)S(1)} all-gather(bf16[2,256,128]{2,1,0:T(8,128)(2,1)S(1)} %get-tuple-element.14), channel_id=2, replica_groups=mesh['zl'=2,'y'=8,'x'=4,'c'=2,'zh'=4] {'zh'}, dimensions={0}, use_global_device_ids=true | all-gather | bytes 655360 | tf_op jit(solution)/shard_map/all_gather | solution.py:229
  116.6 1.2 share.1
  117.8 7.6 %all-to-all-start.3 = ((bf16[16,16,512]{2,1,0:T(8,128)(2,1)}), bf16[16,16,512]{2,1,0:T(8,128)(2,1)S(1)}, u32[]{:S(2)}, u32[]{:S(2)}) async-start(bf16[16,16,512]{2,1,0:T(8,128)(2,1)} %bitcast.16), calls=%async_computation.3 | async-start | bytes 524288 | tf_op jit(solution)/shard_map/all_to_all | solution.py:231
  125.4 8.9 %all-to-all-done.3 = bf16[16,16,512]{2,1,0:T(8,128)(2,1)S(1)} async-done(((bf16[16,16,512]{2,1,0:T(8,128)(2,1)}), bf16[16,16,512]{2,1,0:T(8,128)(2,1)S(1)}, u32[]{:S(2)}, u32[]{:S(2)}) %all-to-all-start.3) | async-done | bytes 262176 | tf_op jit(solution)/shard_map/all_to_all | solution.py:231
  134.3 0.1 divide_reduce_fusion
  134.4 0.6 broadcast_multiply_fusion
  (8 shorter events, 0.1 us)
Async XLA Ops:
  0.8 7.0 %collective-permute-start = (bf16[2,32,512]{2,1,0:T(8,128)(2,1)S(1)}, bf16[2,32,512]{2,1,0:T(8,128)(2,1)S(1)}, u32[]{:S(2)}, u32[]{:S(2)}) collective-permute-start(bf16[2,32,512]{2,1,0:T(8,128)(2,1)S(1)} %pad_maximum_fusion.2.refs_0_), channel_id=1, source_target_pairs={{0,256},{256,0},{1,257},{257,1},{2,258},{258,2},{3,259},{259,3},{4... | collective-permute-start | bytes 196616 | tf_op jit(solution)/shard_map/ppermute | solution.py:21
  7.8 60.7 %all-to-all-start = ((bf16[16,2,128,256]{3,2,1,0:T(8,128)(2,1)}), bf16[16,2,128,256]{3,2,1,0:T(8,128)(2,1)S(1)}, u32[]{:S(2)}, u32[]{:S(2)}) async-start(bf16[16,2,128,256]{3,2,1,0:T(8,128)(2,1)} %bitcast.26), calls=%async_computation | async-start | bytes 4194304 | tf_op jit(solution)/shard_map/all_to_all | solution.py:212
  20.2 48.2 %copy-start = (s32[2]{0:T(128)S(1)}, s32[2]{0:T(128)}, u32[]{:S(2)}) copy-start(s32[2]{0:T(128)} %lengths.1) | copy-start | bytes 28
  20.7 12.8 %collective-permute-start.1 = (bf16[2,2,32,512]{3,2,1,0:T(8,128)(2,1)S(1)}, bf16[2,2,32,512]{3,2,1,0:T(8,128)(2,1)S(1)}, u32[]{:S(2)}, u32[]{:S(2)}) collective-permute-start(bf16[2,2,32,512]{3,2,1,0:T(8,128)(2,1)S(1)} %arrange_bases.1), channel_id=1, source_target_pairs={{0,128},{32,160},{64,192},{96,224},{128,0},{160,32},{192,64},{224,... | collective-permute-start | bytes 393224 | tf_op jit(solution)/shard_map/ppermute | solution.py:199
  33.6 12.6 %collective-permute-start.2 = (bf16[2,2,2,32,512]{4,3,2,1,0:T(8,128)(2,1)S(1)}, bf16[2,2,2,32,512]{4,3,2,1,0:T(8,128)(2,1)S(1)}, u32[]{:S(2)}, u32[]{:S(2)}) collective-permute-start(bf16[2,2,2,32,512]{4,3,2,1,0:T(8,128)(2,1)S(1)} %get-tuple-element.16), channel_id=1, source_target_pairs={{0,64},{32,96},{64,0},{96,32},{128,192},{160,224},{192,128},{224,1... | collective-permute-start | bytes 786440 | tf_op jit(solution)/shard_map/ppermute | solution.py:199
  46.2 14.6 %collective-permute-start.3 = (bf16[2,2,2,2,32,512]{5,4,3,2,1,0:T(8,128)(2,1)S(1)}, bf16[2,2,2,2,32,512]{5,4,3,2,1,0:T(8,128)(2,1)S(1)}, u32[]{:S(2)}, u32[]{:S(2)}) collective-permute-start(bf16[2,2,2,2,32,512]{5,4,3,2,1,0:T(8,128)(2,1)S(1)} %pad_maximum_fusion.low), channel_id=1, source_target_pairs={{0,32},{32,0},{64,96},{96,64},{128,160},{160,128},{192,224},{224,1... | collective-permute-start | bytes 1572872 | tf_op jit(solution)/shard_map/ppermute | solution.py:199
  49.7 13.2 %collective-permute-start.4 = (bf16[2,2,2,2,32,512]{5,4,3,2,1,0:T(8,128)(2,1)S(1)}, bf16[2,2,2,2,32,512]{5,4,3,2,1,0:T(8,128)(2,1)}, u32[]{:S(2)}, u32[]{:S(2)}) collective-permute-start(bf16[2,2,2,2,32,512]{5,4,3,2,1,0:T(8,128)(2,1)S(1)} %pad_maximum_fusion.low), channel_id=1, source_target_pairs={{0,4},{4,0},{1,5},{5,1},{2,6},{6,2},{3,7},{7,3},{8,12},{12,8},{9,1... | collective-permute-start | bytes 1572872 | tf_op jit(solution)/shard_map/ppermute | solution.py:21
  60.9 3.9 %collective-permute-start.5 = (bf16[2,2,2,2,32,512]{5,4,3,2,1,0:T(8,128)(2,1)S(1)}, bf16[2,2,2,2,32,512]{5,4,3,2,1,0:T(8,128)(2,1)}, u32[]{:S(2)}, u32[]{:S(2)}) collective-permute-start(bf16[2,2,2,2,32,512]{5,4,3,2,1,0:T(8,128)(2,1)S(1)} %collective-permute-done.3.high), channel_id=1, source_target_pairs={{0,4},{4,0},{1,5},{5,1},{2,6},{6,2},{3,7},{7,3},{8,12},{12,8},{9,1... | collective-permute-start | bytes 1572872 | tf_op jit(solution)/shard_map/ppermute | solution.py:21
  92.9 23.7 %all-to-all-start.2 = ((bf16[8,2,256,128]{3,2,1,0:T(8,128)(2,1)}), bf16[8,2,256,128]{3,2,1,0:T(8,128)(2,1)S(1)}, u32[]{:S(2)}, u32[]{:S(2)}) async-start(bf16[8,2,256,128]{3,2,1,0:T(8,128)(2,1)} %broadcast_in_dim.2), calls=%async_computation.2 | async-start | bytes 2097152 | tf_op jit(solution)/shard_map/all_to_all | solution.py:226
  117.8 16.5 %all-to-all-start.3 = ((bf16[16,16,512]{2,1,0:T(8,128)(2,1)}), bf16[16,16,512]{2,1,0:T(8,128)(2,1)S(1)}, u32[]{:S(2)}, u32[]{:S(2)}) async-start(bf16[16,16,512]{2,1,0:T(8,128)(2,1)} %bitcast.16), calls=%async_computation.3 | async-start | bytes 524288 | tf_op jit(solution)/shard_map/all_to_all | solution.py:231

commit v19 on v18

--- a/solution.py
+++ b/solution.py
@@ -104,13 +104,12 @@
     )(act, grad)
 
 
-def rotate_kernel(place, lengths, tokens, low, high, core_low, core_high, out, whole):
+def rotate_kernel(place, lengths, tokens, low, high, core_low, core_high, out, *wholes):
     n_x, n_zh, _, toks, width = tokens.shape
     rows, cols = low.shape[4], low.shape[5]
     group, part = n_x * toks, cols // n_x
     zl, y, c = place[0], place[1], place[2]
-    sums = []
-    for which in range(2):
+    for which, whole in enumerate(wholes):
         for one, pair in enumerate(((low, core_low), (high, core_high))):
             for two in range(2):
                 for four in range(2):
@@ -119,11 +118,13 @@
                         owner = (zl ^ far) * 2 + from_y // 4
                         for ref, core in zip(pair, (c, 1 - c)):
                             at = pl.multiple_of((from_y % 4 * 2 + core) * rows, rows)
-                            whole[which, owner, pl.ds(at, rows)] = ref[two, four, far, which]
+                            whole[owner, pl.ds(at, rows)] = ref[two, four, far, which]
+    sums = []
+    for which, whole in enumerate(wholes):
         total = None
         for owner in range(n_zh):
             left = tokens[:, owner, which].reshape(group, width)
-            product = jnp.dot(left, whole[which, owner], preferred_element_type=F32)
+            product = jnp.dot(left, whole[owner], preferred_element_type=F32)
             total = product if total is None else total + product
         sums.append(total)
     index = lax.broadcasted_iota(jnp.int32, (group, 1), 0)
@@ -151,7 +152,7 @@
         out_shape=jax.ShapeDtypeStruct((2 * n_x, n_x * toks + TILE, cols // n_x), F32),
         in_specs=[SMEM] * 2 + [VMEM] * len(arrays),
         out_specs=VMEM,
-        scratch_shapes=[pltpu.VMEM((2, n_zh, width, cols), BF16)],
+        scratch_shapes=[pltpu.VMEM((n_zh, width, cols), BF16)] * 2,
         compiler_params=pltpu.CompilerParams(vmem_limit_bytes=40 * 2**20),
         cost_estimate=pl.CostEstimate(
             flops=4 * n_x * n_zh * toks * width * cols, bytes_accessed=8 * 2**20, transcendentals=0

time: 136 us -> 136 us (level)
  no operation moved by 1% of the time
where the time goes in v19:
time: 136 us; the launch traced here: 135 us
  starting transfers between devices  47.1 us (35%)
  waiting for transfers between devices  38.5 us (28%)
  blocking collectives  38.4 us (28%)
  Pallas kernels  7.44 us (5%)
  other arithmetic  2.06 us (2%)
  local copies, waits for them, and re-layouts  1.4 us (1%)
    ppermute x3, waiting for transfers between devices, partner(): return lax.ppermute(value, 'y', [(i, i ^ step) for i in range(n_y)])  23.9 us
    all_to_all x1, blocking collectives, on_device(): partial = lax.all_to_all(partial, ('c', 'x'), 0, 0, tiled=True)  19.5 us
    all_gather x1, blocking collectives, on_device(): wide_grad = lax.all_gather(rot_grad, 'zh', axis=0)  18.9 us
    ppermute x3, starting transfers between devices, partner(): return lax.ppermute(value, 'y', [(i, i ^ step) for i in range(n_y)])  14.2 us
    all_to_all x1, starting transfers between devices, on_device(): lax.all_to_all(tokens.reshape(n_x * n_zh, *tokens.shape[2:]), ('x', 'zh')...  12.5 us
    all_to_all x1, waiting for transfers between devices, on_device(): received = lax.all_to_all(share, ('zl', 'y'), 0, 0, tiled=True)  8.93 us
    ppermute x3, starting transfers between devices, shift(): return lax.ppermute(value, axis, [(i, (i + step) % n) for i in range(n)])  8.1 us
    all_to_all x1, starting transfers between devices, on_device(): received = lax.all_to_all(share, ('zl', 'y'), 0, 0, tiled=True)  7.56 us
  transfers between devices with their start and end apart: 9, of which 6 were waited for; matrix products, arithmetic and copies ran while one was open for 0% of the time, Pallas kernels for 2%

profile of v19, /device:TPU:10, one launch (start us, length us, event | category | flops | bytes accessed | tf_op | source)
XLA Modules:
  0.0 135.0 jit_solution(6231878263107193749)
XLA Ops:
  0.0 0.8 pad_maximum_fusion.2.refs_0_
  0.8 4.3 %collective-permute-start = (bf16[2,32,512]{2,1,0:T(8,128)(2,1)S(1)}, bf16[2,32,512]{2,1,0:T(8,128)(2,1)S(1)}, u32[]{:S(2)}, u32[]{:S(2)}) collective-permute-start(bf16[2,32,512]{2,1,0:T(8,128)(2,1)S(1)} %pad_maximum_fusion.2.refs_0_), channel_id=1, source_target_pairs={{0,256},{256,0},{1,257},{257,1},{2,258},{258,2},{3,259},{259,3},{4... | collective-permute-start | bytes 196616 | tf_op jit(solution)/shard_map/ppermute | solution.py:21
  5.1 2.7 %arrange_tokens.1 = bf16[4,4,2,128,256]{4,3,2,1,0:T(8,128)(2,1)} custom-call(bf16[128,1024]{1,0:T(8,128)(2,1)} %refs_0_, bf16[128,1024]{1,0:T(8,128)(2,1)} %refs_1_.1), custom_call_target="tpu_custom_call" | custom-call | flops 131072 | bytes 1048576 | tf_op jit(solution)/shard_map/arrange_tokens/pallas_call | solution.py:88
  7.8 12.5 %all-to-all-start = ((bf16[16,2,128,256]{3,2,1,0:T(8,128)(2,1)}), bf16[16,2,128,256]{3,2,1,0:T(8,128)(2,1)S(1)}, u32[]{:S(2)}, u32[]{:S(2)}) async-start(bf16[16,2,128,256]{3,2,1,0:T(8,128)(2,1)} %bitcast.26), calls=%async_computation | async-start | bytes 4194304 | tf_op jit(solution)/shard_map/all_to_all | solution.py:213
  20.3 0.5 arrange_bases.1
  20.7 6.8 %collective-permute-start.1 = (bf16[2,2,32,512]{3,2,1,0:T(8,128)(2,1)S(1)}, bf16[2,2,32,512]{3,2,1,0:T(8,128)(2,1)S(1)}, u32[]{:S(2)}, u32[]{:S(2)}) collective-permute-start(bf16[2,2,32,512]{3,2,1,0:T(8,128)(2,1)S(1)} %arrange_bases.1), channel_id=1, source_target_pairs={{0,128},{32,160},{64,192},{96,224},{128,0},{160,32},{192,64},{224,... | collective-permute-start | bytes 393224 | tf_op jit(solution)/shard_map/ppermute | solution.py:200
  27.6 6.0 %collective-permute-done.1 = bf16[2,2,32,512]{3,2,1,0:T(8,128)(2,1)S(1)} collective-permute-done((bf16[2,2,32,512]{3,2,1,0:T(8,128)(2,1)S(1)}, bf16[2,2,32,512]{3,2,1,0:T(8,128)(2,1)S(1)}, u32[]{:S(2)}, u32[]{:S(2)}) %collective-permute-start.1) | collective-permute-done | bytes 131104 | tf_op jit(solution)/shard_map/ppermute | solution.py:200
  33.6 3.9 %collective-permute-start.2 = (bf16[2,2,2,32,512]{4,3,2,1,0:T(8,128)(2,1)S(1)}, bf16[2,2,2,32,512]{4,3,2,1,0:T(8,128)(2,1)S(1)}, u32[]{:S(2)}, u32[]{:S(2)}) collective-permute-start(bf16[2,2,2,32,512]{4,3,2,1,0:T(8,128)(2,1)S(1)} %get-tuple-element.16), channel_id=1, source_target_pairs={{0,64},{32,96},{64,0},{96,32},{128,192},{160,224},{192,128},{224,1... | collective-permute-start | bytes 786440 | tf_op jit(solution)/shard_map/ppermute | solution.py:200
  37.5 8.7 %collective-permute-done.2 = bf16[2,2,2,32,512]{4,3,2,1,0:T(8,128)(2,1)S(1)} collective-permute-done((bf16[2,2,2,32,512]{4,3,2,1,0:T(8,128)(2,1)S(1)}, bf16[2,2,2,32,512]{4,3,2,1,0:T(8,128)(2,1)S(1)}, u32[]{:S(2)}, u32[]{:S(2)}) %collective-permute-start.2) | collective-permute-done | bytes 262176 | tf_op jit(solution)/shard_map/ppermute | solution.py:200
  46.2 0.1 pad_maximum_fusion.low
  46.2 3.4 %collective-permute-start.3 = (bf16[2,2,2,2,32,512]{5,4,3,2,1,0:T(8,128)(2,1)S(1)}, bf16[2,2,2,2,32,512]{5,4,3,2,1,0:T(8,128)(2,1)S(1)}, u32[]{:S(2)}, u32[]{:S(2)}) collective-permute-start(bf16[2,2,2,2,32,512]{5,4,3,2,1,0:T(8,128)(2,1)S(1)} %pad_maximum_fusion.low), channel_id=1, source_target_pairs={{0,32},{32,0},{64,96},{96,64},{128,160},{160,128},{192,224},{224,1... | collective-permute-start | bytes 1572872 | tf_op jit(solution)/shard_map/ppermute | solution.py:200
  49.7 1.9 %collective-permute-start.4 = (bf16[2,2,2,2,32,512]{5,4,3,2,1,0:T(8,128)(2,1)S(1)}, bf16[2,2,2,2,32,512]{5,4,3,2,1,0:T(8,128)(2,1)}, u32[]{:S(2)}, u32[]{:S(2)}) collective-permute-start(bf16[2,2,2,2,32,512]{5,4,3,2,1,0:T(8,128)(2,1)S(1)} %pad_maximum_fusion.low), channel_id=1, source_target_pairs={{0,4},{4,0},{1,5},{5,1},{2,6},{6,2},{3,7},{7,3},{8,12},{12,8},{9,1... | collective-permute-start | bytes 1572872 | tf_op jit(solution)/shard_map/ppermute | solution.py:21
  51.6 9.3 %collective-permute-done.3.high = bf16[2,2,2,2,32,512]{5,4,3,2,1,0:T(8,128)(2,1)S(1)} collective-permute-done((bf16[2,2,2,2,32,512]{5,4,3,2,1,0:T(8,128)(2,1)S(1)}, bf16[2,2,2,2,32,512]{5,4,3,2,1,0:T(8,128)(2,1)S(1)}, u32[]{:S(2)}, u32[]{:S(2)}) %collective-permute-start.3) | collective-permute-done | bytes 524320 | tf_op jit(solution)/shard_map/ppermute | solution.py:200
  60.9 1.9 %collective-permute-start.5 = (bf16[2,2,2,2,32,512]{5,4,3,2,1,0:T(8,128)(2,1)S(1)}, bf16[2,2,2,2,32,512]{5,4,3,2,1,0:T(8,128)(2,1)}, u32[]{:S(2)}, u32[]{:S(2)}) collective-permute-start(bf16[2,2,2,2,32,512]{5,4,3,2,1,0:T(8,128)(2,1)S(1)} %collective-permute-done.3.high), channel_id=1, source_target_pairs={{0,4},{4,0},{1,5},{5,1},{2,6},{6,2},{3,7},{7,3},{8,12},{12,8},{9,1... | collective-permute-start | bytes 1572872 | tf_op jit(solution)/shard_map/ppermute | solution.py:21
  62.8 0.1 pad_add_fusion.place
  62.9 0.0 collective-permute-done.4.core_low
  62.9 1.9 %collective-permute-done.5.core_high = bf16[2,2,2,2,32,512]{5,4,3,2,1,0:T(8,128)(2,1)} collective-permute-done((bf16[2,2,2,2,32,512]{5,4,3,2,1,0:T(8,128)(2,1)S(1)}, bf16[2,2,2,2,32,512]{5,4,3,2,1,0:T(8,128)(2,1)}, u32[]{:S(2)}, u32[]{:S(2)}) %collective-permute-start.5) | collective-permute-done | bytes 524320 | tf_op jit(solution)/shard_map/ppermute | solution.py:21
  64.8 3.7 %all-to-all-done = bf16[16,2,128,256]{3,2,1,0:T(8,128)(2,1)S(1)} async-done(((bf16[16,2,128,256]{3,2,1,0:T(8,128)(2,1)}), bf16[16,2,128,256]{3,2,1,0:T(8,128)(2,1)S(1)}, u32[]{:S(2)}, u32[]{:S(2)}) %all-to-all-start) | async-done | bytes 2097184 | tf_op jit(solution)/shard_map/all_to_all | solution.py:213
  68.4 3.1 %rotate.1 = f32[8,528,128]{2,1,0:T(8,128)S(1)} custom-call(s32[3]{0:T(128)S(1)} %pad_add_fusion.place, s32[2]{0:T(128)S(1)} %copy-done, bf16[4,4,2,128,256]{4,3,2,1,0:T(8,128)(2,1)S(1)} %bitcast.22, bf16[2,2,2,2,32,512]{5,4,3,2,1,0:T(8,128)(2,1)S(1)} %pad_maximum_fusion.low, bf16[2,2,2,2,32,512]{5,4,3,2,1,0:T(8,128)(2,1)S(1)} %collective-permute-done.3.high, ...), custom_call_target="tpu_custom_call" | custom-call | flops 1073741824 | bytes 8388608 | tf_op jit(solution)/shard_map/rotate/pallas_call | solution.py:150
  71.6 0.1 convert_element_type.25
  71.7 19.5 %all_to_all.20 = f16[8,528,128]{2,1,0:T(8,128)(2,1)S(1)} all-to-all(f16[8,528,128]{2,1,0:T(8,128)(2,1)S(1)} %convert_element_type.25), channel_id=1, replica_groups=mesh['zl'=2,'y'=8,'x'=4,'c'=2,'zh'=4] {'c','x'}, dimensions={0} | all-to-all | bytes 2162688 | tf_op jit(solution)/shard_map/all_to_all | solution.py:220
  91.2 0.2 slice.16
  91.5 0.2 fusion
  91.7 1.2 broadcast_in_dim.2
  92.9 4.8 %all-to-all-start.2 = ((bf16[8,2,256,128]{3,2,1,0:T(8,128)(2,1)}), bf16[8,2,256,128]{3,2,1,0:T(8,128)(2,1)S(1)}, u32[]{:S(2)}, u32[]{:S(2)}) async-start(bf16[8,2,256,128]{3,2,1,0:T(8,128)(2,1)} %broadcast_in_dim.2), calls=%async_computation.2 | async-start | bytes 2097152 | tf_op jit(solution)/shard_map/all_to_all | solution.py:227
  97.7 18.9 %all-gather = bf16[8,256,128]{2,1,0:T(8,128)(2,1)S(1)} all-gather(bf16[2,256,128]{2,1,0:T(8,128)(2,1)S(1)} %get-tuple-element.14), channel_id=2, replica_groups=mesh['zl'=2,'y'=8,'x'=4,'c'=2,'zh'=4] {'zh'}, dimensions={0}, use_global_device_ids=true | all-gather | bytes 655360 | tf_op jit(solution)/shard_map/all_gather | solution.py:230
  116.6 0.0 all-to-all-done.2
  116.6 1.2 share.1
  117.8 7.6 %all-to-all-start.3 = ((bf16[16,16,512]{2,1,0:T(8,128)(2,1)}), bf16[16,16,512]{2,1,0:T(8,128)(2,1)S(1)}, u32[]{:S(2)}, u32[]{:S(2)}) async-start(bf16[16,16,512]{2,1,0:T(8,128)(2,1)} %bitcast.16), calls=%async_computation.3 | async-start | bytes 524288 | tf_op jit(solution)/shard_map/all_to_all | solution.py:232
  125.4 8.9 %all-to-all-done.3 = bf16[16,16,512]{2,1,0:T(8,128)(2,1)S(1)} async-done(((bf16[16,16,512]{2,1,0:T(8,128)(2,1)}), bf16[16,16,512]{2,1,0:T(8,128)(2,1)S(1)}, u32[]{:S(2)}, u32[]{:S(2)}) %all-to-all-start.3) | async-done | bytes 262176 | tf_op jit(solution)/shard_map/all_to_all | solution.py:232
  134.3 0.1 divide_reduce_fusion
  134.4 0.6 broadcast_multiply_fusion
  (8 shorter events, 0.1 us)
Async XLA Ops:
  0.8 7.0 %collective-permute-start = (bf16[2,32,512]{2,1,0:T(8,128)(2,1)S(1)}, bf16[2,32,512]{2,1,0:T(8,128)(2,1)S(1)}, u32[]{:S(2)}, u32[]{:S(2)}) collective-permute-start(bf16[2,32,512]{2,1,0:T(8,128)(2,1)S(1)} %pad_maximum_fusion.2.refs_0_), channel_id=1, source_target_pairs={{0,256},{256,0},{1,257},{257,1},{2,258},{258,2},{3,259},{259,3},{4... | collective-permute-start | bytes 196616 | tf_op jit(solution)/shard_map/ppermute | solution.py:21
  7.8 60.7 %all-to-all-start = ((bf16[16,2,128,256]{3,2,1,0:T(8,128)(2,1)}), bf16[16,2,128,256]{3,2,1,0:T(8,128)(2,1)S(1)}, u32[]{:S(2)}, u32[]{:S(2)}) async-start(bf16[16,2,128,256]{3,2,1,0:T(8,128)(2,1)} %bitcast.26), calls=%async_computation | async-start | bytes 4194304 | tf_op jit(solution)/shard_map/all_to_all | solution.py:213
  20.2 48.2 %copy-start = (s32[2]{0:T(128)S(1)}, s32[2]{0:T(128)}, u32[]{:S(2)}) copy-start(s32[2]{0:T(128)} %lengths.1) | copy-start | bytes 28
  20.7 12.8 %collective-permute-start.1 = (bf16[2,2,32,512]{3,2,1,0:T(8,128)(2,1)S(1)}, bf16[2,2,32,512]{3,2,1,0:T(8,128)(2,1)S(1)}, u32[]{:S(2)}, u32[]{:S(2)}) collective-permute-start(bf16[2,2,32,512]{3,2,1,0:T(8,128)(2,1)S(1)} %arrange_bases.1), channel_id=1, source_target_pairs={{0,128},{32,160},{64,192},{96,224},{128,0},{160,32},{192,64},{224,... | collective-permute-start | bytes 393224 | tf_op jit(solution)/shard_map/ppermute | solution.py:200
  33.6 12.6 %collective-permute-start.2 = (bf16[2,2,2,32,512]{4,3,2,1,0:T(8,128)(2,1)S(1)}, bf16[2,2,2,32,512]{4,3,2,1,0:T(8,128)(2,1)S(1)}, u32[]{:S(2)}, u32[]{:S(2)}) collective-permute-start(bf16[2,2,2,32,512]{4,3,2,1,0:T(8,128)(2,1)S(1)} %get-tuple-element.16), channel_id=1, source_target_pairs={{0,64},{32,96},{64,0},{96,32},{128,192},{160,224},{192,128},{224,1... | collective-permute-start | bytes 786440 | tf_op jit(solution)/shard_map/ppermute | solution.py:200
  46.2 14.6 %collective-permute-start.3 = (bf16[2,2,2,2,32,512]{5,4,3,2,1,0:T(8,128)(2,1)S(1)}, bf16[2,2,2,2,32,512]{5,4,3,2,1,0:T(8,128)(2,1)S(1)}, u32[]{:S(2)}, u32[]{:S(2)}) collective-permute-start(bf16[2,2,2,2,32,512]{5,4,3,2,1,0:T(8,128)(2,1)S(1)} %pad_maximum_fusion.low), channel_id=1, source_target_pairs={{0,32},{32,0},{64,96},{96,64},{128,160},{160,128},{192,224},{224,1... | collective-permute-start | bytes 1572872 | tf_op jit(solution)/shard_map/ppermute | solution.py:200
  49.7 13.2 %collective-permute-start.4 = (bf16[2,2,2,2,32,512]{5,4,3,2,1,0:T(8,128)(2,1)S(1)}, bf16[2,2,2,2,32,512]{5,4,3,2,1,0:T(8,128)(2,1)}, u32[]{:S(2)}, u32[]{:S(2)}) collective-permute-start(bf16[2,2,2,2,32,512]{5,4,3,2,1,0:T(8,128)(2,1)S(1)} %pad_maximum_fusion.low), channel_id=1, source_target_pairs={{0,4},{4,0},{1,5},{5,1},{2,6},{6,2},{3,7},{7,3},{8,12},{12,8},{9,1... | collective-permute-start | bytes 1572872 | tf_op jit(solution)/shard_map/ppermute | solution.py:21
  60.9 3.9 %collective-permute-start.5 = (bf16[2,2,2,2,32,512]{5,4,3,2,1,0:T(8,128)(2,1)S(1)}, bf16[2,2,2,2,32,512]{5,4,3,2,1,0:T(8,128)(2,1)}, u32[]{:S(2)}, u32[]{:S(2)}) collective-permute-start(bf16[2,2,2,2,32,512]{5,4,3,2,1,0:T(8,128)(2,1)S(1)} %collective-permute-done.3.high), channel_id=1, source_target_pairs={{0,4},{4,0},{1,5},{5,1},{2,6},{6,2},{3,7},{7,3},{8,12},{12,8},{9,1... | collective-permute-start | bytes 1572872 | tf_op jit(solution)/shard_map/ppermute | solution.py:21
  92.9 23.7 %all-to-all-start.2 = ((bf16[8,2,256,128]{3,2,1,0:T(8,128)(2,1)}), bf16[8,2,256,128]{3,2,1,0:T(8,128)(2,1)S(1)}, u32[]{:S(2)}, u32[]{:S(2)}) async-start(bf16[8,2,256,128]{3,2,1,0:T(8,128)(2,1)} %broadcast_in_dim.2), calls=%async_computation.2 | async-start | bytes 2097152 | tf_op jit(solution)/shard_map/all_to_all | solution.py:227
  117.8 16.5 %all-to-all-start.3 = ((bf16[16,16,512]{2,1,0:T(8,128)(2,1)}), bf16[16,16,512]{2,1,0:T(8,128)(2,1)S(1)}, u32[]{:S(2)}, u32[]{:S(2)}) async-start(bf16[16,16,512]{2,1,0:T(8,128)(2,1)} %bitcast.16), calls=%async_computation.3 | async-start | bytes 524288 | tf_op jit(solution)/shard_map/all_to_all | solution.py:232

commit v20 on v19

--- a/solution.py
+++ b/solution.py
@@ -191,6 +191,27 @@
     )(grad, act)
 
 
+def copies_kernel(value, out, sems):
+    copies = [pltpu.make_async_copy(value, out.at[i], sems.at[i]) for i in range(out.shape[0])]
+    for copy in copies:
+        copy.start()
+    for copy in copies:
+        copy.wait()
+
+
+def copies_of(value, count):
+    return pl.pallas_call(
+        copies_kernel,
+        out_shape=jax.ShapeDtypeStruct((count, *value.shape), value.dtype),
+        in_specs=[VMEM],
+        out_specs=pl.BlockSpec(memory_space=pl.ANY),
+        scratch_shapes=[pltpu.SemaphoreType.DMA((count,))],
+        compiler_params=pltpu.CompilerParams(vmem_limit_bytes=16 * 2**20),
+        cost_estimate=pl.CostEstimate(flops=0, bytes_accessed=2**20, transcendentals=0),
+        name="copies",
+    )(value)
+
+
 def on_device(activations, gradients, basis_act, basis_grad, lengths):
     n_zl, n_y, n_x, n_c, n_zh = (lax.axis_size(a) for a in ("zl", "y", "x", "c", "zh"))
     zl, y, c = (lax.axis_index(a) for a in ("zl", "y", "c"))
@@ -225,7 +246,7 @@
     rot_act, rot_grad = rotated[:, : group // 2], rotated[:, group // 2 :]
 
     wide_act = lax.all_to_all(
-        jnp.broadcast_to(rot_act[None], (n_c * n_x, *rot_act.shape)), ("c", "x"), 0, 0, tiled=True
+        copies_of(rot_act, n_c * n_x), ("c", "x"), 0, 0, tiled=True
     ).reshape(n_c, n_x, *rot_act.shape)
     wide_grad = lax.all_gather(rot_grad, "zh", axis=0)
     share = share_of(wide_grad, wide_act).reshape(n_zl * n_y, -1, cols)

time: 136 us -> 136 us (level)
  no operation moved by 1% of the time
where the time goes in v20:
time: 136 us; the launch traced here: 135 us
  starting transfers between devices  47.1 us (35%)
  waiting for transfers between devices  38.5 us (28%)
  blocking collectives  38.4 us (28%)
  Pallas kernels  8.49 us (6%)
  other arithmetic  2.06 us (2%)
    ppermute x3, waiting for transfers between devices, partner(): return lax.ppermute(value, 'y', [(i, i ^ step) for i in range(n_y)])  23.9 us
    all_to_all x1, blocking collectives, on_device(): partial = lax.all_to_all(partial, ('c', 'x'), 0, 0, tiled=True)  19.5 us
    all_gather x1, blocking collectives, on_device(): wide_grad = lax.all_gather(rot_grad, 'zh', axis=0)  18.9 us
    ppermute x3, starting transfers between devices, partner(): return lax.ppermute(value, 'y', [(i, i ^ step) for i in range(n_y)])  14.2 us
    all_to_all x1, starting transfers between devices, on_device(): lax.all_to_all(tokens.reshape(n_x * n_zh, *tokens.shape[2:]), ('x', 'zh')...  12.5 us
    all_to_all x1, waiting for transfers between devices, on_device(): received = lax.all_to_all(share, ('zl', 'y'), 0, 0, tiled=True)  8.93 us
    ppermute x3, starting transfers between devices, shift(): return lax.ppermute(value, axis, [(i, (i + step) % n) for i in range(n)])  8.1 us
    all_to_all x1, starting transfers between devices, on_device(): received = lax.all_to_all(share, ('zl', 'y'), 0, 0, tiled=True)  7.56 us
  transfers between devices with their start and end apart: 9, of which 6 were waited for; matrix products, arithmetic and copies ran while one was open for 0% of the time, Pallas kernels for 2%

profile of v20, /device:TPU:10, one launch (start us, length us, event | category | flops | bytes accessed | tf_op | source)
XLA Modules:
  0.0 134.9 jit_solution(14273147318074678744)
XLA Ops:
  0.0 0.8 pad_maximum_fusion.2.refs_0_
  0.8 4.3 %collective-permute-start = (bf16[2,32,512]{2,1,0:T(8,128)(2,1)S(1)}, bf16[2,32,512]{2,1,0:T(8,128)(2,1)S(1)}, u32[]{:S(2)}, u32[]{:S(2)}) collective-permute-start(bf16[2,32,512]{2,1,0:T(8,128)(2,1)S(1)} %pad_maximum_fusion.2.refs_0_), channel_id=1, source_target_pairs={{0,256},{256,0},{1,257},{257,1},{2,258},{258,2},{3,259},{259,3},{4... | collective-permute-start | bytes 196616 | tf_op jit(solution)/shard_map/ppermute | solution.py:21
  5.1 2.7 %arrange_tokens.1 = bf16[4,4,2,128,256]{4,3,2,1,0:T(8,128)(2,1)} custom-call(bf16[128,1024]{1,0:T(8,128)(2,1)} %refs_0_, bf16[128,1024]{1,0:T(8,128)(2,1)} %refs_1_.1), custom_call_target="tpu_custom_call" | custom-call | flops 131072 | bytes 1048576 | tf_op jit(solution)/shard_map/arrange_tokens/pallas_call | solution.py:88
  7.8 0.0 collective-permute-done.refs_1_
  7.8 12.5 %all-to-all-start = ((bf16[16,2,128,256]{3,2,1,0:T(8,128)(2,1)}), bf16[16,2,128,256]{3,2,1,0:T(8,128)(2,1)S(1)}, u32[]{:S(2)}, u32[]{:S(2)}) async-start(bf16[16,2,128,256]{3,2,1,0:T(8,128)(2,1)} %bitcast.26), calls=%async_computation | async-start | bytes 4194304 | tf_op jit(solution)/shard_map/all_to_all | solution.py:234
  20.3 0.5 arrange_bases.1
  20.7 6.8 %collective-permute-start.1 = (bf16[2,2,32,512]{3,2,1,0:T(8,128)(2,1)S(1)}, bf16[2,2,32,512]{3,2,1,0:T(8,128)(2,1)S(1)}, u32[]{:S(2)}, u32[]{:S(2)}) collective-permute-start(bf16[2,2,32,512]{3,2,1,0:T(8,128)(2,1)S(1)} %arrange_bases.1), channel_id=1, source_target_pairs={{0,128},{32,160},{64,192},{96,224},{128,0},{160,32},{192,64},{224,... | collective-permute-start | bytes 393224 | tf_op jit(solution)/shard_map/ppermute | solution.py:221
  27.6 6.0 %collective-permute-done.1 = bf16[2,2,32,512]{3,2,1,0:T(8,128)(2,1)S(1)} collective-permute-done((bf16[2,2,32,512]{3,2,1,0:T(8,128)(2,1)S(1)}, bf16[2,2,32,512]{3,2,1,0:T(8,128)(2,1)S(1)}, u32[]{:S(2)}, u32[]{:S(2)}) %collective-permute-start.1) | collective-permute-done | bytes 131104 | tf_op jit(solution)/shard_map/ppermute | solution.py:221
  33.6 3.9 %collective-permute-start.2 = (bf16[2,2,2,32,512]{4,3,2,1,0:T(8,128)(2,1)S(1)}, bf16[2,2,2,32,512]{4,3,2,1,0:T(8,128)(2,1)S(1)}, u32[]{:S(2)}, u32[]{:S(2)}) collective-permute-start(bf16[2,2,2,32,512]{4,3,2,1,0:T(8,128)(2,1)S(1)} %get-tuple-element.16), channel_id=1, source_target_pairs={{0,64},{32,96},{64,0},{96,32},{128,192},{160,224},{192,128},{224,1... | collective-permute-start | bytes 786440 | tf_op jit(solution)/shard_map/ppermute | solution.py:221
  37.5 8.7 %collective-permute-done.2 = bf16[2,2,2,32,512]{4,3,2,1,0:T(8,128)(2,1)S(1)} collective-permute-done((bf16[2,2,2,32,512]{4,3,2,1,0:T(8,128)(2,1)S(1)}, bf16[2,2,2,32,512]{4,3,2,1,0:T(8,128)(2,1)S(1)}, u32[]{:S(2)}, u32[]{:S(2)}) %collective-permute-start.2) | collective-permute-done | bytes 262176 | tf_op jit(solution)/shard_map/ppermute | solution.py:221
  46.2 0.1 pad_maximum_fusion.low
  46.2 3.4 %collective-permute-start.3 = (bf16[2,2,2,2,32,512]{5,4,3,2,1,0:T(8,128)(2,1)S(1)}, bf16[2,2,2,2,32,512]{5,4,3,2,1,0:T(8,128)(2,1)S(1)}, u32[]{:S(2)}, u32[]{:S(2)}) collective-permute-start(bf16[2,2,2,2,32,512]{5,4,3,2,1,0:T(8,128)(2,1)S(1)} %pad_maximum_fusion.low), channel_id=1, source_target_pairs={{0,32},{32,0},{64,96},{96,64},{128,160},{160,128},{192,224},{224,1... | collective-permute-start | bytes 1572872 | tf_op jit(solution)/shard_map/ppermute | solution.py:221
  49.7 1.9 %collective-permute-start.4 = (bf16[2,2,2,2,32,512]{5,4,3,2,1,0:T(8,128)(2,1)S(1)}, bf16[2,2,2,2,32,512]{5,4,3,2,1,0:T(8,128)(2,1)}, u32[]{:S(2)}, u32[]{:S(2)}) collective-permute-start(bf16[2,2,2,2,32,512]{5,4,3,2,1,0:T(8,128)(2,1)S(1)} %pad_maximum_fusion.low), channel_id=1, source_target_pairs={{0,4},{4,0},{1,5},{5,1},{2,6},{6,2},{3,7},{7,3},{8,12},{12,8},{9,1... | collective-permute-start | bytes 1572872 | tf_op jit(solution)/shard_map/ppermute | solution.py:21
  51.6 9.3 %collective-permute-done.3.high = bf16[2,2,2,2,32,512]{5,4,3,2,1,0:T(8,128)(2,1)S(1)} collective-permute-done((bf16[2,2,2,2,32,512]{5,4,3,2,1,0:T(8,128)(2,1)S(1)}, bf16[2,2,2,2,32,512]{5,4,3,2,1,0:T(8,128)(2,1)S(1)}, u32[]{:S(2)}, u32[]{:S(2)}) %collective-permute-start.3) | collective-permute-done | bytes 524320 | tf_op jit(solution)/shard_map/ppermute | solution.py:221
  60.9 1.9 %collective-permute-start.5 = (bf16[2,2,2,2,32,512]{5,4,3,2,1,0:T(8,128)(2,1)S(1)}, bf16[2,2,2,2,32,512]{5,4,3,2,1,0:T(8,128)(2,1)}, u32[]{:S(2)}, u32[]{:S(2)}) collective-permute-start(bf16[2,2,2,2,32,512]{5,4,3,2,1,0:T(8,128)(2,1)S(1)} %collective-permute-done.3.high), channel_id=1, source_target_pairs={{0,4},{4,0},{1,5},{5,1},{2,6},{6,2},{3,7},{7,3},{8,12},{12,8},{9,1... | collective-permute-start | bytes 1572872 | tf_op jit(solution)/shard_map/ppermute | solution.py:21
  62.8 0.1 pad_add_fusion.place
  62.9 0.0 collective-permute-done.4.core_low
  62.9 1.9 %collective-permute-done.5.core_high = bf16[2,2,2,2,32,512]{5,4,3,2,1,0:T(8,128)(2,1)} collective-permute-done((bf16[2,2,2,2,32,512]{5,4,3,2,1,0:T(8,128)(2,1)S(1)}, bf16[2,2,2,2,32,512]{5,4,3,2,1,0:T(8,128)(2,1)}, u32[]{:S(2)}, u32[]{:S(2)}) %collective-permute-start.5) | collective-permute-done | bytes 524320 | tf_op jit(solution)/shard_map/ppermute | solution.py:21
  64.8 3.7 %all-to-all-done = bf16[16,2,128,256]{3,2,1,0:T(8,128)(2,1)S(1)} async-done(((bf16[16,2,128,256]{3,2,1,0:T(8,128)(2,1)}), bf16[16,2,128,256]{3,2,1,0:T(8,128)(2,1)S(1)}, u32[]{:S(2)}, u32[]{:S(2)}) %all-to-all-start) | async-done | bytes 2097184 | tf_op jit(solution)/shard_map/all_to_all | solution.py:234
  68.4 3.1 %rotate.1 = f32[8,528,128]{2,1,0:T(8,128)S(1)} custom-call(s32[3]{0:T(128)S(1)} %pad_add_fusion.place, s32[2]{0:T(128)S(1)} %copy-done, bf16[4,4,2,128,256]{4,3,2,1,0:T(8,128)(2,1)S(1)} %bitcast.22, bf16[2,2,2,2,32,512]{5,4,3,2,1,0:T(8,128)(2,1)S(1)} %pad_maximum_fusion.low, bf16[2,2,2,2,32,512]{5,4,3,2,1,0:T(8,128)(2,1)S(1)} %collective-permute-done.3.high, ...), custom_call_target="tpu_custom_call" | custom-call | flops 1073741824 | bytes 8388608 | tf_op jit(solution)/shard_map/rotate/pallas_call | solution.py:150
  71.6 0.1 convert_element_type.25
  71.7 19.5 %all_to_all.20 = f16[8,528,128]{2,1,0:T(8,128)(2,1)S(1)} all-to-all(f16[8,528,128]{2,1,0:T(8,128)(2,1)S(1)} %convert_element_type.25), channel_id=1, replica_groups=mesh['zl'=2,'y'=8,'x'=4,'c'=2,'zh'=4] {'c','x'}, dimensions={0} | all-to-all | bytes 2162688 | tf_op jit(solution)/shard_map/all_to_all | solution.py:241
  91.2 0.2 slice.16
  91.5 0.2 fusion
  91.7 1.0 copies.1
  92.8 4.9 %all-to-all-start.2 = ((bf16[8,2,256,128]{3,2,1,0:T(8,128)(2,1)}), bf16[8,2,256,128]{3,2,1,0:T(8,128)(2,1)S(1)}, u32[]{:S(2)}, u32[]{:S(2)}) async-start(bf16[8,2,256,128]{3,2,1,0:T(8,128)(2,1)} %copies.1), calls=%async_computation.2 | async-start | bytes 2097152 | tf_op jit(solution)/shard_map/all_to_all | solution.py:248
  97.6 18.9 %all-gather = bf16[8,256,128]{2,1,0:T(8,128)(2,1)S(1)} all-gather(bf16[2,256,128]{2,1,0:T(8,128)(2,1)S(1)} %get-tuple-element.14), channel_id=2, replica_groups=mesh['zl'=2,'y'=8,'x'=4,'c'=2,'zh'=4] {'zh'}, dimensions={0}, use_global_device_ids=true | all-gather | bytes 655360 | tf_op jit(solution)/shard_map/all_gather | solution.py:251
  116.5 1.2 share.1
  117.7 7.6 %all-to-all-start.3 = ((bf16[16,16,512]{2,1,0:T(8,128)(2,1)}), bf16[16,16,512]{2,1,0:T(8,128)(2,1)S(1)}, u32[]{:S(2)}, u32[]{:S(2)}) async-start(bf16[16,16,512]{2,1,0:T(8,128)(2,1)} %bitcast.16), calls=%async_computation.3 | async-start | bytes 524288 | tf_op jit(solution)/shard_map/all_to_all | solution.py:253
  125.3 8.9 %all-to-all-done.3 = bf16[16,16,512]{2,1,0:T(8,128)(2,1)S(1)} async-done(((bf16[16,16,512]{2,1,0:T(8,128)(2,1)}), bf16[16,16,512]{2,1,0:T(8,128)(2,1)S(1)}, u32[]{:S(2)}, u32[]{:S(2)}) %all-to-all-start.3) | async-done | bytes 262176 | tf_op jit(solution)/shard_map/all_to_all | solution.py:253
  134.2 0.1 divide_reduce_fusion
  134.3 0.6 broadcast_multiply_fusion
  (8 shorter events, 0.1 us)
Async XLA Ops:
  0.8 7.0 %collective-permute-start = (bf16[2,32,512]{2,1,0:T(8,128)(2,1)S(1)}, bf16[2,32,512]{2,1,0:T(8,128)(2,1)S(1)}, u32[]{:S(2)}, u32[]{:S(2)}) collective-permute-start(bf16[2,32,512]{2,1,0:T(8,128)(2,1)S(1)} %pad_maximum_fusion.2.refs_0_), channel_id=1, source_target_pairs={{0,256},{256,0},{1,257},{257,1},{2,258},{258,2},{3,259},{259,3},{4... | collective-permute-start | bytes 196616 | tf_op jit(solution)/shard_map/ppermute | solution.py:21
  7.8 60.7 %all-to-all-start = ((bf16[16,2,128,256]{3,2,1,0:T(8,128)(2,1)}), bf16[16,2,128,256]{3,2,1,0:T(8,128)(2,1)S(1)}, u32[]{:S(2)}, u32[]{:S(2)}) async-start(bf16[16,2,128,256]{3,2,1,0:T(8,128)(2,1)} %bitcast.26), calls=%async_computation | async-start | bytes 4194304 | tf_op jit(solution)/shard_map/all_to_all | solution.py:234
  20.2 48.2 %copy-start = (s32[2]{0:T(128)S(1)}, s32[2]{0:T(128)}, u32[]{:S(2)}) copy-start(s32[2]{0:T(128)} %lengths.1) | copy-start | bytes 28
  20.7 12.8 %collective-permute-start.1 = (bf16[2,2,32,512]{3,2,1,0:T(8,128)(2,1)S(1)}, bf16[2,2,32,512]{3,2,1,0:T(8,128)(2,1)S(1)}, u32[]{:S(2)}, u32[]{:S(2)}) collective-permute-start(bf16[2,2,32,512]{3,2,1,0:T(8,128)(2,1)S(1)} %arrange_bases.1), channel_id=1, source_target_pairs={{0,128},{32,160},{64,192},{96,224},{128,0},{160,32},{192,64},{224,... | collective-permute-start | bytes 393224 | tf_op jit(solution)/shard_map/ppermute | solution.py:221
  33.6 12.6 %collective-permute-start.2 = (bf16[2,2,2,32,512]{4,3,2,1,0:T(8,128)(2,1)S(1)}, bf16[2,2,2,32,512]{4,3,2,1,0:T(8,128)(2,1)S(1)}, u32[]{:S(2)}, u32[]{:S(2)}) collective-permute-start(bf16[2,2,2,32,512]{4,3,2,1,0:T(8,128)(2,1)S(1)} %get-tuple-element.16), channel_id=1, source_target_pairs={{0,64},{32,96},{64,0},{96,32},{128,192},{160,224},{192,128},{224,1... | collective-permute-start | bytes 786440 | tf_op jit(solution)/shard_map/ppermute | solution.py:221
  46.2 14.6 %collective-permute-start.3 = (bf16[2,2,2,2,32,512]{5,4,3,2,1,0:T(8,128)(2,1)S(1)}, bf16[2,2,2,2,32,512]{5,4,3,2,1,0:T(8,128)(2,1)S(1)}, u32[]{:S(2)}, u32[]{:S(2)}) collective-permute-start(bf16[2,2,2,2,32,512]{5,4,3,2,1,0:T(8,128)(2,1)S(1)} %pad_maximum_fusion.low), channel_id=1, source_target_pairs={{0,32},{32,0},{64,96},{96,64},{128,160},{160,128},{192,224},{224,1... | collective-permute-start | bytes 1572872 | tf_op jit(solution)/shard_map/ppermute | solution.py:221
  49.7 13.2 %collective-permute-start.4 = (bf16[2,2,2,2,32,512]{5,4,3,2,1,0:T(8,128)(2,1)S(1)}, bf16[2,2,2,2,32,512]{5,4,3,2,1,0:T(8,128)(2,1)}, u32[]{:S(2)}, u32[]{:S(2)}) collective-permute-start(bf16[2,2,2,2,32,512]{5,4,3,2,1,0:T(8,128)(2,1)S(1)} %pad_maximum_fusion.low), channel_id=1, source_target_pairs={{0,4},{4,0},{1,5},{5,1},{2,6},{6,2},{3,7},{7,3},{8,12},{12,8},{9,1... | collective-permute-start | bytes 1572872 | tf_op jit(solution)/shard_map/ppermute | solution.py:21
  60.9 3.9 %collective-permute-start.5 = (bf16[2,2,2,2,32,512]{5,4,3,2,1,0:T(8,128)(2,1)S(1)}, bf16[2,2,2,2,32,512]{5,4,3,2,1,0:T(8,128)(2,1)}, u32[]{:S(2)}, u32[]{:S(2)}) collective-permute-start(bf16[2,2,2,2,32,512]{5,4,3,2,1,0:T(8,128)(2,1)S(1)} %collective-permute-done.3.high), channel_id=1, source_target_pairs={{0,4},{4,0},{1,5},{5,1},{2,6},{6,2},{3,7},{7,3},{8,12},{12,8},{9,1... | collective-permute-start | bytes 1572872 | tf_op jit(solution)/shard_map/ppermute | solution.py:21
  92.8 23.7 %all-to-all-start.2 = ((bf16[8,2,256,128]{3,2,1,0:T(8,128)(2,1)}), bf16[8,2,256,128]{3,2,1,0:T(8,128)(2,1)S(1)}, u32[]{:S(2)}, u32[]{:S(2)}) async-start(bf16[8,2,256,128]{3,2,1,0:T(8,128)(2,1)} %copies.1), calls=%async_computation.2 | async-start | bytes 2097152 | tf_op jit(solution)/shard_map/all_to_all | solution.py:248
  117.7 16.5 %all-to-all-start.3 = ((bf16[16,16,512]{2,1,0:T(8,128)(2,1)}), bf16[16,16,512]{2,1,0:T(8,128)(2,1)S(1)}, u32[]{:S(2)}, u32[]{:S(2)}) async-start(bf16[16,16,512]{2,1,0:T(8,128)(2,1)} %bitcast.16), calls=%async_computation.3 | async-start | bytes 524288 | tf_op jit(solution)/shard_map/all_to_all | solution.py:253
